TPU v7x, 32 devices: a whole 2x2x4 slice. The times are simulated.
32 devices in a mesh: dp: 4 (over x, core), seq: 8 (over z, y).
Axes of the slice: x: 2, y: 2, z: 4, core: 2. Of those that a mesh axis runs over, the one named last changes fastest.
Arguments:
- tokens: bfloat16 [16, 1024, 1152], P('dp', 'seq'), may hold values from -6 to 6
- segment_ids: int32 [16, 1024], P('dp', 'seq'), may hold values from 0 to 3, never falling along the last dimension, each value on 1 to 512 neighbouring positions
- w_query: float32 [1152, 1024], P(('dp', 'seq')), may hold values from -0.1875 to 0.1875
- w_key: float32 [1152, 256], P(('dp', 'seq')), may hold values from -0.1875 to 0.1875
- w_value: float32 [1152, 256], P(('dp', 'seq')), may hold values from -0.1875 to 0.1875
- w_out: float32 [1024, 1152], P(('dp', 'seq')), may hold values from -0.1875 to 0.1875
- w_gate: float32 [1152, 6912], P(('dp', 'seq')), may hold values from -0.1875 to 0.1875
- w_up: float32 [1152, 6912], P(('dp', 'seq')), may hold values from -0.1875 to 0.1875
- w_down: float32 [6912, 1152], P(('dp', 'seq')), may hold values from -0.078125 to 0.078125
- g_in: float32 [1152], P(('dp', 'seq')), may hold values from 0.25 to 1.75
- g_post_attn: float32 [1152], P(('dp', 'seq')), may hold values from 0.25 to 1.75
- g_pre_ffn: float32 [1152], P(('dp', 'seq')), may hold values from 0.25 to 1.75
- g_post_ffn: float32 [1152], P(('dp', 'seq')), may hold values from 0.25 to 1.75
- g_query: float32 [256], P(('dp', 'seq')), may hold values from 0.25 to 1.75
- g_key: float32 [256], P(('dp', 'seq')), may hold values from 0.25 to 1.75
- cotangent: bfloat16 [16, 1024, 1152], P('dp', 'seq'), may hold values from -6 to 6
Outputs:
- output: bfloat16 [16, 1024, 1152], P('dp', 'seq')
- grad_tokens: bfloat16 [16, 1024, 1152], P('dp', 'seq')
- grad_query: float32 [1152, 1024], P(('dp', 'seq'))
- grad_key: float32 [1152, 256], P(('dp', 'seq'))
- grad_value: float32 [1152, 256], P(('dp', 'seq'))
- grad_out: float32 [1024, 1152], P(('dp', 'seq'))
- grad_gate: float32 [1152, 6912], P(('dp', 'seq'))
- grad_up: float32 [1152, 6912], P(('dp', 'seq'))
- grad_down: float32 [6912, 1152], P(('dp', 'seq'))
- grad_in_norm: float32 [1152], P(('dp', 'seq'))
- grad_post_attn_norm: float32 [1152], P(('dp', 'seq'))
- grad_pre_ffn_norm: float32 [1152], P(('dp', 'seq'))
- grad_post_ffn_norm: float32 [1152], P(('dp', 'seq'))
- grad_query_norm: float32 [256], P(('dp', 'seq'))
- grad_key_norm: float32 [256], P(('dp', 'seq'))
Inputs may be any that keep to these rules, and one draw needn't show every extreme that they name: `segment_ids`: in each row the ids start at 0 and never fall; every id of 0 to 3 appears, and each document has 1 to 512 positions.
All inputs are finite; a program needn't handle non-finite values.
Results may differ from a plain program's by a relative error of at most 0.018.
The roundings to bfloat16 on the way count: a program that leaves them out, or rounds other values in their place, can miss the bound.
Values may be sent and summed in bfloat16 or wider, within the bound.
No kernel may reach another device: no remote copies, remote signals or barrier semaphores. Data moves between devices by JAX's collectives and lax.ppermute only.
A program may use at most 320 MiB of HBM per device.

v0:
```python
import jax
import jax.numpy as jnp
from jax import lax
from jax.sharding import PartitionSpec as P

HEADS = 4
HEAD = 256


EPSILON = 1e-06
ROPE_BASE = 1000000.0
NEG_FILL = -1e30


def rms_scale(values, gain_vec):
    return (
        values * lax.rsqrt(jnp.mean(values * values, axis=-1, keepdims=True) + EPSILON) * gain_vec
    )


def rope_tables(positions, head_width):
    half_width = head_width // 2
    inverse = ROPE_BASE ** (-(jnp.arange(half_width, dtype=jnp.float32) * 2.0 / head_width))
    angles = positions.astype(jnp.float32)[..., None] * inverse
    return (jnp.cos(angles), jnp.sin(angles))


def rotate(values, cosine, sine_part):
    half_width = values.shape[-1] // 2
    first_half = values[..., :half_width]
    second_half = values[..., half_width:]
    return jnp.concatenate(
        [
            first_half * cosine - second_half * sine_part,
            second_half * cosine + first_half * sine_part,
        ],
        axis=-1,
    )


def masked_scores(query_row, keys_row, allowed_row, score_scale):
    raw_scores = (
        jnp.einsum("chd,kd->hck", query_row, keys_row, preferred_element_type=jnp.float32)
        * score_scale
    )
    return jnp.where(allowed_row[None], raw_scores, NEG_FILL)


def middle_part(inputs_f, attn_out, gain_post, gain_pre):
    residual = inputs_f + rms_scale(attn_out, gain_post)
    return (residual, rms_scale(residual, gain_pre))


def gated_gelu(gate_in, up_in):
    return jax.nn.gelu(gate_in, approximate=True) * up_in


def finish_layer(residual, ffn_out, gain_vec):
    return residual + rms_scale(ffn_out, gain_vec)


def on_device(
    tokens,
    segment_ids,
    w_query,
    w_key,
    w_value,
    w_out,
    w_gate,
    w_up,
    w_down,
    g_in,
    g_post_attn,
    g_pre_ffn,
    g_post_ffn,
    g_query,
    g_key,
    cotangent,
):
    row_count, local_len, model_width = tokens.shape
    token_count = row_count * local_len
    score_scale = HEAD ** (-0.5)
    f32 = jnp.float32
    bf16 = jnp.bfloat16
    query_index = lax.axis_index("seq") * local_len + jnp.arange(local_len, dtype=jnp.int32)
    all_segments = lax.all_gather(segment_ids, "seq", axis=1, tiled=True)
    key_index = jnp.arange(all_segments.shape[1], dtype=jnp.int32)
    starts = jnp.sum((all_segments[:, None, :] < segment_ids[:, :, None]).astype(jnp.int32), axis=2)
    cosine, sine_part = rope_tables((query_index[None, :] - starts).reshape(token_count), HEAD)
    allowed = (all_segments[:, None, :] == segment_ids[:, :, None]) & (
        key_index[None, None, :] <= query_index[None, :, None]
    )
    shards_low = [
        shard_item.astype(bf16)
        for shard_item in (
            w_query,
            w_key,
            w_value,
            w_out,
            w_gate,
            w_up,
            w_down,
            g_in,
            g_post_attn,
            g_pre_ffn,
            g_post_ffn,
            g_query,
            g_key,
        )
    ]
    full_set = (
        lax.all_gather(shards_low[0], ("dp", "seq"), axis=0, tiled=True),
        lax.all_gather(shards_low[1], ("dp", "seq"), axis=0, tiled=True),
        lax.all_gather(shards_low[2], ("dp", "seq"), axis=0, tiled=True),
        lax.all_gather(shards_low[3], ("dp", "seq"), axis=0, tiled=True),
        lax.all_gather(shards_low[4], ("dp", "seq"), axis=0, tiled=True),
        lax.all_gather(shards_low[5], ("dp", "seq"), axis=0, tiled=True),
        lax.all_gather(shards_low[6], ("dp", "seq"), axis=0, tiled=True),
        lax.all_gather(shards_low[7], ("dp", "seq"), axis=0, tiled=True),
        lax.all_gather(shards_low[8], ("dp", "seq"), axis=0, tiled=True),
        lax.all_gather(shards_low[9], ("dp", "seq"), axis=0, tiled=True),
        lax.all_gather(shards_low[10], ("dp", "seq"), axis=0, tiled=True),
        lax.all_gather(shards_low[11], ("dp", "seq"), axis=0, tiled=True),
        lax.all_gather(shards_low[12], ("dp", "seq"), axis=0, tiled=True),
    )
    full_query, full_key, full_value, full_out, full_gate, full_up, full_down = full_set[:7]
    gain_list = [gain_item.astype(f32) for gain_item in full_set[7:]]
    gain_in, gain_post_attn, gain_pre_ffn, gain_post_ffn, gain_query, gain_key = gain_list
    inputs_f = tokens.astype(f32).reshape(token_count, model_width)
    h_in_f, in_pull = jax.vjp(rms_scale, inputs_f, gain_in)
    h_in = h_in_f.astype(bf16)
    q_proj = jnp.dot(h_in, full_query, preferred_element_type=f32).reshape(token_count, HEADS, HEAD)
    k_proj = jnp.dot(h_in, full_key, preferred_element_type=f32)
    value_rows = (
        jnp.dot(h_in, full_value, preferred_element_type=f32)
        .astype(bf16)
        .reshape(row_count, local_len, HEAD)
    )

    def query_key(q_in, k_in, gain_q, gain_k):
        query_rot = rotate(rms_scale(q_in, gain_q), cosine[:, None, :], sine_part[:, None, :])
        key_rot = rotate(rms_scale(k_in, gain_k), cosine, sine_part)
        return (query_rot, key_rot)

    (query_rot, key_rot), rotary_pull = jax.vjp(query_key, q_proj, k_proj, gain_query, gain_key)
    query_low = query_rot.astype(bf16).reshape(row_count, local_len, HEADS, HEAD)
    key_low = key_rot.astype(bf16).reshape(row_count, local_len, HEAD)
    keys_all, values_all = (
        lax.all_gather(key_low, "seq", axis=1, tiled=True),
        lax.all_gather(value_rows, "seq", axis=1, tiled=True),
    )

    def attend(arguments):
        query_row, keys_row, values_row, allowed_row = arguments
        scores = masked_scores(query_row, keys_row, allowed_row, score_scale)
        top_score = jnp.max(scores, axis=-1, keepdims=True)
        log_total = top_score + jnp.log(
            jnp.sum(jnp.exp(scores - top_score), axis=-1, keepdims=True)
        )
        probs_low = jnp.exp(scores - log_total).astype(bf16)
        mixed_row = jnp.einsum("hck,kd->chd", probs_low, values_row, preferred_element_type=f32)
        return (mixed_row.astype(bf16), log_total)

    mixed_low, log_totals = lax.map(attend, (query_low, keys_all, values_all, allowed))
    mixed_flat = mixed_low.reshape(token_count, HEADS * HEAD)
    attn_out = jnp.dot(mixed_flat, full_out, preferred_element_type=f32)
    (residual, h_ffn_f), middle_pull = jax.vjp(
        middle_part, inputs_f, attn_out, gain_post_attn, gain_pre_ffn
    )
    h_ffn = h_ffn_f.astype(bf16)
    gate_proj = jnp.dot(h_ffn, full_gate, preferred_element_type=f32)
    up_proj = jnp.dot(h_ffn, full_up, preferred_element_type=f32)
    hidden_f, act_pull = jax.vjp(gated_gelu, gate_proj, up_proj)
    hidden_low = hidden_f.astype(bf16)
    ffn_out = jnp.dot(hidden_low, full_down, preferred_element_type=f32)
    final_f, final_pull = jax.vjp(finish_layer, residual, ffn_out, gain_post_ffn)
    output = final_f.astype(bf16).reshape(row_count, local_len, model_width)
    back_set = (
        lax.all_gather(shards_low[0], ("dp", "seq"), axis=0, tiled=True),
        lax.all_gather(shards_low[1], ("dp", "seq"), axis=0, tiled=True),
        lax.all_gather(shards_low[2], ("dp", "seq"), axis=0, tiled=True),
        lax.all_gather(shards_low[3], ("dp", "seq"), axis=0, tiled=True),
        lax.all_gather(shards_low[4], ("dp", "seq"), axis=0, tiled=True),
        lax.all_gather(shards_low[5], ("dp", "seq"), axis=0, tiled=True),
        lax.all_gather(shards_low[6], ("dp", "seq"), axis=0, tiled=True),
    )
    back_query, back_key, back_value, back_out, back_gate, back_up, back_down = back_set
    d_final = cotangent.astype(f32).reshape(token_count, model_width)
    d_resid_a, d_ffn_f, grad_post_ffn = final_pull(d_final)
    d_ffn = d_ffn_f.astype(bf16)
    grad_down = jnp.einsum("tf,td->fd", hidden_low, d_ffn, preferred_element_type=f32)
    d_hidden = jnp.einsum("td,fd->tf", d_ffn, back_down, preferred_element_type=f32)
    d_gate_f, d_up_f = act_pull(d_hidden)
    d_gate = d_gate_f.astype(bf16)
    d_up = d_up_f.astype(bf16)
    grad_gate = jnp.einsum("td,tf->df", h_ffn, d_gate, preferred_element_type=f32)
    grad_up = jnp.einsum("td,tf->df", h_ffn, d_up, preferred_element_type=f32)
    d_hffn = jnp.einsum("tf,df->td", d_gate, back_gate, preferred_element_type=f32) + jnp.einsum(
        "tf,df->td", d_up, back_up, preferred_element_type=f32
    )
    d_inputs_a, d_attn_f, grad_post_attn, grad_pre_ffn = middle_pull((d_resid_a, d_hffn))
    d_attn = d_attn_f.astype(bf16)
    grad_out = jnp.einsum("tc,td->cd", mixed_flat, d_attn, preferred_element_type=f32)
    d_mixed = (
        jnp.einsum("td,cd->tc", d_attn, back_out, preferred_element_type=f32)
        .astype(bf16)
        .reshape(row_count, local_len, HEADS, HEAD)
    )
    keys_back, values_back = (
        lax.all_gather(key_low, "seq", axis=1, tiled=True),
        lax.all_gather(value_rows, "seq", axis=1, tiled=True),
    )

    def attend_back(arguments):
        query_row, keys_row, values_row, allowed_row, log_row, d_mixed_row = arguments
        scores = masked_scores(query_row, keys_row, allowed_row, score_scale)
        probs_f = jnp.exp(scores - log_row)
        probs_low = probs_f.astype(bf16)
        d_probs = jnp.einsum("chd,kd->hck", d_mixed_row, values_row, preferred_element_type=f32)
        d_scores = (
            probs_f * (d_probs - jnp.sum(d_probs * probs_f, axis=-1, keepdims=True))
        ).astype(bf16)
        d_query_row = (
            jnp.einsum("hck,kd->chd", d_scores, keys_row, preferred_element_type=f32) * score_scale
        )
        key_term = (
            jnp.einsum("hck,chd->kd", d_scores, query_row, preferred_element_type=f32) * score_scale
        )
        value_term = jnp.einsum("hck,chd->kd", probs_low, d_mixed_row, preferred_element_type=f32)
        return (d_query_row, key_term, value_term)

    d_query, key_terms, value_terms = lax.map(
        attend_back, (query_low, keys_back, values_back, allowed, log_totals, d_mixed)
    )
    d_key, d_value_f = (
        lax.psum_scatter(
            key_terms.astype(jnp.bfloat16), "seq", scatter_dimension=1, tiled=True
        ).astype(jnp.float32),
        lax.psum_scatter(
            value_terms.astype(jnp.bfloat16), "seq", scatter_dimension=1, tiled=True
        ).astype(jnp.float32),
    )
    d_value = d_value_f.reshape(token_count, HEAD).astype(bf16)
    d_qproj_f, d_kproj_f, grad_query_norm, grad_key_norm = rotary_pull(
        (d_query.reshape(token_count, HEADS, HEAD), d_key.reshape(token_count, HEAD))
    )
    d_qproj = d_qproj_f.reshape(token_count, HEADS * HEAD).astype(bf16)
    d_kproj = d_kproj_f.astype(bf16)
    grad_query = jnp.einsum("td,tc->dc", h_in, d_qproj, preferred_element_type=f32)
    grad_key = jnp.einsum("td,tc->dc", h_in, d_kproj, preferred_element_type=f32)
    grad_value = jnp.einsum("td,tc->dc", h_in, d_value, preferred_element_type=f32)
    d_hin = (
        jnp.einsum("tc,dc->td", d_qproj, back_query, preferred_element_type=f32)
        + jnp.einsum("tc,dc->td", d_kproj, back_key, preferred_element_type=f32)
        + jnp.einsum("tc,dc->td", d_value, back_value, preferred_element_type=f32)
    )
    d_inputs_b, grad_in_norm = in_pull(d_hin)
    grad_tokens = (d_inputs_a + d_inputs_b).astype(bf16).reshape(row_count, local_len, model_width)
    shares = (
        lax.psum_scatter(grad_query, ("dp", "seq"), scatter_dimension=0, tiled=True),
        lax.psum_scatter(grad_key, ("dp", "seq"), scatter_dimension=0, tiled=True),
        lax.psum_scatter(grad_value, ("dp", "seq"), scatter_dimension=0, tiled=True),
        lax.psum_scatter(grad_out, ("dp", "seq"), scatter_dimension=0, tiled=True),
        lax.psum_scatter(grad_gate, ("dp", "seq"), scatter_dimension=0, tiled=True),
        lax.psum_scatter(grad_up, ("dp", "seq"), scatter_dimension=0, tiled=True),
        lax.psum_scatter(grad_down, ("dp", "seq"), scatter_dimension=0, tiled=True),
        lax.psum_scatter(grad_in_norm, ("dp", "seq"), scatter_dimension=0, tiled=True),
        lax.psum_scatter(grad_post_attn, ("dp", "seq"), scatter_dimension=0, tiled=True),
        lax.psum_scatter(grad_pre_ffn, ("dp", "seq"), scatter_dimension=0, tiled=True),
        lax.psum_scatter(grad_post_ffn, ("dp", "seq"), scatter_dimension=0, tiled=True),
        lax.psum_scatter(grad_query_norm, ("dp", "seq"), scatter_dimension=0, tiled=True),
        lax.psum_scatter(grad_key_norm, ("dp", "seq"), scatter_dimension=0, tiled=True),
    )
    return (
        output,
        grad_tokens,
        shares[0],
        shares[1],
        shares[2],
        shares[3],
        shares[4],
        shares[5],
        shares[6],
        shares[7],
        shares[8],
        shares[9],
        shares[10],
        shares[11],
        shares[12],
    )


def solution(mesh):
    in_specs = (
        P("dp", "seq", None),
        P("dp", "seq"),
        P(("dp", "seq"), None),
        P(("dp", "seq"), None),
        P(("dp", "seq"), None),
        P(("dp", "seq"), None),
        P(("dp", "seq"), None),
        P(("dp", "seq"), None),
        P(("dp", "seq"), None),
        P(("dp", "seq")),
        P(("dp", "seq")),
        P(("dp", "seq")),
        P(("dp", "seq")),
        P(("dp", "seq")),
        P(("dp", "seq")),
        P("dp", "seq", None),
    )
    out_specs = (
        P("dp", "seq", None),
        P("dp", "seq", None),
        P(("dp", "seq"), None),
        P(("dp", "seq"), None),
        P(("dp", "seq"), None),
        P(("dp", "seq"), None),
        P(("dp", "seq"), None),
        P(("dp", "seq"), None),
        P(("dp", "seq"), None),
        P(("dp", "seq")),
        P(("dp", "seq")),
        P(("dp", "seq")),
        P(("dp", "seq")),
        P(("dp", "seq")),
        P(("dp", "seq")),
    )
    return jax.shard_map(
        on_device, mesh=mesh, in_specs=in_specs, out_specs=out_specs, check_vma=False
    )
```

profile of v0, /device:TPU:0, one launch (start us, length us, event | category | flops | bytes accessed | tf_op | source)
XLA Modules:
  0.0 3033.1 jit_solution(5956225543729877244)
XLA Ops:
  14.2 42.5 %all-reduce.28 = (bf16[1152]{0:T(1024)(128)(2,1)S(1)}, bf16[256]{0:T(256)(128)(2,1)S(1)}, bf16[256]{0:T(256)(128)(2,1)S(1)}, bf16[1152]{0:T(1024)(128)(2,1)S(1)}...) all-reduce(bf16[1152]{0:T(1024)(128)(2,1)S(1)} %dynamic-update-slic, ...), channel_id=1, replica_groups=mesh['dp'=4,'seq'=8] {'dp','seq'}, use_global_device_ids=true, to_apply=%add.4 | all-reduce | flops 5120 | bytes 20480
  57.5 70.1 %all-gather = bf16[32,36,256]{2,1,0:T(8,128)(2,1)S(1)} all-gather(bf16[1,36,256]{2,1,0:T(8,128)(2,1)S(1)} %convert_bitcast_fusion.4), channel_id=1, replica_groups=mesh['dp'=4,'seq'=8] {'dp','seq'}, dimensions={0}, use_global_device_ids=true | all-gather | bytes 608256 | tf_op jit(solution)/shard_map/all_gather | solution.py:114
  129.8 69.9 %all-gather.1 = bf16[32,36,256]{2,1,0:T(8,128)(2,1)S(1)} all-gather(bf16[1,36,256]{2,1,0:T(8,128)(2,1)S(1)} %convert_bitcast_fusion.3), channel_id=1, replica_groups=mesh['dp'=4,'seq'=8] {'dp','seq'}, dimensions={0}, use_global_device_ids=true | all-gather | bytes 608256 | tf_op jit(solution)/shard_map/all_gather | solution.py:113
  200.6 26.0 all_gather.60
  253.6 26.3 all-gather.15.cloned.1.call-done
  279.9 23.5 while.26
  306.2 32.9 %all-gather.17.cloned.1.call-done = bf16[1024,1152]{1,0:T(8,128)(2,1)} async-done(((bf16[32,1152]{1,0:T(8,128)(2,1)}), bf16[1024,1152]{1,0:T(8,128)(2,1)}) %all-gather.17.cloned.1.call-update) | async-done | bytes 2359312 | tf_op jit(solution)/shard_map/all_gather | solution.py:115
  345.1 115.5 %all-gather.23.cloned.1.call-done = bf16[32,36,6912]{2,1,0:T(8,128)(2,1)} async-done(((bf16[1,36,6912]{2,1,0:T(8,128)(2,1)}), bf16[32,36,6912]{2,1,0:T(8,128)(2,1)}) %all-gather.23.cloned.1.call-update) | async-done | bytes 15925264 | tf_op jit(solution)/shard_map/all_gather | solution.py:116
  460.6 18.5 reshape.402
  479.1 102.4 %all-gather.25.cloned.1.call-done = bf16[32,36,6912]{2,1,0:T(8,128)(2,1)} async-done(((bf16[1,36,6912]{2,1,0:T(8,128)(2,1)}), bf16[32,36,6912]{2,1,0:T(8,128)(2,1)}) %all-gather.25.cloned.1.call-update) | async-done | bytes 15925264 | tf_op jit(solution)/shard_map/all_gather | solution.py:117
  581.5 18.5 reshape.404
  615.8 21.7 multiply_convert_fusion.1
  637.5 56.0 %all-gather.19.cloned.1.call-done = bf16[6912,1152]{1,0:T(8,128)(2,1)} async-done(((bf16[216,1152]{1,0:T(8,128)(2,1)}), bf16[6912,1152]{1,0:T(8,128)(2,1)}) %all-gather.19.cloned.1.call-update) | async-done | bytes 15925264 | tf_op jit(solution)/shard_map/all_gather | solution.py:118
  711.8 28.4 multiply_convert_fusion
  754.6 16.3 multiply_reduce_fusion
  778.1 62.5 %while.27 = (s32[]{:T(128)}, f32[4,128,4,256]{3,1,0,2:T(8,128)}, bf16[4,1024,256]{2,1,0:T(8,128)(2,1)}, bf16[4,1024,256]{2,1,0:T(8,128)(2,1)}, bf16[4,1024,256]{...) while((s32[]{:T(128)}, f32[4,128,4,256]{3,1,0,2:T(8,128)}, ...), condition=%wide.region_16.17_spmd, body=%wide.region_14.16_spmd.sunk | while | flops 1347288576 | bytes 49164516 | solution.py:232
  847.1 19.0 fusion.97
  867.5 17.0 fusion.96
  884.4 870.8 %fusion.4 = f32[40,6912]{1,0:T(8,128)S(1)} fusion(f32[1152,6912]{1,0:T(8,128)} %fusion.96), kind=kCustom, calls=%all-reduce-scatter.4 | all-reduce-scatter fusion | flops 8847361 | bytes 32956416
  1772.4 16.9 fusion.95
  1810.5 22.2 concatenate.29
  1843.4 950.1 %fusion.87 = (f32[40,1024]{1,0:T(8,128)}, f32[40,256]{1,0:T(8,128)}, f32[40,256]{1,0:T(8,128)S(1)}, f32[40,6912]{1,0:T(8,128)S(1)}) fusion(f32[1152,1024]{1,0:T(8,128)} %fusion.92, f32[1152,256]{1,0:T(8,128)S(1)} %fusion.93, f32[1152,256]{1,0:T(8,128)S(1)} %convolution_bitcast_fusion.2, f32[1152,6912]{1,0:T(8,128)} %fusion.95), kind=kCustom, calls=%all-reduce-scatter.5 | all-reduce-scatter fusion | flops 10813441 | bytes 40280064
  2851.5 105.8 %all-reduce.27 = (f32[1152]{0:T(1024)}, f32[1152]{0:T(1024)}, f32[1152]{0:T(1024)}, f32[1152]{0:T(1024)}, f32[256]{0:T(256)}, /*index=5*/f32[256]{0:T(256)}) all-reduce(f32[1152]{0:T(1024)S(1)} %get-tuple-element.171, f32[1152]{0:T(1024)S(1)} %get-tuple-element.165, ...), channel_id=11, replica_groups=mesh['dp'=4,'seq'=8] {'dp','seq'}, use_global_device_ids=true, to_apply=%region_30.31.clone | all-reduce | flops 5120 | bytes 40960
  3001.8 21.9 concatenate.28
  (450 shorter events, 348.7 us)
Async XLA Ops:
  7.2 235.3 %all-gather.21.cloned.1.call-start = ((), (), s32[]{:S(2)}) async-start(), calls=%async_computation.11 | async-start | bytes 2703360 | tf_op jit(solution)/shard_map/all_gather | solution.py:112
  8.9 244.7 %all-gather.13.cloned.1.call-start = ((), (), s32[]{:S(2)}) async-start(), calls=%async_computation.4 | async-start | bytes 2359296 | tf_op jit(solution)/shard_map/all_gather | solution.py:150
  129.7 150.2 %all-gather.15.cloned.1.call-start = ((), (), s32[]{:S(2)}) async-start(), calls=%async_computation.5 | async-start | bytes 2359296 | tf_op jit(solution)/shard_map/all_gather | solution.py:149
  232.8 106.3 %all-gather.17.cloned.1.call-start = ((), (), s32[]{:S(2)}) async-start(), calls=%async_computation.6 | async-start | bytes 2433024 | tf_op jit(solution)/shard_map/all_gather | solution.py:115
  234.4 226.2 %all-gather.23.cloned.1.call-start = ((), (), s32[]{:S(2)}) async-start(), calls=%async_computation.12 | async-start | bytes 18247680 | tf_op jit(solution)/shard_map/all_gather | solution.py:116
  235.4 346.1 %all-gather.25.cloned.1.call-start = ((), (), s32[]{:S(2)}) async-start(), calls=%async_computation.13 | async-start | bytes 18247680 | tf_op jit(solution)/shard_map/all_gather | solution.py:117
  236.3 457.2 %all-gather.19.cloned.1.call-start = ((), (), s32[]{:S(2)}) async-start(), calls=%async_computation.7 | async-start | bytes 16422912 | tf_op jit(solution)/shard_map/all_gather | solution.py:118
  237.6 1597.6 %reduce-scatter.17.cloned.1.call-start = ((), (), s32[]{:S(2)}) async-start(), calls=%async_computation.8 | async-start | bytes 2359296 | tf_op jit(solution)/shard_map/reduce_scatter | solution.py:236
  840.6 997.6 %reduce-scatter.19.cloned.1.call-start = ((), (), s32[]{:S(2)}) async-start(), calls=%async_computation.9 | async-start | bytes 2359296 | tf_op jit(solution)/shard_map/reduce_scatter | solution.py:239
  841.3 2184.7 %reduce-scatter.21.cloned.1.call-start = ((), (), s32[]{:S(2)}) async-start(), calls=%async_computation.10 | async-start | bytes 4866048 | tf_op jit(solution)/shard_map/reduce_scatter | solution.py:263
  845.9 2180.2 %reduce-scatter.23.cloned.1.call-start = ((), (), s32[]{:S(2)}) async-start(), calls=%async_computation.14 | async-start | bytes 32845824
  1755.2 55.3 %collective-permute-start.18 = (f32[40,6912]{1,0:T(8,128)S(1)}, f32[40,6912]{1,0:T(8,128)}, u32[]{:S(2)}, u32[]{:S(2)}) collective-permute-start(f32[40,6912]{1,0:T(8,128)S(1)} %fusion.4), channel_id=1, source_target_pairs={{0,3},{1,4},{2,5},{3,6},{4,7},{5,8},{6,9},{7,10},{8,11},{9,12},{10... | collective-permute-start | bytes 3317768
  1761.4 49.2 %collective-permute-start.17 = (f32[40,6912]{1,0:T(8,128)S(1)}, f32[40,6912]{1,0:T(8,128)}, u32[]{:S(2)}, u32[]{:S(2)}) collective-permute-start(f32[40,6912]{1,0:T(8,128)S(1)} %fusion.4), channel_id=1, source_target_pairs={{0,2},{1,3},{2,4},{3,5},{4,6},{5,7},{6,8},{7,9},{8,10},{9,11},{10,... | collective-permute-start | bytes 3317768
  1763.6 46.9 %collective-permute-start.16 = (f32[40,6912]{1,0:T(8,128)S(1)}, f32[40,6912]{1,0:T(8,128)}, u32[]{:S(2)}, u32[]{:S(2)}) collective-permute-start(f32[40,6912]{1,0:T(8,128)S(1)} %fusion.4), channel_id=1, source_target_pairs={{0,1},{1,2},{2,3},{3,4},{4,5},{5,6},{6,7},{7,8},{8,9},{9,10},{10,1... | collective-permute-start | bytes 3317768
  1791.5 19.1 collective-permute-start.19
  2794.2 39.4 %collective-permute-start.6 = (f32[40,256]{1,0:T(8,128)}, f32[40,256]{1,0:T(8,128)S(1)}, u32[]{:S(2)}, u32[]{:S(2)}) collective-permute-start(f32[40,256]{1,0:T(8,128)} %get-tuple-element.226), channel_id=1, source_target_pairs={{0,3},{1,4},{2,5},{3,6},{4,7},{5,8},{6,9},{7,10},{8,11},{9,12},{10... | collective-permute-start | bytes 122888
  2795.5 40.3 %collective-permute-start.5 = (f32[40,256]{1,0:T(8,128)}, f32[40,256]{1,0:T(8,128)S(1)}, u32[]{:S(2)}, u32[]{:S(2)}) collective-permute-start(f32[40,256]{1,0:T(8,128)} %get-tuple-element.226), channel_id=1, source_target_pairs={{0,2},{1,3},{2,4},{3,5},{4,6},{5,7},{6,8},{7,9},{8,10},{9,11},{10,... | collective-permute-start | bytes 122888
  2812.4 19.3 collective-permute-start.3
  2833.7 140.8 %collective-permute-start.2 = (f32[40,1024]{1,0:T(8,128)S(1)}, f32[40,1024]{1,0:T(8,128)}, u32[]{:S(2)}, u32[]{:S(2)}) collective-permute-start(f32[40,1024]{1,0:T(8,128)S(1)} %copy-done.39), channel_id=1, source_target_pairs={{0,3},{1,4},{2,5},{3,6},{4,7},{5,8},{6,9},{7,10},{8,11},{9,12},{10... | collective-permute-start | bytes 491528
  2835.8 136.1 %collective-permute-start.8 = (f32[40,256]{1,0:T(8,128)S(1)}, f32[40,256]{1,0:T(8,128)}, u32[]{:S(2)}, u32[]{:S(2)}) collective-permute-start(f32[40,256]{1,0:T(8,128)S(1)} %get-tuple-element.227), channel_id=1, source_target_pairs={{0,1},{1,2},{2,3},{3,4},{4,5},{5,6},{6,7},{7,8},{8,9},{9,10},{10,1... | collective-permute-start | bytes 122888
  2841.2 160.6 %collective-permute-start.14 = (f32[40,6912]{1,0:T(8,128)S(1)}, f32[40,6912]{1,0:T(8,128)S(1)}, u32[]{:S(2)}, u32[]{:S(2)}) collective-permute-start(f32[40,6912]{1,0:T(8,128)S(1)} %get-tuple-element.228), channel_id=1, source_target_pairs={{0,3},{1,4},{2,5},{3,6},{4,7},{5,8},{6,9},{7,10},{8,11},{9,12},{10... | collective-permute-start | bytes 3317768
  2842.5 159.3 %collective-permute-start.13 = (f32[40,6912]{1,0:T(8,128)S(1)}, f32[40,6912]{1,0:T(8,128)S(1)}, u32[]{:S(2)}, u32[]{:S(2)}) collective-permute-start(f32[40,6912]{1,0:T(8,128)S(1)} %get-tuple-element.228), channel_id=1, source_target_pairs={{0,2},{1,3},{2,4},{3,5},{4,6},{5,7},{6,8},{7,9},{8,10},{9,11},{10,... | collective-permute-start | bytes 3317768
  2844.9 156.9 %collective-permute-start.12 = (f32[40,6912]{1,0:T(8,128)S(1)}, f32[40,6912]{1,0:T(8,128)}, u32[]{:S(2)}, u32[]{:S(2)}) collective-permute-start(f32[40,6912]{1,0:T(8,128)S(1)} %get-tuple-element.228), channel_id=1, source_target_pairs={{0,1},{1,2},{2,3},{3,4},{4,5},{5,6},{6,7},{7,8},{8,9},{9,10},{10,1... | collective-permute-start | bytes 3317768
  2974.4 18.0 collective-permute-start
  (102 other events, 3550.5 us)
Sparse Core Ops, SparseCore 0:
  11.5 61.4 all-gather.20
  129.8 50.4 all-gather.12
  232.9 46.9 all-gather.14
  283.3 55.8 all-gather.16
  342.4 118.1 all-gather.22
  464.0 117.4 all-gather.24
  584.3 109.1 all-gather.18
  840.7 90.6 reduce-scatter.16
  935.0 104.1 reduce-scatter.18
  1045.0 153.0 reduce-scatter.20
  1206.2 518.8 reduce-scatter.22
where the time goes:
time: 3050 us; the launch traced here: 3030 us
  blocking collectives  2140 us (70%)
  waiting for transfers between devices  344 us (11%)
  matrix products  235 us (8%)
  local copies, waits for them, and re-layouts  187 us (6%)
  starting transfers between devices  75.7 us (2%)
  other arithmetic  41 us (1%)
    unnamed x4, blocking collectives  1970 us
    unnamed x205, local copies, waits for them, and re-layouts  141 us
    all_gather x1, waiting for transfers between devices, on_device(): lax.all_gather(shards_low[4], ('dp', 'seq'), axis=0, tiled=True)  116 us
    all_gather x1, waiting for transfers between devices, on_device(): lax.all_gather(shards_low[5], ('dp', 'seq'), axis=0, tiled=True)  102 us
    unnamed x21, starting transfers between devices  75.1 us
    all_gather x1, blocking collectives, on_device(): lax.all_gather(shards_low[2], ('dp', 'seq'), axis=0, tiled=True)  70.1 us
    all_gather x1, blocking collectives, on_device(): lax.all_gather(shards_low[1], ('dp', 'seq'), axis=0, tiled=True)  69.9 us
  transfers between devices with their start and end apart: 31, of which 6 were waited for; matrix products, arithmetic and copies ran while one was open for 70% of the time, Pallas kernels for 0%

commit v1 on v0

v1 whole, which is shorter than its diff:
```python
import math

import jax
import jax.numpy as jnp
from jax import lax
from jax.sharding import Mesh
from jax.sharding import PartitionSpec as P

HEADS = 4
HEAD = 256
DOC_LIMIT = 512
EPSILON = 1e-06
ROPE_BASE = 1000000.0
NEG_FILL = -1e30
F32 = jnp.float32
BF16 = jnp.bfloat16
PLANE = ("x", "y")
AXES = ("x", "core", "z", "y")
SWAP = [(0, 1), (1, 0)]


def dot(left, right, dims):
    return lax.dot_general(left, right, (dims, ((), ())), preferred_element_type=F32)


def mm(left, right):
    return dot(left, right, ((1,), (0,)))


def mm_t(left, right):
    return dot(left, right, ((1,), (1,)))


def t_mm(left, right):
    return dot(left, right, ((0,), (0,)))


def inv_rms(values):
    return lax.rsqrt(jnp.mean(values * values, axis=-1, keepdims=True) + EPSILON)


def rms_back(values, gain_vec, d_norm):
    scale = inv_rms(values)
    unit = values * scale
    weighted = d_norm * gain_vec
    d_values = scale * (weighted - unit * jnp.mean(weighted * unit, axis=-1, keepdims=True))
    return d_values, d_norm * unit


def rope_tables(positions):
    half_width = HEAD // 2
    inverse = ROPE_BASE ** (-(jnp.arange(half_width, dtype=F32) * 2.0 / HEAD))
    angles = positions.astype(F32)[..., None] * inverse
    return jnp.cos(angles), jnp.sin(angles)


def rotate(values, cosine, sine):
    half_width = values.shape[-1] // 2
    first, second = values[..., :half_width], values[..., half_width:]
    return jnp.concatenate([first * cosine - second * sine, second * cosine + first * sine], axis=-1)


class Links:
    def __init__(self, mesh):
        self.size = dict(mesh.shape)
        self.pairs_only = self.size["x"] == 2 and self.size["y"] == 2

    def index(self, axis):
        return lax.axis_index(axis)

    def swap(self, array, axis):
        return lax.ppermute(array, axis, SWAP)

    def shift(self, array, step):
        depth = self.size["z"]
        pairs = [(i, i + step) for i in range(depth) if 0 <= i + step < depth]
        return lax.ppermute(array, "z", pairs)

    def turn(self, array, step):
        depth = self.size["z"]
        return lax.ppermute(array, "z", [(i, (i + step) % depth) for i in range(depth)])

    def ordered(self, own, other, axis):
        first = self.index(axis) == 0
        return jnp.where(first, jnp.stack([own, other]), jnp.stack([other, own]))

    def gather_axis(self, array, axis):
        if self.size[axis] == 2:
            return self.ordered(array, self.swap(array, axis), axis)
        return lax.all_gather(array, axis, axis=0)

    def unrolled(self, pieces):
        depth = self.size["z"]
        back = jnp.stack(pieces[::-1] + pieces[::-1])
        return lax.dynamic_slice_in_dim(back, depth - 1 - self.index("z"), depth)

    def gather_z(self, array):
        pieces = [array] + [self.turn(array, k) for k in range(1, self.size["z"])]
        return self.unrolled(pieces)

    def gather_all(self, array):
        along = self.gather_z(array)
        if self.pairs_only:
            half = array.shape[1] // 2 // 128 * 128
            left, right = along[..., :half], along[..., half:]
            left = self.gather_axis(self.gather_axis(left, "x"), "y")
            right = self.gather_axis(self.gather_axis(right, "y"), "x")
            plane = jnp.concatenate([left, jnp.swapaxes(right, 0, 1)], axis=-1)
        else:
            plane = self.gather_axis(self.gather_axis(along, "x"), "y")
        both = self.gather_axis(plane, "core")
        return jnp.transpose(both, (2, 0, 3, 1, 4, 5))

    def gather_cz(self, array):
        depth = self.size["z"]
        own = [array]
        for _ in range(depth - 1):
            own.append(self.turn(own[-1], 1))
        other = [self.swap(piece, "core") for piece in own]
        z, core = self.index("z"), self.index("core")
        out = jnp.zeros((2, depth) + array.shape, array.dtype)
        for k in range(depth):
            place = jnp.remainder(z - k, depth)
            rest = (0,) * array.ndim
            out = lax.dynamic_update_slice(out, own[k][None, None], (core, place) + rest)
            out = lax.dynamic_update_slice(out, other[k][None, None], (1 - core, place) + rest)
        return out

    def sum_halves(self, array, axis, dim):
        if self.size[axis] == 2:
            at = self.index(axis)
            sent = self.swap(lax.dynamic_index_in_dim(array, 1 - at, dim, False), axis)
            kept = lax.dynamic_index_in_dim(array, at, dim, False)
            return (kept.astype(F32) + sent.astype(F32)).astype(array.dtype)
        return lax.psum_scatter(array, axis, scatter_dimension=dim, tiled=False)

    def sum_ring(self, array, dim):
        depth = self.size["z"]
        z = self.index("z")

        def block(k):
            return lax.dynamic_index_in_dim(array, jnp.remainder(z + k, depth), dim, False)

        total = block(depth - 1)
        for k in range(depth - 1):
            moved = self.turn(total, 1)
            total = (moved.astype(F32) + block(2 * depth - 2 - k).astype(F32)).astype(array.dtype)
        return total

    def sum_cz(self, array):
        return self.sum_ring(self.sum_halves(array, "core", 0), 0)

    def sum_all(self, array):
        array = self.sum_halves(array, "core", 1)
        array = self.sum_halves(array, "x", 0)
        return self.sum_halves(self.sum_ring(array, 0), "y", 0)

    def exchange(self, array):
        if self.pairs_only:
            x, y = self.index("x"), self.index("y")
            sent = self.swap(lax.dynamic_index_in_dim(array, 1 - x, 0, False), "x")
            array = self.ordered(lax.dynamic_index_in_dim(array, x, 0, False), sent, "x")
            sent = self.swap(lax.dynamic_index_in_dim(array, 1 - y, 1, False), "y")
            array = self.ordered(lax.dynamic_index_in_dim(array, y, 1, False), sent, "y")
            return jnp.swapaxes(array, 0, 1)
        count = self.size["x"] * self.size["y"]
        flat = array.reshape((count,) + array.shape[2:])
        return lax.all_to_all(flat, PLANE, 0, 0, tiled=True).reshape(array.shape)

    def gather_plane(self, rows):
        if not self.pairs_only:
            return lax.all_gather(rows, PLANE, axis=0, tiled=True)
        half = rows.shape[0] // 2
        upper, lower = rows[:half], rows[half:]
        upper = jnp.concatenate([upper, self.swap(upper, "x")])
        lower = jnp.concatenate([lower, self.swap(lower, "y")])
        return jnp.concatenate([upper, self.swap(upper, "y"), lower, self.swap(lower, "x")])

    def sum_plane(self, rows):
        if not self.pairs_only:
            return lax.psum_scatter(rows, PLANE, scatter_dimension=0, tiled=True).astype(F32)
        part = rows.shape[0] // 8
        at = [rows[k * part : (k + 1) * part] for k in range(8)]
        up = self.swap(rows[2 * part : 4 * part], "y").astype(F32)
        low = self.swap(rows[6 * part :], "x").astype(F32)
        up_far = self.swap((at[1].astype(F32) + up[part:]).astype(BF16), "x")
        low_far = self.swap((at[5].astype(F32) + low[part:]).astype(BF16), "y")
        return jnp.concatenate(
            [
                at[0].astype(F32) + up[:part] + up_far.astype(F32),
                at[4].astype(F32) + low[:part] + low_far.astype(F32),
            ]
        )

    def window(self, array, length):
        z, y, wide = self.index("z"), self.index("y"), self.size["y"]
        span = wide * length
        reach = -(-(DOC_LIMIT - 1) // span)
        base = z * span + y * length
        if wide == 2 and reach == 2:
            first = y == 0
            one = self.shift(array, 1)
            two = self.shift(one, 1)
            near = self.swap(jnp.where(first, array, one), "y")
            far = self.swap(jnp.where(first, one, two), "y")
            cross = jnp.where(first, z * span - length, z * span)
            bases = [base, base - span, base - 2 * span, cross, cross - span]
            return [array, one, two, near, far], bases
        along = lax.all_gather(array, "y", axis=0)
        blocks, bases = [], []
        for k in range(reach + 1):
            moved = along if k == 0 else self.shift(moved, 1)
            blocks += [moved[j] for j in range(wide)]
            bases += [(z - k) * span + j * length for j in range(wide)]
        return blocks, bases

    def window_back(self, terms, length):
        wide = self.size["y"]
        span = wide * length
        reach = -(-(DOC_LIMIT - 1) // span)
        y = self.index("y")

        def send(array, axis, step):
            low = array.astype(BF16)
            moved = self.swap(low, "y") if axis == "y" else self.shift(low, step)
            return moved.astype(F32)

        if wide == 2 and reach == 2:
            first = y == 0
            own, one, two, near, far = terms
            far = send(far, "y", 0)
            near = send(near, "y", 0)
            two = two + jnp.where(first, 0.0, far)
            one = one + jnp.where(first, far, near)
            own = own + jnp.where(first, near, 0.0)
            one = one + send(two, "z", -1)
            return own + send(one, "z", -1)
        total = None
        for k in range(reach, -1, -1):
            level = jnp.stack(terms[k * wide : (k + 1) * wide])
            total = level if total is None else level + send(total, "z", -1)
        return lax.psum_scatter(total.astype(BF16), "y", scatter_dimension=0, tiled=False).astype(F32)


def on_device(
    links,
    tokens,
    segment_ids,
    w_query,
    w_key,
    w_value,
    w_out,
    w_gate,
    w_up,
    w_down,
    g_in,
    g_post_attn,
    g_pre_ffn,
    g_post_ffn,
    g_query,
    g_key,
    cotangent,
):
    rows, length, width = tokens.shape
    count = rows * length
    size = links.size
    sx, sc, sz, sy = (size[axis] for axis in AXES)
    parts = sx * sc * sz * sy
    score_scale = HEAD ** (-0.5)
    shard = w_gate.shape[0]
    hidden_shard = w_down.shape[0]
    hidden_own = sc * sz * hidden_shard
    head_shard = g_query.shape[0]
    qkv = HEADS * HEAD + 2 * HEAD

    seg_blocks, bases = links.window(segment_ids, length)
    seg_window = jnp.concatenate(seg_blocks, axis=1)
    pos_window = jnp.concatenate([base + jnp.arange(length, dtype=jnp.int32) for base in bases])
    pos_own = bases[0] + jnp.arange(length, dtype=jnp.int32) if size["y"] == 2 else (
        links.index("z") * sy * length + links.index("y") * length + jnp.arange(length, dtype=jnp.int32)
    )
    same = (segment_ids[:, :, None] == seg_window[:, None, :]) & (pos_window >= 0)[None, None, :]
    allowed = same & (pos_window[None, None, :] <= pos_own[None, :, None])
    positions = jnp.sum(allowed.astype(jnp.int32), axis=2) - 1
    cosine, sine = rope_tables(positions.reshape(count))

    gains_low = jnp.concatenate([g_in, g_post_attn, g_pre_ffn, g_post_ffn, g_query, g_key]).astype(BF16)
    packed = -(-gains_low.shape[0] // 256) * 256
    gains_low = jnp.pad(gains_low, (0, packed - gains_low.shape[0]))[None]
    gains = links.gather_all(gains_low).reshape(parts, packed)
    gain_in, gain_post_attn, gain_pre_ffn, gain_post_ffn = (
        gains[:, k * shard : (k + 1) * shard].reshape(1, width).astype(F32) for k in range(4)
    )
    gain_query, gain_key = (
        gains[:, 4 * shard + k * head_shard : 4 * shard + (k + 1) * head_shard].reshape(1, HEAD).astype(F32)
        for k in range(2)
    )
    kv_shard = jnp.concatenate([w_key.astype(BF16), w_value.astype(BF16)], axis=1)
    full_kv = links.gather_all(kv_shard).reshape(width, 2 * HEAD)
    full_query = links.gather_all(w_query.astype(BF16)).reshape(width, HEADS * HEAD)
    full_out = links.gather_all(w_out.astype(BF16)).reshape(HEADS * HEAD, width)
    full_down = links.gather_cz(w_down.astype(BF16)).reshape(hidden_own, width)

    def columns(weight):
        split = weight.astype(BF16).reshape(shard, sx, sc, sz, sy, hidden_shard)
        return jnp.transpose(split, (1, 4, 0, 2, 3, 5)).reshape(sx, sy, shard, hidden_own)

    def whole_columns(pieces):
        gathered = links.gather_cz(pieces.reshape(sx, sy * shard, hidden_own))
        return jnp.transpose(gathered, (2, 0, 1, 3, 4)).reshape(width, hidden_own)

    full_gate = whole_columns(links.exchange(columns(w_gate)))
    full_up = whole_columns(links.exchange(columns(w_up)))

    inputs_f = tokens.astype(F32).reshape(count, width)
    h_in = (inputs_f * inv_rms(inputs_f) * gain_in).astype(BF16)
    kv_proj = mm(h_in, full_kv)
    k_proj = kv_proj[:, :HEAD]
    value_low = kv_proj[:, HEAD:].astype(BF16)
    key_low = rotate(k_proj * inv_rms(k_proj) * gain_key, cosine, sine).astype(BF16)
    kv_low = jnp.concatenate([key_low, value_low], axis=1).reshape(rows, length, 2 * HEAD)
    kv_window = jnp.concatenate(links.window(kv_low, length)[0], axis=1)
    q_proj = mm(h_in, full_query).reshape(count, HEADS, HEAD)
    query_low = rotate(
        q_proj * inv_rms(q_proj) * gain_query, cosine[:, None, :], sine[:, None, :]
    ).astype(BF16).reshape(rows, length, HEADS, HEAD)
    keys, values = kv_window[..., :HEAD], kv_window[..., HEAD:]
    raw = jnp.einsum("rchd,rkd->rhck", query_low, keys, preferred_element_type=F32) * score_scale
    scores = jnp.where(allowed[:, None], raw, NEG_FILL)
    top = jnp.max(scores, axis=-1, keepdims=True)
    powers = jnp.exp(scores - top)
    probs = powers / jnp.sum(powers, axis=-1, keepdims=True)
    probs_low = probs.astype(BF16)
    mixed = jnp.einsum("rhck,rkd->rchd", probs_low, values, preferred_element_type=F32).astype(BF16)
    mixed_flat = mixed.reshape(count, HEADS * HEAD)
    attn_out = mm(mixed_flat, full_out)
    residual = inputs_f + attn_out * inv_rms(attn_out) * gain_post_attn
    h_ffn = (residual * inv_rms(residual) * gain_pre_ffn).astype(BF16)

    h_all = links.gather_plane(h_ffn)
    gate = mm(h_all, full_gate)
    up = mm(h_all, full_up)
    slope = math.sqrt(2.0 / math.pi)
    bent = jnp.tanh(slope * (gate + 0.044715 * gate * gate * gate))
    act = 0.5 * gate * (1.0 + bent)
    d_act = 0.5 * (1.0 + bent) + 0.5 * gate * (1.0 - bent * bent) * slope * (1.0 + 3 * 0.044715 * gate * gate)
    hidden = (act * up).astype(BF16)
    act_low = act.astype(BF16)
    turn_low = (up * d_act).astype(BF16)
    ffn = links.sum_plane(mm(hidden, full_down).astype(BF16))
    output = (residual + ffn * inv_rms(ffn) * gain_post_ffn).astype(BF16).reshape(tokens.shape)

    d_final = cotangent.astype(F32).reshape(count, width)
    d_ffn_f, post_ffn_terms = rms_back(ffn, gain_post_ffn, d_final)
    d_all = links.gather_plane(d_ffn_f.astype(BF16))
    d_hidden = mm_t(d_all, full_down)
    d_gate = (d_hidden * turn_low.astype(F32)).astype(BF16)
    d_up = (d_hidden * act_low.astype(F32)).astype(BF16)
    d_hffn = links.sum_plane((mm_t(d_gate, full_gate) + mm_t(d_up, full_up)).astype(BF16))

    def by_owner(grad):
        split = grad.astype(BF16).reshape(sx, sc, sz, sy * shard, hidden_own)
        return links.sum_cz(jnp.transpose(split, (1, 2, 0, 3, 4)))

    def own_rows(sums):
        got = links.exchange(sums.reshape(sx, sy, shard, hidden_own))
        got = got.reshape(sx, sy, shard, sc, sz, hidden_shard)
        return jnp.transpose(got, (2, 0, 3, 4, 1, 5)).reshape(shard, parts * hidden_shard).astype(F32)

    grad_down = links.sum_cz(t_mm(hidden, d_all).astype(BF16).reshape(sc, sz, hidden_shard, width)).astype(F32)
    grad_gate = own_rows(by_owner(t_mm(h_all, d_gate)))
    grad_up = own_rows(by_owner(t_mm(h_all, d_up)))

    d_normed, pre_ffn_terms = rms_back(residual, gain_pre_ffn, d_hffn)
    d_residual = d_final + d_normed
    d_attn_f, post_attn_terms = rms_back(attn_out, gain_post_attn, d_residual)
    d_attn = d_attn_f.astype(BF16)

    def summed(grad):
        split = grad.astype(BF16).reshape(sx, sc, sz, sy, -1, grad.shape[1])
        return links.sum_all(split).astype(F32)

    grad_out = summed(t_mm(mixed_flat, d_attn))
    d_mixed = mm_t(d_attn, full_out).astype(BF16).reshape(rows, length, HEADS, HEAD)
    d_probs = jnp.einsum("rchd,rkd->rhck", d_mixed, values, preferred_element_type=F32)
    d_scores = (probs * (d_probs - jnp.sum(d_probs * probs, axis=-1, keepdims=True))).astype(BF16)
    d_query = jnp.einsum("rhck,rkd->rchd", d_scores, keys, preferred_element_type=F32) * score_scale
    key_terms = jnp.einsum("rhck,rchd->rkd", d_scores, query_low, preferred_element_type=F32) * score_scale
    value_terms = jnp.einsum("rhck,rchd->rkd", probs_low, d_mixed, preferred_element_type=F32)
    terms = jnp.concatenate([key_terms, value_terms], axis=-1)
    d_kv = links.window_back(
        [terms[:, k * length : (k + 1) * length] for k in range(terms.shape[1] // length)], length
    ).reshape(count, 2 * HEAD)
    d_value = d_kv[:, HEAD:].astype(BF16)
    d_qproj_f, query_norm_terms = rms_back(
        q_proj, gain_query, rotate(d_query.reshape(count, HEADS, HEAD), cosine[:, None, :], -sine[:, None, :])
    )
    d_kproj_f, key_norm_terms = rms_back(k_proj, gain_key, rotate(d_kv[:, :HEAD], cosine, -sine))
    d_qkv = jnp.concatenate(
        [d_qproj_f.reshape(count, HEADS * HEAD).astype(BF16), d_kproj_f.astype(BF16), d_value], axis=1
    )
    grad_qkv = summed(t_mm(h_in, d_qkv))
    d_hin = mm_t(d_qkv[:, : HEADS * HEAD], full_query) + mm_t(d_qkv[:, HEADS * HEAD :], full_kv)
    d_inputs, in_terms = rms_back(inputs_f, gain_in, d_hin)
    grad_tokens = (d_residual + d_inputs).astype(BF16).reshape(tokens.shape)

    gain_grads = [
        jnp.sum(terms, axis=0).reshape(parts, shard)
        for terms in (in_terms, post_attn_terms, pre_ffn_terms, post_ffn_terms)
    ] + [
        jnp.sum(query_norm_terms, axis=(0, 1)).reshape(parts, head_shard),
        jnp.sum(key_norm_terms, axis=0).reshape(parts, head_shard),
    ]
    gain_grads = jnp.concatenate(gain_grads, axis=1)
    gain_grads = jnp.pad(gain_grads, ((0, 0), (0, packed - gain_grads.shape[1])))
    own = links.sum_all(gain_grads.reshape(sx, sc, sz, sy, 1, packed))[0]
    gain_out = [own[k * shard : (k + 1) * shard] for k in range(4)]
    gain_out += [own[4 * shard + k * head_shard : 4 * shard + (k + 1) * head_shard] for k in range(2)]
    return (
        output,
        grad_tokens,
        grad_qkv[:, : HEADS * HEAD],
        grad_qkv[:, HEADS * HEAD : HEADS * HEAD + HEAD],
        grad_qkv[:, HEADS * HEAD + HEAD :],
        grad_out,
        grad_gate,
        grad_up,
        grad_down,
        *gain_out,
    )


def solution(mesh):
    plane = mesh.shape["dp"] // 2
    by_chip = Mesh(mesh.devices.reshape(plane, 2, -1, plane), AXES)
    links = Links(by_chip)
    placed = P(("x", "core"), ("z", "y"), None)
    matrix = P(AXES, None)
    vector = P(AXES)
    in_specs = (placed, P(("x", "core"), ("z", "y"))) + (matrix,) * 7 + (vector,) * 6 + (placed,)
    out_specs = (placed, placed) + (matrix,) * 7 + (vector,) * 6

    def step(*arguments):
        return on_device(links, *arguments)

    return jax.shard_map(step, mesh=by_chip, in_specs=in_specs, out_specs=out_specs, check_vma=False)
```

time: 3050 us -> 943 us (0.31)
  blocking collectives: 2140 us -> 0 us
  matrix products: 235 us -> 177 us
  other arithmetic: 41 us -> 94.2 us
  starting transfers between devices: 75.7 us -> 125 us
    unnamed x4 -> x0, blocking collectives: 1970 us -> none
    ppermute x0 -> x119, waiting for transfers between devices: none -> 354 us  [the longest x74 237 us: swap(): return lax.ppermute(array, axis, SWAP)]
    all_gather x7 -> x0, waiting for transfers between devices: 333 us -> none  [the longest x1 116 us: on_device(): lax.all_gather(shards_low[4], ('dp', 'seq'), axis=0, tiled=True)]
    all_gather x3 -> x0, blocking collectives: 166 us -> none  [the longest x1 70.1 us: on_device(): lax.all_gather(shards_low[2], ('dp', 'seq'), axis=0, tiled=True)]
    ppermute x0 -> x119, starting transfers between devices: none -> 125 us  [the longest x74 57.7 us: swap(): return lax.ppermute(array, axis, SWAP)]
    unnamed x205 -> x258, local copies, waits for them, and re-layouts: 141 us -> 30.6 us
    unnamed x21 -> x0, starting transfers between devices: 75.1 us -> none
    dot_general x49 -> x23, matrix products: 235 us -> 177 us  [the longest x17 166 us: dot(): lax.dot_general(left, right, (dims, ((), ())), preferred_element_type=F32)]
  transfers between devices with their start and end apart: 31 -> 119, of which waited for: 6 -> 54; matrix products, arithmetic and copies ran while one was open for 70% -> 32% of each run, Pallas kernels for 0% -> 0%
where the time goes in v1:
time: 943 us; the launch traced here: 932 us
  waiting for transfers between devices  354 us (38%)
  local copies, waits for them, and re-layouts  179 us (19%)
  matrix products  177 us (19%)
  starting transfers between devices  125 us (13%)
  other arithmetic  94.2 us (10%)
    ppermute x74, waiting for transfers between devices, swap(): return lax.ppermute(array, axis, SWAP)  237 us
    dot_general x17, matrix products, dot(): lax.dot_general(left, right, (dims, ((), ())), preferred_element_type=F32)  166 us
    ppermute x39, waiting for transfers between devices, turn(): lax.ppermute(array, 'z', [(i, (i + step) % depth) for i in range(depth)])  95.9 us
    ppermute x74, starting transfers between devices, swap(): return lax.ppermute(array, axis, SWAP)  57.7 us
    ppermute x39, starting transfers between devices, turn(): lax.ppermute(array, 'z', [(i, (i + step) % depth) for i in range(depth)])  49.6 us
    unnamed x258, local copies, waits for them, and re-layouts  30.6 us
    ppermute x6, waiting for transfers between devices, shift(): return lax.ppermute(array, 'z', pairs)  20.7 us
  transfers between devices with their start and end apart: 119, of which 54 were waited for; matrix products, arithmetic and copies ran while one was open for 32% of the time, Pallas kernels for 0%

profile of v1, /device:TPU:0, one launch (start us, length us, event | category | flops | bytes accessed | tf_op | source)
XLA Modules:
  0.0 932.5 jit_solution(101418058266644400)
XLA Ops:
  264.3 8.9 collective-permute-done.22
  273.3 10.6 %collective-permute-done.23 = bf16[4,128,512]{2,1,0:T(8,128)(2,1)S(1)} collective-permute-done((bf16[4,128,512]{2,1,0:T(8,128)(2,1)S(1)}, bf16[4,128,512]{2,1,0:T(8,128)(2,1)S(1)}, u32[]{:S(2)}, u32[]{:S(2)}) %collective-permute-start.23) | collective-permute-done | bytes 524320 | tf_op jit(solution)/shard_map/ppermute | solution.py:72
  303.6 9.2 collective-permute-done.40
  320.2 23.8 %collective-permute-done.41 = bf16[512,1152]{1,0:T(8,128)(2,1)S(1)} collective-permute-done((bf16[512,1152]{1,0:T(8,128)(2,1)S(1)}, bf16[512,1152]{1,0:T(8,128)(2,1)S(1)}, u32[]{:S(2)}, u32[]{:S(2)}) %collective-permute-start.41) | collective-permute-done | bytes 1179680 | tf_op jit(solution)/shard_map/ppermute | solution.py:72
  346.1 12.7 %fusion.157 = f32[2048,1728]{0,1:T(8,128)} fusion(bf16[2048,1152]{1,0:T(8,128)(2,1)S(1)} %constant_dynamic-update-slice_fusion.35, bf16[1152,1728]{1,0:T(8,128)(2,1)S(1)} %bitcast.584), kind=kOutput, calls=%fused_computation.489 | convolution fusion | flops 8153726976 | bytes 22855680 | tf_op jit(solution)/shard_map/dot_general | solution.py:23
  358.8 22.0 %multiply_convert_fusion.2 = (bf16[2048,1728]{0,1:T(8,128)(2,1)}, f32[2048,1728]{0,1:T(8,128)}) fusion(f32[2048,1728]{0,1:T(8,128)} %fusion.157, bf16[2048,1152]{1,0:T(8,128)(2,1)} %copy-done.86, bf16[1152,1728]{1,0:T(8,128)(2,1)} %bitcast.586), kind=kOutput, calls=%fused_computation.12 | convolution fusion | flops 8189116416 | bytes 44089344 | tf_op jit(solution)/shard_map/dot_general | solution.py:23
  380.9 13.5 %convolution_convert_fusion = bf16[2048,1152]{1,0:T(8,128)(2,1)S(1)} fusion(bf16[2048,1728]{0,1:T(8,128)(2,1)} %get-tuple-element.134, bf16[1728,1152]{1,0:T(8,128)(2,1)} %bitcast.138), kind=kOutput, calls=%fused_computation.22 | convolution fusion | flops 8156086272 | bytes 15777792 | tf_op jit(solution)/shard_map/dot_general | solution.py:23
  395.8 24.3 %collective-permute-done.69 = bf16[512,1152]{1,0:T(8,128)(2,1)S(1)} collective-permute-done((bf16[512,1152]{1,0:T(8,128)(2,1)S(1)}, bf16[512,1152]{1,0:T(8,128)(2,1)S(1)}, u32[]{:S(2)}, u32[]{:S(2)}) %collective-permute-start.69) | collective-permute-done | bytes 1179680 | tf_op jit(solution)/shard_map/ppermute | solution.py:72
  421.0 11.8 %collective-permute-done.70 = bf16[256,1152]{1,0:T(8,128)(2,1)S(1)} collective-permute-done((bf16[256,1152]{1,0:T(8,128)(2,1)S(1)}, bf16[256,1152]{1,0:T(8,128)(2,1)S(1)}, u32[]{:S(2)}, u32[]{:S(2)}) %collective-permute-start.70) | collective-permute-done | bytes 589856 | tf_op jit(solution)/shard_map/ppermute | solution.py:72
  436.4 10.6 %collective-permute-done.72 = bf16[256,1152]{1,0:T(8,128)(2,1)} collective-permute-done((bf16[256,1152]{1,0:T(8,128)(2,1)}, bf16[256,1152]{1,0:T(8,128)(2,1)}, u32[]{:S(2)}, u32[]{:S(2)}) %collective-permute-start.72) | collective-permute-done | bytes 589856 | tf_op jit(solution)/shard_map/ppermute | solution.py:72
  454.0 11.8 %collective-permute-done.73 = bf16[256,1152]{1,0:T(8,128)(2,1)S(1)} collective-permute-done((bf16[256,1152]{1,0:T(8,128)(2,1)S(1)}, bf16[256,1152]{1,0:T(8,128)(2,1)S(1)}, u32[]{:S(2)}, u32[]{:S(2)}) %collective-permute-start.73) | collective-permute-done | bytes 589856 | tf_op jit(solution)/shard_map/ppermute | solution.py:72
  469.7 33.8 %collective-permute-done.75 = bf16[256,1152]{1,0:T(8,128)(2,1)S(1)} collective-permute-done((bf16[256,1152]{1,0:T(8,128)(2,1)}, bf16[256,1152]{1,0:T(8,128)(2,1)S(1)}, u32[]{:S(2)}, u32[]{:S(2)}) %collective-permute-start.75) | collective-permute-done | bytes 589856 | tf_op jit(solution)/shard_map/ppermute | solution.py:72
  510.3 17.2 %collective-permute-done.76 = bf16[512,1152]{1,0:T(8,128)(2,1)S(1)} collective-permute-done((bf16[512,1152]{1,0:T(8,128)(2,1)S(1)}, bf16[512,1152]{1,0:T(8,128)(2,1)S(1)}, u32[]{:S(2)}, u32[]{:S(2)}) %collective-permute-start.76) | collective-permute-done | bytes 1179680 | tf_op jit(solution)/shard_map/ppermute | solution.py:72
  528.6 26.8 %multiply_convert_fusion.1 = (bf16[2048,1728]{0,1:T(8,128)(2,1)}, bf16[2048,1728]{0,1:T(8,128)(2,1)}) fusion(f32[2048,1728]{0,1:T(8,128)} %get-tuple-element.135, f32[2048,1728]{0,1:T(8,128)} %fusion.157, bf16[2048,1152]{1,0:T(8,128)(2,1)} %constant_dynamic-update-slice_fusion.41, bf16[1728,1152]{1,0:T(8,128)(2,1)} %bitcast.138), kind=kOutput, calls=%fused_computation.11 | convolution fusion | flops 8249278464 | bytes 51167232 | tf_op jit(solution)/shard_map/dot_general | solution.py:23
  555.4 14.7 %fusion.158 = f32[2048,1152]{1,0:T(8,128)} fusion(bf16[2048,1728]{0,1:T(8,128)(2,1)} %get-tuple-element.35, bf16[1152,1728]{1,0:T(8,128)(2,1)S(1)} %bitcast.587), kind=kOutput, calls=%fused_computation.490 | convolution fusion | flops 8153726976 | bytes 20496384 | tf_op jit(solution)/shard_map/dot_general | solution.py:23
  570.2 10.8 %convolution_convert_fusion.3 = bf16[1152,1728]{0,1:T(8,128)(2,1)} fusion(bf16[2048,1728]{0,1:T(8,128)(2,1)S(1)} %copy-done.107, bf16[2048,1152]{1,0:T(8,128)(2,1)S(1)} %bitcast.662), kind=kOutput, calls=%fused_computation.25 | convolution fusion | flops 8155717632 | bytes 15777792 | tf_op jit(solution)/shard_map/dot_general | solution.py:23
  581.0 13.6 %add_convert_fusion = bf16[2048,1152]{1,0:T(8,128)(2,1)S(1)} fusion(f32[2048,1152]{1,0:T(8,128)} %fusion.158, bf16[2048,1728]{0,1:T(8,128)(2,1)} %get-tuple-element.34, bf16[1152,1728]{1,0:T(8,128)(2,1)S(1)} %bitcast.585), kind=kOutput, calls=%fused_computation.14 | convolution fusion | flops 8158445568 | bytes 25214976 | tf_op jit(solution)/shard_map/dot_general | solution.py:23
  599.1 13.0 %convolution_convert_fusion.2 = bf16[1152,1728]{0,1:T(8,128)(2,1)} fusion(bf16[2048,1728]{0,1:T(8,128)(2,1)} %get-tuple-element.35, bf16[2048,1152]{1,0:T(8,128)(2,1)S(1)} %bitcast.662), kind=kOutput, calls=%fused_computation.24 | convolution fusion | flops 8155717632 | bytes 15777792 | tf_op jit(solution)/shard_map/dot_general | solution.py:23
  635.0 12.9 %convolution_convert_fusion.4 = bf16[1728,1152]{1,0:T(8,128)(2,1)S(1)} fusion(bf16[2048,1728]{0,1:T(8,128)(2,1)} %get-tuple-element.134, bf16[2048,1152]{1,0:T(8,128)(2,1)} %constant_dynamic-update-slice_fusion.41), kind=kOutput, calls=%fused_computation.26 | convolution fusion | flops 8155717632 | bytes 15777792 | tf_op jit(solution)/shard_map/dot_general | solution.py:23
  709.6 8.8 collective-permute-done.82
  722.7 8.4 collective-permute-done.105
  732.1 9.5 %collective-permute-done.111 = bf16[216,1152]{1,0:T(8,128)(2,1)S(1)} collective-permute-done((bf16[216,1152]{1,0:T(8,128)(2,1)S(1)}, bf16[216,1152]{1,0:T(8,128)(2,1)S(1)}, u32[]{:S(2)}, u32[]{:S(2)}) %collective-permute-start.111) | collective-permute-done | bytes 497696 | tf_op jit(solution)/shard_map/ppermute | solution.py:81
  743.4 9.3 collective-permute-done.83
  755.4 8.7 collective-permute-done.100
  (801 shorter events, 582.0 us)
Async XLA Ops:
  13.6 59.2 %collective-permute-start.8 = (bf16[36,512]{1,0:T(8,128)(2,1)}, bf16[36,512]{1,0:T(8,128)(2,1)S(1)}, u32[]{:S(2)}, u32[]{:S(2)}) collective-permute-start(bf16[36,512]{1,0:T(8,128)(2,1)} %pad_maximum_fusion.16), channel_id=1, source_target_pairs={{0,6},{2,0},{4,2},{6,4},{1,7},{3,1},{5,3},{7,5},{8,14},{10,8},{12,... | collective-permute-start | bytes 110600 | tf_op jit(solution)/shard_map/ppermute | solution.py:81
  16.4 58.4 %collective-permute-start.9 = (bf16[36,512]{1,0:T(8,128)(2,1)}, bf16[36,512]{1,0:T(8,128)(2,1)}, u32[]{:S(2)}, u32[]{:S(2)}) collective-permute-start(bf16[36,512]{1,0:T(8,128)(2,1)} %pad_maximum_fusion.16), channel_id=1, source_target_pairs={{0,4},{2,6},{4,0},{6,2},{1,5},{3,7},{5,1},{7,3},{8,12},{10,14},{12... | collective-permute-start | bytes 110600 | tf_op jit(solution)/shard_map/ppermute | solution.py:81
  34.0 43.5 %collective-permute-start.10 = (bf16[36,512]{1,0:T(8,128)(2,1)}, bf16[36,512]{1,0:T(8,128)(2,1)S(1)}, u32[]{:S(2)}, u32[]{:S(2)}) collective-permute-start(bf16[36,512]{1,0:T(8,128)(2,1)} %pad_maximum_fusion.16), channel_id=1, source_target_pairs={{0,2},{2,4},{4,6},{6,0},{1,3},{3,5},{5,7},{7,1},{8,10},{10,12},{12... | collective-permute-start | bytes 110600 | tf_op jit(solution)/shard_map/ppermute | solution.py:81
  45.5 41.8 %collective-permute-start.24 = (bf16[36,1024]{1,0:T(8,128)(2,1)S(1)}, bf16[36,1024]{1,0:T(8,128)(2,1)S(1)}, u32[]{:S(2)}, u32[]{:S(2)}) collective-permute-start(bf16[36,1024]{1,0:T(8,128)(2,1)S(1)} %convert_element_type.633), channel_id=1, source_target_pairs={{0,6},{2,0},{4,2},{6,4},{1,7},{3,1},{5,3},{7,5},{8,14},{10,8},{12,... | collective-permute-start | bytes 221192 | tf_op jit(solution)/shard_map/ppermute | solution.py:81
  83.7 65.3 %collective-permute-start.62 = (bf16[216,1152]{1,0:T(8,128)(2,1)}, bf16[216,1152]{1,0:T(8,128)(2,1)S(1)}, u32[]{:S(2)}, u32[]{:S(2)}) collective-permute-start(bf16[216,1152]{1,0:T(8,128)(2,1)} %get-tuple-element.29), channel_id=1, source_target_pairs={{0,8},{8,0},{1,9},{9,1},{2,10},{10,2},{3,11},{11,3},{4,12},{12,4},... | collective-permute-start | bytes 1493000 | tf_op jit(solution)/shard_map/ppermute | solution.py:72
  86.9 64.5 %collective-permute-start.63 = (bf16[216,1152]{1,0:T(8,128)(2,1)}, bf16[216,1152]{1,0:T(8,128)(2,1)}, u32[]{:S(2)}, u32[]{:S(2)}) collective-permute-start(bf16[216,1152]{1,0:T(8,128)(2,1)} %get-tuple-element.29), channel_id=1, source_target_pairs={{0,2},{2,4},{4,6},{6,0},{1,3},{3,5},{5,7},{7,1},{8,10},{10,12},{12... | collective-permute-start | bytes 1493000 | tf_op jit(solution)/shard_map/ppermute | solution.py:81
  88.9 39.6 %collective-permute-start.44 = (bf16[2,36,1728]{2,0,1:T(2,128)(2,1)}, bf16[2,36,1728]{2,0,1:T(2,128)(2,1)S(1)}, u32[]{:S(2)}, u32[]{:S(2)}) collective-permute-start(bf16[2,36,1728]{2,0,1:T(2,128)(2,1)} %get-tuple-element.89), channel_id=1, source_target_pairs={{0,16},{16,0},{1,17},{17,1},{2,18},{18,2},{3,19},{19,3},{4,20},{20... | collective-permute-start | bytes 746504 | tf_op jit(solution)/shard_map/ppermute | solution.py:72
  181.8 55.2 %collective-permute-start.31 = (bf16[2,2,4,36,1024]{4,2,3,1,0:T(4,128)(2,1)}, bf16[2,2,4,36,1024]{4,2,3,1,0:T(4,128)(2,1)S(1)}, u32[]{:S(2)}, u32[]{:S(2)}) collective-permute-start(bf16[2,2,4,36,1024]{4,2,3,1,0:T(4,128)(2,1)} %copy.329), channel_id=1, source_target_pairs={{0,8},{8,0},{1,9},{9,1},{2,10},{10,2},{3,11},{11,3},{4,12},{12,4},... | collective-permute-start | bytes 3538952 | tf_op jit(solution)/shard_map/ppermute | solution.py:72
  183.6 67.1 %collective-permute-start.39 = (bf16[2,2,4,32,1152]{4,3,0,2,1:T(8,128)(2,1)}, bf16[2,2,4,32,1152]{4,3,0,2,1:T(8,128)(2,1)}, u32[]{:S(2)}, u32[]{:S(2)}) collective-permute-start(bf16[2,2,4,32,1152]{4,3,0,2,1:T(8,128)(2,1)} %get-tuple-element.64), channel_id=1, source_target_pairs={{0,8},{8,0},{1,9},{9,1},{2,10},{10,2},{3,11},{11,3},{4,12},{12,4},... | collective-permute-start | bytes 3538952 | tf_op jit(solution)/shard_map/ppermute | solution.py:72
  237.0 61.6 %collective-permute-start.50 = (bf16[2,72,1728]{2,0,1:T(2,128)(2,1)}, bf16[2,72,1728]{2,0,1:T(2,128)(2,1)}, u32[]{:S(2)}, u32[]{:S(2)}) collective-permute-start(bf16[2,72,1728]{2,0,1:T(2,128)(2,1)} %collective-permute-done.49), channel_id=1, source_target_pairs={{0,8},{8,0},{1,9},{9,1},{2,10},{10,2},{3,11},{11,3},{4,12},{12,4},... | collective-permute-start | bytes 1493000 | tf_op jit(solution)/shard_map/ppermute | solution.py:72
  250.8 50.2 %collective-permute-start.51 = (bf16[2,72,1728]{2,0,1:T(2,128)(2,1)}, bf16[2,72,1728]{2,0,1:T(2,128)(2,1)}, u32[]{:S(2)}, u32[]{:S(2)}) collective-permute-start(bf16[2,72,1728]{2,0,1:T(2,128)(2,1)} %collective-permute-done.49), channel_id=1, source_target_pairs={{0,2},{2,4},{4,6},{6,0},{1,3},{3,5},{5,7},{7,1},{8,10},{10,12},{12... | collective-permute-start | bytes 1493000 | tf_op jit(solution)/shard_map/ppermute | solution.py:81
  256.7 44.8 %collective-permute-start.68 = (bf16[216,1152]{1,0:T(8,128)(2,1)}, bf16[216,1152]{1,0:T(8,128)(2,1)}, u32[]{:S(2)}, u32[]{:S(2)}) collective-permute-start(bf16[216,1152]{1,0:T(8,128)(2,1)} %collective-permute-done.67), channel_id=1, source_target_pairs={{0,8},{8,0},{1,9},{9,1},{2,10},{10,2},{3,11},{11,3},{4,12},{12,4},... | collective-permute-start | bytes 1493000 | tf_op jit(solution)/shard_map/ppermute | solution.py:72
  466.9 39.2 %collective-permute-start.74 = (bf16[512,1152]{1,0:T(8,128)(2,1)}, bf16[512,1152]{1,0:T(8,128)(2,1)}, u32[]{:S(2)}, u32[]{:S(2)}) collective-permute-start(bf16[512,1152]{1,0:T(8,128)(2,1)} %pad_maximum_fusion.8), channel_id=1, source_target_pairs={{0,1},{1,0},{2,3},{3,2},{4,5},{5,4},{6,7},{7,6},{8,9},{9,8},{10,11... | collective-permute-start | bytes 3538952 | tf_op jit(solution)/shard_map/ppermute | solution.py:72
  654.7 47.2 %collective-permute-start.98 = (bf16[2,72,1728]{2,1,0:T(8,128)(2,1)}, bf16[2,72,1728]{2,1,0:T(8,128)(2,1)}, u32[]{:S(2)}, u32[]{:S(2)}) collective-permute-start(bf16[2,72,1728]{2,1,0:T(8,128)(2,1)} %dynamic-slice_bitcast_fusion.8), channel_id=1, source_target_pairs={{0,2},{2,4},{4,6},{6,0},{1,3},{3,5},{5,7},{7,1},{8,10},{10,12},{12... | collective-permute-start | bytes 1493000 | tf_op jit(solution)/shard_map/ppermute | solution.py:81
  658.6 44.8 %collective-permute-start.104 = (bf16[2,72,1728]{2,1,0:T(8,128)(2,1)}, bf16[2,72,1728]{2,1,0:T(8,128)(2,1)}, u32[]{:S(2)}, u32[]{:S(2)}) collective-permute-start(bf16[2,72,1728]{2,1,0:T(8,128)(2,1)} %dynamic-slice_bitcast_fusion.7), channel_id=1, source_target_pairs={{0,2},{2,4},{4,6},{6,0},{1,3},{3,5},{5,7},{7,1},{8,10},{10,12},{12... | collective-permute-start | bytes 1493000 | tf_op jit(solution)/shard_map/ppermute | solution.py:81
  661.0 46.2 %collective-permute-start.110 = (bf16[216,1152]{1,0:T(8,128)(2,1)}, bf16[216,1152]{1,0:T(8,128)(2,1)}, u32[]{:S(2)}, u32[]{:S(2)}) collective-permute-start(bf16[216,1152]{1,0:T(8,128)(2,1)} %dynamic-slice_bitcast_fusion.9), channel_id=1, source_target_pairs={{0,2},{2,4},{4,6},{6,0},{1,3},{3,5},{5,7},{7,1},{8,10},{10,12},{12... | collective-permute-start | bytes 1493000 | tf_op jit(solution)/shard_map/ppermute | solution.py:81
  694.4 48.0 %collective-permute-start.81 = (bf16[4,128,512]{2,1,0:T(8,128)(2,1)}, bf16[4,128,512]{2,1,0:T(8,128)(2,1)}, u32[]{:S(2)}, u32[]{:S(2)}) collective-permute-start(bf16[4,128,512]{2,1,0:T(8,128)(2,1)} %get-tuple-element.45), channel_id=1, source_target_pairs={{0,1},{1,0},{2,3},{3,2},{4,5},{5,4},{6,7},{7,6},{8,9},{9,8},{10,11... | collective-permute-start | bytes 1572872 | tf_op jit(solution)/shard_map/ppermute | solution.py:72
  701.9 84.8 %collective-permute-start.91 = (bf16[2,4,2,32,1152]{4,3,2,1,0:T(8,128)(2,1)}, bf16[2,4,2,32,1152]{4,3,2,1,0:T(8,128)(2,1)S(1)}, u32[]{:S(2)}, u32[]{:S(2)}) collective-permute-start(bf16[2,4,2,32,1152]{4,3,2,1,0:T(8,128)(2,1)} %dynamic-slice_bitcast_fusion.4), channel_id=1, source_target_pairs={{0,8},{8,0},{1,9},{9,1},{2,10},{10,2},{3,11},{11,3},{4,12},{12,4},... | collective-permute-start | bytes 3538952 | tf_op jit(solution)/shard_map/ppermute | solution.py:72
  742.4 43.3 %collective-permute-start.112 = (bf16[216,1152]{1,0:T(8,128)(2,1)S(1)}, bf16[216,1152]{1,0:T(8,128)(2,1)S(1)}, u32[]{:S(2)}, u32[]{:S(2)}) collective-permute-start(bf16[216,1152]{1,0:T(8,128)(2,1)S(1)} %fusion.80), channel_id=1, source_target_pairs={{0,2},{2,4},{4,6},{6,0},{1,3},{3,5},{5,7},{7,1},{8,10},{10,12},{12... | collective-permute-start | bytes 1493000 | tf_op jit(solution)/shard_map/ppermute | solution.py:81
  754.1 42.2 %collective-permute-start.84 = (bf16[4,128,512]{2,1,0:T(8,128)(2,1)S(1)}, bf16[4,128,512]{2,1,0:T(8,128)(2,1)S(1)}, u32[]{:S(2)}, u32[]{:S(2)}) collective-permute-start(bf16[4,128,512]{2,1,0:T(8,128)(2,1)S(1)} %fusion.65), channel_id=1, source_target_pairs={{2,0},{4,2},{6,4},{3,1},{5,3},{7,5},{10,8},{12,10},{14,12},{11,9},... | collective-permute-start | bytes 1572872 | tf_op jit(solution)/shard_map/ppermute | solution.py:77
  777.7 50.8 %collective-permute-start.107 = (bf16[2,36,1728]{2,0,1:T(2,128)(2,1)}, bf16[2,36,1728]{2,0,1:T(2,128)(2,1)}, u32[]{:S(2)}, u32[]{:S(2)}) collective-permute-start(bf16[2,36,1728]{2,0,1:T(2,128)(2,1)} %bitcast.560), channel_id=1, source_target_pairs={{0,16},{16,0},{1,17},{17,1},{2,18},{18,2},{3,19},{19,3},{4,20},{20... | collective-permute-start | bytes 746504 | tf_op jit(solution)/shard_map/ppermute | solution.py:72
  788.0 84.4 %collective-permute-start.92 = (bf16[4,2,32,1152]{3,2,1,0:T(8,128)(2,1)}, bf16[4,2,32,1152]{3,2,1,0:T(8,128)(2,1)}, u32[]{:S(2)}, u32[]{:S(2)}) collective-permute-start(bf16[4,2,32,1152]{3,2,1,0:T(8,128)(2,1)} %dynamic-slice_bitcast_fusion.6), channel_id=1, source_target_pairs={{0,16},{16,0},{1,17},{17,1},{2,18},{18,2},{3,19},{19,3},{4,20},{20... | collective-permute-start | bytes 1769480 | tf_op jit(solution)/shard_map/ppermute | solution.py:72
  792.4 72.1 %collective-permute-start.102 = (bf16[2,36,1728]{2,0,1:T(2,128)(2,1)}, bf16[2,36,1728]{2,0,1:T(2,128)(2,1)}, u32[]{:S(2)}, u32[]{:S(2)}) collective-permute-start(bf16[2,36,1728]{2,0,1:T(2,128)(2,1)} %bitcast.561), channel_id=1, source_target_pairs={{0,1},{1,0},{2,3},{3,2},{4,5},{5,4},{6,7},{7,6},{8,9},{9,8},{10,11... | collective-permute-start | bytes 746504 | tf_op jit(solution)/shard_map/ppermute | solution.py:72
  836.0 43.4 %collective-permute-start.108 = (bf16[2,36,1728]{2,0,1:T(2,128)(2,1)}, bf16[2,36,1728]{2,0,1:T(2,128)(2,1)}, u32[]{:S(2)}, u32[]{:S(2)}) collective-permute-start(bf16[2,36,1728]{2,0,1:T(2,128)(2,1)} %bitcast.558), channel_id=1, source_target_pairs={{0,1},{1,0},{2,3},{3,2},{4,5},{5,4},{6,7},{7,6},{8,9},{9,8},{10,11... | collective-permute-start | bytes 746504 | tf_op jit(solution)/shard_map/ppermute | solution.py:72
  (205 other events, 2903.3 us)

commit v2 on v1

v2 whole, which is shorter than its diff:
```python
import functools
import math

import jax
import jax.numpy as jnp
from jax import lax
from jax.experimental import pallas as pl
from jax.experimental.pallas import tpu as pltpu
from jax.sharding import Mesh
from jax.sharding import PartitionSpec as P

HEADS = 4
HEAD = 256
HALF = HEAD // 2
DOC_LIMIT = 512
EPSILON = 1e-06
ROPE_BASE = 1000000.0
NEG_FILL = -1e30
SCORE_SCALE = HEAD ** (-0.5)
SLOPE = math.sqrt(2.0 / math.pi)
F32 = jnp.float32
BF16 = jnp.bfloat16
PLANE = ("x", "y")
AXES = ("x", "core", "z", "y")
SWAP = [(0, 1), (1, 0)]
IN, POST_ATTN, PRE_FFN, POST_FFN = range(4)
SMALL = 128
ROOM = 58 << 20


def dot(left, right, dims):
    return lax.dot_general(left, right, (dims, ((), ())), preferred_element_type=F32)


def mm(left, right):
    return dot(left, right, ((1,), (0,)))


def mm_t(left, right):
    return dot(left, right, ((1,), (1,)))


def t_mm(left, right):
    return dot(left, right, ((0,), (0,)))


def inv_rms(values):
    return lax.rsqrt(jnp.mean(values * values, axis=-1, keepdims=True) + EPSILON)


def rms_back(values, gain_vec, d_norm):
    scale = inv_rms(values)
    unit = values * scale
    weighted = d_norm * gain_vec
    d_values = scale * (weighted - unit * jnp.mean(weighted * unit, axis=-1, keepdims=True))
    return d_values, d_norm * unit


def rope_tables(positions):
    inverse = ROPE_BASE ** (-(jnp.arange(HALF, dtype=F32) * 2.0 / HEAD))
    angles = positions.astype(F32)[..., None] * inverse
    return jnp.cos(angles), jnp.sin(angles)


def rotate(values, cosine, sine):
    first, second = values[:, :HALF], values[:, HALF:]
    return jnp.concatenate([first * cosine - second * sine, second * cosine + first * sine], axis=-1)


def column_sum(terms):
    return jnp.sum(terms, axis=0, keepdims=True)


def call(body, grid, in_specs, out_specs, out_shape, flops, scratch=()):
    moved = sum(math.prod(one.shape) * one.dtype.itemsize for one in jax.tree.leaves(out_shape))
    return pl.pallas_call(
        body,
        grid=grid,
        in_specs=in_specs,
        out_specs=out_specs,
        out_shape=out_shape,
        scratch_shapes=list(scratch),
        compiler_params=pltpu.CompilerParams(vmem_limit_bytes=ROOM),
        cost_estimate=pl.CostEstimate(flops=flops, bytes_accessed=2 * moved, transcendentals=0),
    )


def shaped(*shape, dtype=F32):
    return jax.ShapeDtypeStruct(shape, dtype)


def whole(*shape):
    return pl.BlockSpec(shape, lambda i: (0,) * len(shape))


def rows_of(tile, width):
    return pl.BlockSpec((tile, width), lambda i: (i, 0))


def row_block(*shape):
    return pl.BlockSpec((1,) + shape, lambda i: (i,) + (0,) * len(shape))


def kv_body(tok_ref, wkv_ref, gains_ref, head_ref, cos_ref, sin_ref, h_ref, kproj_ref, kv_ref):
    tokens = tok_ref[...].astype(F32)
    h = (tokens * inv_rms(tokens) * gains_ref[IN : IN + 1]).astype(BF16)
    h_ref[...] = h
    proj = mm(h, wkv_ref[...])
    k_proj = proj[:, :HEAD]
    kproj_ref[...] = k_proj
    key = rotate(k_proj * inv_rms(k_proj) * head_ref[1:2], cos_ref[...], sin_ref[...])
    kv_ref[0, :, :HEAD] = key.astype(BF16)
    kv_ref[0, :, HEAD:] = proj[:, HEAD:].astype(BF16)


def kv_step(rows, length, tokens, wkv, gains, heads, cosine, sine):
    count, width = tokens.shape
    return call(
        kv_body,
        (rows,),
        [rows_of(length, width), whole(*wkv.shape), whole(*gains.shape), whole(*heads.shape)]
        + [rows_of(length, HALF)] * 2,
        [rows_of(length, width), rows_of(length, HEAD), row_block(length, 2 * HEAD)],
        [shaped(count, width, dtype=BF16), shaped(count, HEAD), shaped(rows, length, 2 * HEAD, dtype=BF16)],
        2 * count * width * 2 * HEAD,
    )(tokens, wkv, gains, heads, cosine, sine)


def by_head(array):
    return jnp.concatenate([array[:, h * HEAD : (h + 1) * HEAD] for h in range(HEADS)], axis=0)


def by_lane(array):
    part = array.shape[0] // HEADS
    return jnp.concatenate([array[h * part : (h + 1) * part] for h in range(HEADS)], axis=1)


def probs_of(query, keys, segq_ref, posq_ref, segk_ref, posk_ref):
    allowed = (segq_ref[...] == segk_ref[0]) & (posk_ref[...] <= posq_ref[...])
    allowed = jnp.concatenate([allowed.astype(F32)] * HEADS, axis=0) > 0.5
    scores = jnp.where(allowed, mm_t(query, keys) * SCORE_SCALE, NEG_FILL)
    powers = jnp.exp(scores - jnp.max(scores, axis=-1, keepdims=True))
    return powers / jnp.sum(powers, axis=-1, keepdims=True)


def attend_body(blocks, *refs):
    (h_ref, tok_ref, wq_ref, wo_ref, gains_ref, head_ref, cos_ref, sin_ref) = refs[:8]
    masks, kv_refs = refs[8:12], refs[12 : 12 + blocks]
    qproj_ref, query_ref, mixed_ref, attn_ref, resid_ref, hffn_ref = refs[12 + blocks :]
    proj = mm(h_ref[...], wq_ref[...])
    qproj_ref[...] = proj
    cosine, sine = cos_ref[...], sin_ref[...]
    query = []
    for h in range(HEADS):
        one = proj[:, h * HEAD : (h + 1) * HEAD]
        query.append(rotate(one * inv_rms(one) * head_ref[0:1], cosine, sine).astype(BF16))
    query_ref[...] = jnp.concatenate(query, axis=1)
    keys = jnp.concatenate([one[0, :, :HEAD] for one in kv_refs], axis=0)
    values = jnp.concatenate([one[0, :, HEAD:] for one in kv_refs], axis=0)
    probs = probs_of(jnp.concatenate(query, axis=0), keys, *masks).astype(BF16)
    mixed = by_lane(mm(probs, values).astype(BF16))
    mixed_ref[...] = mixed
    attn = mm(mixed, wo_ref[...])
    attn_ref[...] = attn
    resid = tok_ref[...].astype(F32) + attn * inv_rms(attn) * gains_ref[POST_ATTN : POST_ATTN + 1]
    resid_ref[...] = resid
    hffn_ref[...] = (resid * inv_rms(resid) * gains_ref[PRE_FFN : PRE_FFN + 1]).astype(BF16)


def mask_specs(length, window):
    return [rows_of(length, 1), whole(length, 1), row_block(1, window), whole(1, window)]


def attend(rows, length, h, tokens, wq, wo, gains, heads, cosine, sine, masks, kv):
    count, width = tokens.shape
    wide = HEADS * HEAD
    window = len(kv) * length
    return call(
        functools.partial(attend_body, len(kv)),
        (rows,),
        [rows_of(length, width)] * 2
        + [whole(*one.shape) for one in (wq, wo, gains, heads)]
        + [rows_of(length, HALF)] * 2
        + mask_specs(length, window)
        + [row_block(length, 2 * HEAD)] * len(kv),
        [rows_of(length, wide)] * 3 + [rows_of(length, width)] * 3,
        [
            shaped(count, wide),
            shaped(count, wide, dtype=BF16),
            shaped(count, wide, dtype=BF16),
            shaped(count, width),
            shaped(count, width),
            shaped(count, width, dtype=BF16),
        ],
        4 * count * wide * (width + window),
    )(h, tokens, wq, wo, gains, heads, cosine, sine, *masks, *kv)


def attend_back_body(blocks, *refs):
    (dh_ref, cot_ref, resid_ref, attn_ref, qproj_ref, query_ref, wo_ref, gains_ref, head_ref, cos_ref, sin_ref) = refs[:11]
    masks, kv_refs = refs[11:15], refs[15 : 15 + blocks]
    dres_ref, dattn_ref, dq_ref, sums_ref, head_sums_ref = refs[15 + blocks : 20 + blocks]
    term_refs = refs[20 + blocks :]
    d_norm, pre_terms = rms_back(resid_ref[...], gains_ref[PRE_FFN : PRE_FFN + 1], dh_ref[...])
    d_res = cot_ref[...].astype(F32) + d_norm
    dres_ref[...] = d_res
    d_attn, post_terms = rms_back(attn_ref[...], gains_ref[POST_ATTN : POST_ATTN + 1], d_res)
    d_attn = d_attn.astype(BF16)
    dattn_ref[...] = d_attn
    d_mixed = by_head(mm_t(d_attn, wo_ref[...]).astype(BF16))
    query = by_head(query_ref[...])
    keys = jnp.concatenate([one[0, :, :HEAD] for one in kv_refs], axis=0)
    values = jnp.concatenate([one[0, :, HEAD:] for one in kv_refs], axis=0)
    probs = probs_of(query, keys, *masks)
    d_probs = mm_t(d_mixed, values)
    d_scores = (probs * (d_probs - jnp.sum(d_probs * probs, axis=-1, keepdims=True))).astype(BF16)
    key_terms = t_mm(d_scores, query) * SCORE_SCALE
    value_terms = t_mm(probs.astype(BF16), d_mixed)
    length = query_ref.shape[0]
    for k, ref in enumerate(term_refs):
        at = slice(k * length, (k + 1) * length)
        ref[0, :, :HEAD] = key_terms[at].astype(ref.dtype)
        ref[0, :, HEAD:] = value_terms[at].astype(ref.dtype)
    d_query = mm(d_scores, keys) * SCORE_SCALE
    cosine, sine = cos_ref[...], -sin_ref[...]
    head_sum = jnp.zeros((1, HEAD), F32)
    for h in range(HEADS):
        turned = rotate(d_query[h * length : (h + 1) * length], cosine, sine)
        lanes = slice(h * HEAD, (h + 1) * HEAD)
        d_proj, terms = rms_back(qproj_ref[:, lanes], head_ref[0:1], turned)
        dq_ref[:, lanes] = d_proj.astype(BF16)
        head_sum += column_sum(terms)

    @pl.when(pl.program_id(0) == 0)
    def _():
        sums_ref[...] = jnp.zeros_like(sums_ref)
        head_sums_ref[...] = jnp.zeros_like(head_sums_ref)

    sums_ref[POST_ATTN : POST_ATTN + 1] += column_sum(post_terms)
    sums_ref[PRE_FFN : PRE_FFN + 1] += column_sum(pre_terms)
    head_sums_ref[0:1] += head_sum


def attend_back(rows, length, dh, cot, resid, attn, qproj, query, wo, gains, heads, cosine, sine, masks, kv, kinds):
    count, width = dh.shape
    wide = HEADS * HEAD
    window = len(kv) * length
    return call(
        functools.partial(attend_back_body, len(kv)),
        (rows,),
        [rows_of(length, width)] * 4
        + [rows_of(length, wide)] * 2
        + [whole(*one.shape) for one in (wo, gains, heads)]
        + [rows_of(length, HALF)] * 2
        + mask_specs(length, window)
        + [row_block(length, 2 * HEAD)] * len(kv),
        [rows_of(length, width)] * 2
        + [rows_of(length, wide), whole(8, width), whole(8, HEAD)]
        + [row_block(length, 2 * HEAD)] * len(kv),
        [
            shaped(count, width),
            shaped(count, width, dtype=BF16),
            shaped(count, wide, dtype=BF16),
            shaped(8, width),
            shaped(8, HEAD),
        ]
        + [shaped(rows, length, 2 * HEAD, dtype=kind) for kind in kinds],
        2 * count * wide * (width + 5 * window),
    )(dh, cot, resid, attn, qproj, query, wo, gains, heads, cosine, sine, *masks, *kv)


def finish_body(dkv_ref, kproj_ref, dq_ref, tok_ref, dres_ref, wq_ref, wkv_ref, gains_ref, head_ref, cos_ref, sin_ref,
                dkvp_ref, grad_ref, sums_ref, head_sums_ref):
    d_kv = dkv_ref[0]
    turned = rotate(d_kv[:, :HEAD], cos_ref[...], -sin_ref[...])
    d_key, key_terms = rms_back(kproj_ref[...], head_ref[1:2], turned)
    d_proj = jnp.concatenate([d_key.astype(BF16), d_kv[:, HEAD:].astype(BF16)], axis=1)
    dkvp_ref[...] = d_proj
    d_hin = mm_t(dq_ref[...], wq_ref[...]) + mm_t(d_proj, wkv_ref[...])
    d_tokens, in_terms = rms_back(tok_ref[...].astype(F32), gains_ref[IN : IN + 1], d_hin)
    grad_ref[...] = (dres_ref[...] + d_tokens).astype(BF16)

    @pl.when(pl.program_id(0) == 0)
    def _():
        sums_ref[...] = jnp.zeros_like(sums_ref)
        head_sums_ref[...] = jnp.zeros_like(head_sums_ref)

    sums_ref[IN : IN + 1] += column_sum(in_terms)
    head_sums_ref[1:2] += column_sum(key_terms)


def finish(rows, length, dkv, kproj, dq, tokens, dres, wq, wkv, gains, heads, cosine, sine):
    count, width = tokens.shape
    wide = HEADS * HEAD
    return call(
        finish_body,
        (rows,),
        [row_block(length, 2 * HEAD), rows_of(length, HEAD), rows_of(length, wide)]
        + [rows_of(length, width)] * 2
        + [whole(*one.shape) for one in (wq, wkv, gains, heads)]
        + [rows_of(length, HALF)] * 2,
        [rows_of(length, 2 * HEAD), rows_of(length, width), whole(8, width), whole(8, HEAD)],
        [shaped(count, 2 * HEAD, dtype=BF16), shaped(count, width, dtype=BF16), shaped(8, width), shaped(8, HEAD)],
        2 * count * width * (wide + 2 * HEAD),
    )(dkv, kproj, dq, tokens, dres, wq, wkv, gains, heads, cosine, sine)


def pieces_of(total, step):
    return [(k, min(step, total - k)) for k in range(0, total, step)]


def up_body(step, h_ref, pair_ref, down_ref, hidden_ref, turn_ref, act_ref, out_ref):
    h = h_ref[...]
    for at, wide in pieces_of(hidden_ref.shape[1], step):
        cols = pl.ds(at, wide)
        gate = mm(h, pair_ref[0, :, cols])
        up = mm(h, pair_ref[1, :, cols])
        square = gate * gate
        bent = jnp.tanh(gate * (SLOPE + SLOPE * 0.044715 * square))
        half = 0.5 + 0.5 * bent
        act = gate * half
        d_act = half + 0.5 * gate * (1.0 - bent * bent) * (SLOPE + 3 * SLOPE * 0.044715 * square)
        hidden_ref[:, cols] = (act * up).astype(BF16)
        turn_ref[:, cols] = (up * d_act).astype(BF16)
        act_ref[:, cols] = act.astype(BF16)
    out_ref[...] = mm(hidden_ref[...], down_ref[...]).astype(BF16)


def ffn_forward(h, pair, down, tile=256, step=256):
    count, width = h.shape
    units = pair.shape[2]
    return call(
        functools.partial(up_body, step),
        (count // tile,),
        [rows_of(tile, width), whole(2, width, units), whole(units, width)],
        [rows_of(tile, units)] * 3 + [rows_of(tile, width)],
        [shaped(count, units, dtype=BF16)] * 3 + [shaped(count, width, dtype=BF16)],
        6 * count * width * units,
    )(h, pair, down)


def down_body(step, d_ref, turn_ref, act_ref, pair_ref, down_ref, pair_out, out_ref):
    d = d_ref[...]
    for at, wide in pieces_of(turn_ref.shape[1], step):
        cols = pl.ds(at, wide)
        d_hidden = mm_t(d, down_ref[cols, :])
        pair_out[0, :, cols] = (d_hidden * turn_ref[:, cols].astype(F32)).astype(BF16)
        pair_out[1, :, cols] = (d_hidden * act_ref[:, cols].astype(F32)).astype(BF16)
    out_ref[...] = (mm_t(pair_out[0], pair_ref[0]) + mm_t(pair_out[1], pair_ref[1])).astype(BF16)


def ffn_backward(d, turn, act, pair, down, tile=256, step=256):
    count, width = d.shape
    units = pair.shape[2]
    return call(
        functools.partial(down_body, step),
        (count // tile,),
        [rows_of(tile, width), rows_of(tile, units), rows_of(tile, units), whole(2, width, units), whole(units, width)],
        [pl.BlockSpec((2, tile, units), lambda i: (0, i, 0)), rows_of(tile, width)],
        [shaped(2, count, units, dtype=BF16), shaped(count, width, dtype=BF16)],
        6 * count * width * units,
    )(d, turn, act, pair, down)


def grads_body(left_ref, right_ref, out_ref):
    out_ref[0] = t_mm(left_ref[...], right_ref[0]).astype(BF16)


def weight_grads(left, right, tile):
    count, rows = left.shape
    many, _, cols = right.shape
    return call(
        grads_body,
        (many, rows // tile),
        [
            pl.BlockSpec((count, tile), lambda k, i: (0, i)),
            pl.BlockSpec((1, count, cols), lambda k, i: (k, 0, 0)),
        ],
        pl.BlockSpec((1, tile, cols), lambda k, i: (k, i, 0)),
        shaped(many, rows, cols, dtype=BF16),
        2 * many * count * rows * cols,
    )(left, right)


def middle_body(ffn_ref, resid_ref, cot_ref, gains_ref, out_ref, dffn_ref, sums_ref):
    ffn = ffn_ref[...]
    gain = gains_ref[POST_FFN : POST_FFN + 1]
    out_ref[...] = (resid_ref[...] + ffn * inv_rms(ffn) * gain).astype(BF16)
    d_ffn, terms = rms_back(ffn, gain, cot_ref[...].astype(F32))
    dffn_ref[...] = d_ffn.astype(BF16)

    @pl.when(pl.program_id(0) == 0)
    def _():
        sums_ref[...] = jnp.zeros_like(sums_ref)

    sums_ref[POST_FFN : POST_FFN + 1] += column_sum(terms)


def middle(rows, length, ffn, resid, cot, gains):
    count, width = ffn.shape
    return call(
        middle_body,
        (rows,),
        [rows_of(length, width)] * 3 + [whole(*gains.shape)],
        [rows_of(length, width)] * 2 + [whole(8, width)],
        [shaped(count, width, dtype=BF16), shaped(count, width, dtype=BF16), shaped(8, width)],
        20 * count * width,
    )(ffn, resid, cot, gains)


def place_body(links, shard, parts, own_ref, other_ref, *refs):
    outs, scratch = refs[:-1], refs[-1]
    depth = links.size["z"]
    at_x, at_c, at_z, at_y = (links.index(axis) for axis in AXES)
    total = scratch.shape[0]
    number = 0
    for x in range(2):
        for core in range(2):
            for z in range(depth):
                for y in range(2):
                    slot = jnp.abs(at_x - x) + 2 * jnp.abs(at_y - y)
                    slot = slot * depth + jnp.remainder(at_z - z + depth, depth)
                    mine = own_ref[slot].astype(F32)
                    theirs = other_ref[slot].astype(F32)
                    piece = jnp.where(at_c == core, mine, theirs)
                    scratch[number] = piece
                    number += 1
    for (first, count, lanes), out in zip(parts, outs, strict=True):
        for k in range(number):
            out[k * count : (k + 1) * count, :] = scratch[k, first : first + count, :lanes].astype(out.dtype)


def placed(links, own, other, parts):
    slots, rows, lanes = own.shape
    number = 2 * slots
    return pl.pallas_call(
        functools.partial(place_body, links, rows, parts),
        out_shape=[shaped(number * count, wide, dtype=BF16) for _, count, wide in parts],
        scratch_shapes=[pltpu.VMEM((number, rows, lanes), F32)],
        compiler_params=pltpu.CompilerParams(vmem_limit_bytes=ROOM),
    )(own, other)


class Links:
    def __init__(self, mesh):
        self.size = dict(mesh.shape)
        self.pairs_only = self.size["x"] == 2 and self.size["y"] == 2

    def index(self, axis):
        return lax.axis_index(axis)

    def swap(self, array, axis):
        return lax.ppermute(array, axis, SWAP)

    def shift(self, array, step):
        depth = self.size["z"]
        pairs = [(i, i + step) for i in range(depth) if 0 <= i + step < depth]
        return lax.ppermute(array, "z", pairs)

    def turn(self, array, step):
        depth = self.size["z"]
        return lax.ppermute(array, "z", [(i, (i + step) % depth) for i in range(depth)])

    def ordered(self, own, other, axis):
        first = self.index(axis) == 0
        return jnp.where(first, jnp.stack([own, other]), jnp.stack([other, own]))

    def gather_all(self, array, parts):
        depth = self.size["z"]
        along = jnp.stack([array] + [self.turn(array, k) for k in range(1, depth)])
        if self.pairs_only:
            across = lax.ppermute(along, PLANE, [(k, 3 - k) for k in range(4)])
            own = jnp.concatenate([along, self.swap(along, "x"), self.swap(along, "y"), across])
            return placed(self, own, self.swap(own, "core"), parts)
        full = lax.all_gather(array, AXES, axis=0)
        return [full[:, at : at + count, :lanes].reshape(-1, lanes) for at, count, lanes in parts]

    def gather_cz(self, array, dim):
        return lax.all_gather(array, ("core", "z"), axis=dim, tiled=True)

    def sum_halves(self, array, axis, dim):
        if self.size[axis] == 2:
            at = self.index(axis)
            sent = self.swap(lax.dynamic_index_in_dim(array, 1 - at, dim, False), axis)
            kept = lax.dynamic_index_in_dim(array, at, dim, False)
            return (kept.astype(F32) + sent.astype(F32)).astype(array.dtype)
        return lax.psum_scatter(array, axis, scatter_dimension=dim, tiled=False)

    def sum_z(self, array, dim):
        depth = self.size["z"]
        z = self.index("z")

        def block(k):
            return lax.dynamic_index_in_dim(array, jnp.remainder(z + k, depth), dim, False)

        total = block(0).astype(F32)
        for k in range(1, depth):
            total = total + self.turn(block(k), k).astype(F32)
        return total

    def sum_cz(self, array):
        mine = jnp.swapaxes(self.sum_halves(array, "core", 1), 0, 1)
        return lax.psum_scatter(mine.reshape(-1, array.shape[-1]), "z", scatter_dimension=0, tiled=True)

    def sum_all(self, array):
        array = self.sum_halves(array, "core", 1)
        array = self.sum_halves(array, "x", 0)
        return self.sum_halves(self.sum_z(array, 0).astype(BF16), "y", 0).astype(F32)

    def sum_all_small(self, array):
        array = self.sum_halves(array, "core", 1)
        sent = array.reshape((-1,) + array.shape[3:])
        got = lax.all_to_all(sent, ("x", "z", "y"), 0, 0, tiled=True)
        return jnp.sum(got.astype(F32), axis=0)

    def exchange(self, array):
        count = self.size["x"] * self.size["y"]
        flat = array.reshape((count,) + array.shape[2:])
        return lax.all_to_all(flat, PLANE, 0, 0, tiled=True).reshape(array.shape)

    def gather_plane(self, rows):
        if not self.pairs_only:
            return lax.all_gather(rows, PLANE, axis=0, tiled=True)
        half = rows.shape[0] // 2
        upper, lower = lax.optimization_barrier((rows[:half], rows[half:]))
        near = lax.optimization_barrier((self.swap(upper, "x"), self.swap(lower, "y")))
        upper = jnp.concatenate([upper, near[0]])
        lower = jnp.concatenate([lower, near[1]])
        upper, lower = lax.optimization_barrier((upper, lower))
        far = lax.optimization_barrier((self.swap(upper, "y"), self.swap(lower, "x")))
        return jnp.concatenate([upper, far[0], lower, far[1]])

    def sum_plane(self, rows):
        if not self.pairs_only:
            return lax.psum_scatter(rows, PLANE, scatter_dimension=0, tiled=True).astype(F32)
        part = rows.shape[0] // 8
        at = [rows[k * part : (k + 1) * part] for k in range(8)]
        up, low = lax.optimization_barrier((self.swap(rows[2 * part : 4 * part], "y"), self.swap(rows[6 * part :], "x")))
        up_far = (at[1].astype(F32) + up[part:].astype(F32)).astype(BF16)
        low_far = (at[5].astype(F32) + low[part:].astype(F32)).astype(BF16)
        up_far, low_far = lax.optimization_barrier((up_far, low_far))
        up_far, low_far = lax.optimization_barrier((self.swap(up_far, "x"), self.swap(low_far, "y")))
        return jnp.concatenate(
            [
                at[0].astype(F32) + up[:part].astype(F32) + up_far.astype(F32),
                at[4].astype(F32) + low[:part].astype(F32) + low_far.astype(F32),
            ]
        )

    def window_bases(self, length):
        z, y, wide = self.index("z"), self.index("y"), self.size["y"]
        span = wide * length
        reach = -(-(DOC_LIMIT - 1) // span)
        base = z * span + y * length
        if wide == 2 and reach == 2:
            cross = jnp.where(y == 0, z * span - length, z * span)
            return [base, base - span, base - 2 * span, cross, cross - span]
        return [(z - k) * span + j * length for k in range(reach + 1) for j in range(wide)]

    def window(self, array, length):
        wide = self.size["y"]
        reach = -(-(DOC_LIMIT - 1) // (wide * length))
        if wide == 2 and reach == 2:
            first = self.index("y") == 0
            one = self.shift(array, 1)
            two = self.shift(one, 1)
            near = self.swap(jnp.where(first, array, one), "y")
            far = self.swap(jnp.where(first, one, two), "y")
            return [array, one, two, near, far]
        along = [lax.all_gather(array, "y", axis=0)]
        for _ in range(reach):
            along.append(self.shift(along[-1], 1))
        return [level[j] for level in along for j in range(wide)]

    def window_kinds(self, length):
        if self.size["y"] == 2 and 2 * length * 2 >= DOC_LIMIT - 1 > 2 * length:
            return [F32, F32, F32, BF16, BF16]
        return [F32] * len(self.window_bases(length))

    def window_back(self, terms, length):
        wide = self.size["y"]
        span = wide * length
        reach = -(-(DOC_LIMIT - 1) // span)
        y = self.index("y")

        def send(array, axis, step):
            low = array.astype(BF16)
            moved = self.swap(low, "y") if axis == "y" else self.shift(low, step)
            return moved.astype(F32)

        if wide == 2 and reach == 2:
            first = y == 0
            own, one, two, near, far = terms
            far = send(far, "y", 0)
            near = send(near, "y", 0)
            two = two + jnp.where(first, 0.0, far)
            one = one + jnp.where(first, far, near)
            own = own + jnp.where(first, near, 0.0)
            one = one + send(two, "z", -1)
            return own + send(one, "z", -1)
        total = None
        for k in range(reach, -1, -1):
            level = jnp.stack(terms[k * wide : (k + 1) * wide])
            total = level if total is None else level + send(total, "z", -1)
        return lax.psum_scatter(total.astype(BF16), "y", scatter_dimension=0, tiled=False).astype(F32)


def on_device(
    links,
    tokens,
    segment_ids,
    w_query,
    w_key,
    w_value,
    w_out,
    w_gate,
    w_up,
    w_down,
    g_in,
    g_post_attn,
    g_pre_ffn,
    g_post_ffn,
    g_query,
    g_key,
    cotangent,
):
    rows, length, width = tokens.shape
    count = rows * length
    size = links.size
    sx, sc, sz, sy = (size[axis] for axis in AXES)
    parts = sx * sc * sz * sy
    shard = w_gate.shape[0]
    hidden_shard = w_down.shape[0]
    chunk = -(-hidden_shard // 16) * 16
    units = sc * sz * chunk
    head_shard = g_query.shape[0]
    tokens_flat = tokens.reshape(count, width)
    cot_flat = cotangent.reshape(count, width)

    def columns(weight):
        split = weight.astype(BF16).reshape(shard, sx, sc, sz, sy, hidden_shard)
        split = jnp.pad(split, ((0, 0),) * 5 + ((0, chunk - hidden_shard),))
        return jnp.transpose(split, (1, 4, 0, 2, 3, 5)).reshape(sx, sy, shard, units)

    pair = jnp.stack([columns(w_gate), columns(w_up)], axis=2)
    pair = jnp.transpose(links.exchange(pair), (2, 0, 1, 3, 4)).reshape(2 * sx, sy * shard, units)
    full_pair = links.gather_cz(pair, 1).reshape(2, width, units)
    full_down = links.gather_cz(jnp.pad(w_down.astype(BF16), ((0, chunk - hidden_shard), (0, 0))), 0)

    lanes = 2 * HEAD + SMALL
    seg_row = jnp.pad(segment_ids.astype(BF16), ((0, 0), (0, lanes - length)))
    gain_columns = jnp.stack([g_in, g_post_attn, g_pre_ffn, g_post_ffn], axis=1)
    head_columns = jnp.pad(jnp.stack([g_query, g_key], axis=1), ((0, shard - head_shard), (0, 0)))
    kv_shard = jnp.concatenate(
        [gain_columns, head_columns, jnp.zeros((shard, SMALL - 6), F32), w_key, w_value], axis=1
    ).astype(BF16)
    first, seg_all = links.gather_all(
        jnp.concatenate([kv_shard, seg_row]), ((0, shard, lanes), (shard, rows, length))
    )
    full_kv = first[:, SMALL:]
    small = jnp.transpose(first[:, :SMALL]).astype(F32)
    gains = small[:8]
    heads = jnp.pad(small[4:6].reshape(2, parts, shard)[..., :head_shard].reshape(2, HEAD), ((0, 6), (0, 0)))
    seg_all = seg_all.reshape(sx, sc, sz, sy, rows, length)
    seg_all = lax.dynamic_slice(
        seg_all, (links.index("x"), links.index("core"), 0, 0, 0, 0), (1, 1, sz, sy, rows, length)
    )
    seg_flat = jnp.transpose(seg_all[0, 0], (2, 0, 1, 3)).reshape(rows, -1).astype(jnp.int32)
    bases = links.window_bases(length)
    seg_window = jnp.concatenate(
        [lax.dynamic_slice_in_dim(seg_flat, jnp.maximum(base, 0), length, 1) for base in bases], axis=1
    )
    step = jnp.arange(length, dtype=jnp.int32)
    pos_window = jnp.concatenate([base + step for base in bases])
    pos_own = links.index("z") * sy * length + links.index("y") * length + step
    seg_window = jnp.where((pos_window >= 0)[None], seg_window, -1)
    allowed = (segment_ids[:, :, None] == seg_window[:, None, :]) & (pos_window[None, None, :] <= pos_own[None, :, None])
    positions = jnp.sum(allowed.astype(jnp.int32), axis=2) - 1
    cosine, sine = rope_tables(positions.reshape(count))
    masks = (segment_ids.reshape(count, 1), pos_own[:, None], seg_window[:, None, :], pos_window[None])

    wide = max(width, HEADS * HEAD)
    q_shard = jnp.pad(w_query.astype(BF16), ((0, 0), (0, wide - HEADS * HEAD)))
    o_shard = jnp.pad(w_out.astype(BF16), ((0, 0), (0, wide - width)))
    out_shard = w_out.shape[0]
    full_out, full_query = links.gather_all(
        jnp.concatenate([o_shard, q_shard]), ((0, out_shard, width), (out_shard, shard, HEADS * HEAD))
    )

    h_in, k_proj, kv_low = kv_step(rows, length, tokens_flat, full_kv, gains, heads, cosine, sine)
    kv = links.window(kv_low, length)
    q_proj, query, mixed, attn, resid, h_ffn = attend(
        rows, length, h_in, tokens_flat, full_query, full_out, gains, heads, cosine, sine, masks, kv
    )
    h_all = links.gather_plane(h_ffn)
    hidden, turn, act, ffn_terms = ffn_forward(h_all, full_pair, full_down)
    ffn = links.sum_plane(ffn_terms)
    output, d_ffn, sums_ffn = middle(rows, length, ffn, resid, cot_flat, gains)

    d_all = links.gather_plane(d_ffn)
    d_pair, d_terms = ffn_backward(d_all, turn, act, full_pair, full_down)
    d_hffn = links.sum_plane(d_terms)
    grad_down = weight_grads(hidden, d_all[None], units // 7 if units % 7 == 0 else units)
    grad_down = links.sum_cz(grad_down.reshape(1, sc, sz, chunk, width))[:hidden_shard].astype(F32)
    grad_pair = weight_grads(h_all, d_pair, 384)
    sums = jnp.stack([links.sum_cz(grad_pair[k].reshape(sx, sc, sz, sy * shard, units)) for k in range(2)])
    sums = jnp.transpose(sums.reshape(2, sx, sy, shard, units), (1, 2, 0, 3, 4))
    got = links.exchange(sums).reshape(sx, sy, 2, shard, sc, sz, chunk)[..., :hidden_shard]
    got = jnp.transpose(got, (2, 3, 0, 4, 5, 1, 6)).reshape(2, shard, parts * hidden_shard).astype(F32)

    d_res, d_attn, d_qproj, sums_attn, heads_attn, *terms = attend_back(
        rows, length, d_hffn, cot_flat, resid, attn, q_proj, query, full_out, gains, heads, cosine, sine, masks, kv,
        links.window_kinds(length),
    )
    d_kv = links.window_back(terms, length)
    grad_out = weight_grads(mixed, d_attn[None], 512)[0]
    grad_query = weight_grads(h_in, d_qproj[None], 384)[0]
    wide_q = jnp.pad(grad_query, ((0, 0), (0, wide - HEADS * HEAD))).reshape(sx, sc, sz, sy, shard, wide)
    wide_o = jnp.pad(grad_out, ((0, 0), (0, wide - width))).reshape(sx, sc, sz, sy, out_shard, wide)
    second_sum = links.sum_all(jnp.concatenate([wide_o, wide_q], axis=4))

    d_kvproj, grad_tokens, sums_in, heads_in = finish(
        rows, length, d_kv, k_proj, d_qproj, tokens_flat, d_res, full_query, full_kv, gains, heads, cosine, sine
    )
    grad_kv = weight_grads(h_in, d_kvproj[None], 384)[0]
    gain_terms = (sums_ffn + sums_attn + sums_in)[:4]
    head_terms = (heads_attn + heads_in)[:2].reshape(2, parts, head_shard)
    head_terms = jnp.pad(head_terms, ((0, 0), (0, 0), (0, shard - head_shard))).reshape(2, width)
    small_terms = jnp.pad(jnp.concatenate([gain_terms, head_terms]), ((0, SMALL - 6), (0, 0)))
    first_grad = jnp.concatenate([jnp.transpose(small_terms).astype(BF16), grad_kv], axis=1)
    first_sum = links.sum_all_small(first_grad.reshape(sx, sc, sz, sy, shard, lanes))
    return (
        output.reshape(tokens.shape),
        grad_tokens.reshape(tokens.shape),
        second_sum[out_shard:, : HEADS * HEAD],
        first_sum[:, SMALL : SMALL + HEAD],
        first_sum[:, SMALL + HEAD :],
        second_sum[:out_shard, :width],
        got[0],
        got[1],
        grad_down,
        *(first_sum[:, k] for k in range(4)),
        *(first_sum[:head_shard, 4 + k] for k in range(2)),
    )


def solution(mesh):
    plane = mesh.shape["dp"] // 2
    by_chip = Mesh(mesh.devices.reshape(plane, 2, -1, plane), AXES)
    links = Links(by_chip)
    placed = P(("x", "core"), ("z", "y"), None)
    matrix = P(AXES, None)
    vector = P(AXES)
    in_specs = (placed, P(("x", "core"), ("z", "y"))) + (matrix,) * 7 + (vector,) * 6 + (placed,)
    out_specs = (placed, placed) + (matrix,) * 7 + (vector,) * 6

    def step(*arguments):
        return on_device(links, *arguments)

    return jax.shard_map(step, mesh=by_chip, in_specs=in_specs, out_specs=out_specs, check_vma=False)
```

time: 943 us -> 769 us (0.82)
  Pallas kernels: 0 us -> 192 us
  matrix products: 177 us -> 0 us
  local copies, waits for them, and re-layouts: 179 us -> 95.9 us
  other arithmetic: 94.2 us -> 46.7 us
  starting transfers between devices: 125 us -> 85.2 us
  waiting for transfers between devices: 354 us -> 321 us
  between operations: 3.75 us -> 15.3 us
    pallas_call x0 -> x14, Pallas kernels: none -> 192 us  [the longest x5 51.8 us: weight_grads(): call(grads_body, (many, rows // tile), [pl.BlockSpec((count, tile), lambd...]
    dot_general x23 -> x0, matrix products: 177 us -> none  [the longest x17 166 us: dot(): lax.dot_general(left, right, (dims, ((), ())), preferred_element_type=F32)]
    ppermute x39 -> x9, waiting for transfers between devices: 95.9 us -> 31.8 us  [turn(): lax.ppermute(array, 'z', [(i, (i + step) % depth) for i in range(depth)])]
    all_to_all x0 -> x3, waiting for transfers between devices: none -> 57.7 us  [the longest x1 34.6 us: sum_all_small(): got = lax.all_to_all(sent, ('x', 'z', 'y'), 0, 0, tiled=True)]
    ppermute x74 -> x33, waiting for transfers between devices: 237 us -> 183 us  [swap(): return lax.ppermute(array, axis, SWAP)]
    ppermute x74 -> x33, starting transfers between devices: 57.7 us -> 24.6 us  [swap(): return lax.ppermute(array, axis, SWAP)]
    convert_element_type x18 -> x1, local copies, waits for them, and re-layouts: 33.5 us -> 0.89 us  [on_device(): jnp.transpose(small_terms).astype(BF16)]
    ppermute x39 -> x9, starting transfers between devices: 49.6 us -> 17.1 us  [turn(): lax.ppermute(array, 'z', [(i, (i + step) % depth) for i in range(depth)])]
  transfers between devices with their start and end apart: 119 -> 56, of which waited for: 54 -> 30; matrix products, arithmetic and copies ran while one was open for 32% -> 15% of each run, Pallas kernels for 0% -> 11%
where the time goes in v2:
time: 769 us; the launch traced here: 756 us
  waiting for transfers between devices  321 us (42%)
  Pallas kernels  192 us (25%)
  local copies, waits for them, and re-layouts  95.9 us (12%)
  starting transfers between devices  85.2 us (11%)
  other arithmetic  46.7 us (6%)
  between operations  15.3 us (2%)
    ppermute x33, waiting for transfers between devices, swap(): return lax.ppermute(array, axis, SWAP)  183 us
    pallas_call x5, Pallas kernels, weight_grads(): call(grads_body, (many, rows // tile), [pl.BlockSpec((count, tile), lambd...  51.8 us
    ppermute x4, waiting for transfers between devices, shift(): return lax.ppermute(array, 'z', pairs)  48.4 us
    pallas_call x1, Pallas kernels, ffn_backward(): call(functools.partial(down_body, step), (count // tile,), [rows_of(tile,...  41.9 us
    pallas_call x1, Pallas kernels, ffn_forward(): call(functools.partial(up_body, step), (count // tile,), [rows_of(tile, w...  36.5 us
    all_to_all x1, waiting for transfers between devices, sum_all_small(): got = lax.all_to_all(sent, ('x', 'z', 'y'), 0, 0, tiled=True)  34.6 us
    ppermute x9, waiting for transfers between devices, turn(): lax.ppermute(array, 'z', [(i, (i + step) % depth) for i in range(depth)])  31.8 us
    ppermute x33, starting transfers between devices, swap(): return lax.ppermute(array, axis, SWAP)  24.6 us
  transfers between devices with their start and end apart: 56, of which 30 were waited for; matrix products, arithmetic and copies ran while one was open for 15% of the time, Pallas kernels for 11%

profile of v2, /device:TPU:0, one launch (start us, length us, event | category | flops | bytes accessed | tf_op | source)
XLA Modules:
  0.0 756.0 jit_solution(16677515802825392483)
XLA Ops:
  24.3 13.0 %all-to-all-done = bf16[4,2,36,1792]{3,1,2,0:T(2,128)(2,1)S(1)} async-done(((bf16[4,2,36,1792]{3,1,2,0:T(2,128)(2,1)}), bf16[4,2,36,1792]{3,1,2,0:T(2,128)(2,1)S(1)}, u32[]{:S(2)}, u32[]{:S(2)}) %all-to-all-start) | async-done | bytes 1032224 | tf_op jit(solution)/shard_map/all_to_all | solution.py:519
  79.1 11.4 %collective-permute-done.10 = bf16[4,68,1152]{2,0,1:T(4,128)(2,1)S(1)} collective-permute-done((bf16[4,68,1152]{2,0,1:T(4,128)(2,1)S(1)}, bf16[4,68,1152]{2,0,1:T(4,128)(2,1)S(1)}, u32[]{:S(2)}, u32[]{:S(2)}) %collective-permute-start.10) | collective-permute-done | bytes 626720 | tf_op jit(solution)/shard_map/ppermute | solution.py:453
  90.6 12.7 %collective-permute-done.11 = bf16[4,68,1152]{2,0,1:T(4,128)(2,1)S(1)} collective-permute-done((bf16[4,68,1152]{2,0,1:T(4,128)(2,1)S(1)}, bf16[4,68,1152]{2,0,1:T(4,128)(2,1)S(1)}, u32[]{:S(2)}, u32[]{:S(2)}) %collective-permute-start.11) | collective-permute-done | bytes 626720 | tf_op jit(solution)/shard_map/ppermute | solution.py:453
  130.6 23.6 %collective-permute-done.14.refs_13_.refs_16_ = bf16[4,128,512]{2,1,0:T(8,128)(2,1)S(1)} collective-permute-done((bf16[4,128,512]{2,1,0:T(8,128)(2,1)}, bf16[4,128,512]{2,1,0:T(8,128)(2,1)S(1)}, u32[]{:S(2)}, u32[]{:S(2)}) %collective-permute-start.14) | collective-permute-done | bytes 524320 | tf_op jit(solution)/shard_map/ppermute | solution.py:458
  154.2 11.9 %collective-permute-start.15 = (bf16[4,128,512]{2,1,0:T(8,128)(2,1)S(1)}, bf16[4,128,512]{2,1,0:T(8,128)(2,1)S(1)}, u32[]{:S(2)}, u32[]{:S(2)}) collective-permute-start(bf16[4,128,512]{2,1,0:T(8,128)(2,1)S(1)} %collective-permute-done.14.refs_13_.refs_16_), channel_id=1, source_target_pairs={{0,2},{2,4},{4,6},{1,3},{3,5},{5,7},{8,10},{10,12},{12,14},{9,11},... | collective-permute-start | bytes 1572872 | tf_op jit(solution)/shard_map/ppermute | solution.py:458
  204.2 14.9 %shard_map.274 = (f32[512,1024]{1,0:T(8,128)}, bf16[512,1024]{1,0:T(8,128)(2,1)}, bf16[512,1024]{1,0:T(8,128)(2,1)}, f32[512,1152]{1,0:T(8,128)}, f32[512,1152]{1,0:T(8,128)}, /*index=5*/bf16[512,1152]{1,0:T(8,128)(2,1)}) custom-call(bf16[512,1152]{1,0:T(8,128)(2,1)} %get-tuple-element.81.refs_0_.left_ref, bf16[512,1152]{1,0:T(8,128)(2,1)} %bitcast.151, ...), custom_call_target="tpu_custom_call" | custom-call | flops 3758096384 | bytes 20185088 | tf_op jit(solution)/shard_map/pallas_call | solution.py:178
  222.4 11.7 %collective-permute-done.18 = bf16[256,1152]{1,0:T(8,128)(2,1)S(1)} collective-permute-done((bf16[256,1152]{1,0:T(8,128)(2,1)S(1)}, bf16[256,1152]{1,0:T(8,128)(2,1)S(1)}, u32[]{:S(2)}, u32[]{:S(2)}) %collective-permute-start.18) | collective-permute-done | bytes 589856 | tf_op jit(solution)/shard_map/ppermute | solution.py:453
  237.8 22.9 %collective-permute-done.20 = bf16[512,1152]{1,0:T(8,128)(2,1)S(1)} collective-permute-done((bf16[512,1152]{1,0:T(8,128)(2,1)S(1)}, bf16[512,1152]{1,0:T(8,128)(2,1)S(1)}, u32[]{:S(2)}, u32[]{:S(2)}) %collective-permute-start.20) | collective-permute-done | bytes 1179680 | tf_op jit(solution)/shard_map/ppermute | solution.py:453
  264.6 36.5 %shard_map.275 = (bf16[2048,1792]{1,0:T(8,128)(2,1)}, bf16[2048,1792]{1,0:T(8,128)(2,1)}, bf16[2048,1792]{1,0:T(8,128)(2,1)}, bf16[2048,1152]{1,0:T(8,128)(2,1)}) custom-call(bf16[2048,1152]{1,0:T(8,128)(2,1)} %constant_dynamic-update-slice_fusion.22.h_ref.left_ref, bf16[2,1152,1792]{2,1,0:T(8,128)(2,1)} %bitcast.180, ...), custom_call_target="tpu_custom_call" | custom-call | flops 25367150592 | bytes 53477376 | tf_op jit(solution)/shard_map/pallas_call | solution.py:332
  304.8 23.4 %collective-permute-done.22 = bf16[512,1152]{1,0:T(8,128)(2,1)S(1)} collective-permute-done((bf16[512,1152]{1,0:T(8,128)(2,1)S(1)}, bf16[512,1152]{1,0:T(8,128)(2,1)S(1)}, u32[]{:S(2)}, u32[]{:S(2)}) %collective-permute-start.22) | collective-permute-done | bytes 1179680 | tf_op jit(solution)/shard_map/ppermute | solution.py:453
  351.9 10.0 %collective-permute-done.26 = bf16[256,1152]{1,0:T(8,128)(2,1)S(1)} collective-permute-done((bf16[256,1152]{1,0:T(8,128)(2,1)S(1)}, bf16[256,1152]{1,0:T(8,128)(2,1)S(1)}, u32[]{:S(2)}, u32[]{:S(2)}) %collective-permute-start.26) | collective-permute-done | bytes 589856 | tf_op jit(solution)/shard_map/ppermute | solution.py:453
  367.2 19.1 %collective-permute-done.28 = bf16[512,1152]{1,0:T(8,128)(2,1)} collective-permute-done((bf16[512,1152]{1,0:T(8,128)(2,1)S(1)}, bf16[512,1152]{1,0:T(8,128)(2,1)}, u32[]{:S(2)}, u32[]{:S(2)}) %collective-permute-start.28) | collective-permute-done | bytes 1179680 | tf_op jit(solution)/shard_map/ppermute | solution.py:453
  390.3 41.9 %shard_map.277 = (bf16[2,2048,1792]{2,1,0:T(8,128)(2,1)}, bf16[2048,1152]{1,0:T(8,128)(2,1)}) custom-call(bf16[2048,1152]{1,0:T(8,128)(2,1)} %copy-done.19, bf16[2048,1792]{1,0:T(8,128)(2,1)} %get-tuple-element.112.turn_ref, bf16[2048,1792]{1,0:T(8,128)(2,1)} %get-tuple-element.113.act_ref, bf16[2,1152,1792]{2,1,0:T(8,128)(2,1)} %bitcast.181, ...), custom_call_target="tpu_custom_call" | custom-call | flops 25367150592 | bytes 38797312 | tf_op jit(solution)/shard_map/pallas_call | solution.py:355
  432.2 24.1 %shard_map.283 = bf16[2,1152,1792]{2,1,0:T(8,128)(2,1)} custom-call(bf16[2048,1152]{1,0:T(8,128)(2,1)} %constant_dynamic-update-slice_fusion.22.h_ref.left_ref, bf16[2,2048,1792]{2,1,0:T(8,128)(2,1)} %get-tuple-element.141.right_ref), custom_call_target="tpu_custom_call" | custom-call | flops 16911433728 | bytes 16515072 | tf_op jit(solution)/shard_map/pallas_call | solution.py:372
  472.5 19.6 %collective-permute-done.30 = bf16[512,1152]{1,0:T(8,128)(2,1)} collective-permute-done((bf16[512,1152]{1,0:T(8,128)(2,1)}, bf16[512,1152]{1,0:T(8,128)(2,1)}, u32[]{:S(2)}, u32[]{:S(2)}) %collective-permute-start.30) | collective-permute-done | bytes 1179680 | tf_op jit(solution)/shard_map/ppermute | solution.py:453
  496.2 11.1 %collective-permute-done.32 = bf16[256,1152]{1,0:T(8,128)(2,1)S(1)} collective-permute-done((bf16[256,1152]{1,0:T(8,128)(2,1)S(1)}, bf16[256,1152]{1,0:T(8,128)(2,1)S(1)}, u32[]{:S(2)}, u32[]{:S(2)}) %collective-permute-start.32) | collective-permute-done | bytes 589856 | tf_op jit(solution)/shard_map/ppermute | solution.py:453
  511.1 17.5 %shard_map.278 = (f32[512,1152]{1,0:T(8,128)}, bf16[512,1152]{1,0:T(8,128)(2,1)}, bf16[512,1024]{1,0:T(8,128)(2,1)}, f32[8,1152]{1,0:T(8,128)}, f32[8,256]{1,0:T...) custom-call(f32[512,1152]{1,0:T(8,128)} %pad_maximum_fusion.1.refs_0, ...), custom_call_target="tpu_custom_call" | custom-call | flops 4563402752 | bytes 17653760 | tf_op jit(solution)/shard_map/pallas_call | solution.py:248
  532.6 11.1 %collective-permute-done.35 = bf16[4,128,512]{2,1,0:T(8,128)(2,1)S(1)} collective-permute-done((bf16[4,128,512]{2,1,0:T(8,128)(2,1)}, bf16[4,128,512]{2,1,0:T(8,128)(2,1)S(1)}, u32[]{:S(2)}, u32[]{:S(2)}) %collective-permute-start.35) | collective-permute-done | bytes 524320 | tf_op jit(solution)/shard_map/ppermute | solution.py:453
  545.2 14.5 %shard_map.284 = bf16[1,1792,1152]{2,1,0:T(8,128)(2,1)} custom-call(bf16[2048,1792]{1,0:T(8,128)(2,1)} %get-tuple-element.142.left_ref, bf16[1,2048,1152]{2,1,0:T(8,128)(2,1)} %bitcast.166), custom_call_target="tpu_custom_call" | custom-call | flops 8455716864 | bytes 8257536 | tf_op jit(solution)/shard_map/pallas_call | solution.py:372
  562.8 15.5 %collective-permute-done.36 = bf16[4,128,512]{2,1,0:T(8,128)(2,1)S(1)} collective-permute-done((bf16[4,128,512]{2,1,0:T(8,128)(2,1)S(1)}, bf16[4,128,512]{2,1,0:T(8,128)(2,1)S(1)}, u32[]{:S(2)}, u32[]{:S(2)}) %collective-permute-start.36) | collective-permute-done | bytes 524320 | tf_op jit(solution)/shard_map/ppermute | solution.py:458
  603.2 9.7 %shard_map.279 = (bf16[512,512]{1,0:T(8,128)(2,1)}, bf16[512,1152]{1,0:T(8,128)(2,1)}, f32[8,1152]{1,0:T(8,128)}, f32[8,256]{1,0:T(8,128)}) custom-call(f32[4,128,512]{2,1,0:T(8,128)} %fusion.11.dkv_ref, f32[512,256]{1,0:T(8,128)} %get-tuple-element.129.kproj_ref, bf16[512,1024]{1,0:T(8,128)(2,1)} %get-tuple-element.130.dq_ref, bf16[512,1152]{1,0:T(8,128)(2,1)} %bitcast.152, ...), custom_call_target="tpu_custom_call" | custom-call | flops 1811939328 | bytes 3497984 | tf_op jit(solution)/shard_map/pallas_call | solution.py:295
  648.9 34.6 %all-to-all-done.1 = bf16[16,36,640]{2,1,0:T(8,128)(2,1)} async-done(((bf16[16,36,640]{2,1,0:T(8,128)(2,1)}), bf16[16,36,640]{2,1,0:T(8,128)(2,1)}, u32[]{:S(2)}, u32[]{:S(2)}) %all-to-all-start.1) | async-done | bytes 737312 | tf_op jit(solution)/shard_map/all_to_all | solution.py:513
  699.8 16.1 %collective-permute-done.41 = bf16[2,68,1152]{2,1,0:T(8,128)(2,1)S(1)} collective-permute-done((bf16[2,68,1152]{2,1,0:T(8,128)(2,1)S(1)}, bf16[2,68,1152]{2,1,0:T(8,128)(2,1)S(1)}, u32[]{:S(2)}, u32[]{:S(2)}) %collective-permute-start.41) | collective-permute-done | bytes 313376 | tf_op jit(solution)/shard_map/ppermute | solution.py:462
  729.5 10.1 %all-to-all-done.2 = bf16[4,2,36,1792]{3,1,2,0:T(2,128)(2,1)S(1)} async-done(((bf16[4,2,36,1792]{3,1,2,0:T(2,128)(2,1)}), bf16[4,2,36,1792]{3,1,2,0:T(2,128)(2,1)S(1)}, u32[]{:S(2)}, u32[]{:S(2)}) %all-to-all-start.2) | async-done | bytes 1032224 | tf_op jit(solution)/shard_map/all_to_all | solution.py:519
  (351 shorter events, 303.8 us)
Async XLA Ops:
  7.2 257.4 %all-gather.5.cloned.1.call-start = ((), (), s32[]{:S(2)}) async-start(), calls=%async_computation.7 | async-start | bytes 4644864 | tf_op jit(solution)/shard_map/all_gather | solution.py:479
  23.8 240.8 %all-gather.3.cloned.1.call-start = ((), (), s32[]{:S(2)}) async-start(), calls=%async_computation.6 | async-start | bytes 9289728 | tf_op jit(solution)/shard_map/all_gather | solution.py:479
  38.6 679.2 %reduce-scatter.4.cloned.1.call-start = ((), (), s32[]{:S(2)}) async-start(), calls=%async_computation.8 | async-start | bytes 2580480 | tf_op jit(solution)/shard_map/reduce_scatter | solution.py:503
  74.9 28.4 %collective-permute-start.11 = (bf16[4,68,1152]{2,0,1:T(4,128)(2,1)S(1)}, bf16[4,68,1152]{2,0,1:T(4,128)(2,1)S(1)}, u32[]{:S(2)}, u32[]{:S(2)}) collective-permute-start(bf16[4,68,1152]{2,0,1:T(4,128)(2,1)S(1)} %copy.186), channel_id=1, source_target_pairs={{0,1},{1,0},{2,3},{3,2},{4,5},{5,4},{6,7},{7,6},{8,9},{9,8},{10,11... | collective-permute-start | bytes 1880072 | tf_op jit(solution)/shard_map/ppermute | solution.py:453
  77.6 25.8 %collective-permute-start.12 = (bf16[4,68,1152]{2,0,1:T(4,128)(2,1)S(1)}, bf16[4,68,1152]{2,0,1:T(4,128)(2,1)S(1)}, u32[]{:S(2)}, u32[]{:S(2)}) collective-permute-start(bf16[4,68,1152]{2,0,1:T(4,128)(2,1)S(1)} %copy.186), channel_id=1, source_target_pairs={{0,17},{1,16},{16,1},{17,0},{2,19},{3,18},{18,3},{19,2},{4,21},{5,... | collective-permute-start | bytes 1880072 | tf_op jit(solution)/shard_map/ppermute | solution.py:472
  79.1 26.8 %collective-permute-start.6 = (bf16[16,40,640]{2,1,0:T(8,128)(2,1)S(1)}, bf16[16,40,640]{2,1,0:T(8,128)(2,1)S(1)}, u32[]{:S(2)}, u32[]{:S(2)}) collective-permute-start(bf16[16,40,640]{2,1,0:T(8,128)(2,1)S(1)} %constant_dynamic-update-slice_fusion.own_ref), channel_id=1, source_target_pairs={{0,8},{8,0},{1,9},{9,1},{2,10},{10,2},{3,11},{11,3},{4,12},{12,4},... | collective-permute-start | bytes 2457608 | tf_op jit(solution)/shard_map/ppermute | solution.py:453
  105.8 75.8 %collective-permute-start.13 = (bf16[16,68,1152]{2,0,1:T(8,128)(2,1)}, bf16[16,68,1152]{2,0,1:T(8,128)(2,1)}, u32[]{:S(2)}, u32[]{:S(2)}) collective-permute-start(bf16[16,68,1152]{2,0,1:T(8,128)(2,1)} %copy.192), channel_id=1, source_target_pairs={{0,8},{8,0},{1,9},{9,1},{2,10},{10,2},{3,11},{11,3},{4,12},{12,4},... | collective-permute-start | bytes 7520264 | tf_op jit(solution)/shard_map/ppermute | solution.py:453
  123.5 30.7 %collective-permute-start.14 = (bf16[4,128,512]{2,1,0:T(8,128)(2,1)}, bf16[4,128,512]{2,1,0:T(8,128)(2,1)S(1)}, u32[]{:S(2)}, u32[]{:S(2)}) collective-permute-start(bf16[4,128,512]{2,1,0:T(8,128)(2,1)} %get-tuple-element.84.refs_12_.refs_15_), channel_id=1, source_target_pairs={{0,2},{2,4},{4,6},{1,3},{3,5},{5,7},{8,10},{10,12},{12,14},{9,11},... | collective-permute-start | bytes 1572872 | tf_op jit(solution)/shard_map/ppermute | solution.py:458
  235.6 25.1 %collective-permute-start.20 = (bf16[512,1152]{1,0:T(8,128)(2,1)S(1)}, bf16[512,1152]{1,0:T(8,128)(2,1)S(1)}, u32[]{:S(2)}, u32[]{:S(2)}) collective-permute-start(bf16[512,1152]{1,0:T(8,128)(2,1)S(1)} %pad_maximum_fusion.2), channel_id=1, source_target_pairs={{0,1},{1,0},{2,3},{3,2},{4,5},{5,4},{6,7},{7,6},{8,9},{9,8},{10,11... | collective-permute-start | bytes 3538952 | tf_op jit(solution)/shard_map/ppermute | solution.py:453
  236.2 25.0 %collective-permute-start.21 = (bf16[512,1152]{1,0:T(8,128)(2,1)S(1)}, bf16[512,1152]{1,0:T(8,128)(2,1)S(1)}, u32[]{:S(2)}, u32[]{:S(2)}) collective-permute-start(bf16[512,1152]{1,0:T(8,128)(2,1)S(1)} %pad_maximum_fusion.3), channel_id=1, source_target_pairs={{0,16},{16,0},{1,17},{17,1},{2,18},{18,2},{3,19},{19,3},{4,20},{20... | collective-permute-start | bytes 3538952 | tf_op jit(solution)/shard_map/ppermute | solution.py:453
  303.0 25.2 %collective-permute-start.22 = (bf16[512,1152]{1,0:T(8,128)(2,1)S(1)}, bf16[512,1152]{1,0:T(8,128)(2,1)S(1)}, u32[]{:S(2)}, u32[]{:S(2)}) collective-permute-start(bf16[512,1152]{1,0:T(8,128)(2,1)S(1)} %get-tuple-element.174), channel_id=1, source_target_pairs={{0,1},{1,0},{2,3},{3,2},{4,5},{5,4},{6,7},{7,6},{8,9},{9,8},{10,11... | collective-permute-start | bytes 3538952 | tf_op jit(solution)/shard_map/ppermute | solution.py:453
  304.3 25.8 %collective-permute-start.23 = (bf16[512,1152]{1,0:T(8,128)(2,1)S(1)}, bf16[512,1152]{1,0:T(8,128)(2,1)S(1)}, u32[]{:S(2)}, u32[]{:S(2)}) collective-permute-start(bf16[512,1152]{1,0:T(8,128)(2,1)S(1)} %get-tuple-element.173), channel_id=1, source_target_pairs={{0,16},{16,0},{1,17},{17,1},{2,18},{18,2},{3,19},{19,3},{4,20},{20... | collective-permute-start | bytes 3538952 | tf_op jit(solution)/shard_map/ppermute | solution.py:453
  465.2 26.8 %collective-permute-start.30 = (bf16[512,1152]{1,0:T(8,128)(2,1)}, bf16[512,1152]{1,0:T(8,128)(2,1)}, u32[]{:S(2)}, u32[]{:S(2)}) collective-permute-start(bf16[512,1152]{1,0:T(8,128)(2,1)} %get-tuple-element.168), channel_id=1, source_target_pairs={{0,1},{1,0},{2,3},{3,2},{4,5},{5,4},{6,7},{7,6},{8,9},{9,8},{10,11... | collective-permute-start | bytes 3538952 | tf_op jit(solution)/shard_map/ppermute | solution.py:453
  466.1 26.6 %collective-permute-start.31 = (bf16[512,1152]{1,0:T(8,128)(2,1)}, bf16[512,1152]{1,0:T(8,128)(2,1)}, u32[]{:S(2)}, u32[]{:S(2)}) collective-permute-start(bf16[512,1152]{1,0:T(8,128)(2,1)} %get-tuple-element.167), channel_id=1, source_target_pairs={{0,16},{16,0},{1,17},{17,1},{2,18},{18,2},{3,19},{19,3},{4,20},{20... | collective-permute-start | bytes 3538952 | tf_op jit(solution)/shard_map/ppermute | solution.py:453
  468.5 250.4 %reduce-scatter.6.cloned.1.call-start = ((), (), s32[]{:S(2)}) async-start(), calls=%async_computation.9 | async-start | bytes 2580480 | tf_op jit(solution)/shard_map/reduce_scatter | solution.py:503
  472.5 58.2 %collective-permute-start.46 = (bf16[2,4,72,1792]{3,2,0,1:T(8,128)(2,1)}, bf16[2,4,72,1792]{3,2,0,1:T(8,128)(2,1)S(1)}, u32[]{:S(2)}, u32[]{:S(2)}) collective-permute-start(bf16[2,4,72,1792]{3,2,0,1:T(8,128)(2,1)} %bitcast.138), channel_id=1, source_target_pairs={{0,8},{8,0},{1,9},{9,1},{2,10},{10,2},{3,11},{11,3},{4,12},{12,4},... | collective-permute-start | bytes 6193160 | tf_op jit(solution)/shard_map/ppermute | solution.py:453
  529.7 33.1 %collective-permute-start.34 = (bf16[4,128,512]{2,1,0:T(8,128)(2,1)}, bf16[4,128,512]{2,1,0:T(8,128)(2,1)S(1)}, u32[]{:S(2)}, u32[]{:S(2)}) collective-permute-start(bf16[4,128,512]{2,1,0:T(8,128)(2,1)} %get-tuple-element.125), channel_id=1, source_target_pairs={{0,1},{1,0},{2,3},{3,2},{4,5},{5,4},{6,7},{7,6},{8,9},{9,8},{10,11... | collective-permute-start | bytes 1572872 | tf_op jit(solution)/shard_map/ppermute | solution.py:453
  532.5 194.9 %reduce-scatter.8.cloned.1.call-start = ((), (), s32[]{:S(2)}) async-start(), calls=%async_computation.10 | async-start | bytes 2580480 | tf_op jit(solution)/shard_map/reduce_scatter | solution.py:503
  543.9 34.4 %collective-permute-start.36 = (bf16[4,128,512]{2,1,0:T(8,128)(2,1)S(1)}, bf16[4,128,512]{2,1,0:T(8,128)(2,1)S(1)}, u32[]{:S(2)}, u32[]{:S(2)}) collective-permute-start(bf16[4,128,512]{2,1,0:T(8,128)(2,1)S(1)} %fusion.16), channel_id=1, source_target_pairs={{2,0},{4,2},{6,4},{3,1},{5,3},{7,5},{10,8},{12,10},{14,12},{11,9},... | collective-permute-start | bytes 1572872 | tf_op jit(solution)/shard_map/ppermute | solution.py:458
  562.8 64.0 %collective-permute-start.47 = (bf16[1,4,224,1152]{3,2,1,0:T(8,128)(2,1)}, bf16[1,4,224,1152]{3,2,1,0:T(8,128)(2,1)}, u32[]{:S(2)}, u32[]{:S(2)}) collective-permute-start(bf16[1,4,224,1152]{3,2,1,0:T(8,128)(2,1)} %dynamic-slice_bitcast_fusion), channel_id=1, source_target_pairs={{0,8},{8,0},{1,9},{9,1},{2,10},{10,2},{3,11},{11,3},{4,12},{12,4},... | collective-permute-start | bytes 6193160 | tf_op jit(solution)/shard_map/ppermute | solution.py:453
  600.9 42.0 %collective-permute-start.38 = (bf16[2,4,2,68,1152]{4,1,3,2,0:T(4,128)(2,1)}, bf16[2,4,2,68,1152]{4,1,3,2,0:T(4,128)(2,1)}, u32[]{:S(2)}, u32[]{:S(2)}) collective-permute-start(bf16[2,4,2,68,1152]{4,1,3,2,0:T(4,128)(2,1)} %copy.200), channel_id=1, source_target_pairs={{0,8},{8,0},{1,9},{9,1},{2,10},{10,2},{3,11},{11,3},{4,12},{12,4},... | collective-permute-start | bytes 7520264 | tf_op jit(solution)/shard_map/ppermute | solution.py:453
  633.3 50.2 %all-to-all-start.1 = ((bf16[16,36,640]{2,1,0:T(8,128)(2,1)}), bf16[16,36,640]{2,1,0:T(8,128)(2,1)}, u32[]{:S(2)}, u32[]{:S(2)}) async-start(bf16[16,36,640]{2,1,0:T(8,128)(2,1)} %bitcast.161), calls=%async_computation.1 | async-start | bytes 1638400 | tf_op jit(solution)/shard_map/all_to_all | solution.py:513
  647.0 38.5 %collective-permute-start.39 = (bf16[4,2,68,1152]{3,0,2,1:T(4,128)(2,1)S(1)}, bf16[4,2,68,1152]{3,0,2,1:T(4,128)(2,1)S(1)}, u32[]{:S(2)}, u32[]{:S(2)}) collective-permute-start(bf16[4,2,68,1152]{3,0,2,1:T(4,128)(2,1)S(1)} %copy.202), channel_id=1, source_target_pairs={{0,16},{16,0},{1,17},{17,1},{2,18},{18,2},{3,19},{19,3},{4,20},{20... | collective-permute-start | bytes 3760136 | tf_op jit(solution)/shard_map/ppermute | solution.py:453
  691.2 24.7 %collective-permute-start.41 = (bf16[2,68,1152]{2,1,0:T(8,128)(2,1)S(1)}, bf16[2,68,1152]{2,1,0:T(8,128)(2,1)S(1)}, u32[]{:S(2)}, u32[]{:S(2)}) collective-permute-start(bf16[2,68,1152]{2,1,0:T(8,128)(2,1)S(1)} %get-tuple-element.183), channel_id=1, source_target_pairs={{0,4},{2,6},{4,0},{6,2},{1,5},{3,7},{5,1},{7,3},{8,12},{10,14},{12... | collective-permute-start | bytes 940040 | tf_op jit(solution)/shard_map/ppermute | solution.py:462
  (69 other events, 801.9 us)
Sparse Core Ops, SparseCore 0:
  9.6 65.6 all-gather.4
  77.5 85.3 all-gather.2
  468.7 44.6 reduce-scatter.3
  532.7 61.4 reduce-scatter.5
  631.0 63.0 reduce-scatter.7

commit v3 on v2

--- a/solution.py
+++ b/solution.py
@@ -119,7 +119,7 @@
         kv_body,
         (rows,),
         [rows_of(length, width), whole(*wkv.shape), whole(*gains.shape), whole(*heads.shape)]
-        + [rows_of(length, HALF)] * 2,
+        + [whole(length, HALF)] * 2,
         [rows_of(length, width), rows_of(length, HEAD), row_block(length, 2 * HEAD)],
         [shaped(count, width, dtype=BF16), shaped(count, HEAD), shaped(rows, length, 2 * HEAD, dtype=BF16)],
         2 * count * width * 2 * HEAD,
@@ -135,18 +135,28 @@
     return jnp.concatenate([array[h * part : (h + 1) * part] for h in range(HEADS)], axis=1)
 
 
-def probs_of(query, keys, segq_ref, posq_ref, segk_ref, posk_ref):
-    allowed = (segq_ref[...] == segk_ref[0]) & (posk_ref[...] <= posq_ref[...])
+def probs_of(links, query, keys, own_ref, seg_ref):
+    length = own_ref.shape[0]
+    bases = links.window_bases(length)
+    here = links.position(length)
+    step = lax.broadcasted_iota(jnp.int32, (1, length), 1)
+    segs, later = [], []
+    for base in bases:
+        row = seg_ref[0, pl.ds(jnp.maximum(base, 0) // length, 1), :]
+        segs.append(jnp.where(base >= 0, row, -1.0))
+        later.append(base - here + step)
+    own_step = lax.broadcasted_iota(jnp.int32, (length, 1), 0)
+    allowed = (own_ref[...] == jnp.concatenate(segs, axis=1)) & (jnp.concatenate(later, axis=1) <= own_step)
     allowed = jnp.concatenate([allowed.astype(F32)] * HEADS, axis=0) > 0.5
     scores = jnp.where(allowed, mm_t(query, keys) * SCORE_SCALE, NEG_FILL)
     powers = jnp.exp(scores - jnp.max(scores, axis=-1, keepdims=True))
     return powers / jnp.sum(powers, axis=-1, keepdims=True)
 
 
-def attend_body(blocks, *refs):
+def attend_body(links, blocks, *refs):
     (h_ref, tok_ref, wq_ref, wo_ref, gains_ref, head_ref, cos_ref, sin_ref) = refs[:8]
-    masks, kv_refs = refs[8:12], refs[12 : 12 + blocks]
-    qproj_ref, query_ref, mixed_ref, attn_ref, resid_ref, hffn_ref = refs[12 + blocks :]
+    masks, kv_refs = refs[8:10], refs[10 : 10 + blocks]
+    qproj_ref, query_ref, mixed_ref, attn_ref, resid_ref, hffn_ref = refs[10 + blocks :]
     proj = mm(h_ref[...], wq_ref[...])
     qproj_ref[...] = proj
     cosine, sine = cos_ref[...], sin_ref[...]
@@ -157,7 +167,7 @@
     query_ref[...] = jnp.concatenate(query, axis=1)
     keys = jnp.concatenate([one[0, :, :HEAD] for one in kv_refs], axis=0)
     values = jnp.concatenate([one[0, :, HEAD:] for one in kv_refs], axis=0)
-    probs = probs_of(jnp.concatenate(query, axis=0), keys, *masks).astype(BF16)
+    probs = probs_of(links, jnp.concatenate(query, axis=0), keys, *masks).astype(BF16)
     mixed = by_lane(mm(probs, values).astype(BF16))
     mixed_ref[...] = mixed
     attn = mm(mixed, wo_ref[...])
@@ -167,21 +177,22 @@
     hffn_ref[...] = (resid * inv_rms(resid) * gains_ref[PRE_FFN : PRE_FFN + 1]).astype(BF16)
 
 
-def mask_specs(length, window):
-    return [rows_of(length, 1), whole(length, 1), row_block(1, window), whole(1, window)]
-
-
-def attend(rows, length, h, tokens, wq, wo, gains, heads, cosine, sine, masks, kv):
+def mask_specs(masks):
+    own, segs = masks
+    return [rows_of(own.shape[0] // segs.shape[0], 1), row_block(*segs.shape[1:])]
+
+
+def attend(links, rows, length, h, tokens, wq, wo, gains, heads, cosine, sine, masks, kv):
     count, width = tokens.shape
     wide = HEADS * HEAD
     window = len(kv) * length
     return call(
-        functools.partial(attend_body, len(kv)),
+        functools.partial(attend_body, links, len(kv)),
         (rows,),
         [rows_of(length, width)] * 2
         + [whole(*one.shape) for one in (wq, wo, gains, heads)]
-        + [rows_of(length, HALF)] * 2
-        + mask_specs(length, window)
+        + [whole(length, HALF)] * 2
+        + mask_specs(masks)
         + [row_block(length, 2 * HEAD)] * len(kv),
         [rows_of(length, wide)] * 3 + [rows_of(length, width)] * 3,
         [
@@ -196,11 +207,11 @@
     )(h, tokens, wq, wo, gains, heads, cosine, sine, *masks, *kv)
 
 
-def attend_back_body(blocks, *refs):
+def attend_back_body(links, blocks, *refs):
     (dh_ref, cot_ref, resid_ref, attn_ref, qproj_ref, query_ref, wo_ref, gains_ref, head_ref, cos_ref, sin_ref) = refs[:11]
-    masks, kv_refs = refs[11:15], refs[15 : 15 + blocks]
-    dres_ref, dattn_ref, dq_ref, sums_ref, head_sums_ref = refs[15 + blocks : 20 + blocks]
-    term_refs = refs[20 + blocks :]
+    masks, kv_refs = refs[11:13], refs[13 : 13 + blocks]
+    dres_ref, dattn_ref, dq_ref, sums_ref, head_sums_ref = refs[13 + blocks : 18 + blocks]
+    term_refs = refs[18 + blocks :]
     d_norm, pre_terms = rms_back(resid_ref[...], gains_ref[PRE_FFN : PRE_FFN + 1], dh_ref[...])
     d_res = cot_ref[...].astype(F32) + d_norm
     dres_ref[...] = d_res
@@ -211,7 +222,7 @@
     query = by_head(query_ref[...])
     keys = jnp.concatenate([one[0, :, :HEAD] for one in kv_refs], axis=0)
     values = jnp.concatenate([one[0, :, HEAD:] for one in kv_refs], axis=0)
-    probs = probs_of(query, keys, *masks)
+    probs = probs_of(links, query, keys, *masks)
     d_probs = mm_t(d_mixed, values)
     d_scores = (probs * (d_probs - jnp.sum(d_probs * probs, axis=-1, keepdims=True))).astype(BF16)
     key_terms = t_mm(d_scores, query) * SCORE_SCALE
@@ -241,18 +252,18 @@
     head_sums_ref[0:1] += head_sum
 
 
-def attend_back(rows, length, dh, cot, resid, attn, qproj, query, wo, gains, heads, cosine, sine, masks, kv, kinds):
+def attend_back(links, rows, length, dh, cot, resid, attn, qproj, query, wo, gains, heads, cosine, sine, masks, kv, kinds):
     count, width = dh.shape
     wide = HEADS * HEAD
     window = len(kv) * length
     return call(
-        functools.partial(attend_back_body, len(kv)),
+        functools.partial(attend_back_body, links, len(kv)),
         (rows,),
         [rows_of(length, width)] * 4
         + [rows_of(length, wide)] * 2
         + [whole(*one.shape) for one in (wo, gains, heads)]
-        + [rows_of(length, HALF)] * 2
-        + mask_specs(length, window)
+        + [whole(length, HALF)] * 2
+        + mask_specs(masks)
         + [row_block(length, 2 * HEAD)] * len(kv),
         [rows_of(length, width)] * 2
         + [rows_of(length, wide), whole(8, width), whole(8, HEAD)]
@@ -298,7 +309,7 @@
         [row_block(length, 2 * HEAD), rows_of(length, HEAD), rows_of(length, wide)]
         + [rows_of(length, width)] * 2
         + [whole(*one.shape) for one in (wq, wkv, gains, heads)]
-        + [rows_of(length, HALF)] * 2,
+        + [whole(length, HALF)] * 2,
         [rows_of(length, 2 * HEAD), rows_of(length, width), whole(8, width), whole(8, HEAD)],
         [shaped(count, 2 * HEAD, dtype=BF16), shaped(count, width, dtype=BF16), shaped(8, width), shaped(8, HEAD)],
         2 * count * width * (wide + 2 * HEAD),
@@ -362,24 +373,100 @@
     )(d, turn, act, pair, down)
 
 
-def grads_body(left_ref, right_ref, out_ref):
-    out_ref[0] = t_mm(left_ref[...], right_ref[0]).astype(BF16)
-
-
-def weight_grads(left, right, tile):
-    count, rows = left.shape
-    many, _, cols = right.shape
+def put(kept_ref, sent_ref, core, index, value):
+    @pl.when(lax.axis_index("core") == core)
+    def _():
+        kept_ref[index] = value
+
+    @pl.when(lax.axis_index("core") != core)
+    def _():
+        sent_ref[index] = value
+
+
+def grads_body(places, sets, *refs):
+    kept_ref, sent_ref = refs[2 * sets :]
+    total = None
+    for left_ref, right_ref in zip(refs[:sets], refs[sets : 2 * sets], strict=True):
+        term = t_mm(left_ref[...], right_ref[0])
+        total = term if total is None else total + term
+    total = total.astype(BF16)
+    tile = total.shape[0]
+    for k in range(sum(count for _, _, _, count in places) // tile):
+
+        @pl.when(pl.program_id(0) == k)
+        def _(k=k):
+            for core, at, row, count in places:
+                begin, end = max(row, k * tile), min(row + count, (k + 1) * tile)
+                if begin < end:
+                    to = at + begin - row
+                    index = (slice(to, to + end - begin), slice(None))
+                    put(kept_ref, sent_ref, core, index, total[begin - k * tile : end - k * tile])
+
+
+def weight_grads(lefts, rights, which, places):
+    rows, cols = lefts[0].shape[1], rights[0].shape[2]
+    count = sum(one.shape[0] for one in lefts)
+    tile = 384 if rows % 384 == 0 else 256
     return call(
-        grads_body,
-        (many, rows // tile),
-        [
-            pl.BlockSpec((count, tile), lambda k, i: (0, i)),
-            pl.BlockSpec((1, count, cols), lambda k, i: (k, 0, 0)),
-        ],
-        pl.BlockSpec((1, tile, cols), lambda k, i: (k, i, 0)),
-        shaped(many, rows, cols, dtype=BF16),
-        2 * many * count * rows * cols,
-    )(left, right)
+        functools.partial(grads_body, places, len(lefts)),
+        (rows // tile,),
+        [pl.BlockSpec((one.shape[0], tile), lambda i: (0, i)) for one in lefts]
+        + [pl.BlockSpec((1,) + one.shape[1:], lambda i: (which, 0, 0)) for one in rights],
+        [whole(rows // 2, cols)] * 2,
+        [shaped(rows // 2, cols, dtype=BF16)] * 2,
+        2 * count * rows * cols,
+    )(*lefts, *rights)
+
+
+def outer_body(order, shards, mixed_ref, dattn_ref, h_ref, dq_ref, kept_ref, sent_ref):
+    lanes = kept_ref.shape[2]
+    at = 0
+    for rows, left, right in ((shards[0], mixed_ref, dattn_ref), (shards[1], h_ref, dq_ref)):
+        total = t_mm(left[...], right[...]).astype(BF16)
+        wide = total.shape[1]
+        for core, place, number in order:
+            index = (place, slice(at, at + rows), slice(0, wide))
+            put(kept_ref, sent_ref, core, index, total[number * rows : (number + 1) * rows])
+        if wide < lanes:
+            empty = jnp.zeros((kept_ref.shape[0], rows, lanes - wide), BF16)
+            kept_ref[:, at : at + rows, wide:] = empty
+            sent_ref[:, at : at + rows, wide:] = empty
+        at += rows
+
+
+def outer_grads(order, shards, mixed, d_attn, h, d_q):
+    count = mixed.shape[0]
+    shape = (len(order) // 2, sum(shards), max(d_attn.shape[1], d_q.shape[1]))
+    return call(
+        functools.partial(outer_body, order, shards),
+        (1,),
+        [whole(*one.shape) for one in (mixed, d_attn, h, d_q)],
+        [whole(*shape)] * 2,
+        [shaped(*shape, dtype=BF16)] * 2,
+        2 * count * (mixed.shape[1] * d_attn.shape[1] + h.shape[1] * d_q.shape[1]),
+    )(mixed, d_attn, h, d_q)
+
+
+def first_body(order, shard, h_ref, dkv_ref, small_ref, kept_ref, sent_ref):
+    small = small_ref[...].T.astype(BF16)
+    total = t_mm(h_ref[...], dkv_ref[...]).astype(BF16)
+    for core, place, number in order:
+        rows = slice(number * shard, (number + 1) * shard)
+        put(kept_ref, sent_ref, core, (place, slice(None), slice(0, SMALL)), small[rows])
+        put(kept_ref, sent_ref, core, (place, slice(None), slice(SMALL, None)), total[rows])
+
+
+def first_grads(order, shard, h, d_kv, small):
+    count, rows = h.shape
+    shape = (len(order) // 2, shard, d_kv.shape[1] + SMALL)
+    return call(
+        functools.partial(first_body, order, shard),
+        (1,),
+        [whole(*one.shape) for one in (h, d_kv, small)],
+        [whole(*shape)] * 2,
+        [shaped(*shape, dtype=BF16)] * 2,
+        2 * count * rows * d_kv.shape[1],
+    )(h, d_kv, small)
 
 
 def middle_body(ffn_ref, resid_ref, cot_ref, gains_ref, out_ref, dffn_ref, sums_ref):
@@ -412,7 +499,6 @@
     outs, scratch = refs[:-1], refs[-1]
     depth = links.size["z"]
     at_x, at_c, at_z, at_y = (links.index(axis) for axis in AXES)
-    total = scratch.shape[0]
     number = 0
     for x in range(2):
         for core in range(2):
@@ -425,9 +511,23 @@
                     piece = jnp.where(at_c == core, mine, theirs)
                     scratch[number] = piece
                     number += 1
-    for (first, count, lanes), out in zip(parts, outs, strict=True):
+    for part, out in zip(parts, outs, strict=True):
         for k in range(number):
-            out[k * count : (k + 1) * count, :] = scratch[k, first : first + count, :lanes].astype(out.dtype)
+            if len(part) == 4:
+                first, count, at, lanes = part
+                out[k * count : (k + 1) * count, :] = scratch[k, first : first + count, at : at + lanes].astype(out.dtype)
+                continue
+            if len(part) == 3:
+                first, count, lanes = part
+                if k < 2 * depth:
+                    ids = scratch[(at_x * 2 + at_c) * 2 * depth + k]
+                    for row in range(count):
+                        out[row, k : k + 1, :] = ids[first + row : first + row + 1, :lanes]
+                continue
+            row, at, lanes, vectors = part[:4]
+            for v in range(vectors):
+                begin = at + v * lanes
+                out[v : v + 1, k * lanes : (k + 1) * lanes] = scratch[k, row : row + 1, begin : begin + lanes]
 
 
 def placed(links, own, other, parts):
@@ -435,7 +535,14 @@
     number = 2 * slots
     return pl.pallas_call(
         functools.partial(place_body, links, rows, parts),
-        out_shape=[shaped(number * count, wide, dtype=BF16) for _, count, wide in parts],
+        out_shape=[
+            shaped(number * part[1], part[3], dtype=BF16)
+            if len(part) == 4
+            else shaped(part[1], slots // 2, part[2])
+            if len(part) == 3
+            else shaped(8, number * part[2])
+            for part in parts
+        ],
         scratch_shapes=[pltpu.VMEM((number, rows, lanes), F32)],
         compiler_params=pltpu.CompilerParams(vmem_limit_bytes=ROOM),
     )(own, other)
@@ -465,15 +572,49 @@
         first = self.index(axis) == 0
         return jnp.where(first, jnp.stack([own, other]), jnp.stack([other, own]))
 
-    def gather_all(self, array, parts):
-        depth = self.size["z"]
-        along = jnp.stack([array] + [self.turn(array, k) for k in range(1, depth)])
+    def along_z(self, array):
+        return jnp.stack([array] + [self.turn(array, k) for k in range(1, self.size["z"])])
+
+    def across_plane(self, along):
+        if not self.pairs_only:
+            return along
+        across = lax.ppermute(along, PLANE, [(k, 3 - k) for k in range(4)])
+        return jnp.concatenate([along, self.swap(along, "x"), self.swap(along, "y"), across])
+
+    def placed(self, array, own, parts, other=None):
         if self.pairs_only:
-            across = lax.ppermute(along, PLANE, [(k, 3 - k) for k in range(4)])
-            own = jnp.concatenate([along, self.swap(along, "x"), self.swap(along, "y"), across])
-            return placed(self, own, self.swap(own, "core"), parts)
+            other = self.swap(own, "core") if other is None else other
+            return placed(self, own, other, parts)
         full = lax.all_gather(array, AXES, axis=0)
-        return [full[:, at : at + count, :lanes].reshape(-1, lanes) for at, count, lanes in parts]
+        cuts = []
+        for part in parts:
+            if len(part) == 4:
+                r, n, c, w = part
+                cuts.append(full[:, r : r + n, c : c + w].reshape(-1, w))
+            elif len(part) == 3:
+                r, n, w = part
+                blocks = self.size["z"] * self.size["y"]
+                at = (self.index("x") * 2 + self.index("core")) * blocks
+                ids = lax.dynamic_slice_in_dim(full[:, r : r + n, :w], at, blocks)
+                cuts.append(jnp.swapaxes(ids, 0, 1).astype(F32))
+            else:
+                r, c, w, n = part[:4]
+                rows = jnp.swapaxes(full[:, r, c : c + n * w].reshape(-1, n, w), 0, 1).reshape(n, -1)
+                cuts.append(jnp.pad(rows.astype(F32), ((0, 8 - n), (0, 0))))
+        return cuts
+
+    def order(self, axes):
+        found = []
+        counts = [self.size[axis] for axis in AXES]
+        for number in range(math.prod(counts)):
+            at, rest = {}, number
+            for axis, many in zip(AXES[::-1], counts[::-1], strict=True):
+                at[axis], rest = rest % many, rest // many
+            place = 0
+            for axis in axes:
+                place = place * self.size[axis] + at[axis]
+            found.append((at["core"], place, number))
+        return found
 
     def gather_cz(self, array, dim):
         return lax.all_gather(array, ("core", "z"), axis=dim, tiled=True)
@@ -486,6 +627,9 @@
             return (kept.astype(F32) + sent.astype(F32)).astype(array.dtype)
         return lax.psum_scatter(array, axis, scatter_dimension=dim, tiled=False)
 
+    def sum_cores(self, kept, sent):
+        return (kept.astype(F32) + self.swap(sent, "core").astype(F32)).astype(kept.dtype)
+
     def sum_z(self, array, dim):
         depth = self.size["z"]
         z = self.index("z")
@@ -498,19 +642,15 @@
             total = total + self.turn(block(k), k).astype(F32)
         return total
 
-    def sum_cz(self, array):
-        mine = jnp.swapaxes(self.sum_halves(array, "core", 1), 0, 1)
-        return lax.psum_scatter(mine.reshape(-1, array.shape[-1]), "z", scatter_dimension=0, tiled=True)
-
-    def sum_all(self, array):
-        array = self.sum_halves(array, "core", 1)
-        array = self.sum_halves(array, "x", 0)
-        return self.sum_halves(self.sum_z(array, 0).astype(BF16), "y", 0).astype(F32)
+    def sum_z_low(self, array):
+        return lax.psum_scatter(array, "z", scatter_dimension=0, tiled=True)
+
+    def planes(self, array):
+        sx, sy, sz = (self.size[axis] for axis in "xyz")
+        return self.sum_halves(array.reshape((sx, sy, sz) + array.shape[1:]), "x", 0)
 
     def sum_all_small(self, array):
-        array = self.sum_halves(array, "core", 1)
-        sent = array.reshape((-1,) + array.shape[3:])
-        got = lax.all_to_all(sent, ("x", "z", "y"), 0, 0, tiled=True)
+        got = lax.all_to_all(array, ("x", "z", "y"), 0, 0, tiled=True)
         return jnp.sum(got.astype(F32), axis=0)
 
     def exchange(self, array):
@@ -518,91 +658,99 @@
         flat = array.reshape((count,) + array.shape[2:])
         return lax.all_to_all(flat, PLANE, 0, 0, tiled=True).reshape(array.shape)
 
-    def gather_plane(self, rows):
+    def over_plane(self, rows, first, then=None):
         if not self.pairs_only:
-            return lax.all_gather(rows, PLANE, axis=0, tiled=True)
+            return [first(lax.all_gather(rows, PLANE, axis=0, tiled=True))]
         half = rows.shape[0] // 2
         upper, lower = lax.optimization_barrier((rows[:half], rows[half:]))
         near = lax.optimization_barrier((self.swap(upper, "x"), self.swap(lower, "y")))
-        upper = jnp.concatenate([upper, near[0]])
-        lower = jnp.concatenate([lower, near[1]])
+        near = jnp.concatenate([upper, near[0], lower, near[1]])
+        upper, lower, near = lax.optimization_barrier((near[: 2 * half], near[2 * half :], near))
+        upper, lower, done = lax.optimization_barrier((self.swap(upper, "y"), self.swap(lower, "x"), first(near)))
+        return [done, first(jnp.concatenate([upper, lower]))]
+
+    def sum_plane(self, parts, beside=(None, None)):
+        works = [work or (lambda *given: ()) for work in beside]
+        if not self.pairs_only:
+            total = lax.psum_scatter(parts[0], PLANE, scatter_dimension=0, tiled=True).astype(F32)
+            return total, works[1](*works[0]())
+        near, far = parts
+        half = far.shape[0] // 2
+        quarter = half // 2
+        upper, lower = lax.optimization_barrier((far[:half], far[half:]))
+        upper, lower, extra = lax.optimization_barrier((self.swap(upper, "y"), self.swap(lower, "x"), works[0]()))
+        at = [near[k * quarter : (k + 1) * quarter].astype(F32) for k in range(4)]
+        own = (at[0] + upper[:quarter].astype(F32), at[2] + lower[:quarter].astype(F32))
+        upper = (at[1] + upper[quarter:].astype(F32)).astype(BF16)
+        lower = (at[3] + lower[quarter:].astype(F32)).astype(BF16)
         upper, lower = lax.optimization_barrier((upper, lower))
-        far = lax.optimization_barrier((self.swap(upper, "y"), self.swap(lower, "x")))
-        return jnp.concatenate([upper, far[0], lower, far[1]])
-
-    def sum_plane(self, rows):
-        if not self.pairs_only:
-            return lax.psum_scatter(rows, PLANE, scatter_dimension=0, tiled=True).astype(F32)
-        part = rows.shape[0] // 8
-        at = [rows[k * part : (k + 1) * part] for k in range(8)]
-        up, low = lax.optimization_barrier((self.swap(rows[2 * part : 4 * part], "y"), self.swap(rows[6 * part :], "x")))
-        up_far = (at[1].astype(F32) + up[part:].astype(F32)).astype(BF16)
-        low_far = (at[5].astype(F32) + low[part:].astype(F32)).astype(BF16)
-        up_far, low_far = lax.optimization_barrier((up_far, low_far))
-        up_far, low_far = lax.optimization_barrier((self.swap(up_far, "x"), self.swap(low_far, "y")))
-        return jnp.concatenate(
-            [
-                at[0].astype(F32) + up[:part].astype(F32) + up_far.astype(F32),
-                at[4].astype(F32) + low[:part].astype(F32) + low_far.astype(F32),
-            ]
-        )
+        upper, lower, extra = lax.optimization_barrier((self.swap(upper, "x"), self.swap(lower, "y"), works[1](*extra)))
+        return jnp.concatenate([own[0] + upper.astype(F32), own[1] + lower.astype(F32)]), extra
+
+    def position(self, length):
+        return (self.index("z") * self.size["y"] + self.index("y")) * length
 
     def window_bases(self, length):
         z, y, wide = self.index("z"), self.index("y"), self.size["y"]
         span = wide * length
         reach = -(-(DOC_LIMIT - 1) // span)
-        base = z * span + y * length
+        base = self.position(length)
         if wide == 2 and reach == 2:
             cross = jnp.where(y == 0, z * span - length, z * span)
             return [base, base - span, base - 2 * span, cross, cross - span]
         return [(z - k) * span + j * length for k in range(reach + 1) for j in range(wide)]
 
-    def window(self, array, length):
+    def window(self, array, length, beside):
         wide = self.size["y"]
         reach = -(-(DOC_LIMIT - 1) // (wide * length))
         if wide == 2 and reach == 2:
             first = self.index("y") == 0
-            one = self.shift(array, 1)
-            two = self.shift(one, 1)
+            one, extra = lax.optimization_barrier((self.shift(array, 1), beside[0]()))
             near = self.swap(jnp.where(first, array, one), "y")
+            two, near, extra = lax.optimization_barrier((self.shift(one, 1), near, beside[1](extra)))
             far = self.swap(jnp.where(first, one, two), "y")
-            return [array, one, two, near, far]
+            return [array, one, two, near, far], extra
         along = [lax.all_gather(array, "y", axis=0)]
         for _ in range(reach):
             along.append(self.shift(along[-1], 1))
-        return [level[j] for level in along for j in range(wide)]
+        return [level[j] for level in along for j in range(wide)], beside[1](beside[0]())
 
     def window_kinds(self, length):
         if self.size["y"] == 2 and 2 * length * 2 >= DOC_LIMIT - 1 > 2 * length:
             return [F32, F32, F32, BF16, BF16]
         return [F32] * len(self.window_bases(length))
 
-    def window_back(self, terms, length):
+    def window_back(self, terms, length, beside=()):
         wide = self.size["y"]
         span = wide * length
         reach = -(-(DOC_LIMIT - 1) // span)
-        y = self.index("y")
-
-        def send(array, axis, step):
-            low = array.astype(BF16)
-            moved = self.swap(low, "y") if axis == "y" else self.shift(low, step)
-            return moved.astype(F32)
+        results = []
+
+        def follow(*arrays):
+            if len(results) < len(beside):
+                results.append(beside[len(results)](*(results[-1] if results else ())))
+                *arrays, results[-1] = lax.optimization_barrier((*arrays, results[-1]))
+            return arrays
 
         if wide == 2 and reach == 2:
-            first = y == 0
+            first = self.index("y") == 0
             own, one, two, near, far = terms
-            far = send(far, "y", 0)
-            near = send(near, "y", 0)
-            two = two + jnp.where(first, 0.0, far)
-            one = one + jnp.where(first, far, near)
+            (far,) = follow(self.swap(far, "y"))
+            two = (two + jnp.where(first, 0.0, far.astype(F32))).astype(BF16)
+            two, near = follow(self.shift(two, -1), self.swap(near, "y"))
+            near = near.astype(F32)
+            one = (one + jnp.where(first, far.astype(F32), near) + two.astype(F32)).astype(BF16)
             own = own + jnp.where(first, near, 0.0)
-            one = one + send(two, "z", -1)
-            return own + send(one, "z", -1)
+            (own,) = follow(own + self.shift(one, -1).astype(F32))
+            return own, results
         total = None
         for k in range(reach, -1, -1):
             level = jnp.stack(terms[k * wide : (k + 1) * wide])
-            total = level if total is None else level + send(total, "z", -1)
-        return lax.psum_scatter(total.astype(BF16), "y", scatter_dimension=0, tiled=False).astype(F32)
+            total = level if total is None else level + self.shift(total.astype(BF16), -1).astype(F32)
+        total = lax.psum_scatter(total.astype(BF16), "y", scatter_dimension=0, tiled=False).astype(F32)
+        for _ in beside:
+            (total,) = follow(total)
+        return total, results
 
 
 def on_device(
@@ -637,98 +785,137 @@
     tokens_flat = tokens.reshape(count, width)
     cot_flat = cotangent.reshape(count, width)
 
+    step = jnp.arange(length, dtype=jnp.int32)
+    pos_own = links.position(length) + step
+    cosine, sine = rope_tables(pos_own)
+
+    lanes = 2 * HEAD + SMALL
+    vectors = jnp.concatenate([g_in, g_post_attn, g_pre_ffn, g_post_ffn, g_query, g_key])
+    vectors = lax.optimization_barrier(jnp.pad(vectors, (0, 2 * HEAD - vectors.shape[0])))[None]
+    seg_rows = jnp.pad(segment_ids.astype(F32), ((0, 0), (0, 2 * HEAD - length)))
+    kv_shard = jnp.concatenate([jnp.concatenate([w_key, w_value], axis=1), seg_rows, vectors]).astype(BF16)
+    own_ids = segment_ids.astype(F32).reshape(count, 1)
+    kv_shard, own_ids, w_gate, w_up, w_down, w_query, w_out = lax.optimization_barrier(
+        (kv_shard, own_ids, w_gate, w_up, w_down, w_query, w_out)
+    )
+    kv_along = links.along_z(kv_shard)
+    full_down = links.gather_cz(jnp.pad(w_down.astype(BF16), ((0, chunk - hidden_shard), (0, 0))), 0)
+
     def columns(weight):
         split = weight.astype(BF16).reshape(shard, sx, sc, sz, sy, hidden_shard)
         split = jnp.pad(split, ((0, 0),) * 5 + ((0, chunk - hidden_shard),))
         return jnp.transpose(split, (1, 4, 0, 2, 3, 5)).reshape(sx, sy, shard, units)
 
     pair = jnp.stack([columns(w_gate), columns(w_up)], axis=2)
-    pair = jnp.transpose(links.exchange(pair), (2, 0, 1, 3, 4)).reshape(2 * sx, sy * shard, units)
-    full_pair = links.gather_cz(pair, 1).reshape(2, width, units)
-    full_down = links.gather_cz(jnp.pad(w_down.astype(BF16), ((0, chunk - hidden_shard), (0, 0))), 0)
-
-    lanes = 2 * HEAD + SMALL
-    seg_row = jnp.pad(segment_ids.astype(BF16), ((0, 0), (0, lanes - length)))
-    gain_columns = jnp.stack([g_in, g_post_attn, g_pre_ffn, g_post_ffn], axis=1)
-    head_columns = jnp.pad(jnp.stack([g_query, g_key], axis=1), ((0, shard - head_shard), (0, 0)))
-    kv_shard = jnp.concatenate(
-        [gain_columns, head_columns, jnp.zeros((shard, SMALL - 6), F32), w_key, w_value], axis=1
-    ).astype(BF16)
-    first, seg_all = links.gather_all(
-        jnp.concatenate([kv_shard, seg_row]), ((0, shard, lanes), (shard, rows, length))
-    )
-    full_kv = first[:, SMALL:]
-    small = jnp.transpose(first[:, :SMALL]).astype(F32)
-    gains = small[:8]
-    heads = jnp.pad(small[4:6].reshape(2, parts, shard)[..., :head_shard].reshape(2, HEAD), ((0, 6), (0, 0)))
-    seg_all = seg_all.reshape(sx, sc, sz, sy, rows, length)
-    seg_all = lax.dynamic_slice(
-        seg_all, (links.index("x"), links.index("core"), 0, 0, 0, 0), (1, 1, sz, sy, rows, length)
-    )
-    seg_flat = jnp.transpose(seg_all[0, 0], (2, 0, 1, 3)).reshape(rows, -1).astype(jnp.int32)
-    bases = links.window_bases(length)
-    seg_window = jnp.concatenate(
-        [lax.dynamic_slice_in_dim(seg_flat, jnp.maximum(base, 0), length, 1) for base in bases], axis=1
-    )
-    step = jnp.arange(length, dtype=jnp.int32)
-    pos_window = jnp.concatenate([base + step for base in bases])
-    pos_own = links.index("z") * sy * length + links.index("y") * length + step
-    seg_window = jnp.where((pos_window >= 0)[None], seg_window, -1)
-    allowed = (segment_ids[:, :, None] == seg_window[:, None, :]) & (pos_window[None, None, :] <= pos_own[None, :, None])
-    positions = jnp.sum(allowed.astype(jnp.int32), axis=2) - 1
-    cosine, sine = rope_tables(positions.reshape(count))
-    masks = (segment_ids.reshape(count, 1), pos_own[:, None], seg_window[:, None, :], pos_window[None])
-
     wide = max(width, HEADS * HEAD)
     q_shard = jnp.pad(w_query.astype(BF16), ((0, 0), (0, wide - HEADS * HEAD)))
     o_shard = jnp.pad(w_out.astype(BF16), ((0, 0), (0, wide - width)))
     out_shard = w_out.shape[0]
-    full_out, full_query = links.gather_all(
-        jnp.concatenate([o_shard, q_shard]), ((0, out_shard, width), (out_shard, shard, HEADS * HEAD))
-    )
-
+    qo_shard = jnp.concatenate([o_shard, q_shard])
+    pair, qo_shard, kv_along = lax.optimization_barrier((pair, qo_shard, kv_along))
+    pair = jnp.transpose(links.exchange(pair), (2, 0, 1, 3, 4)).reshape(2 * sx, sy * shard, units)
+    kv_own, pair, qo_shard = lax.optimization_barrier((links.across_plane(kv_along), pair, qo_shard))
+    full_kv, gains, heads, seg_all = links.placed(
+        kv_shard,
+        kv_own,
+        (
+            (0, shard, 0, 2 * HEAD),
+            (shard + rows, 0, shard, 4, True),
+            (shard + rows, 4 * shard, head_shard, 2, True),
+            (shard, rows, length),
+        ),
+    )
     h_in, k_proj, kv_low = kv_step(rows, length, tokens_flat, full_kv, gains, heads, cosine, sine)
-    kv = links.window(kv_low, length)
+    kv_low, qo_along = lax.optimization_barrier((kv_low, links.along_z(qo_shard)))
+    kv, qo = links.window(
+        kv_low,
+        length,
+        (
+            lambda: (links.across_plane(qo_along),),
+            lambda qo: (qo[0], links.swap(qo[0], "core") if links.pairs_only else qo[0]),
+        ),
+    )
+    masks = (own_ids, seg_all)
+    full_pair = links.gather_cz(pair, 1).reshape(2, width, units)
+    full_out, full_query = links.placed(
+        qo_shard, qo[0], ((0, out_shard, 0, width), (out_shard, shard, 0, HEADS * HEAD)), qo[1]
+    )
+
     q_proj, query, mixed, attn, resid, h_ffn = attend(
-        rows, length, h_in, tokens_flat, full_query, full_out, gains, heads, cosine, sine, masks, kv
-    )
-    h_all = links.gather_plane(h_ffn)
-    hidden, turn, act, ffn_terms = ffn_forward(h_all, full_pair, full_down)
-    ffn = links.sum_plane(ffn_terms)
+        links, rows, length, h_in, tokens_flat, full_query, full_out, gains, heads, cosine, sine, masks, kv
+    )
+    parts_up = links.over_plane(h_ffn, lambda part: (part, *ffn_forward(part, full_pair, full_down)))
+    h_parts, hidden, turn, act, ffn_terms = zip(*parts_up, strict=True)
+    ffn, _ = links.sum_plane(ffn_terms)
     output, d_ffn, sums_ffn = middle(rows, length, ffn, resid, cot_flat, gains)
 
-    d_all = links.gather_plane(d_ffn)
-    d_pair, d_terms = ffn_backward(d_all, turn, act, full_pair, full_down)
-    d_hffn = links.sum_plane(d_terms)
-    grad_down = weight_grads(hidden, d_all[None], units // 7 if units % 7 == 0 else units)
-    grad_down = links.sum_cz(grad_down.reshape(1, sc, sz, chunk, width))[:hidden_shard].astype(F32)
-    grad_pair = weight_grads(h_all, d_pair, 384)
-    sums = jnp.stack([links.sum_cz(grad_pair[k].reshape(sx, sc, sz, sy * shard, units)) for k in range(2)])
-    sums = jnp.transpose(sums.reshape(2, sx, sy, shard, units), (1, 2, 0, 3, 4))
-    got = links.exchange(sums).reshape(sx, sy, 2, shard, sc, sz, chunk)[..., :hidden_shard]
-    got = jnp.transpose(got, (2, 3, 0, 4, 5, 1, 6)).reshape(2, shard, parts * hidden_shard).astype(F32)
+    pending = list(zip(turn, act, strict=True))
+
+    def back(part):
+        return (part, *ffn_backward(part, *pending.pop(0), full_pair, full_down))
+
+    d_parts, d_pairs, d_terms = zip(*links.over_plane(d_ffn, back), strict=True)
+    block = sy * shard
+    places = sorted(
+        (c, (z * sx + x) * block, ((x * sc + c) * sz + z) * block, block)
+        for x in range(sx)
+        for c in range(sc)
+        for z in range(sz)
+    )
+    half = units // 2
+    down_places = [(c, 0, c * half, half) for c in range(sc)]
+
+    def gate_up():
+        grad_gate = weight_grads(h_parts, d_pairs, 0, places)
+        return (links.sum_cores(*grad_gate), *weight_grads(h_parts, d_pairs, 1, places))
+
+    def up_down(half_gate, *grad_up):
+        grad_down = weight_grads(hidden, [part[None] for part in d_parts], 0, down_places)
+        return (half_gate, links.sum_cores(*grad_up), *grad_down)
+
+    d_hffn, (half_gate, half_up, *grad_down) = links.sum_plane(d_terms, (gate_up, up_down))
+
+    def owned(sums):
+        return links.exchange(sums.reshape(sx, sy, shard, units))
+
+    def unpacked(got):
+        got = got.reshape(sx, sy, shard, sc, sz, chunk)[..., :hidden_shard]
+        return jnp.transpose(got, (2, 0, 3, 4, 1, 5)).reshape(shard, parts * hidden_shard).astype(F32)
 
     d_res, d_attn, d_qproj, sums_attn, heads_attn, *terms = attend_back(
-        rows, length, d_hffn, cot_flat, resid, attn, q_proj, query, full_out, gains, heads, cosine, sine, masks, kv,
+        links, rows, length, d_hffn, cot_flat, resid, attn, q_proj, query, full_out, gains, heads, cosine, sine, masks, kv,
         links.window_kinds(length),
     )
-    d_kv = links.window_back(terms, length)
-    grad_out = weight_grads(mixed, d_attn[None], 512)[0]
-    grad_query = weight_grads(h_in, d_qproj[None], 384)[0]
-    wide_q = jnp.pad(grad_query, ((0, 0), (0, wide - HEADS * HEAD))).reshape(sx, sc, sz, sy, shard, wide)
-    wide_o = jnp.pad(grad_out, ((0, 0), (0, wide - width))).reshape(sx, sc, sz, sy, out_shard, wide)
-    second_sum = links.sum_all(jnp.concatenate([wide_o, wide_q], axis=4))
+    d_kv, beside = links.window_back(
+        terms,
+        length,
+        (
+            lambda: (
+                links.sum_cores(*outer_grads(links.order("xyz"), (out_shard, shard), mixed, d_attn, h_in, d_qproj)),
+                links.sum_cores(*grad_down),
+                links.sum_z_low(half_gate),
+            ),
+            lambda second, low, gate: (second, low, owned(gate)),
+            lambda second, low, gate: (links.planes(second), low, unpacked(gate), links.sum_z_low(half_up)),
+        ),
+    )
+    second, low, grad_gate, up = beside[2]
 
     d_kvproj, grad_tokens, sums_in, heads_in = finish(
         rows, length, d_kv, k_proj, d_qproj, tokens_flat, d_res, full_query, full_kv, gains, heads, cosine, sine
     )
-    grad_kv = weight_grads(h_in, d_kvproj[None], 384)[0]
     gain_terms = (sums_ffn + sums_attn + sums_in)[:4]
     head_terms = (heads_attn + heads_in)[:2].reshape(2, parts, head_shard)
     head_terms = jnp.pad(head_terms, ((0, 0), (0, 0), (0, shard - head_shard))).reshape(2, width)
     small_terms = jnp.pad(jnp.concatenate([gain_terms, head_terms]), ((0, SMALL - 6), (0, 0)))
-    first_grad = jnp.concatenate([jnp.transpose(small_terms).astype(BF16), grad_kv], axis=1)
-    first_sum = links.sum_all_small(first_grad.reshape(sx, sc, sz, sy, shard, lanes))
+    first_grad = first_grads(links.order("xzy"), shard, h_in, d_kvproj, small_terms)
+    first_core, second, got_up = lax.optimization_barrier(
+        (links.sum_cores(*first_grad), links.sum_halves(second, "y", 0), owned(up))
+    )
+    first_sum = links.sum_all_small(first_core)
+    second_sum = links.sum_z(second, 0)
+    grad_up = unpacked(got_up)
+    grad_down = links.sum_z_low(low)[:hidden_shard].astype(F32)
     return (
         output.reshape(tokens.shape),
         grad_tokens.reshape(tokens.shape),
@@ -736,8 +923,8 @@
         first_sum[:, SMALL : SMALL + HEAD],
         first_sum[:, SMALL + HEAD :],
         second_sum[:out_shard, :width],
-        got[0],
-        got[1],
+        grad_gate,
+        grad_up,
         grad_down,
         *(first_sum[:, k] for k in range(4)),
         *(first_sum[:head_shard, 4 + k] for k in range(2)),

time: 769 us -> 682 us (0.89)
  waiting for transfers between devices: 321 us -> 249 us
  local copies, waits for them, and re-layouts: 95.9 us -> 54.1 us
  Pallas kernels: 192 us -> 214 us
    ppermute x33, waiting for transfers between devices: 183 us -> 129 us  [swap(): return lax.ppermute(array, axis, SWAP)]
    all_to_all x1, waiting for transfers between devices: 34.6 us -> 0.01 us  [sum_all_small(): got = lax.all_to_all(array, ('x', 'z', 'y'), 0, 0, tiled=True)]
    convert_element_type x12 -> x13, other arithmetic: 7.15 us -> 24.4 us  [the longest x5 13.1 us: sum_cores(): (kept.astype(F32) + self.swap(sent, 'core').astype(F32)).astype(kept.dtype)]
    unnamed x99 -> x56, local copies, waits for them, and re-layouts: 17.7 us -> 3.94 us
    ppermute x4, waiting for transfers between devices: 48.4 us -> 58.9 us  [shift(): return lax.ppermute(array, 'z', pairs)]
    convert_element_type x6 -> x2, other arithmetic: 14.3 us -> 3.8 us  [sum_halves(): return (kept.astype(F32) + sent.astype(F32)).astype(array.dtype)]
    reduce_scatter x3, waiting for transfers between devices: 0.02 us -> 9.75 us  [sum_z_low(): return lax.psum_scatter(array, 'z', scatter_dimension=0, tiled=True)]
    slice x11 -> x4, local copies, waits for them, and re-layouts: 15.3 us -> 6.28 us  [the longest x2 3.61 us: sum_plane(): upper, lower = lax.optimization_barrier((far[:half], far[half:]))]
  transfers between devices with their start and end apart: 56 -> 57, of which waited for: 30 -> 32; matrix products, arithmetic and copies ran while one was open for 15% -> 13% of each run, Pallas kernels for 11% -> 22%
where the time goes in v3:
time: 682 us; the launch traced here: 672 us
  waiting for transfers between devices  249 us (37%)
  Pallas kernels  214 us (31%)
  starting transfers between devices  87.9 us (13%)
  local copies, waits for them, and re-layouts  54.1 us (8%)
  other arithmetic  52.8 us (8%)
  between operations  14.8 us (2%)
    ppermute x33, waiting for transfers between devices, swap(): return lax.ppermute(array, axis, SWAP)  129 us
    ppermute x4, waiting for transfers between devices, shift(): return lax.ppermute(array, 'z', pairs)  58.9 us
    pallas_call x2, Pallas kernels, ffn_backward(): call(functools.partial(down_body, step), (count // tile,), [rows_of(tile,...  49.1 us
    pallas_call x3, Pallas kernels, weight_grads(): call(functools.partial(grads_body, places, len(lefts)), (rows // tile,),...  47.5 us
    pallas_call x2, Pallas kernels, ffn_forward(): call(functools.partial(up_body, step), (count // tile,), [rows_of(tile, w...  42.3 us
    ppermute x9, waiting for transfers between devices, turn(): lax.ppermute(array, 'z', [(i, (i + step) % depth) for i in range(depth)])  33.2 us
    ppermute x33, starting transfers between devices, swap(): return lax.ppermute(array, axis, SWAP)  26.2 us
    ppermute x4, starting transfers between devices, shift(): return lax.ppermute(array, 'z', pairs)  21 us
  transfers between devices with their start and end apart: 57, of which 32 were waited for; matrix products, arithmetic and copies ran while one was open for 13% of the time, Pallas kernels for 22%

profile of v3, /device:TPU:0, one launch (start us, length us, event | category | flops | bytes accessed | tf_op | source)
XLA Modules:
  0.0 672.2 jit_solution(15950319807097360872)
XLA Ops:
  37.3 15.5 %collective-permute-done.3 = bf16[4,41,512]{2,1,0:T(8,128)(2,1)S(1)} collective-permute-done((bf16[4,41,512]{2,1,0:T(8,128)(2,1)S(1)}, bf16[4,41,512]{2,1,0:T(8,128)(2,1)S(1)}, u32[]{:S(2)}, u32[]{:S(2)}) %collective-permute-start.3) | collective-permute-done | bytes 167968 | tf_op jit(solution)/shard_map/ppermute | solution.py:560
  100.5 11.4 %collective-permute-done.12 = bf16[4,68,1152]{2,0,1:T(4,128)(2,1)S(1)} collective-permute-done((bf16[4,68,1152]{2,0,1:T(4,128)(2,1)S(1)}, bf16[4,68,1152]{2,0,1:T(4,128)(2,1)S(1)}, u32[]{:S(2)}, u32[]{:S(2)}) %collective-permute-start.12) | collective-permute-done | bytes 626720 | tf_op jit(solution)/shard_map/ppermute | solution.py:560
  118.0 12.8 %collective-permute-start.14 = (bf16[4,128,512]{2,1,0:T(8,128)(2,1)S(1)}, bf16[4,128,512]{2,1,0:T(8,128)(2,1)S(1)}, u32[]{:S(2)}, u32[]{:S(2)}) collective-permute-start(bf16[4,128,512]{2,1,0:T(8,128)(2,1)S(1)} %collective-permute-done.10.refs_11_.refs_14_), channel_id=1, source_target_pairs={{0,2},{2,4},{4,6},{1,3},{3,5},{5,7},{8,10},{10,12},{12,14},{9,11},... | collective-permute-start | bytes 1572872 | tf_op jit(solution)/shard_map/ppermute | solution.py:565
  131.7 22.3 %collective-permute-done.14.refs_12_.refs_15_ = bf16[4,128,512]{2,1,0:T(8,128)(2,1)S(1)} collective-permute-done((bf16[4,128,512]{2,1,0:T(8,128)(2,1)S(1)}, bf16[4,128,512]{2,1,0:T(8,128)(2,1)S(1)}, u32[]{:S(2)}, u32[]{:S(2)}) %collective-permute-start.14) | collective-permute-done | bytes 524320 | tf_op jit(solution)/shard_map/ppermute | solution.py:565
  169.2 14.9 %shard_map.274 = (f32[512,1024]{1,0:T(8,128)}, bf16[512,1024]{1,0:T(8,128)(2,1)}, bf16[512,1024]{1,0:T(8,128)(2,1)}, f32[512,1152]{1,0:T(8,128)}, f32[512,1152]{1,0:T(8,128)}, /*index=5*/bf16[512,1152]{1,0:T(8,128)(2,1)}) custom-call(bf16[512,1152]{1,0:T(8,128)(2,1)} %get-tuple-element.168.refs_0_.h_ref, bf16[512,1152]{1,0:T(8,128)(2,1)} %bitcast.58, ...), custom_call_target="tpu_custom_call" | custom-call | flops 3758096384 | bytes 20185088 | tf_op jit(solution)/shard_map/pallas_call | solution.py:189
  187.6 11.7 %collective-permute-done.18 = bf16[256,1152]{1,0:T(8,128)(2,1)S(1)} collective-permute-done((bf16[256,1152]{1,0:T(8,128)(2,1)S(1)}, bf16[256,1152]{1,0:T(8,128)(2,1)S(1)}, u32[]{:S(2)}, u32[]{:S(2)}) %collective-permute-start.18) | collective-permute-done | bytes 589856 | tf_op jit(solution)/shard_map/ppermute | solution.py:560
  204.7 21.2 %shard_map.275 = (bf16[1024,1792]{1,0:T(8,128)(2,1)}, bf16[1024,1792]{1,0:T(8,128)(2,1)}, bf16[1024,1792]{1,0:T(8,128)(2,1)}, bf16[1024,1152]{1,0:T(8,128)(2,1)}) custom-call(bf16[1024,1152]{1,0:T(8,128)(2,1)} %pad_maximum_fusion.1.h_ref.refs_0_, bf16[2,1152,1792]{2,1,0:T(8,128)(2,1)} %bitcast.77, bf16[1792,1152]{1,0:T(8,128)(2,1)} %all-gather.5.cloned.1.call-done.down_ref), custom_call_target="tpu_custom_call" | custom-call | flops 12683575296 | bytes 26738688 | tf_op jit(solution)/shard_map/pallas_call | solution.py:343
  230.3 21.1 %shard_map.276 = (bf16[1024,1792]{1,0:T(8,128)(2,1)}, bf16[1024,1792]{1,0:T(8,128)(2,1)}, bf16[1024,1792]{1,0:T(8,128)(2,1)}, bf16[1024,1152]{1,0:T(8,128)(2,1)}) custom-call(bf16[1024,1152]{1,0:T(8,128)(2,1)} %copy-done.16, bf16[2,1152,1792]{2,1,0:T(8,128)(2,1)} %bitcast.78, bf16[1792,1152]{1,0:T(8,128)(2,1)} %all-gather.5.cloned.1.call-done.down_ref), custom_call_target="tpu_custom_call" | custom-call | flops 12683575296 | bytes 26738688 | tf_op jit(solution)/shard_map/pallas_call | solution.py:343
  255.5 22.5 %collective-permute-done.22 = bf16[512,1152]{1,0:T(8,128)(2,1)S(1)} collective-permute-done((bf16[512,1152]{1,0:T(8,128)(2,1)S(1)}, bf16[512,1152]{1,0:T(8,128)(2,1)S(1)}, u32[]{:S(2)}, u32[]{:S(2)}) %collective-permute-start.22) | collective-permute-done | bytes 1179680 | tf_op jit(solution)/shard_map/ppermute | solution.py:560
  302.5 10.0 %collective-permute-done.26 = bf16[256,1152]{1,0:T(8,128)(2,1)S(1)} collective-permute-done((bf16[256,1152]{1,0:T(8,128)(2,1)S(1)}, bf16[256,1152]{1,0:T(8,128)(2,1)S(1)}, u32[]{:S(2)}, u32[]{:S(2)}) %collective-permute-start.26) | collective-permute-done | bytes 589856 | tf_op jit(solution)/shard_map/ppermute | solution.py:560
  318.6 24.4 %shard_map.278 = (bf16[2,1024,1792]{2,1,0:T(8,128)(2,1)}, bf16[1024,1152]{1,0:T(8,128)(2,1)}) custom-call(bf16[1024,1152]{1,0:T(8,128)(2,1)} %pad_maximum_fusion.3.d_ref, bf16[1024,1792]{1,0:T(8,128)(2,1)} %get-tuple-element.219.turn_ref, bf16[1024,1792]{1,0:T(8,128)(2,1)} %get-tuple-element.220.act_ref, bf16[2,1152,1792]{2,1,0:T(8,128)(2,1)} %bitcast.79, ...), custom_call_target="tpu_custom_call" | custom-call | flops 12683575296 | bytes 19398656 | tf_op jit(solution)/shard_map/pallas_call | solution.py:366
  344.8 24.6 %shard_map.279 = (bf16[2,1024,1792]{2,1,0:T(8,128)(2,1)}, bf16[1024,1152]{1,0:T(8,128)(2,1)}) custom-call(bf16[1024,1152]{1,0:T(8,128)(2,1)} %copy-done.17, bf16[1024,1792]{1,0:T(8,128)(2,1)} %get-tuple-element.226.turn_ref, bf16[1024,1792]{1,0:T(8,128)(2,1)} %get-tuple-element.227.act_ref, bf16[2,1152,1792]{2,1,0:T(8,128)(2,1)} %bitcast.80, ...), custom_call_target="tpu_custom_call" | custom-call | flops 12683575296 | bytes 19398656 | tf_op jit(solution)/shard_map/pallas_call | solution.py:366
  369.4 15.4 %shard_map.280 = (bf16[576,1792]{1,0:T(8,128)(2,1)}, bf16[576,1792]{1,0:T(8,128)(2,1)}) custom-call(bf16[1024,1152]{1,0:T(8,128)(2,1)} %pad_maximum_fusion.1.h_ref.refs_0_, bf16[1024,1152]{1,0:T(8,128)(2,1)} %copy-done.16, bf16[2,1024,1792]{2,1,0:T(8,128)(2,1)} %get-tuple-element.232.refs_2_, bf16[2,1024,1792]{2,1,0:T(8,128)(2,1)} %get-tuple-element.233.refs_3_), custom_call_target="tpu_custom_call" | custom-call | flops 8455716864 | bytes 8257536 | tf_op jit(solution)/shard_map/pallas_call | solution.py:410
  389.2 15.5 %shard_map.281 = (bf16[576,1792]{1,0:T(8,128)(2,1)}, bf16[576,1792]{1,0:T(8,128)(2,1)}) custom-call(bf16[1024,1152]{1,0:T(8,128)(2,1)} %pad_maximum_fusion.1.h_ref.refs_0_, bf16[1024,1152]{1,0:T(8,128)(2,1)} %copy-done.16, bf16[2,1024,1792]{2,1,0:T(8,128)(2,1)} %get-tuple-element.232.refs_2_, bf16[2,1024,1792]{2,1,0:T(8,128)(2,1)} %get-tuple-element.233.refs_3_), custom_call_target="tpu_custom_call" | custom-call | flops 8455716864 | bytes 8257536 | tf_op jit(solution)/shard_map/pallas_call | solution.py:410
  415.9 16.6 %shard_map.282 = (bf16[896,1152]{1,0:T(8,128)(2,1)}, bf16[896,1152]{1,0:T(8,128)(2,1)}) custom-call(bf16[1024,1792]{1,0:T(8,128)(2,1)} %get-tuple-element.245.refs_0_, bf16[1024,1792]{1,0:T(8,128)(2,1)} %get-tuple-element.246.refs_1_, bf16[1,1024,1152]{2,1,0:T(8,128)(2,1)} %bitcast.62, bf16[1,1024,1152]{2,1,0:T(8,128)(2,1)} %bitcast.68), custom_call_target="tpu_custom_call" | custom-call | flops 8455716864 | bytes 8257536 | tf_op jit(solution)/shard_map/pallas_call | solution.py:410
  439.3 11.8 %collective-permute-done.33 = bf16[256,1152]{1,0:T(8,128)(2,1)} collective-permute-done((bf16[256,1152]{1,0:T(8,128)(2,1)}, bf16[256,1152]{1,0:T(8,128)(2,1)}, u32[]{:S(2)}, u32[]{:S(2)}) %collective-permute-start.33) | collective-permute-done | bytes 589856 | tf_op jit(solution)/shard_map/ppermute | solution.py:560
  456.0 17.4 %shard_map.283 = (f32[512,1152]{1,0:T(8,128)}, bf16[512,1152]{1,0:T(8,128)(2,1)}, bf16[512,1024]{1,0:T(8,128)(2,1)}, f32[8,1152]{1,0:T(8,128)}, f32[8,256]{1,0:T...) custom-call(f32[512,1152]{1,0:T(8,128)} %pad_maximum_fusion.4.refs_0, ...), custom_call_target="tpu_custom_call" | custom-call | flops 4563402752 | bytes 17653760 | tf_op jit(solution)/shard_map/pallas_call | solution.py:259
  499.9 9.7 %reduce-scatter.4.cloned.1.call-done = bf16[144,1792]{1,0:T(8,128)(2,1)} async-done(((bf16[576,1792]{1,0:T(8,128)(2,1)}), bf16[144,1792]{1,0:T(8,128)(2,1)}) %reduce-scatter.4.cloned.1.call-update) | async-done | bytes 516112 | tf_op jit(solution)/shard_map/reduce_scatter | solution.py:646
  527.2 23.7 %collective-permute-done.39 = bf16[4,128,512]{2,1,0:T(8,128)(2,1)} collective-permute-done((bf16[4,128,512]{2,1,0:T(8,128)(2,1)}, bf16[4,128,512]{2,1,0:T(8,128)(2,1)}, u32[]{:S(2)}, u32[]{:S(2)}) %collective-permute-start.39) | collective-permute-done | bytes 524320 | tf_op jit(solution)/shard_map/ppermute | solution.py:565
  563.8 11.3 %collective-permute-done.41 = bf16[4,128,512]{2,1,0:T(8,128)(2,1)} collective-permute-done((bf16[4,128,512]{2,1,0:T(8,128)(2,1)}, bf16[4,128,512]{2,1,0:T(8,128)(2,1)}, u32[]{:S(2)}, u32[]{:S(2)}) %collective-permute-start.41) | collective-permute-done | bytes 524320 | tf_op jit(solution)/shard_map/ppermute | solution.py:565
  582.9 9.6 %shard_map.285 = (bf16[512,512]{1,0:T(8,128)(2,1)}, bf16[512,1152]{1,0:T(8,128)(2,1)}, f32[8,1152]{1,0:T(8,128)}, f32[8,256]{1,0:T(8,128)}) custom-call(f32[4,128,512]{2,1,0:T(8,128)} %fusion.5.dkv_ref, f32[512,256]{1,0:T(8,128)} %get-tuple-element.279.kproj_ref, bf16[512,1024]{1,0:T(8,128)(2,1)} %get-tuple-element.260.dq_ref, bf16[512,1152]{1,0:T(8,128)(2,1)} %bitcast.59, ...), custom_call_target="tpu_custom_call" | custom-call | flops 1811939328 | bytes 3497984 | tf_op jit(solution)/shard_map/pallas_call | solution.py:306
  615.6 10.4 %all-to-all-start.3 = ((bf16[16,36,640]{2,1,0:T(8,128)(2,1)}), bf16[16,36,640]{2,1,0:T(8,128)(2,1)S(1)}, u32[]{:S(2)}, u32[]{:S(2)}) async-start(bf16[16,36,640]{2,1,0:T(8,128)(2,1)} %add_convert_fusion.4), calls=%async_computation.5 | async-start | bytes 1638400 | tf_op jit(solution)/shard_map/all_to_all | solution.py:653
  636.3 12.1 %collective-permute-done.45 = bf16[68,1152]{1,0:T(8,128)(2,1)S(1)} collective-permute-done((bf16[68,1152]{1,0:T(8,128)(2,1)S(1)}, bf16[68,1152]{1,0:T(8,128)(2,1)S(1)}, u32[]{:S(2)}, u32[]{:S(2)}) %collective-permute-start.45) | collective-permute-done | bytes 156704 | tf_op jit(solution)/shard_map/ppermute | solution.py:569
  648.4 10.5 %collective-permute-done.46 = bf16[68,1152]{1,0:T(8,128)(2,1)S(1)} collective-permute-done((bf16[68,1152]{1,0:T(8,128)(2,1)S(1)}, bf16[68,1152]{1,0:T(8,128)(2,1)S(1)}, u32[]{:S(2)}, u32[]{:S(2)}) %collective-permute-start.46) | collective-permute-done | bytes 156704 | tf_op jit(solution)/shard_map/ppermute | solution.py:569
  (269 shorter events, 280.9 us)
Async XLA Ops:
  7.2 197.5 %all-gather.5.cloned.1.call-start = ((), (), s32[]{:S(2)}) async-start(), calls=%async_computation.8 | async-start | bytes 4644864 | tf_op jit(solution)/shard_map/all_gather | solution.py:620
  30.1 25.8 %all-to-all-start = ((bf16[4,2,36,1792]{3,1,2,0:T(2,128)(2,1)}), bf16[4,2,36,1792]{3,1,2,0:T(2,128)(2,1)S(1)}, u32[]{:S(2)}, u32[]{:S(2)}) async-start(bf16[4,2,36,1792]{3,1,2,0:T(2,128)(2,1)} %bitcast.8), calls=%async_computation | async-start | bytes 2064384 | tf_op jit(solution)/shard_map/all_to_all | solution.py:659
  33.8 170.8 %all-gather.3.cloned.1.call-start = ((), (), s32[]{:S(2)}) async-start(), calls=%async_computation.7 | async-start | bytes 9289728 | tf_op jit(solution)/shard_map/all_gather | solution.py:620
  57.2 452.5 %reduce-scatter.4.cloned.1.call-start = ((), (), s32[]{:S(2)}) async-start(), calls=%async_computation.9 | async-start | bytes 2580480 | tf_op jit(solution)/shard_map/reduce_scatter | solution.py:646
  83.9 28.0 %collective-permute-start.12 = (bf16[4,68,1152]{2,0,1:T(4,128)(2,1)S(1)}, bf16[4,68,1152]{2,0,1:T(4,128)(2,1)S(1)}, u32[]{:S(2)}, u32[]{:S(2)}) collective-permute-start(bf16[4,68,1152]{2,0,1:T(4,128)(2,1)S(1)} %copy.105), channel_id=1, source_target_pairs={{0,1},{1,0},{2,3},{3,2},{4,5},{5,4},{6,7},{7,6},{8,9},{9,8},{10,11... | collective-permute-start | bytes 1880072 | tf_op jit(solution)/shard_map/ppermute | solution.py:560
  84.5 27.5 %collective-permute-start.13 = (bf16[4,68,1152]{2,0,1:T(4,128)(2,1)S(1)}, bf16[4,68,1152]{2,0,1:T(4,128)(2,1)S(1)}, u32[]{:S(2)}, u32[]{:S(2)}) collective-permute-start(bf16[4,68,1152]{2,0,1:T(4,128)(2,1)S(1)} %copy.105), channel_id=1, source_target_pairs={{0,17},{1,16},{16,1},{17,0},{2,19},{3,18},{18,3},{19,2},{4,21},{5,... | collective-permute-start | bytes 1880072 | tf_op jit(solution)/shard_map/ppermute | solution.py:581
  86.8 28.7 %collective-permute-start.10 = (bf16[4,128,512]{2,1,0:T(8,128)(2,1)}, bf16[4,128,512]{2,1,0:T(8,128)(2,1)S(1)}, u32[]{:S(2)}, u32[]{:S(2)}) collective-permute-start(bf16[4,128,512]{2,1,0:T(8,128)(2,1)} %get-tuple-element.171.refs_10_.refs_13_), channel_id=1, source_target_pairs={{0,2},{2,4},{4,6},{1,3},{3,5},{5,7},{8,10},{10,12},{12,14},{9,11},... | collective-permute-start | bytes 1572872 | tf_op jit(solution)/shard_map/ppermute | solution.py:565
  117.3 36.8 %collective-permute-start.16 = (bf16[16,68,1152]{2,0,1:T(8,128)(2,1)}, bf16[16,68,1152]{2,0,1:T(8,128)(2,1)S(1)}, u32[]{:S(2)}, u32[]{:S(2)}) collective-permute-start(bf16[16,68,1152]{2,0,1:T(8,128)(2,1)} %copy.111), channel_id=1, source_target_pairs={{0,8},{8,0},{1,9},{9,1},{2,10},{10,2},{3,11},{11,3},{4,12},{12,4},... | collective-permute-start | bytes 7520264 | tf_op jit(solution)/shard_map/ppermute | solution.py:560
  118.0 36.0 %collective-permute-start.14 = (bf16[4,128,512]{2,1,0:T(8,128)(2,1)S(1)}, bf16[4,128,512]{2,1,0:T(8,128)(2,1)S(1)}, u32[]{:S(2)}, u32[]{:S(2)}) collective-permute-start(bf16[4,128,512]{2,1,0:T(8,128)(2,1)S(1)} %collective-permute-done.10.refs_11_.refs_14_), channel_id=1, source_target_pairs={{0,2},{2,4},{4,6},{1,3},{3,5},{5,7},{8,10},{10,12},{12,14},{9,11},... | collective-permute-start | bytes 1572872 | tf_op jit(solution)/shard_map/ppermute | solution.py:565
  203.0 25.3 %collective-permute-start.20 = (bf16[512,1152]{1,0:T(8,128)(2,1)}, bf16[512,1152]{1,0:T(8,128)(2,1)S(1)}, u32[]{:S(2)}, u32[]{:S(2)}) collective-permute-start(bf16[512,1152]{1,0:T(8,128)(2,1)} %get-tuple-element.188), channel_id=1, source_target_pairs={{0,1},{1,0},{2,3},{3,2},{4,5},{5,4},{6,7},{7,6},{8,9},{9,8},{10,11... | collective-permute-start | bytes 3538952 | tf_op jit(solution)/shard_map/ppermute | solution.py:560
  254.7 25.8 %collective-permute-start.23 = (bf16[512,1152]{1,0:T(8,128)(2,1)S(1)}, bf16[512,1152]{1,0:T(8,128)(2,1)S(1)}, u32[]{:S(2)}, u32[]{:S(2)}) collective-permute-start(bf16[512,1152]{1,0:T(8,128)(2,1)S(1)} %get-tuple-element.202), channel_id=1, source_target_pairs={{0,16},{16,0},{1,17},{17,1},{2,18},{18,2},{3,19},{19,3},{4,20},{20... | collective-permute-start | bytes 3538952 | tf_op jit(solution)/shard_map/ppermute | solution.py:560
  317.2 25.8 %collective-permute-start.28 = (bf16[512,1152]{1,0:T(8,128)(2,1)S(1)}, bf16[512,1152]{1,0:T(8,128)(2,1)S(1)}, u32[]{:S(2)}, u32[]{:S(2)}) collective-permute-start(bf16[512,1152]{1,0:T(8,128)(2,1)S(1)} %pad_maximum_fusion.7), channel_id=1, source_target_pairs={{0,1},{1,0},{2,3},{3,2},{4,5},{5,4},{6,7},{7,6},{8,9},{9,8},{10,11... | collective-permute-start | bytes 3538952 | tf_op jit(solution)/shard_map/ppermute | solution.py:560
  318.0 25.0 %collective-permute-start.29 = (bf16[512,1152]{1,0:T(8,128)(2,1)S(1)}, bf16[512,1152]{1,0:T(8,128)(2,1)S(1)}, u32[]{:S(2)}, u32[]{:S(2)}) collective-permute-start(bf16[512,1152]{1,0:T(8,128)(2,1)S(1)} %pad_maximum_fusion.8), channel_id=1, source_target_pairs={{0,16},{16,0},{1,17},{17,1},{2,18},{18,2},{3,19},{19,3},{4,20},{20... | collective-permute-start | bytes 3538952 | tf_op jit(solution)/shard_map/ppermute | solution.py:560
  386.4 28.6 %collective-permute-start.30 = (bf16[512,1152]{1,0:T(8,128)(2,1)}, bf16[512,1152]{1,0:T(8,128)(2,1)S(1)}, u32[]{:S(2)}, u32[]{:S(2)}) collective-permute-start(bf16[512,1152]{1,0:T(8,128)(2,1)} %get-tuple-element.229), channel_id=1, source_target_pairs={{0,1},{1,0},{2,3},{3,2},{4,5},{5,4},{6,7},{7,6},{8,9},{9,8},{10,11... | collective-permute-start | bytes 3538952 | tf_op jit(solution)/shard_map/ppermute | solution.py:560
  387.5 28.4 %collective-permute-start.31 = (bf16[512,1152]{1,0:T(8,128)(2,1)}, bf16[512,1152]{1,0:T(8,128)(2,1)}, u32[]{:S(2)}, u32[]{:S(2)}) collective-permute-start(bf16[512,1152]{1,0:T(8,128)(2,1)} %get-tuple-element.230), channel_id=1, source_target_pairs={{0,16},{16,0},{1,17},{17,1},{2,18},{18,2},{3,19},{19,3},{4,20},{20... | collective-permute-start | bytes 3538952 | tf_op jit(solution)/shard_map/ppermute | solution.py:560
  452.5 127.9 %reduce-scatter.6.cloned.1.call-start = ((), (), s32[]{:S(2)}) async-start(), calls=%async_computation.10 | async-start | bytes 2580480 | tf_op jit(solution)/shard_map/reduce_scatter | solution.py:646
  452.5 34.4 %collective-permute-start.38 = (bf16[896,1152]{1,0:T(8,128)(2,1)}, bf16[896,1152]{1,0:T(8,128)(2,1)}, u32[]{:S(2)}, u32[]{:S(2)}) collective-permute-start(bf16[896,1152]{1,0:T(8,128)(2,1)} %get-tuple-element.264), channel_id=1, source_target_pairs={{0,8},{8,0},{1,9},{9,1},{2,10},{10,2},{3,11},{11,3},{4,12},{12,4},... | collective-permute-start | bytes 6193160 | tf_op jit(solution)/shard_map/ppermute | solution.py:560
  485.7 33.1 %collective-permute-start.40 = (bf16[4,128,512]{2,1,0:T(8,128)(2,1)}, bf16[4,128,512]{2,1,0:T(8,128)(2,1)}, u32[]{:S(2)}, u32[]{:S(2)}) collective-permute-start(bf16[4,128,512]{2,1,0:T(8,128)(2,1)} %get-tuple-element.267), channel_id=1, source_target_pairs={{0,1},{1,0},{2,3},{3,2},{4,5},{5,4},{6,7},{7,6},{8,9},{9,8},{10,11... | collective-permute-start | bytes 1572872 | tf_op jit(solution)/shard_map/ppermute | solution.py:560
  511.9 39.0 %collective-permute-start.39 = (bf16[4,128,512]{2,1,0:T(8,128)(2,1)}, bf16[4,128,512]{2,1,0:T(8,128)(2,1)}, u32[]{:S(2)}, u32[]{:S(2)}) collective-permute-start(bf16[4,128,512]{2,1,0:T(8,128)(2,1)} %fusion.3), channel_id=1, source_target_pairs={{2,0},{4,2},{6,4},{3,1},{5,3},{7,5},{10,8},{12,10},{14,12},{11,9},... | collective-permute-start | bytes 1572872 | tf_op jit(solution)/shard_map/ppermute | solution.py:565
  518.8 144.7 %reduce-scatter.8.cloned.1.call-start = ((), (), s32[]{:S(2)}) async-start(), calls=%async_computation.11 | async-start | bytes 2580480 | tf_op jit(solution)/shard_map/reduce_scatter | solution.py:646
  552.6 25.3 %collective-permute-start.42 = (bf16[2,4,68,1152]{3,1,2,0:T(4,128)(2,1)}, bf16[2,4,68,1152]{3,1,2,0:T(4,128)(2,1)}, u32[]{:S(2)}, u32[]{:S(2)}) collective-permute-start(bf16[2,4,68,1152]{3,1,2,0:T(4,128)(2,1)} %copy.117), channel_id=1, source_target_pairs={{0,16},{16,0},{1,17},{17,1},{2,18},{18,2},{3,19},{19,3},{4,20},{20... | collective-permute-start | bytes 3760136 | tf_op jit(solution)/shard_map/ppermute | solution.py:560
  615.6 45.6 %all-to-all-start.3 = ((bf16[16,36,640]{2,1,0:T(8,128)(2,1)}), bf16[16,36,640]{2,1,0:T(8,128)(2,1)S(1)}, u32[]{:S(2)}, u32[]{:S(2)}) async-start(bf16[16,36,640]{2,1,0:T(8,128)(2,1)} %add_convert_fusion.4), calls=%async_computation.5 | async-start | bytes 1638400 | tf_op jit(solution)/shard_map/all_to_all | solution.py:653
  628.9 29.9 %collective-permute-start.46 = (bf16[68,1152]{1,0:T(8,128)(2,1)S(1)}, bf16[68,1152]{1,0:T(8,128)(2,1)S(1)}, u32[]{:S(2)}, u32[]{:S(2)}) collective-permute-start(bf16[68,1152]{1,0:T(8,128)(2,1)S(1)} %get-tuple-element.321), channel_id=1, source_target_pairs={{0,4},{2,6},{4,0},{6,2},{1,5},{3,7},{5,1},{7,3},{8,12},{10,14},{12... | collective-permute-start | bytes 470024 | tf_op jit(solution)/shard_map/ppermute | solution.py:569
  631.3 27.5 %collective-permute-start.47 = (bf16[68,1152]{1,0:T(8,128)(2,1)S(1)}, bf16[68,1152]{1,0:T(8,128)(2,1)}, u32[]{:S(2)}, u32[]{:S(2)}) collective-permute-start(bf16[68,1152]{1,0:T(8,128)(2,1)S(1)} %get-tuple-element.320), channel_id=1, source_target_pairs={{0,6},{2,0},{4,2},{6,4},{1,7},{3,1},{5,3},{7,5},{8,14},{10,8},{12,... | collective-permute-start | bytes 470024 | tf_op jit(solution)/shard_map/ppermute | solution.py:569
  (60 other events, 770.1 us)
Sparse Core Ops, SparseCore 0:
  13.3 49.1 all-gather.4
  64.7 104.0 all-gather.2
  452.6 57.0 reduce-scatter.3
  512.0 55.8 reduce-scatter.5
  583.0 48.1 reduce-scatter.7

commit v4 on v3

--- a/solution.py
+++ b/solution.py
@@ -391,30 +391,32 @@
         total = term if total is None else total + term
     total = total.astype(BF16)
     tile = total.shape[0]
-    for k in range(sum(count for _, _, _, count in places) // tile):
-
-        @pl.when(pl.program_id(0) == k)
-        def _(k=k):
-            for core, at, row, count in places:
-                begin, end = max(row, k * tile), min(row + count, (k + 1) * tile)
-                if begin < end:
-                    to = at + begin - row
-                    index = (slice(to, to + end - begin), slice(None))
-                    put(kept_ref, sent_ref, core, index, total[begin - k * tile : end - k * tile])
-
-
-def weight_grads(lefts, rights, which, places):
+    for which, moves in enumerate(places):
+        for k in range(sum(count for _, _, _, count in moves) // tile):
+
+            @pl.when((pl.program_id(0) == which) & (pl.program_id(1) == k))
+            def _(k=k, moves=moves):
+                for core, at, row, count in moves:
+                    begin, end = max(row, k * tile), min(row + count, (k + 1) * tile)
+                    if begin < end:
+                        to = at + begin - row
+                        index = (slice(to, to + end - begin), slice(None))
+                        put(kept_ref, sent_ref, core, index, total[begin - k * tile : end - k * tile])
+
+
+def weight_grads(lefts, rights, places):
     rows, cols = lefts[0].shape[1], rights[0].shape[2]
     count = sum(one.shape[0] for one in lefts)
     tile = 384 if rows % 384 == 0 else 256
+    out = len(places) * rows // 2
     return call(
         functools.partial(grads_body, places, len(lefts)),
-        (rows // tile,),
-        [pl.BlockSpec((one.shape[0], tile), lambda i: (0, i)) for one in lefts]
-        + [pl.BlockSpec((1,) + one.shape[1:], lambda i: (which, 0, 0)) for one in rights],
-        [whole(rows // 2, cols)] * 2,
-        [shaped(rows // 2, cols, dtype=BF16)] * 2,
-        2 * count * rows * cols,
+        (len(places), rows // tile),
+        [pl.BlockSpec((one.shape[0], tile), lambda k, i: (0, i)) for one in lefts]
+        + [pl.BlockSpec((1,) + one.shape[1:], lambda k, i: (k, 0, 0)) for one in rights],
+        [pl.BlockSpec((out, cols), lambda k, i: (0, 0))] * 2,
+        [shaped(out, cols, dtype=BF16)] * 2,
+        2 * len(places) * count * rows * cols,
     )(*lefts, *rights)
 
 
@@ -669,21 +671,21 @@
         upper, lower, done = lax.optimization_barrier((self.swap(upper, "y"), self.swap(lower, "x"), first(near)))
         return [done, first(jnp.concatenate([upper, lower]))]
 
-    def sum_plane(self, parts, beside=(None, None)):
+    def sum_plane(self, parts, held=(), beside=(None, None)):
         works = [work or (lambda *given: ()) for work in beside]
         if not self.pairs_only:
             total = lax.psum_scatter(parts[0], PLANE, scatter_dimension=0, tiled=True).astype(F32)
-            return total, works[1](*works[0]())
+            return total, works[1](*works[0](*held))
         near, far = parts
         half = far.shape[0] // 2
         quarter = half // 2
-        upper, lower = lax.optimization_barrier((far[:half], far[half:]))
-        upper, lower, extra = lax.optimization_barrier((self.swap(upper, "y"), self.swap(lower, "x"), works[0]()))
+        upper, lower, held = lax.optimization_barrier((far[:half], far[half:], tuple(held)))
+        upper, lower, extra = lax.optimization_barrier((self.swap(upper, "y"), self.swap(lower, "x"), works[0](*held)))
         at = [near[k * quarter : (k + 1) * quarter].astype(F32) for k in range(4)]
         own = (at[0] + upper[:quarter].astype(F32), at[2] + lower[:quarter].astype(F32))
         upper = (at[1] + upper[quarter:].astype(F32)).astype(BF16)
         lower = (at[3] + lower[quarter:].astype(F32)).astype(BF16)
-        upper, lower = lax.optimization_barrier((upper, lower))
+        upper, lower, extra = lax.optimization_barrier((upper, lower, extra))
         upper, lower, extra = lax.optimization_barrier((self.swap(upper, "x"), self.swap(lower, "y"), works[1](*extra)))
         return jnp.concatenate([own[0] + upper.astype(F32), own[1] + lower.astype(F32)]), extra
 
@@ -705,10 +707,10 @@
         reach = -(-(DOC_LIMIT - 1) // (wide * length))
         if wide == 2 and reach == 2:
             first = self.index("y") == 0
-            one, extra = lax.optimization_barrier((self.shift(array, 1), beside[0]()))
+            one, two, extra = lax.optimization_barrier((self.shift(array, 1), self.shift(array, 2), beside[0]()))
             near = self.swap(jnp.where(first, array, one), "y")
-            two, near, extra = lax.optimization_barrier((self.shift(one, 1), near, beside[1](extra)))
             far = self.swap(jnp.where(first, one, two), "y")
+            near, far, extra = lax.optimization_barrier((near, far, beside[1](extra)))
             return [array, one, two, near, far], extra
         along = [lax.all_gather(array, "y", axis=0)]
         for _ in range(reach):
@@ -735,13 +737,13 @@
         if wide == 2 and reach == 2:
             first = self.index("y") == 0
             own, one, two, near, far = terms
-            (far,) = follow(self.swap(far, "y"))
-            two = (two + jnp.where(first, 0.0, far.astype(F32))).astype(BF16)
-            two, near = follow(self.shift(two, -1), self.swap(near, "y"))
-            near = near.astype(F32)
-            one = (one + jnp.where(first, far.astype(F32), near) + two.astype(F32)).astype(BF16)
-            own = own + jnp.where(first, near, 0.0)
-            (own,) = follow(own + self.shift(one, -1).astype(F32))
+            far, near = follow(self.swap(far, "y"), self.swap(near, "y"))
+            far, near = far.astype(F32), near.astype(F32)
+            two = (two + jnp.where(first, 0.0, far)).astype(BF16)
+            one = (one + jnp.where(first, far, near)).astype(BF16)
+            two, one = follow(self.shift(two, -2), self.shift(one, -1))
+            own = own + jnp.where(first, near, 0.0) + one.astype(F32) + two.astype(F32)
+            (own,) = follow(own)
             return own, results
         total = None
         for k in range(reach, -1, -1):
@@ -813,7 +815,6 @@
     out_shard = w_out.shape[0]
     qo_shard = jnp.concatenate([o_shard, q_shard])
     pair, qo_shard, kv_along = lax.optimization_barrier((pair, qo_shard, kv_along))
-    pair = jnp.transpose(links.exchange(pair), (2, 0, 1, 3, 4)).reshape(2 * sx, sy * shard, units)
     kv_own, pair, qo_shard = lax.optimization_barrier((links.across_plane(kv_along), pair, qo_shard))
     full_kv, gains, heads, seg_all = links.placed(
         kv_shard,
@@ -826,7 +827,8 @@
         ),
     )
     h_in, k_proj, kv_low = kv_step(rows, length, tokens_flat, full_kv, gains, heads, cosine, sine)
-    kv_low, qo_along = lax.optimization_barrier((kv_low, links.along_z(qo_shard)))
+    kv_low, qo_along, pair = lax.optimization_barrier((kv_low, links.along_z(qo_shard), links.exchange(pair)))
+    pair = jnp.transpose(pair, (2, 0, 1, 3, 4)).reshape(2 * sx, sy * shard, units)
     kv, qo = links.window(
         kv_low,
         length,
@@ -836,6 +838,7 @@
         ),
     )
     masks = (own_ids, seg_all)
+    kv[2], pair = lax.optimization_barrier((kv[2], pair))
     full_pair = links.gather_cz(pair, 1).reshape(2, width, units)
     full_out, full_query = links.placed(
         qo_shard, qo[0], ((0, out_shard, 0, width), (out_shard, shard, 0, HEADS * HEAD)), qo[1]
@@ -856,31 +859,34 @@
 
     d_parts, d_pairs, d_terms = zip(*links.over_plane(d_ffn, back), strict=True)
     block = sy * shard
-    places = sorted(
-        (c, (z * sx + x) * block, ((x * sc + c) * sz + z) * block, block)
-        for x in range(sx)
-        for c in range(sc)
-        for z in range(sz)
-    )
+    places = [
+        [
+            (c, ((z * 2 + k) * sx + x) * block, ((x * sc + c) * sz + z) * block, block)
+            for x in range(sx)
+            for c in range(sc)
+            for z in range(sz)
+        ]
+        for k in range(2)
+    ]
     half = units // 2
     down_places = [(c, 0, c * half, half) for c in range(sc)]
 
-    def gate_up():
-        grad_gate = weight_grads(h_parts, d_pairs, 0, places)
-        return (links.sum_cores(*grad_gate), *weight_grads(h_parts, d_pairs, 1, places))
-
-    def up_down(half_gate, *grad_up):
-        grad_down = weight_grads(hidden, [part[None] for part in d_parts], 0, down_places)
-        return (half_gate, links.sum_cores(*grad_up), *grad_down)
-
-    d_hffn, (half_gate, half_up, *grad_down) = links.sum_plane(d_terms, (gate_up, up_down))
-
-    def owned(sums):
-        return links.exchange(sums.reshape(sx, sy, shard, units))
+    def pair_down(kept, sent):
+        low = weight_grads(hidden, [part[None] for part in d_parts], [down_places])
+        return (kept, links.swap(sent, "core"), *low)
+
+    d_hffn, (kept, got, *grad_down) = links.sum_plane(
+        d_terms, d_pairs, (lambda *pairs: weight_grads(h_parts, pairs, places), pair_down)
+    )
+    d_hffn, half_pair = lax.optimization_barrier((d_hffn, (kept.astype(F32) + got.astype(F32)).astype(BF16)))
+    grad_pair = links.sum_z_low(half_pair)
+
+    def by_member(sums):
+        return jnp.transpose(sums.reshape(2, sx, sy, shard, units), (1, 2, 0, 3, 4))
 
     def unpacked(got):
-        got = got.reshape(sx, sy, shard, sc, sz, chunk)[..., :hidden_shard]
-        return jnp.transpose(got, (2, 0, 3, 4, 1, 5)).reshape(shard, parts * hidden_shard).astype(F32)
+        got = got.reshape(sx, sy, 2, shard, sc, sz, chunk)[..., :hidden_shard]
+        return jnp.transpose(got, (2, 3, 0, 4, 5, 1, 6)).reshape(2, shard, parts * hidden_shard).astype(F32)
 
     d_res, d_attn, d_qproj, sums_attn, heads_attn, *terms = attend_back(
         links, rows, length, d_hffn, cot_flat, resid, attn, q_proj, query, full_out, gains, heads, cosine, sine, masks, kv,
@@ -893,13 +899,12 @@
             lambda: (
                 links.sum_cores(*outer_grads(links.order("xyz"), (out_shard, shard), mixed, d_attn, h_in, d_qproj)),
                 links.sum_cores(*grad_down),
-                links.sum_z_low(half_gate),
             ),
-            lambda second, low, gate: (second, low, owned(gate)),
-            lambda second, low, gate: (links.planes(second), low, unpacked(gate), links.sum_z_low(half_up)),
+            lambda second, low: (links.planes(second), low, grad_pair),
         ),
     )
-    second, low, grad_gate, up = beside[2]
+    second, low, grad_pair = beside[1]
+    grad_down = links.sum_z_low(low)[:hidden_shard].astype(F32)
 
     d_kvproj, grad_tokens, sums_in, heads_in = finish(
         rows, length, d_kv, k_proj, d_qproj, tokens_flat, d_res, full_query, full_kv, gains, heads, cosine, sine
@@ -908,14 +913,14 @@
     head_terms = (heads_attn + heads_in)[:2].reshape(2, parts, head_shard)
     head_terms = jnp.pad(head_terms, ((0, 0), (0, 0), (0, shard - head_shard))).reshape(2, width)
     small_terms = jnp.pad(jnp.concatenate([gain_terms, head_terms]), ((0, SMALL - 6), (0, 0)))
+    d_kvproj, second, got_pair = lax.optimization_barrier(
+        (d_kvproj, links.sum_halves(second, "y", 0), links.exchange(by_member(grad_pair)))
+    )
     first_grad = first_grads(links.order("xzy"), shard, h_in, d_kvproj, small_terms)
-    first_core, second, got_up = lax.optimization_barrier(
-        (links.sum_cores(*first_grad), links.sum_halves(second, "y", 0), owned(up))
-    )
+    first_core = links.sum_cores(*first_grad)
     first_sum = links.sum_all_small(first_core)
     second_sum = links.sum_z(second, 0)
-    grad_up = unpacked(got_up)
-    grad_down = links.sum_z_low(low)[:hidden_shard].astype(F32)
+    grad_pair = unpacked(got_pair)
     return (
         output.reshape(tokens.shape),
         grad_tokens.reshape(tokens.shape),
@@ -923,8 +928,8 @@
         first_sum[:, SMALL : SMALL + HEAD],
         first_sum[:, SMALL + HEAD :],
         second_sum[:out_shard, :width],
-        grad_gate,
-        grad_up,
+        grad_pair[0],
+        grad_pair[1],
         grad_down,
         *(first_sum[:, k] for k in range(4)),
         *(first_sum[:head_shard, 4 + k] for k in range(2)),

time: 682 us -> 647 us (0.949)
  waiting for transfers between devices: 249 us -> 222 us
    ppermute x4, waiting for transfers between devices: 58.9 us -> 7.59 us  [shift(): return lax.ppermute(array, 'z', pairs)]
    ppermute x33 -> x32, waiting for transfers between devices: 129 us -> 154 us  [swap(): return lax.ppermute(array, axis, SWAP)]
    all_gather x2, waiting for transfers between devices: 0.01 us -> 12.9 us  [gather_cz(): return lax.all_gather(array, ('core', 'z'), axis=dim, tiled=True)]
    all_to_all x3 -> x2, waiting for transfers between devices: 14.4 us -> 2.42 us  [exchange(): return lax.all_to_all(flat, PLANE, 0, 0, tiled=True).reshape(array.shape)]
    ppermute x9, waiting for transfers between devices: 33.2 us -> 43.9 us  [turn(): lax.ppermute(array, 'z', [(i, (i + step) % depth) for i in range(depth)])]
    reduce_scatter x3 -> x2, waiting for transfers between devices: 9.75 us -> 0.01 us  [sum_z_low(): return lax.psum_scatter(array, 'z', scatter_dimension=0, tiled=True)]
    ppermute x4, starting transfers between devices: 21 us -> 11.6 us  [shift(): return lax.ppermute(array, 'z', pairs)]
    convert_element_type x4 -> x0, local copies, waits for them, and re-layouts: 8.56 us -> none  [unpacked(): jnp.transpose(got, (2, 0, 3, 4, 1, 5)).reshape(shard, parts * hidden_shard)]
  transfers between devices with their start and end apart: 57 -> 54, of which waited for: 32 -> 25; matrix products, arithmetic and copies ran while one was open for 13% -> 12% of each run, Pallas kernels for 22% -> 25%
where the time goes in v4:
time: 647 us; the launch traced here: 637 us
  waiting for transfers between devices  222 us (34%)
  Pallas kernels  210 us (32%)
  starting transfers between devices  81.2 us (13%)
  local copies, waits for them, and re-layouts  59.3 us (9%)
  other arithmetic  50.3 us (8%)
  between operations  14.7 us (2%)
    ppermute x32, waiting for transfers between devices, swap(): return lax.ppermute(array, axis, SWAP)  154 us
    pallas_call x2, Pallas kernels, ffn_backward(): call(functools.partial(down_body, step), (count // tile,), [rows_of(tile,...  48.9 us
    ppermute x9, waiting for transfers between devices, turn(): lax.ppermute(array, 'z', [(i, (i + step) % depth) for i in range(depth)])  43.9 us
    pallas_call x2, Pallas kernels, weight_grads(): call(functools.partial(grads_body, places, len(lefts)), (len(places), row...  43.6 us
    pallas_call x2, Pallas kernels, ffn_forward(): call(functools.partial(up_body, step), (count // tile,), [rows_of(tile, w...  42.2 us
    ppermute x32, starting transfers between devices, swap(): return lax.ppermute(array, axis, SWAP)  31.2 us
    pallas_call x1, Pallas kernels, attend_back(): call(functools.partial(attend_back_body, links, len(kv)), (rows,), [rows_...  17.4 us
    ppermute x9, starting transfers between devices, turn(): lax.ppermute(array, 'z', [(i, (i + step) % depth) for i in range(depth)])  16.2 us
  transfers between devices with their start and end apart: 54, of which 25 were waited for; matrix products, arithmetic and copies ran while one was open for 12% of the time, Pallas kernels for 25%

profile of v4, /device:TPU:0, one launch (start us, length us, event | category | flops | bytes accessed | tf_op | source)
XLA Modules:
  0.0 636.9 jit_solution(12474965807755286513)
XLA Ops:
  49.5 15.5 %collective-permute-done.8 = bf16[68,1152]{1,0:T(8,128)(2,1)S(1)} collective-permute-done((bf16[68,1152]{1,0:T(8,128)(2,1)S(1)}, bf16[68,1152]{1,0:T(8,128)(2,1)S(1)}, u32[]{:S(2)}, u32[]{:S(2)}) %collective-permute-start.8) | collective-permute-done | bytes 156704 | tf_op jit(solution)/shard_map/ppermute | solution.py:571
  98.9 12.6 %collective-permute-done.13 = bf16[4,68,1152]{2,0,1:T(4,128)(2,1)} collective-permute-done((bf16[4,68,1152]{2,0,1:T(4,128)(2,1)S(1)}, bf16[4,68,1152]{2,0,1:T(4,128)(2,1)}, u32[]{:S(2)}, u32[]{:S(2)}) %collective-permute-start.13) | collective-permute-done | bytes 626720 | tf_op jit(solution)/shard_map/ppermute | solution.py:562
  122.0 11.8 %collective-permute-done.15.refs_13_.refs_16_ = bf16[4,128,512]{2,1,0:T(8,128)(2,1)S(1)} collective-permute-done((bf16[4,128,512]{2,1,0:T(8,128)(2,1)S(1)}, bf16[4,128,512]{2,1,0:T(8,128)(2,1)S(1)}, u32[]{:S(2)}, u32[]{:S(2)}) %collective-permute-start.15) | collective-permute-done | bytes 524320 | tf_op jit(solution)/shard_map/ppermute | solution.py:562
  133.8 10.8 %collective-permute-done.16.refs_14_.refs_17_ = bf16[4,128,512]{2,1,0:T(8,128)(2,1)S(1)} collective-permute-done((bf16[4,128,512]{2,1,0:T(8,128)(2,1)S(1)}, bf16[4,128,512]{2,1,0:T(8,128)(2,1)S(1)}, u32[]{:S(2)}, u32[]{:S(2)}) %collective-permute-start.16) | collective-permute-done | bytes 524320 | tf_op jit(solution)/shard_map/ppermute | solution.py:562
  154.9 15.0 %shard_map.274 = (f32[512,1024]{1,0:T(8,128)}, bf16[512,1024]{1,0:T(8,128)(2,1)}, bf16[512,1024]{1,0:T(8,128)(2,1)}, f32[512,1152]{1,0:T(8,128)}, f32[512,1152]{1,0:T(8,128)}, /*index=5*/bf16[512,1152]{1,0:T(8,128)(2,1)}) custom-call(bf16[512,1152]{1,0:T(8,128)(2,1)} %get-tuple-element.170.refs_0_.h_ref, bf16[512,1152]{1,0:T(8,128)(2,1)} %bitcast.60, ...), custom_call_target="tpu_custom_call" | custom-call | flops 3758096384 | bytes 20185088 | tf_op jit(solution)/shard_map/pallas_call | solution.py:189
  173.5 12.8 %collective-permute-done.18 = bf16[256,1152]{1,0:T(8,128)(2,1)S(1)} collective-permute-done((bf16[256,1152]{1,0:T(8,128)(2,1)S(1)}, bf16[256,1152]{1,0:T(8,128)(2,1)S(1)}, u32[]{:S(2)}, u32[]{:S(2)}) %collective-permute-start.18) | collective-permute-done | bytes 589856 | tf_op jit(solution)/shard_map/ppermute | solution.py:562
  192.5 12.9 %all-gather.3.cloned.1.call-done = bf16[4,576,1792]{2,1,0:T(8,128)(2,1)} async-done(((bf16[4,72,1792]{2,1,0:T(8,128)(2,1)}), bf16[4,576,1792]{2,1,0:T(8,128)(2,1)}) %all-gather.3.cloned.1.call-update) | async-done | bytes 8257552 | tf_op jit(solution)/shard_map/all_gather | solution.py:622
  205.4 21.1 %shard_map.275 = (bf16[1024,1792]{1,0:T(8,128)(2,1)}, bf16[1024,1792]{1,0:T(8,128)(2,1)}, bf16[1024,1792]{1,0:T(8,128)(2,1)}, bf16[1024,1152]{1,0:T(8,128)(2,1)}) custom-call(bf16[1024,1152]{1,0:T(8,128)(2,1)} %pad_maximum_fusion.1.h_ref.refs_0_, bf16[2,1152,1792]{2,1,0:T(8,128)(2,1)} %bitcast.80, bf16[1792,1152]{1,0:T(8,128)(2,1)} %all-gather.5.cloned.1.call-done.down_ref), custom_call_target="tpu_custom_call" | custom-call | flops 12683575296 | bytes 26738688 | tf_op jit(solution)/shard_map/pallas_call | solution.py:343
  228.2 21.1 %shard_map.276 = (bf16[1024,1792]{1,0:T(8,128)(2,1)}, bf16[1024,1792]{1,0:T(8,128)(2,1)}, bf16[1024,1792]{1,0:T(8,128)(2,1)}, bf16[1024,1152]{1,0:T(8,128)(2,1)}) custom-call(bf16[1024,1152]{1,0:T(8,128)(2,1)} %copy-done.12, bf16[2,1152,1792]{2,1,0:T(8,128)(2,1)} %bitcast.81, bf16[1792,1152]{1,0:T(8,128)(2,1)} %all-gather.5.cloned.1.call-done.down_ref), custom_call_target="tpu_custom_call" | custom-call | flops 12683575296 | bytes 26738688 | tf_op jit(solution)/shard_map/pallas_call | solution.py:343
  254.3 25.2 %collective-permute-done.22 = bf16[512,1152]{1,0:T(8,128)(2,1)S(1)} collective-permute-done((bf16[512,1152]{1,0:T(8,128)(2,1)S(1)}, bf16[512,1152]{1,0:T(8,128)(2,1)S(1)}, u32[]{:S(2)}, u32[]{:S(2)}) %collective-permute-start.22) | collective-permute-done | bytes 1179680 | tf_op jit(solution)/shard_map/ppermute | solution.py:562
  283.0 12.3 %collective-permute-done.24 = bf16[256,1152]{1,0:T(8,128)(2,1)S(1)} collective-permute-done((bf16[256,1152]{1,0:T(8,128)(2,1)S(1)}, bf16[256,1152]{1,0:T(8,128)(2,1)S(1)}, u32[]{:S(2)}, u32[]{:S(2)}) %collective-permute-start.24) | collective-permute-done | bytes 589856 | tf_op jit(solution)/shard_map/ppermute | solution.py:562
  306.7 12.0 %collective-permute-done.26 = bf16[256,1152]{1,0:T(8,128)(2,1)S(1)} collective-permute-done((bf16[256,1152]{1,0:T(8,128)(2,1)S(1)}, bf16[256,1152]{1,0:T(8,128)(2,1)S(1)}, u32[]{:S(2)}, u32[]{:S(2)}) %collective-permute-start.26) | collective-permute-done | bytes 589856 | tf_op jit(solution)/shard_map/ppermute | solution.py:562
  322.9 24.3 %shard_map.278 = (bf16[2,1024,1792]{2,1,0:T(8,128)(2,1)}, bf16[1024,1152]{1,0:T(8,128)(2,1)}) custom-call(bf16[1024,1152]{1,0:T(8,128)(2,1)} %pad_maximum_fusion.3.d_ref, bf16[1024,1792]{1,0:T(8,128)(2,1)} %get-tuple-element.225.turn_ref, bf16[1024,1792]{1,0:T(8,128)(2,1)} %get-tuple-element.226.act_ref, bf16[2,1152,1792]{2,1,0:T(8,128)(2,1)} %bitcast.82, ...), custom_call_target="tpu_custom_call" | custom-call | flops 12683575296 | bytes 19398656 | tf_op jit(solution)/shard_map/pallas_call | solution.py:366
  349.0 24.5 %shard_map.279 = (bf16[2,1024,1792]{2,1,0:T(8,128)(2,1)}, bf16[1024,1152]{1,0:T(8,128)(2,1)}) custom-call(bf16[1024,1152]{1,0:T(8,128)(2,1)} %copy-done.13, bf16[1024,1792]{1,0:T(8,128)(2,1)} %get-tuple-element.232.turn_ref, bf16[1024,1792]{1,0:T(8,128)(2,1)} %get-tuple-element.233.act_ref, bf16[2,1152,1792]{2,1,0:T(8,128)(2,1)} %bitcast.83, ...), custom_call_target="tpu_custom_call" | custom-call | flops 12683575296 | bytes 19398656 | tf_op jit(solution)/shard_map/pallas_call | solution.py:366
  378.8 26.9 %shard_map.280 = (bf16[1152,1792]{1,0:T(8,128)(2,1)}, bf16[1152,1792]{1,0:T(8,128)(2,1)}) custom-call(bf16[1024,1152]{1,0:T(8,128)(2,1)} %pad_maximum_fusion.1.h_ref.refs_0_, bf16[1024,1152]{1,0:T(8,128)(2,1)} %copy-done.12, bf16[2,1024,1792]{2,1,0:T(8,128)(2,1)} %get-tuple-element.240.refs_2_, bf16[2,1024,1792]{2,1,0:T(8,128)(2,1)} %get-tuple-element.241.refs_3_), custom_call_target="tpu_custom_call" | custom-call | flops 16911433728 | bytes 16515072 | tf_op jit(solution)/shard_map/pallas_call | solution.py:412
  409.3 16.7 %shard_map.281 = (bf16[896,1152]{1,0:T(8,128)(2,1)}, bf16[896,1152]{1,0:T(8,128)(2,1)}) custom-call(bf16[1024,1792]{1,0:T(8,128)(2,1)} %get-tuple-element.252.refs_0_, bf16[1024,1792]{1,0:T(8,128)(2,1)} %get-tuple-element.253.refs_1_, bf16[1,1024,1152]{2,1,0:T(8,128)(2,1)} %bitcast.67, bf16[1,1024,1152]{2,1,0:T(8,128)(2,1)} %bitcast.71), custom_call_target="tpu_custom_call" | custom-call | flops 8455716864 | bytes 8257536 | tf_op jit(solution)/shard_map/pallas_call | solution.py:412
  434.8 17.4 %shard_map.282 = (f32[512,1152]{1,0:T(8,128)}, bf16[512,1152]{1,0:T(8,128)(2,1)}, bf16[512,1024]{1,0:T(8,128)(2,1)}, f32[8,1152]{1,0:T(8,128)}, f32[8,256]{1,0:T...) custom-call(f32[512,1152]{1,0:T(8,128)} %pad_maximum_fusion.4.refs_0, ...), custom_call_target="tpu_custom_call" | custom-call | flops 4563402752 | bytes 17653760 | tf_op jit(solution)/shard_map/pallas_call | solution.py:259
  452.2 9.1 %shard_map.283 = (bf16[16,68,1152]{2,1,0:T(8,128)(2,1)}, bf16[16,68,1152]{2,1,0:T(8,128)(2,1)}) custom-call(bf16[512,1024]{1,0:T(8,128)(2,1)} %get-tuple-element.268.mixed_ref, bf16[512,1152]{1,0:T(8,128)(2,1)} %get-tuple-element.269.dattn_ref, bf16[512,1152]{1,0:T(8,128)(2,1)} %get-tuple-element.170.refs_0_.h_ref, bf16[512,1024]{1,0:T(8,128)(2,1)} %get-tuple-element.270.dq_ref), custom_call_target="tpu_custom_call" | custom-call | flops 2415919104 | bytes 10027008 | tf_op jit(solution)/shard_map/pallas_call | solution.py:442
  478.9 10.3 %collective-permute-done.36 = bf16[4,128,512]{2,1,0:T(8,128)(2,1)S(1)} collective-permute-done((bf16[4,128,512]{2,1,0:T(8,128)(2,1)}, bf16[4,128,512]{2,1,0:T(8,128)(2,1)S(1)}, u32[]{:S(2)}, u32[]{:S(2)}) %collective-permute-start.36) | collective-permute-done | bytes 524320 | tf_op jit(solution)/shard_map/ppermute | solution.py:562
  496.2 23.9 %collective-permute-done.41 = bf16[2,4,68,1152]{3,1,2,0:T(4,128)(2,1)} collective-permute-done((bf16[2,4,68,1152]{3,1,2,0:T(4,128)(2,1)}, bf16[2,4,68,1152]{3,1,2,0:T(4,128)(2,1)}, u32[]{:S(2)}, u32[]{:S(2)}) %collective-permute-start.41) | collective-permute-done | bytes 1253408 | tf_op jit(solution)/shard_map/ppermute | solution.py:562
  543.8 9.7 %shard_map.284 = (bf16[512,512]{1,0:T(8,128)(2,1)}, bf16[512,1152]{1,0:T(8,128)(2,1)}, f32[8,1152]{1,0:T(8,128)}, f32[8,256]{1,0:T(8,128)}) custom-call(f32[4,128,512]{2,1,0:T(8,128)} %fusion.4.dkv_ref, f32[512,256]{1,0:T(8,128)} %get-tuple-element.284.kproj_ref, bf16[512,1024]{1,0:T(8,128)(2,1)} %get-tuple-element.270.dq_ref, bf16[512,1152]{1,0:T(8,128)(2,1)} %bitcast.61, ...), custom_call_target="tpu_custom_call" | custom-call | flops 1811939328 | bytes 3497984 | tf_op jit(solution)/shard_map/pallas_call | solution.py:306
  569.5 14.3 %all-to-all-start.2 = ((bf16[16,36,640]{2,1,0:T(8,128)(2,1)}), bf16[16,36,640]{2,1,0:T(8,128)(2,1)S(1)}, u32[]{:S(2)}, u32[]{:S(2)}) async-start(bf16[16,36,640]{2,1,0:T(8,128)(2,1)} %add_convert_fusion.3), calls=%async_computation.3 | async-start | bytes 1638400 | tf_op jit(solution)/shard_map/all_to_all | solution.py:655
  601.0 12.3 %collective-permute-done.43 = bf16[68,1152]{1,0:T(8,128)(2,1)S(1)} collective-permute-done((bf16[68,1152]{1,0:T(8,128)(2,1)}, bf16[68,1152]{1,0:T(8,128)(2,1)S(1)}, u32[]{:S(2)}, u32[]{:S(2)}) %collective-permute-start.43) | collective-permute-done | bytes 156704 | tf_op jit(solution)/shard_map/ppermute | solution.py:571
  613.2 10.2 %collective-permute-done.44 = bf16[68,1152]{1,0:T(8,128)(2,1)} collective-permute-done((bf16[68,1152]{1,0:T(8,128)(2,1)}, bf16[68,1152]{1,0:T(8,128)(2,1)}, u32[]{:S(2)}, u32[]{:S(2)}) %collective-permute-start.44) | collective-permute-done | bytes 156704 | tf_op jit(solution)/shard_map/ppermute | solution.py:571
  (247 shorter events, 239.5 us)
Async XLA Ops:
  7.2 185.3 %all-gather.5.cloned.1.call-start = ((), (), s32[]{:S(2)}) async-start(), calls=%async_computation.6 | async-start | bytes 4644864 | tf_op jit(solution)/shard_map/all_gather | solution.py:622
  41.0 39.2 %all-to-all-start = ((bf16[4,2,36,1792]{3,1,2,0:T(2,128)(2,1)}), bf16[4,2,36,1792]{3,1,2,0:T(2,128)(2,1)S(1)}, u32[]{:S(2)}, u32[]{:S(2)}) async-start(bf16[4,2,36,1792]{3,1,2,0:T(2,128)(2,1)} %bitcast.66), calls=%async_computation | async-start | bytes 2064384 | tf_op jit(solution)/shard_map/all_to_all | solution.py:661
  44.6 160.8 %all-gather.3.cloned.1.call-start = ((), (), s32[]{:S(2)}) async-start(), calls=%async_computation.5 | async-start | bytes 9289728 | tf_op jit(solution)/shard_map/all_gather | solution.py:622
  82.5 28.9 %collective-permute-start.13 = (bf16[4,68,1152]{2,0,1:T(4,128)(2,1)S(1)}, bf16[4,68,1152]{2,0,1:T(4,128)(2,1)}, u32[]{:S(2)}, u32[]{:S(2)}) collective-permute-start(bf16[4,68,1152]{2,0,1:T(4,128)(2,1)S(1)} %copy.100), channel_id=1, source_target_pairs={{0,1},{1,0},{2,3},{3,2},{4,5},{5,4},{6,7},{7,6},{8,9},{9,8},{10,11... | collective-permute-start | bytes 1880072 | tf_op jit(solution)/shard_map/ppermute | solution.py:562
  84.0 28.6 %collective-permute-start.14 = (bf16[4,68,1152]{2,0,1:T(4,128)(2,1)S(1)}, bf16[4,68,1152]{2,0,1:T(4,128)(2,1)}, u32[]{:S(2)}, u32[]{:S(2)}) collective-permute-start(bf16[4,68,1152]{2,0,1:T(4,128)(2,1)S(1)} %copy.100), channel_id=1, source_target_pairs={{0,17},{1,16},{16,1},{17,0},{2,19},{3,18},{18,3},{19,2},{4,21},{5,... | collective-permute-start | bytes 1880072 | tf_op jit(solution)/shard_map/ppermute | solution.py:583
  84.1 31.5 %collective-permute-start.10 = (bf16[4,128,512]{2,1,0:T(8,128)(2,1)}, bf16[4,128,512]{2,1,0:T(8,128)(2,1)}, u32[]{:S(2)}, u32[]{:S(2)}) collective-permute-start(bf16[4,128,512]{2,1,0:T(8,128)(2,1)} %get-tuple-element.174.refs_10_.refs_13_), channel_id=1, source_target_pairs={{0,2},{2,4},{4,6},{1,3},{3,5},{5,7},{8,10},{10,12},{12,14},{9,11},... | collective-permute-start | bytes 1572872 | tf_op jit(solution)/shard_map/ppermute | solution.py:567
  115.6 415.4 %reduce-scatter.3.cloned.1.call-start = ((), (), s32[]{:S(2)}) async-start(), calls=%async_computation.7 | async-start | bytes 5160960 | tf_op jit(solution)/shard_map/reduce_scatter | solution.py:648
  117.9 26.8 %collective-permute-start.17 = (bf16[16,68,1152]{2,0,1:T(8,128)(2,1)}, bf16[16,68,1152]{2,0,1:T(8,128)(2,1)}, u32[]{:S(2)}, u32[]{:S(2)}) collective-permute-start(bf16[16,68,1152]{2,0,1:T(8,128)(2,1)} %copy.106), channel_id=1, source_target_pairs={{0,8},{8,0},{1,9},{9,1},{2,10},{10,2},{3,11},{11,3},{4,12},{12,4},... | collective-permute-start | bytes 7520264 | tf_op jit(solution)/shard_map/ppermute | solution.py:562
  189.6 37.0 %collective-permute-start.20 = (bf16[512,1152]{1,0:T(8,128)(2,1)}, bf16[512,1152]{1,0:T(8,128)(2,1)S(1)}, u32[]{:S(2)}, u32[]{:S(2)}) collective-permute-start(bf16[512,1152]{1,0:T(8,128)(2,1)} %get-tuple-element.194), channel_id=1, source_target_pairs={{0,1},{1,0},{2,3},{3,2},{4,5},{5,4},{6,7},{7,6},{8,9},{9,8},{10,11... | collective-permute-start | bytes 3538952 | tf_op jit(solution)/shard_map/ppermute | solution.py:562
  191.1 35.4 %collective-permute-start.21 = (bf16[512,1152]{1,0:T(8,128)(2,1)S(1)}, bf16[512,1152]{1,0:T(8,128)(2,1)S(1)}, u32[]{:S(2)}, u32[]{:S(2)}) collective-permute-start(bf16[512,1152]{1,0:T(8,128)(2,1)S(1)} %get-tuple-element.195), channel_id=1, source_target_pairs={{0,16},{16,0},{1,17},{17,1},{2,18},{18,2},{3,19},{19,3},{4,20},{20... | collective-permute-start | bytes 3538952 | tf_op jit(solution)/shard_map/ppermute | solution.py:562
  251.3 28.2 %collective-permute-start.22 = (bf16[512,1152]{1,0:T(8,128)(2,1)S(1)}, bf16[512,1152]{1,0:T(8,128)(2,1)S(1)}, u32[]{:S(2)}, u32[]{:S(2)}) collective-permute-start(bf16[512,1152]{1,0:T(8,128)(2,1)S(1)} %get-tuple-element.207), channel_id=1, source_target_pairs={{0,1},{1,0},{2,3},{3,2},{4,5},{5,4},{6,7},{7,6},{8,9},{9,8},{10,11... | collective-permute-start | bytes 3538952 | tf_op jit(solution)/shard_map/ppermute | solution.py:562
  252.8 27.8 %collective-permute-start.23 = (bf16[512,1152]{1,0:T(8,128)(2,1)S(1)}, bf16[512,1152]{1,0:T(8,128)(2,1)S(1)}, u32[]{:S(2)}, u32[]{:S(2)}) collective-permute-start(bf16[512,1152]{1,0:T(8,128)(2,1)S(1)} %get-tuple-element.208), channel_id=1, source_target_pairs={{0,16},{16,0},{1,17},{17,1},{2,18},{18,2},{3,19},{19,3},{4,20},{20... | collective-permute-start | bytes 3538952 | tf_op jit(solution)/shard_map/ppermute | solution.py:562
  320.7 26.5 %collective-permute-start.28 = (bf16[512,1152]{1,0:T(8,128)(2,1)S(1)}, bf16[512,1152]{1,0:T(8,128)(2,1)S(1)}, u32[]{:S(2)}, u32[]{:S(2)}) collective-permute-start(bf16[512,1152]{1,0:T(8,128)(2,1)S(1)} %pad_maximum_fusion.7), channel_id=1, source_target_pairs={{0,1},{1,0},{2,3},{3,2},{4,5},{5,4},{6,7},{7,6},{8,9},{9,8},{10,11... | collective-permute-start | bytes 3538952 | tf_op jit(solution)/shard_map/ppermute | solution.py:562
  376.9 28.8 %collective-permute-start.30 = (bf16[512,1152]{1,0:T(8,128)(2,1)}, bf16[512,1152]{1,0:T(8,128)(2,1)S(1)}, u32[]{:S(2)}, u32[]{:S(2)}) collective-permute-start(bf16[512,1152]{1,0:T(8,128)(2,1)} %get-tuple-element.237), channel_id=1, source_target_pairs={{0,1},{1,0},{2,3},{3,2},{4,5},{5,4},{6,7},{7,6},{8,9},{9,8},{10,11... | collective-permute-start | bytes 3538952 | tf_op jit(solution)/shard_map/ppermute | solution.py:562
  378.2 27.5 %collective-permute-start.31 = (bf16[512,1152]{1,0:T(8,128)(2,1)}, bf16[512,1152]{1,0:T(8,128)(2,1)S(1)}, u32[]{:S(2)}, u32[]{:S(2)}) collective-permute-start(bf16[512,1152]{1,0:T(8,128)(2,1)} %get-tuple-element.238), channel_id=1, source_target_pairs={{0,16},{16,0},{1,17},{17,1},{2,18},{18,2},{3,19},{19,3},{4,20},{20... | collective-permute-start | bytes 3538952 | tf_op jit(solution)/shard_map/ppermute | solution.py:562
  434.7 31.1 %collective-permute-start.38 = (bf16[896,1152]{1,0:T(8,128)(2,1)}, bf16[896,1152]{1,0:T(8,128)(2,1)}, u32[]{:S(2)}, u32[]{:S(2)}) collective-permute-start(bf16[896,1152]{1,0:T(8,128)(2,1)} %get-tuple-element.274), channel_id=1, source_target_pairs={{0,8},{8,0},{1,9},{9,1},{2,10},{10,2},{3,11},{11,3},{4,12},{12,4},... | collective-permute-start | bytes 6193160 | tf_op jit(solution)/shard_map/ppermute | solution.py:562
  490.9 29.2 %collective-permute-start.41 = (bf16[2,4,68,1152]{3,1,2,0:T(4,128)(2,1)}, bf16[2,4,68,1152]{3,1,2,0:T(4,128)(2,1)}, u32[]{:S(2)}, u32[]{:S(2)}) collective-permute-start(bf16[2,4,68,1152]{3,1,2,0:T(4,128)(2,1)} %copy.113), channel_id=1, source_target_pairs={{0,16},{16,0},{1,17},{17,1},{2,18},{18,2},{3,19},{19,3},{4,20},{20... | collective-permute-start | bytes 3760136 | tf_op jit(solution)/shard_map/ppermute | solution.py:562
  493.6 36.7 %collective-permute-start.39 = (bf16[4,128,512]{2,1,0:T(8,128)(2,1)S(1)}, bf16[4,128,512]{2,1,0:T(8,128)(2,1)S(1)}, u32[]{:S(2)}, u32[]{:S(2)}) collective-permute-start(bf16[4,128,512]{2,1,0:T(8,128)(2,1)S(1)} %get-tuple-element.329), channel_id=1, source_target_pairs={{4,0},{6,2},{5,1},{7,3},{12,8},{14,10},{13,9},{15,11},{20,16},{22,... | collective-permute-start | bytes 1572872 | tf_op jit(solution)/shard_map/ppermute | solution.py:567
  494.9 36.2 %collective-permute-start.40 = (bf16[4,128,512]{2,1,0:T(8,128)(2,1)S(1)}, bf16[4,128,512]{2,1,0:T(8,128)(2,1)}, u32[]{:S(2)}, u32[]{:S(2)}) collective-permute-start(bf16[4,128,512]{2,1,0:T(8,128)(2,1)S(1)} %get-tuple-element.328), channel_id=1, source_target_pairs={{2,0},{4,2},{6,4},{3,1},{5,3},{7,5},{10,8},{12,10},{14,12},{11,9},... | collective-permute-start | bytes 1572872 | tf_op jit(solution)/shard_map/ppermute | solution.py:567
  540.8 87.4 %reduce-scatter.5.cloned.1.call-start = ((), (), s32[]{:S(2)}) async-start(), calls=%async_computation.8 | async-start | bytes 2580480 | tf_op jit(solution)/shard_map/reduce_scatter | solution.py:648
  569.5 56.4 %all-to-all-start.2 = ((bf16[16,36,640]{2,1,0:T(8,128)(2,1)}), bf16[16,36,640]{2,1,0:T(8,128)(2,1)S(1)}, u32[]{:S(2)}, u32[]{:S(2)}) async-start(bf16[16,36,640]{2,1,0:T(8,128)(2,1)} %add_convert_fusion.3), calls=%async_computation.3 | async-start | bytes 1638400 | tf_op jit(solution)/shard_map/all_to_all | solution.py:655
  587.1 26.1 %collective-permute-start.43 = (bf16[68,1152]{1,0:T(8,128)(2,1)}, bf16[68,1152]{1,0:T(8,128)(2,1)S(1)}, u32[]{:S(2)}, u32[]{:S(2)}) collective-permute-start(bf16[68,1152]{1,0:T(8,128)(2,1)} %get-tuple-element.325), channel_id=1, source_target_pairs={{0,2},{2,4},{4,6},{6,0},{1,3},{3,5},{5,7},{7,1},{8,10},{10,12},{12... | collective-permute-start | bytes 470024 | tf_op jit(solution)/shard_map/ppermute | solution.py:571
  589.0 34.4 %collective-permute-start.44 = (bf16[68,1152]{1,0:T(8,128)(2,1)}, bf16[68,1152]{1,0:T(8,128)(2,1)}, u32[]{:S(2)}, u32[]{:S(2)}) collective-permute-start(bf16[68,1152]{1,0:T(8,128)(2,1)} %get-tuple-element.327), channel_id=1, source_target_pairs={{0,4},{2,6},{4,0},{6,2},{1,5},{3,7},{5,1},{7,3},{8,12},{10,14},{12... | collective-permute-start | bytes 470024 | tf_op jit(solution)/shard_map/ppermute | solution.py:571
  591.4 32.0 %collective-permute-start.45 = (bf16[68,1152]{1,0:T(8,128)(2,1)S(1)}, bf16[68,1152]{1,0:T(8,128)(2,1)}, u32[]{:S(2)}, u32[]{:S(2)}) collective-permute-start(bf16[68,1152]{1,0:T(8,128)(2,1)S(1)} %get-tuple-element.326), channel_id=1, source_target_pairs={{0,6},{2,0},{4,2},{6,4},{1,7},{3,1},{5,3},{7,5},{8,14},{10,8},{12,... | collective-permute-start | bytes 470024 | tf_op jit(solution)/shard_map/ppermute | solution.py:571
  (52 other events, 667.3 us)
Sparse Core Ops, SparseCore 0:
  12.7 61.9 all-gather.4
  115.8 89.5 all-gather.2
  434.9 82.0 reduce-scatter.2
  543.8 58.4 reduce-scatter.4

commit v5 on v4

--- a/solution.py
+++ b/solution.py
@@ -67,6 +67,10 @@
     return jnp.concatenate([first * cosine - second * sine, second * cosine + first * sine], axis=-1)
 
 
+def eights(rows):
+    return -(-rows // 8) * 8
+
+
 def column_sum(terms):
     return jnp.sum(terms, axis=0, keepdims=True)
 
@@ -99,6 +103,40 @@
 
 def row_block(*shape):
     return pl.BlockSpec((1,) + shape, lambda i: (i,) + (0,) * len(shape))
+
+
+def part_specs(tile, width, arrays):
+    if len(arrays) == 1:
+        return [rows_of(tile, width)]
+    half = arrays[0].shape[0] // tile
+    return [
+        pl.BlockSpec((tile, width), lambda i: (jnp.minimum(i, half - 1), 0)),
+        pl.BlockSpec((tile, width), lambda i: (jnp.maximum(i - half, 0), 0)),
+    ]
+
+
+def in_second():
+    return pl.program_id(0) >= pl.num_programs(0) // 2
+
+
+def load_part(refs):
+    if len(refs) == 1:
+        return refs[0][...]
+    return lax.select_n(in_second(), refs[0][...], refs[1][...])
+
+
+def store_part(refs, value):
+    if len(refs) == 1:
+        refs[0][...] = value
+        return
+
+    @pl.when(in_second() == False)
+    def _():
+        refs[0][...] = value
+
+    @pl.when(in_second())
+    def _():
+        refs[1][...] = value
 
 
 def kv_body(tok_ref, wkv_ref, gains_ref, head_ref, cos_ref, sin_ref, h_ref, kproj_ref, kv_ref):
@@ -156,7 +194,7 @@
 def attend_body(links, blocks, *refs):
     (h_ref, tok_ref, wq_ref, wo_ref, gains_ref, head_ref, cos_ref, sin_ref) = refs[:8]
     masks, kv_refs = refs[8:10], refs[10 : 10 + blocks]
-    qproj_ref, query_ref, mixed_ref, attn_ref, resid_ref, hffn_ref = refs[10 + blocks :]
+    qproj_ref, query_ref, mixed_ref, attn_ref, resid_ref, *hffn_refs = refs[10 + blocks :]
     proj = mm(h_ref[...], wq_ref[...])
     qproj_ref[...] = proj
     cosine, sine = cos_ref[...], sin_ref[...]
@@ -174,7 +212,7 @@
     attn_ref[...] = attn
     resid = tok_ref[...].astype(F32) + attn * inv_rms(attn) * gains_ref[POST_ATTN : POST_ATTN + 1]
     resid_ref[...] = resid
-    hffn_ref[...] = (resid * inv_rms(resid) * gains_ref[PRE_FFN : PRE_FFN + 1]).astype(BF16)
+    store_part(hffn_refs, (resid * inv_rms(resid) * gains_ref[PRE_FFN : PRE_FFN + 1]).astype(BF16))
 
 
 def mask_specs(masks):
@@ -186,6 +224,7 @@
     count, width = tokens.shape
     wide = HEADS * HEAD
     window = len(kv) * length
+    halves = [shaped(count // 2, width, dtype=BF16)] * 2
     return call(
         functools.partial(attend_body, links, len(kv)),
         (rows,),
@@ -194,25 +233,26 @@
         + [whole(length, HALF)] * 2
         + mask_specs(masks)
         + [row_block(length, 2 * HEAD)] * len(kv),
-        [rows_of(length, wide)] * 3 + [rows_of(length, width)] * 3,
+        [rows_of(length, wide)] * 3 + [rows_of(length, width)] * 2 + part_specs(length, width, halves),
         [
             shaped(count, wide),
             shaped(count, wide, dtype=BF16),
             shaped(count, wide, dtype=BF16),
             shaped(count, width),
             shaped(count, width),
-            shaped(count, width, dtype=BF16),
+            *halves,
         ],
         4 * count * wide * (width + window),
     )(h, tokens, wq, wo, gains, heads, cosine, sine, *masks, *kv)
 
 
 def attend_back_body(links, blocks, *refs):
-    (dh_ref, cot_ref, resid_ref, attn_ref, qproj_ref, query_ref, wo_ref, gains_ref, head_ref, cos_ref, sin_ref) = refs[:11]
-    masks, kv_refs = refs[11:13], refs[13 : 13 + blocks]
-    dres_ref, dattn_ref, dq_ref, sums_ref, head_sums_ref = refs[13 + blocks : 18 + blocks]
-    term_refs = refs[18 + blocks :]
-    d_norm, pre_terms = rms_back(resid_ref[...], gains_ref[PRE_FFN : PRE_FFN + 1], dh_ref[...])
+    own_refs, far_refs, refs = refs[:2], refs[2:4], refs[4:]
+    (cot_ref, resid_ref, attn_ref, qproj_ref, query_ref, wo_ref, gains_ref, head_ref, cos_ref, sin_ref) = refs[:10]
+    masks, kv_refs = refs[10:12], refs[12 : 12 + blocks]
+    dres_ref, dattn_ref, dq_ref, sums_ref, head_sums_ref = refs[12 + blocks : 17 + blocks]
+    term_refs = refs[17 + blocks :]
+    d_norm, pre_terms = rms_back(resid_ref[...], gains_ref[PRE_FFN : PRE_FFN + 1], load_part(own_refs) + load_part(far_refs).astype(F32))
     d_res = cot_ref[...].astype(F32) + d_norm
     dres_ref[...] = d_res
     d_attn, post_terms = rms_back(attn_ref[...], gains_ref[POST_ATTN : POST_ATTN + 1], d_res)
@@ -252,14 +292,15 @@
     head_sums_ref[0:1] += head_sum
 
 
-def attend_back(links, rows, length, dh, cot, resid, attn, qproj, query, wo, gains, heads, cosine, sine, masks, kv, kinds):
-    count, width = dh.shape
+def attend_back(links, rows, length, own, far, cot, resid, attn, qproj, query, wo, gains, heads, cosine, sine, masks, kv, kinds):
+    count, width = cot.shape
     wide = HEADS * HEAD
     window = len(kv) * length
     return call(
         functools.partial(attend_back_body, links, len(kv)),
         (rows,),
-        [rows_of(length, width)] * 4
+        part_specs(length, width, own) * 2
+        + [rows_of(length, width)] * 3
         + [rows_of(length, wide)] * 2
         + [whole(*one.shape) for one in (wo, gains, heads)]
         + [whole(length, HALF)] * 2
@@ -277,7 +318,7 @@
         ]
         + [shaped(rows, length, 2 * HEAD, dtype=kind) for kind in kinds],
         2 * count * wide * (width + 5 * window),
-    )(dh, cot, resid, attn, qproj, query, wo, gains, heads, cosine, sine, *masks, *kv)
+    )(*own, *far, cot, resid, attn, qproj, query, wo, gains, heads, cosine, sine, *masks, *kv)
 
 
 def finish_body(dkv_ref, kproj_ref, dq_ref, tok_ref, dres_ref, wq_ref, wkv_ref, gains_ref, head_ref, cos_ref, sin_ref,
@@ -320,8 +361,9 @@
     return [(k, min(step, total - k)) for k in range(0, total, step)]
 
 
-def up_body(step, h_ref, pair_ref, down_ref, hidden_ref, turn_ref, act_ref, out_ref):
-    h = h_ref[...]
+def up_body(step, many, *refs):
+    pair_ref, down_ref, hidden_ref, turn_ref, act_ref = refs[many : many + 5]
+    h = load_part(refs[:many])
     for at, wide in pieces_of(hidden_ref.shape[1], step):
         cols = pl.ds(at, wide)
         gate = mm(h, pair_ref[0, :, cols])
@@ -334,43 +376,48 @@
         hidden_ref[:, cols] = (act * up).astype(BF16)
         turn_ref[:, cols] = (up * d_act).astype(BF16)
         act_ref[:, cols] = act.astype(BF16)
-    out_ref[...] = mm(hidden_ref[...], down_ref[...]).astype(BF16)
+    store_part(refs[many + 5 :], mm(hidden_ref[...], down_ref[...]).astype(BF16))
 
 
 def ffn_forward(h, pair, down, tile=256, step=256):
-    count, width = h.shape
+    count, width = sum(one.shape[0] for one in h), h[0].shape[1]
     units = pair.shape[2]
-    return call(
-        functools.partial(up_body, step),
+    specs = part_specs(tile, width, h)
+    hidden, turn, act, *terms = call(
+        functools.partial(up_body, step, len(h)),
         (count // tile,),
-        [rows_of(tile, width), whole(2, width, units), whole(units, width)],
-        [rows_of(tile, units)] * 3 + [rows_of(tile, width)],
-        [shaped(count, units, dtype=BF16)] * 3 + [shaped(count, width, dtype=BF16)],
+        specs + [whole(2, width, units), whole(units, width)],
+        [rows_of(tile, units)] * 3 + specs,
+        [shaped(count, units, dtype=BF16)] * 3 + [shaped(*one.shape, dtype=BF16) for one in h],
         6 * count * width * units,
-    )(h, pair, down)
-
-
-def down_body(step, d_ref, turn_ref, act_ref, pair_ref, down_ref, pair_out, out_ref):
-    d = d_ref[...]
+    )(*h, pair, down)
+    return hidden, turn, act, terms
+
+
+def down_body(step, many, *refs):
+    turn_ref, act_ref, pair_ref, down_ref, pair_out = refs[many : many + 5]
+    d = load_part(refs[:many])
     for at, wide in pieces_of(turn_ref.shape[1], step):
         cols = pl.ds(at, wide)
         d_hidden = mm_t(d, down_ref[cols, :])
         pair_out[0, :, cols] = (d_hidden * turn_ref[:, cols].astype(F32)).astype(BF16)
         pair_out[1, :, cols] = (d_hidden * act_ref[:, cols].astype(F32)).astype(BF16)
-    out_ref[...] = (mm_t(pair_out[0], pair_ref[0]) + mm_t(pair_out[1], pair_ref[1])).astype(BF16)
+    store_part(refs[many + 5 :], (mm_t(pair_out[0], pair_ref[0]) + mm_t(pair_out[1], pair_ref[1])).astype(BF16))
 
 
 def ffn_backward(d, turn, act, pair, down, tile=256, step=256):
-    count, width = d.shape
+    count, width = sum(one.shape[0] for one in d), d[0].shape[1]
     units = pair.shape[2]
-    return call(
-        functools.partial(down_body, step),
+    specs = part_specs(tile, width, d)
+    d_pair, *terms = call(
+        functools.partial(down_body, step, len(d)),
         (count // tile,),
-        [rows_of(tile, width), rows_of(tile, units), rows_of(tile, units), whole(2, width, units), whole(units, width)],
-        [pl.BlockSpec((2, tile, units), lambda i: (0, i, 0)), rows_of(tile, width)],
-        [shaped(2, count, units, dtype=BF16), shaped(count, width, dtype=BF16)],
+        specs + [rows_of(tile, units), rows_of(tile, units), whole(2, width, units), whole(units, width)],
+        [pl.BlockSpec((2, tile, units), lambda i: (0, i, 0))] + specs,
+        [shaped(2, count, units, dtype=BF16)] + [shaped(*one.shape, dtype=BF16) for one in d],
         6 * count * width * units,
-    )(d, turn, act, pair, down)
+    )(*d, turn, act, pair, down)
+    return d_pair, terms
 
 
 def put(kept_ref, sent_ref, core, index, value):
@@ -384,10 +431,15 @@
 
 
 def grads_body(places, sets, *refs):
-    kept_ref, sent_ref = refs[2 * sets :]
-    total = None
-    for left_ref, right_ref in zip(refs[:sets], refs[sets : 2 * sets], strict=True):
-        term = t_mm(left_ref[...], right_ref[0])
+    kept_ref, sent_ref = refs[-2:]
+    total, at = None, 0
+    for lefts, rights in sets:
+        values = []
+        for many in (lefts, rights):
+            pieces = [ref[...] if len(ref.shape) == 2 else ref[0] for ref in refs[at : at + many]]
+            values.append(jnp.concatenate(pieces, axis=0) if many > 1 else pieces[0])
+            at += many
+        term = t_mm(*values)
         total = term if total is None else total + term
     total = total.astype(BF16)
     tile = total.shape[0]
@@ -404,20 +456,24 @@
                         put(kept_ref, sent_ref, core, index, total[begin - k * tile : end - k * tile])
 
 
-def weight_grads(lefts, rights, places):
-    rows, cols = lefts[0].shape[1], rights[0].shape[2]
-    count = sum(one.shape[0] for one in lefts)
+def weight_grads(sets, places):
+    rows, cols = sets[0][0][0].shape[1], sets[0][1][0].shape[2]
+    count = sum(one.shape[0] for lefts, _ in sets for one in lefts)
     tile = 384 if rows % 384 == 0 else 256
     out = len(places) * rows // 2
+    specs, arrays = [], []
+    for lefts, rights in sets:
+        specs += [pl.BlockSpec((one.shape[0], tile), lambda k, i: (0, i)) for one in lefts]
+        specs += [pl.BlockSpec((1,) + one.shape[1:], lambda k, i: (k, 0, 0)) for one in rights]
+        arrays += [*lefts, *rights]
     return call(
-        functools.partial(grads_body, places, len(lefts)),
+        functools.partial(grads_body, places, [(len(lefts), len(rights)) for lefts, rights in sets]),
         (len(places), rows // tile),
-        [pl.BlockSpec((one.shape[0], tile), lambda k, i: (0, i)) for one in lefts]
-        + [pl.BlockSpec((1,) + one.shape[1:], lambda k, i: (k, 0, 0)) for one in rights],
+        specs,
         [pl.BlockSpec((out, cols), lambda k, i: (0, 0))] * 2,
         [shaped(out, cols, dtype=BF16)] * 2,
         2 * len(places) * count * rows * cols,
-    )(*lefts, *rights)
+    )(*arrays)
 
 
 def outer_body(order, shards, mixed_ref, dattn_ref, h_ref, dq_ref, kept_ref, sent_ref):
@@ -429,16 +485,18 @@
         for core, place, number in order:
             index = (place, slice(at, at + rows), slice(0, wide))
             put(kept_ref, sent_ref, core, index, total[number * rows : (number + 1) * rows])
-        if wide < lanes:
-            empty = jnp.zeros((kept_ref.shape[0], rows, lanes - wide), BF16)
-            kept_ref[:, at : at + rows, wide:] = empty
-            sent_ref[:, at : at + rows, wide:] = empty
+        for ref in (kept_ref, sent_ref):
+            if wide < lanes:
+                ref[:, at : at + rows, wide:] = jnp.zeros((ref.shape[0], rows, lanes - wide), BF16)
         at += rows
+    for ref in (kept_ref, sent_ref):
+        if at < ref.shape[1]:
+            ref[:, at:, :] = jnp.zeros((ref.shape[0], ref.shape[1] - at, lanes), BF16)
 
 
 def outer_grads(order, shards, mixed, d_attn, h, d_q):
     count = mixed.shape[0]
-    shape = (len(order) // 2, sum(shards), max(d_attn.shape[1], d_q.shape[1]))
+    shape = (len(order) // 2, eights(sum(shards)), max(d_attn.shape[1], d_q.shape[1]))
     return call(
         functools.partial(outer_body, order, shards),
         (1,),
@@ -454,13 +512,16 @@
     total = t_mm(h_ref[...], dkv_ref[...]).astype(BF16)
     for core, place, number in order:
         rows = slice(number * shard, (number + 1) * shard)
-        put(kept_ref, sent_ref, core, (place, slice(None), slice(0, SMALL)), small[rows])
-        put(kept_ref, sent_ref, core, (place, slice(None), slice(SMALL, None)), total[rows])
+        put(kept_ref, sent_ref, core, (place, slice(0, shard), slice(0, SMALL)), small[rows])
+        put(kept_ref, sent_ref, core, (place, slice(0, shard), slice(SMALL, None)), total[rows])
+    for ref in (kept_ref, sent_ref):
+        if shard < ref.shape[1]:
+            ref[:, shard:, :] = jnp.zeros((ref.shape[0], ref.shape[1] - shard, ref.shape[2]), BF16)
 
 
 def first_grads(order, shard, h, d_kv, small):
     count, rows = h.shape
-    shape = (len(order) // 2, shard, d_kv.shape[1] + SMALL)
+    shape = (len(order) // 2, eights(shard), d_kv.shape[1] + SMALL)
     return call(
         functools.partial(first_body, order, shard),
         (1,),
@@ -471,12 +532,12 @@
     )(h, d_kv, small)
 
 
-def middle_body(ffn_ref, resid_ref, cot_ref, gains_ref, out_ref, dffn_ref, sums_ref):
-    ffn = ffn_ref[...]
+def middle_body(own_a, own_b, far_a, far_b, resid_ref, cot_ref, gains_ref, out_ref, dffn_a, dffn_b, sums_ref):
+    ffn = load_part((own_a, own_b)) + load_part((far_a, far_b)).astype(F32)
     gain = gains_ref[POST_FFN : POST_FFN + 1]
     out_ref[...] = (resid_ref[...] + ffn * inv_rms(ffn) * gain).astype(BF16)
     d_ffn, terms = rms_back(ffn, gain, cot_ref[...].astype(F32))
-    dffn_ref[...] = d_ffn.astype(BF16)
+    store_part((dffn_a, dffn_b), d_ffn.astype(BF16))
 
     @pl.when(pl.program_id(0) == 0)
     def _():
@@ -485,16 +546,17 @@
     sums_ref[POST_FFN : POST_FFN + 1] += column_sum(terms)
 
 
-def middle(rows, length, ffn, resid, cot, gains):
-    count, width = ffn.shape
+def middle(rows, length, own, far, resid, cot, gains):
+    count, width = resid.shape
+    specs = part_specs(length, width, own)
     return call(
         middle_body,
         (rows,),
-        [rows_of(length, width)] * 3 + [whole(*gains.shape)],
-        [rows_of(length, width)] * 2 + [whole(8, width)],
-        [shaped(count, width, dtype=BF16), shaped(count, width, dtype=BF16), shaped(8, width)],
+        specs * 2 + [rows_of(length, width)] * 2 + [whole(*gains.shape)],
+        [rows_of(length, width)] + specs + [whole(8, width)],
+        [shaped(count, width, dtype=BF16)] + [shaped(count // 2, width, dtype=BF16)] * 2 + [shaped(8, width)],
         20 * count * width,
-    )(ffn, resid, cot, gains)
+    )(*own, *far, resid, cot, gains)
 
 
 def place_body(links, shard, parts, own_ref, other_ref, *refs):
@@ -660,34 +722,35 @@
         flat = array.reshape((count,) + array.shape[2:])
         return lax.all_to_all(flat, PLANE, 0, 0, tiled=True).reshape(array.shape)
 
-    def over_plane(self, rows, first, then=None):
+    def over_plane(self, halves, first):
         if not self.pairs_only:
-            return [first(lax.all_gather(rows, PLANE, axis=0, tiled=True))]
-        half = rows.shape[0] // 2
-        upper, lower = lax.optimization_barrier((rows[:half], rows[half:]))
+            return [first([lax.all_gather(jnp.concatenate(halves), PLANE, axis=0, tiled=True)])]
+        upper, lower = halves
+        size = 2 * upper.shape[0]
         near = lax.optimization_barrier((self.swap(upper, "x"), self.swap(lower, "y")))
         near = jnp.concatenate([upper, near[0], lower, near[1]])
-        upper, lower, near = lax.optimization_barrier((near[: 2 * half], near[2 * half :], near))
-        upper, lower, done = lax.optimization_barrier((self.swap(upper, "y"), self.swap(lower, "x"), first(near)))
-        return [done, first(jnp.concatenate([upper, lower]))]
+        upper, lower, near = lax.optimization_barrier((near[:size], near[size:], near))
+        upper, lower, done = lax.optimization_barrier((self.swap(upper, "y"), self.swap(lower, "x"), first([near])))
+        return [done, first([upper, lower])]
 
     def sum_plane(self, parts, held=(), beside=(None, None)):
         works = [work or (lambda *given: ()) for work in beside]
         if not self.pairs_only:
-            total = lax.psum_scatter(parts[0], PLANE, scatter_dimension=0, tiled=True).astype(F32)
-            return total, works[1](*works[0](*held))
-        near, far = parts
-        half = far.shape[0] // 2
-        quarter = half // 2
-        upper, lower, held = lax.optimization_barrier((far[:half], far[half:], tuple(held)))
+            total = lax.psum_scatter(parts[0][0], PLANE, scatter_dimension=0, tiled=True).astype(F32)
+            half = total.shape[0] // 2
+            empty = [jnp.zeros((half, total.shape[1]), BF16)] * 2
+            return [total[:half], total[half:]], empty, works[1](*works[0](*held))
+        (near,), (upper, lower) = parts
+        quarter = upper.shape[0] // 2
+        upper, lower, held = lax.optimization_barrier((upper, lower, tuple(held)))
         upper, lower, extra = lax.optimization_barrier((self.swap(upper, "y"), self.swap(lower, "x"), works[0](*held)))
         at = [near[k * quarter : (k + 1) * quarter].astype(F32) for k in range(4)]
-        own = (at[0] + upper[:quarter].astype(F32), at[2] + lower[:quarter].astype(F32))
+        own = [at[0] + upper[:quarter].astype(F32), at[2] + lower[:quarter].astype(F32)]
         upper = (at[1] + upper[quarter:].astype(F32)).astype(BF16)
         lower = (at[3] + lower[quarter:].astype(F32)).astype(BF16)
         upper, lower, extra = lax.optimization_barrier((upper, lower, extra))
         upper, lower, extra = lax.optimization_barrier((self.swap(upper, "x"), self.swap(lower, "y"), works[1](*extra)))
-        return jnp.concatenate([own[0] + upper.astype(F32), own[1] + lower.astype(F32)]), extra
+        return own, [upper, lower], extra
 
     def position(self, length):
         return (self.index("z") * self.size["y"] + self.index("y")) * length
@@ -795,7 +858,9 @@
     vectors = jnp.concatenate([g_in, g_post_attn, g_pre_ffn, g_post_ffn, g_query, g_key])
     vectors = lax.optimization_barrier(jnp.pad(vectors, (0, 2 * HEAD - vectors.shape[0])))[None]
     seg_rows = jnp.pad(segment_ids.astype(F32), ((0, 0), (0, 2 * HEAD - length)))
+    used = shard + rows + 1
     kv_shard = jnp.concatenate([jnp.concatenate([w_key, w_value], axis=1), seg_rows, vectors]).astype(BF16)
+    kv_shard = jnp.pad(kv_shard, ((0, eights(used) - used), (0, 0)))
     own_ids = segment_ids.astype(F32).reshape(count, 1)
     kv_shard, own_ids, w_gate, w_up, w_down, w_query, w_out = lax.optimization_barrier(
         (kv_shard, own_ids, w_gate, w_up, w_down, w_query, w_out)
@@ -813,7 +878,8 @@
     q_shard = jnp.pad(w_query.astype(BF16), ((0, 0), (0, wide - HEADS * HEAD)))
     o_shard = jnp.pad(w_out.astype(BF16), ((0, 0), (0, wide - width)))
     out_shard = w_out.shape[0]
-    qo_shard = jnp.concatenate([o_shard, q_shard])
+    used = out_shard + shard
+    qo_shard = jnp.pad(jnp.concatenate([o_shard, q_shard]), ((0, eights(used) - used), (0, 0)))
     pair, qo_shard, kv_along = lax.optimization_barrier((pair, qo_shard, kv_along))
     kv_own, pair, qo_shard = lax.optimization_barrier((links.across_plane(kv_along), pair, qo_shard))
     full_kv, gains, heads, seg_all = links.placed(
@@ -844,13 +910,13 @@
         qo_shard, qo[0], ((0, out_shard, 0, width), (out_shard, shard, 0, HEADS * HEAD)), qo[1]
     )
 
-    q_proj, query, mixed, attn, resid, h_ffn = attend(
+    q_proj, query, mixed, attn, resid, *h_ffn = attend(
         links, rows, length, h_in, tokens_flat, full_query, full_out, gains, heads, cosine, sine, masks, kv
     )
     parts_up = links.over_plane(h_ffn, lambda part: (part, *ffn_forward(part, full_pair, full_down)))
     h_parts, hidden, turn, act, ffn_terms = zip(*parts_up, strict=True)
-    ffn, _ = links.sum_plane(ffn_terms)
-    output, d_ffn, sums_ffn = middle(rows, length, ffn, resid, cot_flat, gains)
+    own, far, _ = links.sum_plane(ffn_terms)
+    output, *d_ffn, sums_ffn = middle(rows, length, own, far, resid, cot_flat, gains)
 
     pending = list(zip(turn, act, strict=True))
 
@@ -872,13 +938,15 @@
     down_places = [(c, 0, c * half, half) for c in range(sc)]
 
     def pair_down(kept, sent):
-        low = weight_grads(hidden, [part[None] for part in d_parts], [down_places])
+        sets = [([left], [one[None] for one in part]) for left, part in zip(hidden, d_parts, strict=True)]
+        low = weight_grads(sets, [down_places])
         return (kept, links.swap(sent, "core"), *low)
 
-    d_hffn, (kept, got, *grad_down) = links.sum_plane(
-        d_terms, d_pairs, (lambda *pairs: weight_grads(h_parts, pairs, places), pair_down)
-    )
-    d_hffn, half_pair = lax.optimization_barrier((d_hffn, (kept.astype(F32) + got.astype(F32)).astype(BF16)))
+    def pair_grads(*pairs):
+        return weight_grads([(part, [pair]) for part, pair in zip(h_parts, pairs, strict=True)], places)
+
+    own, far, (kept, got, *grad_down) = links.sum_plane(d_terms, d_pairs, (pair_grads, pair_down))
+    own, far, half_pair = lax.optimization_barrier((own, far, (kept.astype(F32) + got.astype(F32)).astype(BF16)))
     grad_pair = links.sum_z_low(half_pair)
 
     def by_member(sums):
@@ -889,7 +957,7 @@
         return jnp.transpose(got, (2, 3, 0, 4, 5, 1, 6)).reshape(2, shard, parts * hidden_shard).astype(F32)
 
     d_res, d_attn, d_qproj, sums_attn, heads_attn, *terms = attend_back(
-        links, rows, length, d_hffn, cot_flat, resid, attn, q_proj, query, full_out, gains, heads, cosine, sine, masks, kv,
+        links, rows, length, own, far, cot_flat, resid, attn, q_proj, query, full_out, gains, heads, cosine, sine, masks, kv,
         links.window_kinds(length),
     )
     d_kv, beside = links.window_back(
@@ -924,14 +992,14 @@
     return (
         output.reshape(tokens.shape),
         grad_tokens.reshape(tokens.shape),
-        second_sum[out_shard:, : HEADS * HEAD],
-        first_sum[:, SMALL : SMALL + HEAD],
-        first_sum[:, SMALL + HEAD :],
+        second_sum[out_shard : out_shard + shard, : HEADS * HEAD],
+        first_sum[:shard, SMALL : SMALL + HEAD],
+        first_sum[:shard, SMALL + HEAD :],
         second_sum[:out_shard, :width],
         grad_pair[0],
         grad_pair[1],
         grad_down,
-        *(first_sum[:, k] for k in range(4)),
+        *(first_sum[:shard, k] for k in range(4)),
         *(first_sum[:head_shard, 4 + k] for k in range(2)),
     )
 

time: 647 us -> 641 us (level)
  local copies, waits for them, and re-layouts: 59.3 us -> 36.7 us
  waiting for transfers between devices: 222 us -> 234 us
    all_gather x2, waiting for transfers between devices: 12.9 us -> 20.9 us  [gather_cz(): return lax.all_gather(array, ('core', 'z'), axis=dim, tiled=True)]
    slice x7 -> x3, local copies, waits for them, and re-layouts: 10 us -> 2.05 us  [the longest x1 0.74 us: on_device(): first_sum[:shard, k]]
  transfers between devices with their start and end apart: 54 -> 54, of which waited for: 25 -> 25; matrix products, arithmetic and copies ran while one was open for 12% -> 10% of each run, Pallas kernels for 25% -> 25%
where the time goes in v5:
time: 641 us; the launch traced here: 630 us
  waiting for transfers between devices  234 us (37%)
  Pallas kernels  213 us (33%)
  starting transfers between devices  80.7 us (13%)
  other arithmetic  51 us (8%)
  local copies, waits for them, and re-layouts  36.7 us (6%)
  between operations  14.7 us (2%)
    ppermute x32, waiting for transfers between devices, swap(): return lax.ppermute(array, axis, SWAP)  158 us
    pallas_call x2, Pallas kernels, ffn_backward(): call(functools.partial(down_body, step, len(d)), (count // tile,), specs...  49.6 us
    ppermute x9, waiting for transfers between devices, turn(): lax.ppermute(array, 'z', [(i, (i + step) % depth) for i in range(depth)])  44.6 us
    pallas_call x2, Pallas kernels, ffn_forward(): call(functools.partial(up_body, step, len(h)), (count // tile,), specs +...  43.9 us
    pallas_call x2, Pallas kernels, weight_grads(): call(functools.partial(grads_body, places, [(len(lefts), len(rights)) for...  43.6 us
    ppermute x32, starting transfers between devices, swap(): return lax.ppermute(array, axis, SWAP)  30.1 us
    all_gather x2, waiting for transfers between devices, gather_cz(): return lax.all_gather(array, ('core', 'z'), axis=dim, tiled=True)  20.9 us
    pallas_call x1, Pallas kernels, attend_back(): call(functools.partial(attend_back_body, links, len(kv)), (rows,), part_s...  18.3 us
  transfers between devices with their start and end apart: 54, of which 25 were waited for; matrix products, arithmetic and copies ran while one was open for 10% of the time, Pallas kernels for 25%

profile of v5, /device:TPU:0, one launch (start us, length us, event | category | flops | bytes accessed | tf_op | source)
XLA Modules:
  0.0 630.3 jit_solution(3835262568015254803)
XLA Ops:
  48.8 15.4 %collective-permute-done.8 = bf16[72,1152]{1,0:T(8,128)(2,1)S(1)} collective-permute-done((bf16[72,1152]{1,0:T(8,128)(2,1)S(1)}, bf16[72,1152]{1,0:T(8,128)(2,1)S(1)}, u32[]{:S(2)}, u32[]{:S(2)}) %collective-permute-start.8) | collective-permute-done | bytes 165920 | tf_op jit(solution)/shard_map/ppermute | solution.py:633
  96.6 14.1 %collective-permute-done.13 = bf16[4,72,1152]{2,1,0:T(8,128)(2,1)} collective-permute-done((bf16[4,72,1152]{2,1,0:T(8,128)(2,1)S(1)}, bf16[4,72,1152]{2,1,0:T(8,128)(2,1)}, u32[]{:S(2)}, u32[]{:S(2)}) %collective-permute-start.13) | collective-permute-done | bytes 663584 | tf_op jit(solution)/shard_map/ppermute | solution.py:624
  118.7 12.1 %collective-permute-done.15.refs_13_.refs_19_ = bf16[4,128,512]{2,1,0:T(8,128)(2,1)S(1)} collective-permute-done((bf16[4,128,512]{2,1,0:T(8,128)(2,1)}, bf16[4,128,512]{2,1,0:T(8,128)(2,1)S(1)}, u32[]{:S(2)}, u32[]{:S(2)}) %collective-permute-start.15) | collective-permute-done | bytes 524320 | tf_op jit(solution)/shard_map/ppermute | solution.py:624
  130.9 10.1 %collective-permute-done.16.refs_14_.refs_20_ = bf16[4,128,512]{2,1,0:T(8,128)(2,1)} collective-permute-done((bf16[4,128,512]{2,1,0:T(8,128)(2,1)}, bf16[4,128,512]{2,1,0:T(8,128)(2,1)}, u32[]{:S(2)}, u32[]{:S(2)}) %collective-permute-start.16) | collective-permute-done | bytes 524320 | tf_op jit(solution)/shard_map/ppermute | solution.py:624
  147.2 15.0 %shard_map.274 = (f32[512,1024]{1,0:T(8,128)}, bf16[512,1024]{1,0:T(8,128)(2,1)}, bf16[512,1024]{1,0:T(8,128)(2,1)}, f32[512,1152]{1,0:T(8,128)}, f32[512,1152]{...) custom-call(bf16[512,1152]{1,0:T(8,128)(2,1)} %get-tuple-element.173.refs_0_.h_ref, ...), custom_call_target="tpu_custom_call" | custom-call | flops 3758096384 | bytes 20185088 | tf_op jit(solution)/shard_map/pallas_call | solution.py:228
  164.2 12.3 %collective-permute-done.18 = bf16[256,1152]{1,0:T(8,128)(2,1)S(1)} collective-permute-done((bf16[256,1152]{1,0:T(8,128)(2,1)}, bf16[256,1152]{1,0:T(8,128)(2,1)S(1)}, u32[]{:S(2)}, u32[]{:S(2)}) %collective-permute-start.18) | collective-permute-done | bytes 589856 | tf_op jit(solution)/shard_map/ppermute | solution.py:624
  182.7 20.9 %all-gather.3.cloned.1.call-done = bf16[4,576,1792]{2,1,0:T(8,128)(2,1)} async-done(((bf16[4,72,1792]{2,1,0:T(8,128)(2,1)}), bf16[4,576,1792]{2,1,0:T(8,128)(2,1)}) %all-gather.3.cloned.1.call-update) | async-done | bytes 8257552 | tf_op jit(solution)/shard_map/all_gather | solution.py:684
  203.7 21.1 %shard_map.275 = (bf16[1024,1792]{1,0:T(8,128)(2,1)}, bf16[1024,1792]{1,0:T(8,128)(2,1)}, bf16[1024,1792]{1,0:T(8,128)(2,1)}, bf16[1024,1152]{1,0:T(8,128)(2,1)}) custom-call(bf16[1024,1152]{1,0:T(8,128)(2,1)} %pad_maximum_fusion.1.refs_0_, bf16[2,1152,1792]{2,1,0:T(8,128)(2,1)} %bitcast.79, ...), custom_call_target="tpu_custom_call" | custom-call | flops 12683575296 | bytes 26738688 | tf_op jit(solution)/shard_map/pallas_call | solution.py:386
  225.8 22.8 %shard_map.276 = (bf16[1024,1792]{1,0:T(8,128)(2,1)}, bf16[1024,1792]{1,0:T(8,128)(2,1)}, bf16[1024,1792]{1,0:T(8,128)(2,1)}, bf16[512,1152]{1,0:T(8,128)(2,1)}, bf16[512,1152]{1,0:T(8,128)(2,1)}) custom-call(bf16[512,1152]{1,0:T(8,128)(2,1)} %copy-done.24, bf16[512,1152]{1,0:T(8,128)(2,1)} %collective-permute-done.21.refs_1_.refs_3_, ...), custom_call_target="tpu_custom_call" | custom-call | flops 12683575296 | bytes 26738688 | tf_op jit(solution)/shard_map/pallas_call | solution.py:386
  251.5 25.4 %collective-permute-done.22 = bf16[512,1152]{1,0:T(8,128)(2,1)S(1)} collective-permute-done((bf16[512,1152]{1,0:T(8,128)(2,1)}, bf16[512,1152]{1,0:T(8,128)(2,1)S(1)}, u32[]{:S(2)}, u32[]{:S(2)}) %collective-permute-start.22) | collective-permute-done | bytes 1179680 | tf_op jit(solution)/shard_map/ppermute | solution.py:624
  282.0 12.3 %collective-permute-done.24.far_a = bf16[256,1152]{1,0:T(8,128)(2,1)S(1)} collective-permute-done((bf16[256,1152]{1,0:T(8,128)(2,1)S(1)}, bf16[256,1152]{1,0:T(8,128)(2,1)S(1)}, u32[]{:S(2)}, u32[]{:S(2)}) %collective-permute-start.24) | collective-permute-done | bytes 589856 | tf_op jit(solution)/shard_map/ppermute | solution.py:624
  303.3 12.2 %collective-permute-done.26 = bf16[256,1152]{1,0:T(8,128)(2,1)S(1)} collective-permute-done((bf16[256,1152]{1,0:T(8,128)(2,1)}, bf16[256,1152]{1,0:T(8,128)(2,1)S(1)}, u32[]{:S(2)}, u32[]{:S(2)}) %collective-permute-start.26) | collective-permute-done | bytes 589856 | tf_op jit(solution)/shard_map/ppermute | solution.py:624
  320.9 24.6 %shard_map.278 = (bf16[2,1024,1792]{2,1,0:T(8,128)(2,1)}, bf16[1024,1152]{1,0:T(8,128)(2,1)}) custom-call(bf16[1024,1152]{1,0:T(8,128)(2,1)} %pad_maximum_fusion.2.refs_0_, bf16[1024,1792]{1,0:T(8,128)(2,1)} %get-tuple-element.227.refs_1_, bf16[1024,1792]{1,0:T(8,128)(2,1)} %get-tuple-element.228.refs_2_, bf16[2,1152,1792]{2,1,0:T(8,128)(2,1)} %bitcast.81, ...), custom_call_target="tpu_custom_call" | custom-call | flops 12683575296 | bytes 19398656 | tf_op jit(solution)/shard_map/pallas_call | solution.py:412
  346.9 25.0 %shard_map.279 = (bf16[2,1024,1792]{2,1,0:T(8,128)(2,1)}, bf16[512,1152]{1,0:T(8,128)(2,1)}, bf16[512,1152]{1,0:T(8,128)(2,1)}) custom-call(bf16[512,1152]{1,0:T(8,128)(2,1)} %copy-done.25, bf16[512,1152]{1,0:T(8,128)(2,1)} %copy-done.26, bf16[1024,1792]{1,0:T(8,128)(2,1)} %get-tuple-element.234.refs_2_, bf16[1024,1792]{1,0:T(8,128)(2,1)} %get-tuple-element.235.refs_3_, ...), custom_call_target="tpu_custom_call" | custom-call | flops 12683575296 | bytes 19398656 | tf_op jit(solution)/shard_map/pallas_call | solution.py:412
  374.1 26.9 %shard_map.280 = (bf16[1152,1792]{1,0:T(8,128)(2,1)}, bf16[1152,1792]{1,0:T(8,128)(2,1)}) custom-call(bf16[1024,1152]{1,0:T(8,128)(2,1)} %pad_maximum_fusion.1.refs_0_, bf16[2,1024,1792]{2,1,0:T(8,128)(2,1)} %get-tuple-element.243.refs_1_, bf16[512,1152]{1,0:T(8,128)(2,1)} %copy-done.24, bf16[512,1152]{1,0:T(8,128)(2,1)} %collective-permute-done.21.refs_1_.refs_3_, ...), custom_call_target="tpu_custom_call" | custom-call | flops 16911433728 | bytes 16515072 | tf_op jit(solution)/shard_map/pallas_call | solution.py:469
  404.7 16.7 %shard_map.281 = (bf16[896,1152]{1,0:T(8,128)(2,1)}, bf16[896,1152]{1,0:T(8,128)(2,1)}) custom-call(bf16[1024,1792]{1,0:T(8,128)(2,1)} %get-tuple-element.255.refs_0_, bf16[1,1024,1152]{2,1,0:T(8,128)(2,1)} %bitcast.69, bf16[1024,1792]{1,0:T(8,128)(2,1)} %get-tuple-element.257.refs_2_, bf16[1,512,1152]{2,1,0:T(8,128)(2,1)} %bitcast.85, ...), custom_call_target="tpu_custom_call" | custom-call | flops 8455716864 | bytes 8257536 | tf_op jit(solution)/shard_map/pallas_call | solution.py:469
  427.1 18.3 %shard_map.282 = (f32[512,1152]{1,0:T(8,128)}, bf16[512,1152]{1,0:T(8,128)(2,1)}, bf16[512,1024]{1,0:T(8,128)(2,1)}, f32[8,1152]{1,0:T(8,128)}, f32[8,256]{1,0:T...) custom-call(f32[256,1152]{1,0:T(8,128)} %get-tuple-element.264.refs_, ...), custom_call_target="tpu_custom_call" | custom-call | flops 4563402752 | bytes 17653760 | tf_op jit(solution)/shard_map/pallas_call | solution.py:299
  445.4 9.2 %shard_map.283 = (bf16[16,72,1152]{2,1,0:T(8,128)(2,1)}, bf16[16,72,1152]{2,1,0:T(8,128)(2,1)}) custom-call(bf16[512,1024]{1,0:T(8,128)(2,1)} %get-tuple-element.274.mixed_ref, bf16[512,1152]{1,0:T(8,128)(2,1)} %get-tuple-element.275.dattn_ref, bf16[512,1152]{1,0:T(8,128)(2,1)} %get-tuple-element.173.refs_0_.h_ref, bf16[512,1024]{1,0:T(8,128)(2,1)} %get-tuple-element.276.dq_ref), custom_call_target="tpu_custom_call" | custom-call | flops 2415919104 | bytes 10616832 | tf_op jit(solution)/shard_map/pallas_call | solution.py:500
  470.1 10.3 %collective-permute-done.36 = bf16[4,128,512]{2,1,0:T(8,128)(2,1)S(1)} collective-permute-done((bf16[4,128,512]{2,1,0:T(8,128)(2,1)}, bf16[4,128,512]{2,1,0:T(8,128)(2,1)S(1)}, u32[]{:S(2)}, u32[]{:S(2)}) %collective-permute-start.36) | collective-permute-done | bytes 524320 | tf_op jit(solution)/shard_map/ppermute | solution.py:624
  487.1 25.2 %collective-permute-done.41 = bf16[2,4,72,1152]{3,2,1,0:T(8,128)(2,1)} collective-permute-done((bf16[2,4,72,1152]{3,2,1,0:T(8,128)(2,1)}, bf16[2,4,72,1152]{3,2,1,0:T(8,128)(2,1)}, u32[]{:S(2)}, u32[]{:S(2)}) %collective-permute-start.41) | collective-permute-done | bytes 1327136 | tf_op jit(solution)/shard_map/ppermute | solution.py:624
  537.2 9.7 %shard_map.284 = (bf16[512,512]{1,0:T(8,128)(2,1)}, bf16[512,1152]{1,0:T(8,128)(2,1)}, f32[8,1152]{1,0:T(8,128)}, f32[8,256]{1,0:T(8,128)}) custom-call(f32[4,128,512]{2,1,0:T(8,128)} %fusion.4.dkv_ref, f32[512,256]{1,0:T(8,128)} %get-tuple-element.290.kproj_ref, bf16[512,1024]{1,0:T(8,128)(2,1)} %get-tuple-element.276.dq_ref, bf16[512,1152]{1,0:T(8,128)(2,1)} %bitcast.62, ...), custom_call_target="tpu_custom_call" | custom-call | flops 1811939328 | bytes 3497984 | tf_op jit(solution)/shard_map/pallas_call | solution.py:347
  562.4 14.3 %all-to-all-start.2 = ((bf16[16,40,640]{2,1,0:T(8,128)(2,1)}), bf16[16,40,640]{2,1,0:T(8,128)(2,1)S(1)}, u32[]{:S(2)}, u32[]{:S(2)}) async-start(bf16[16,40,640]{2,1,0:T(8,128)(2,1)} %add_convert_fusion.3), calls=%async_computation.3 | async-start | bytes 1638400 | tf_op jit(solution)/shard_map/all_to_all | solution.py:717
  593.9 12.6 %collective-permute-done.43 = bf16[72,1152]{1,0:T(8,128)(2,1)S(1)} collective-permute-done((bf16[72,1152]{1,0:T(8,128)(2,1)}, bf16[72,1152]{1,0:T(8,128)(2,1)S(1)}, u32[]{:S(2)}, u32[]{:S(2)}) %collective-permute-start.43) | collective-permute-done | bytes 165920 | tf_op jit(solution)/shard_map/ppermute | solution.py:633
  606.5 10.2 %collective-permute-done.44 = bf16[72,1152]{1,0:T(8,128)(2,1)} collective-permute-done((bf16[72,1152]{1,0:T(8,128)(2,1)}, bf16[72,1152]{1,0:T(8,128)(2,1)}, u32[]{:S(2)}, u32[]{:S(2)}) %collective-permute-start.44) | collective-permute-done | bytes 165920 | tf_op jit(solution)/shard_map/ppermute | solution.py:633
  (235 shorter events, 218.8 us)
Async XLA Ops:
  7.2 175.6 %all-gather.5.cloned.1.call-start = ((), (), s32[]{:S(2)}) async-start(), calls=%async_computation.6 | async-start | bytes 4644864 | tf_op jit(solution)/shard_map/all_gather | solution.py:684
  39.3 31.3 %collective-permute-start.6 = (bf16[16,48,512]{2,1,0:T(8,128)(2,1)S(1)}, bf16[16,48,512]{2,1,0:T(8,128)(2,1)}, u32[]{:S(2)}, u32[]{:S(2)}) collective-permute-start(bf16[16,48,512]{2,1,0:T(8,128)(2,1)S(1)} %pad_maximum_fusion.8.own_ref), channel_id=1, source_target_pairs={{0,8},{8,0},{1,9},{9,1},{2,10},{10,2},{3,11},{11,3},{4,12},{12,4},... | collective-permute-start | bytes 2359304 | tf_op jit(solution)/shard_map/ppermute | solution.py:624
  41.1 37.5 %all-to-all-start = ((bf16[4,2,36,1792]{3,1,2,0:T(2,128)(2,1)}), bf16[4,2,36,1792]{3,1,2,0:T(2,128)(2,1)S(1)}, u32[]{:S(2)}, u32[]{:S(2)}) async-start(bf16[4,2,36,1792]{3,1,2,0:T(2,128)(2,1)} %bitcast.12), calls=%async_computation | async-start | bytes 2064384 | tf_op jit(solution)/shard_map/all_to_all | solution.py:723
  44.7 159.0 %all-gather.3.cloned.1.call-start = ((), (), s32[]{:S(2)}) async-start(), calls=%async_computation.5 | async-start | bytes 9289728 | tf_op jit(solution)/shard_map/all_gather | solution.py:684
  80.5 30.2 %collective-permute-start.13 = (bf16[4,72,1152]{2,1,0:T(8,128)(2,1)S(1)}, bf16[4,72,1152]{2,1,0:T(8,128)(2,1)}, u32[]{:S(2)}, u32[]{:S(2)}) collective-permute-start(bf16[4,72,1152]{2,1,0:T(8,128)(2,1)S(1)} %pad_maximum_fusion.9), channel_id=1, source_target_pairs={{0,1},{1,0},{2,3},{3,2},{4,5},{5,4},{6,7},{7,6},{8,9},{9,8},{10,11... | collective-permute-start | bytes 1990664 | tf_op jit(solution)/shard_map/ppermute | solution.py:624
  82.0 28.7 %collective-permute-start.14 = (bf16[4,72,1152]{2,1,0:T(8,128)(2,1)S(1)}, bf16[4,72,1152]{2,1,0:T(8,128)(2,1)}, u32[]{:S(2)}, u32[]{:S(2)}) collective-permute-start(bf16[4,72,1152]{2,1,0:T(8,128)(2,1)S(1)} %pad_maximum_fusion.9), channel_id=1, source_target_pairs={{0,17},{1,16},{16,1},{17,0},{2,19},{3,18},{18,3},{19,2},{4,21},{5,... | collective-permute-start | bytes 1990664 | tf_op jit(solution)/shard_map/ppermute | solution.py:645
  82.2 30.5 %collective-permute-start.10 = (bf16[4,128,512]{2,1,0:T(8,128)(2,1)}, bf16[4,128,512]{2,1,0:T(8,128)(2,1)}, u32[]{:S(2)}, u32[]{:S(2)}) collective-permute-start(bf16[4,128,512]{2,1,0:T(8,128)(2,1)} %get-tuple-element.177.refs_10_.refs_16_), channel_id=1, source_target_pairs={{0,2},{2,4},{4,6},{1,3},{3,5},{5,7},{8,10},{10,12},{12,14},{9,11},... | collective-permute-start | bytes 1572872 | tf_op jit(solution)/shard_map/ppermute | solution.py:629
  112.7 411.1 %reduce-scatter.3.cloned.1.call-start = ((), (), s32[]{:S(2)}) async-start(), calls=%async_computation.7 | async-start | bytes 5160960 | tf_op jit(solution)/shard_map/reduce_scatter | solution.py:710
  112.7 28.2 %collective-permute-start.17 = (bf16[16,72,1152]{2,1,0:T(8,128)(2,1)S(1)}, bf16[16,72,1152]{2,1,0:T(8,128)(2,1)}, u32[]{:S(2)}, u32[]{:S(2)}) collective-permute-start(bf16[16,72,1152]{2,1,0:T(8,128)(2,1)S(1)} %pad_maximum_fusion.own_ref), channel_id=1, source_target_pairs={{0,8},{8,0},{1,9},{9,1},{2,10},{10,2},{3,11},{11,3},{4,12},{12,4},... | collective-permute-start | bytes 7962632 | tf_op jit(solution)/shard_map/ppermute | solution.py:624
  180.4 44.4 %collective-permute-start.20 = (bf16[512,1152]{1,0:T(8,128)(2,1)S(1)}, bf16[512,1152]{1,0:T(8,128)(2,1)S(1)}, u32[]{:S(2)}, u32[]{:S(2)}) collective-permute-start(bf16[512,1152]{1,0:T(8,128)(2,1)S(1)} %get-tuple-element.196), channel_id=1, source_target_pairs={{0,1},{1,0},{2,3},{3,2},{4,5},{5,4},{6,7},{7,6},{8,9},{9,8},{10,11... | collective-permute-start | bytes 3538952 | tf_op jit(solution)/shard_map/ppermute | solution.py:624
  181.2 43.6 %collective-permute-start.21 = (bf16[512,1152]{1,0:T(8,128)(2,1)S(1)}, bf16[512,1152]{1,0:T(8,128)(2,1)}, u32[]{:S(2)}, u32[]{:S(2)}) collective-permute-start(bf16[512,1152]{1,0:T(8,128)(2,1)S(1)} %get-tuple-element.197), channel_id=1, source_target_pairs={{0,16},{16,0},{1,17},{17,1},{2,18},{18,2},{3,19},{19,3},{4,20},{20... | collective-permute-start | bytes 3538952 | tf_op jit(solution)/shard_map/ppermute | solution.py:624
  248.6 28.3 %collective-permute-start.22 = (bf16[512,1152]{1,0:T(8,128)(2,1)}, bf16[512,1152]{1,0:T(8,128)(2,1)S(1)}, u32[]{:S(2)}, u32[]{:S(2)}) collective-permute-start(bf16[512,1152]{1,0:T(8,128)(2,1)} %get-tuple-element.210), channel_id=1, source_target_pairs={{0,1},{1,0},{2,3},{3,2},{4,5},{5,4},{6,7},{7,6},{8,9},{9,8},{10,11... | collective-permute-start | bytes 3538952 | tf_op jit(solution)/shard_map/ppermute | solution.py:624
  250.0 28.0 %collective-permute-start.23 = (bf16[512,1152]{1,0:T(8,128)(2,1)}, bf16[512,1152]{1,0:T(8,128)(2,1)S(1)}, u32[]{:S(2)}, u32[]{:S(2)}) collective-permute-start(bf16[512,1152]{1,0:T(8,128)(2,1)} %get-tuple-element.211), channel_id=1, source_target_pairs={{0,16},{16,0},{1,17},{17,1},{2,18},{18,2},{3,19},{19,3},{4,20},{20... | collective-permute-start | bytes 3538952 | tf_op jit(solution)/shard_map/ppermute | solution.py:624
  318.9 26.6 %collective-permute-start.28 = (bf16[512,1152]{1,0:T(8,128)(2,1)S(1)}, bf16[512,1152]{1,0:T(8,128)(2,1)S(1)}, u32[]{:S(2)}, u32[]{:S(2)}) collective-permute-start(bf16[512,1152]{1,0:T(8,128)(2,1)S(1)} %pad_maximum_fusion.5), channel_id=1, source_target_pairs={{0,1},{1,0},{2,3},{3,2},{4,5},{5,4},{6,7},{7,6},{8,9},{9,8},{10,11... | collective-permute-start | bytes 3538952 | tf_op jit(solution)/shard_map/ppermute | solution.py:624
  371.9 29.1 %collective-permute-start.30 = (bf16[512,1152]{1,0:T(8,128)(2,1)}, bf16[512,1152]{1,0:T(8,128)(2,1)S(1)}, u32[]{:S(2)}, u32[]{:S(2)}) collective-permute-start(bf16[512,1152]{1,0:T(8,128)(2,1)} %get-tuple-element.240), channel_id=1, source_target_pairs={{0,1},{1,0},{2,3},{3,2},{4,5},{5,4},{6,7},{7,6},{8,9},{9,8},{10,11... | collective-permute-start | bytes 3538952 | tf_op jit(solution)/shard_map/ppermute | solution.py:624
  373.3 27.7 %collective-permute-start.31 = (bf16[512,1152]{1,0:T(8,128)(2,1)}, bf16[512,1152]{1,0:T(8,128)(2,1)S(1)}, u32[]{:S(2)}, u32[]{:S(2)}) collective-permute-start(bf16[512,1152]{1,0:T(8,128)(2,1)} %get-tuple-element.241), channel_id=1, source_target_pairs={{0,16},{16,0},{1,17},{17,1},{2,18},{18,2},{3,19},{19,3},{4,20},{20... | collective-permute-start | bytes 3538952 | tf_op jit(solution)/shard_map/ppermute | solution.py:624
  427.1 30.0 %collective-permute-start.38 = (bf16[896,1152]{1,0:T(8,128)(2,1)}, bf16[896,1152]{1,0:T(8,128)(2,1)}, u32[]{:S(2)}, u32[]{:S(2)}) collective-permute-start(bf16[896,1152]{1,0:T(8,128)(2,1)} %get-tuple-element.280), channel_id=1, source_target_pairs={{0,8},{8,0},{1,9},{9,1},{2,10},{10,2},{3,11},{11,3},{4,12},{12,4},... | collective-permute-start | bytes 6193160 | tf_op jit(solution)/shard_map/ppermute | solution.py:624
  481.6 30.7 %collective-permute-start.41 = (bf16[2,4,72,1152]{3,2,1,0:T(8,128)(2,1)}, bf16[2,4,72,1152]{3,2,1,0:T(8,128)(2,1)}, u32[]{:S(2)}, u32[]{:S(2)}) collective-permute-start(bf16[2,4,72,1152]{3,2,1,0:T(8,128)(2,1)} %dynamic-slice_bitcast_fusion), channel_id=1, source_target_pairs={{0,16},{16,0},{1,17},{17,1},{2,18},{18,2},{3,19},{19,3},{4,20},{20... | collective-permute-start | bytes 3981320 | tf_op jit(solution)/shard_map/ppermute | solution.py:624
  484.5 38.4 %collective-permute-start.39 = (bf16[4,128,512]{2,1,0:T(8,128)(2,1)S(1)}, bf16[4,128,512]{2,1,0:T(8,128)(2,1)S(1)}, u32[]{:S(2)}, u32[]{:S(2)}) collective-permute-start(bf16[4,128,512]{2,1,0:T(8,128)(2,1)S(1)} %get-tuple-element.331), channel_id=1, source_target_pairs={{4,0},{6,2},{5,1},{7,3},{12,8},{14,10},{13,9},{15,11},{20,16},{22,... | collective-permute-start | bytes 1572872 | tf_op jit(solution)/shard_map/ppermute | solution.py:629
  485.8 37.9 %collective-permute-start.40 = (bf16[4,128,512]{2,1,0:T(8,128)(2,1)S(1)}, bf16[4,128,512]{2,1,0:T(8,128)(2,1)}, u32[]{:S(2)}, u32[]{:S(2)}) collective-permute-start(bf16[4,128,512]{2,1,0:T(8,128)(2,1)S(1)} %get-tuple-element.330), channel_id=1, source_target_pairs={{2,0},{4,2},{6,4},{3,1},{5,3},{7,5},{10,8},{12,10},{14,12},{11,9},... | collective-permute-start | bytes 1572872 | tf_op jit(solution)/shard_map/ppermute | solution.py:629
  534.2 87.3 %reduce-scatter.5.cloned.1.call-start = ((), (), s32[]{:S(2)}) async-start(), calls=%async_computation.8 | async-start | bytes 2580480 | tf_op jit(solution)/shard_map/reduce_scatter | solution.py:710
  562.4 56.9 %all-to-all-start.2 = ((bf16[16,40,640]{2,1,0:T(8,128)(2,1)}), bf16[16,40,640]{2,1,0:T(8,128)(2,1)S(1)}, u32[]{:S(2)}, u32[]{:S(2)}) async-start(bf16[16,40,640]{2,1,0:T(8,128)(2,1)} %add_convert_fusion.3), calls=%async_computation.3 | async-start | bytes 1638400 | tf_op jit(solution)/shard_map/all_to_all | solution.py:717
  581.9 34.8 %collective-permute-start.44 = (bf16[72,1152]{1,0:T(8,128)(2,1)}, bf16[72,1152]{1,0:T(8,128)(2,1)}, u32[]{:S(2)}, u32[]{:S(2)}) collective-permute-start(bf16[72,1152]{1,0:T(8,128)(2,1)} %get-tuple-element.329), channel_id=1, source_target_pairs={{0,4},{2,6},{4,0},{6,2},{1,5},{3,7},{5,1},{7,3},{8,12},{10,14},{12... | collective-permute-start | bytes 497672 | tf_op jit(solution)/shard_map/ppermute | solution.py:633
  584.3 32.4 %collective-permute-start.45 = (bf16[72,1152]{1,0:T(8,128)(2,1)S(1)}, bf16[72,1152]{1,0:T(8,128)(2,1)}, u32[]{:S(2)}, u32[]{:S(2)}) collective-permute-start(bf16[72,1152]{1,0:T(8,128)(2,1)S(1)} %get-tuple-element.328), channel_id=1, source_target_pairs={{0,6},{2,0},{4,2},{6,4},{1,7},{3,1},{5,3},{7,5},{8,14},{10,8},{12,... | collective-permute-start | bytes 497672 | tf_op jit(solution)/shard_map/ppermute | solution.py:633
  (57 other events, 778.9 us)
Sparse Core Ops, SparseCore 0:
  12.7 62.3 all-gather.4
  112.8 90.8 all-gather.2
  427.2 83.9 reduce-scatter.2
  537.2 58.6 reduce-scatter.4

commit v6 on v5

--- a/solution.py
+++ b/solution.py
@@ -321,9 +321,13 @@
     )(*own, *far, cot, resid, attn, qproj, query, wo, gains, heads, cosine, sine, *masks, *kv)
 
 
-def finish_body(dkv_ref, kproj_ref, dq_ref, tok_ref, dres_ref, wq_ref, wkv_ref, gains_ref, head_ref, cos_ref, sin_ref,
+def finish_body(many, *refs):
+    finish_rows(refs[:many], *refs[many:])
+
+
+def finish_rows(dkv_refs, kproj_ref, dq_ref, tok_ref, dres_ref, wq_ref, wkv_ref, gains_ref, head_ref, cos_ref, sin_ref,
                 dkvp_ref, grad_ref, sums_ref, head_sums_ref):
-    d_kv = dkv_ref[0]
+    d_kv = sum(ref[0].astype(F32) for ref in dkv_refs)
     turned = rotate(d_kv[:, :HEAD], cos_ref[...], -sin_ref[...])
     d_key, key_terms = rms_back(kproj_ref[...], head_ref[1:2], turned)
     d_proj = jnp.concatenate([d_key.astype(BF16), d_kv[:, HEAD:].astype(BF16)], axis=1)
@@ -345,16 +349,17 @@
     count, width = tokens.shape
     wide = HEADS * HEAD
     return call(
-        finish_body,
+        functools.partial(finish_body, len(dkv)),
         (rows,),
-        [row_block(length, 2 * HEAD), rows_of(length, HEAD), rows_of(length, wide)]
+        [row_block(length, 2 * HEAD)] * len(dkv)
+        + [rows_of(length, HEAD), rows_of(length, wide)]
         + [rows_of(length, width)] * 2
         + [whole(*one.shape) for one in (wq, wkv, gains, heads)]
         + [whole(length, HALF)] * 2,
         [rows_of(length, 2 * HEAD), rows_of(length, width), whole(8, width), whole(8, HEAD)],
         [shaped(count, 2 * HEAD, dtype=BF16), shaped(count, width, dtype=BF16), shaped(8, width), shaped(8, HEAD)],
         2 * count * width * (wide + 2 * HEAD),
-    )(dkv, kproj, dq, tokens, dres, wq, wkv, gains, heads, cosine, sine)
+    )(*dkv, kproj, dq, tokens, dres, wq, wkv, gains, heads, cosine, sine)
 
 
 def pieces_of(total, step):
@@ -713,9 +718,10 @@
         sx, sy, sz = (self.size[axis] for axis in "xyz")
         return self.sum_halves(array.reshape((sx, sy, sz) + array.shape[1:]), "x", 0)
 
-    def sum_all_small(self, array):
-        got = lax.all_to_all(array, ("x", "z", "y"), 0, 0, tiled=True)
-        return jnp.sum(got.astype(F32), axis=0)
+    def to_members(self, array):
+        count = self.size["x"] * self.size["y"]
+        got = lax.all_to_all(array.reshape((count, -1) + array.shape[2:]), PLANE, 0, 0, tiled=True)
+        return got.reshape((count, self.size["z"]) + array.shape[1:])
 
     def exchange(self, array):
         count = self.size["x"] * self.size["y"]
@@ -804,10 +810,9 @@
             far, near = far.astype(F32), near.astype(F32)
             two = (two + jnp.where(first, 0.0, far)).astype(BF16)
             one = (one + jnp.where(first, far, near)).astype(BF16)
-            two, one = follow(self.shift(two, -2), self.shift(one, -1))
-            own = own + jnp.where(first, near, 0.0) + one.astype(F32) + two.astype(F32)
-            (own,) = follow(own)
-            return own, results
+            own = own + jnp.where(first, near, 0.0)
+            two, one, own = follow(self.shift(two, -2), self.shift(one, -1), own)
+            return [own, one, two], results
         total = None
         for k in range(reach, -1, -1):
             level = jnp.stack(terms[k * wide : (k + 1) * wide])
@@ -815,7 +820,7 @@
         total = lax.psum_scatter(total.astype(BF16), "y", scatter_dimension=0, tiled=False).astype(F32)
         for _ in beside:
             (total,) = follow(total)
-        return total, results
+        return [total], results
 
 
 def on_device(
@@ -984,10 +989,10 @@
     d_kvproj, second, got_pair = lax.optimization_barrier(
         (d_kvproj, links.sum_halves(second, "y", 0), links.exchange(by_member(grad_pair)))
     )
-    first_grad = first_grads(links.order("xzy"), shard, h_in, d_kvproj, small_terms)
-    first_core = links.sum_cores(*first_grad)
-    first_sum = links.sum_all_small(first_core)
-    second_sum = links.sum_z(second, 0)
+    first_grad = first_grads(links.order("xyz"), shard, h_in, d_kvproj, small_terms)
+    first_core, second, grad_down = lax.optimization_barrier((links.sum_cores(*first_grad), second, grad_down))
+    first_got, second_sum = lax.optimization_barrier((links.to_members(first_core), links.sum_z(second, 0)))
+    first_sum = links.sum_z(jnp.sum(first_got.astype(F32), axis=0).astype(BF16), 0)
     grad_pair = unpacked(got_pair)
     return (
         output.reshape(tokens.shape),

time: 641 us -> 632 us (0.986)
  starting transfers between devices: 80.7 us -> 73.3 us
    ppermute x9 -> x12, waiting for transfers between devices: 44.6 us -> 27.4 us  [turn(): lax.ppermute(array, 'z', [(i, (i + step) % depth) for i in range(depth)])]
    reduce_scatter x2, waiting for transfers between devices: 0.01 us -> 14.3 us  [sum_z_low(): return lax.psum_scatter(array, 'z', scatter_dimension=0, tiled=True)]
    all_to_all x1, starting transfers between devices: 14.3 us -> 4.21 us  [to_members(): lax.all_to_all(array.reshape((count, -1) + array.shape[2:]), PLANE, 0, 0,...]
    ppermute x9 -> x12, starting transfers between devices: 15.9 us -> 18.8 us  [turn(): lax.ppermute(array, 'z', [(i, (i + step) % depth) for i in range(depth)])]
  transfers between devices with their start and end apart: 54 -> 57, of which waited for: 25 -> 27; matrix products, arithmetic and copies ran while one was open for 10% -> 9% of each run, Pallas kernels for 25% -> 26%
where the time goes in v6:
time: 632 us; the launch traced here: 622 us
  waiting for transfers between devices  234 us (37%)
  Pallas kernels  214 us (34%)
  starting transfers between devices  73.3 us (12%)
  other arithmetic  53.1 us (8%)
  local copies, waits for them, and re-layouts  33.5 us (5%)
  between operations  14.7 us (2%)
    ppermute x32, waiting for transfers between devices, swap(): return lax.ppermute(array, axis, SWAP)  159 us
    pallas_call x2, Pallas kernels, ffn_backward(): call(functools.partial(down_body, step, len(d)), (count // tile,), specs...  49.6 us
    pallas_call x2, Pallas kernels, ffn_forward(): call(functools.partial(up_body, step, len(h)), (count // tile,), specs +...  43.9 us
    pallas_call x2, Pallas kernels, weight_grads(): call(functools.partial(grads_body, places, [(len(lefts), len(rights)) for...  43.6 us
    ppermute x32, starting transfers between devices, swap(): return lax.ppermute(array, axis, SWAP)  30.2 us
    ppermute x12, waiting for transfers between devices, turn(): lax.ppermute(array, 'z', [(i, (i + step) % depth) for i in range(depth)])  27.4 us
    all_gather x2, waiting for transfers between devices, gather_cz(): return lax.all_gather(array, ('core', 'z'), axis=dim, tiled=True)  20.9 us
    ppermute x12, starting transfers between devices, turn(): lax.ppermute(array, 'z', [(i, (i + step) % depth) for i in range(depth)])  18.8 us
  transfers between devices with their start and end apart: 57, of which 27 were waited for; matrix products, arithmetic and copies ran while one was open for 9% of the time, Pallas kernels for 26%

profile of v6, /device:TPU:0, one launch (start us, length us, event | category | flops | bytes accessed | tf_op | source)
XLA Modules:
  0.0 622.4 jit_solution(1157188904349113676)
XLA Ops:
  48.9 15.4 %collective-permute-done.8 = bf16[72,1152]{1,0:T(8,128)(2,1)S(1)} collective-permute-done((bf16[72,1152]{1,0:T(8,128)(2,1)S(1)}, bf16[72,1152]{1,0:T(8,128)(2,1)S(1)}, u32[]{:S(2)}, u32[]{:S(2)}) %collective-permute-start.8) | collective-permute-done | bytes 165920 | tf_op jit(solution)/shard_map/ppermute | solution.py:638
  82.2 7.2 %collective-permute-start.10 = (bf16[4,128,512]{2,1,0:T(8,128)(2,1)}, bf16[4,128,512]{2,1,0:T(8,128)(2,1)}, u32[]{:S(2)}, u32[]{:S(2)}) collective-permute-start(bf16[4,128,512]{2,1,0:T(8,128)(2,1)} %get-tuple-element.183.refs_10_.refs_16_), channel_id=1, source_target_pairs={{0,2},{2,4},{4,6},{1,3},{3,5},{5,7},{8,10},{10,12},{12,14},{9,11},... | collective-permute-start | bytes 1572872 | tf_op jit(solution)/shard_map/ppermute | solution.py:634
  96.7 14.1 %collective-permute-done.13 = bf16[4,72,1152]{2,1,0:T(8,128)(2,1)} collective-permute-done((bf16[4,72,1152]{2,1,0:T(8,128)(2,1)S(1)}, bf16[4,72,1152]{2,1,0:T(8,128)(2,1)}, u32[]{:S(2)}, u32[]{:S(2)}) %collective-permute-start.13) | collective-permute-done | bytes 663584 | tf_op jit(solution)/shard_map/ppermute | solution.py:629
  118.8 12.1 %collective-permute-done.15.refs_13_.refs_19_ = bf16[4,128,512]{2,1,0:T(8,128)(2,1)S(1)} collective-permute-done((bf16[4,128,512]{2,1,0:T(8,128)(2,1)}, bf16[4,128,512]{2,1,0:T(8,128)(2,1)S(1)}, u32[]{:S(2)}, u32[]{:S(2)}) %collective-permute-start.15) | collective-permute-done | bytes 524320 | tf_op jit(solution)/shard_map/ppermute | solution.py:629
  130.9 10.1 %collective-permute-done.16.refs_14_.refs_20_ = bf16[4,128,512]{2,1,0:T(8,128)(2,1)} collective-permute-done((bf16[4,128,512]{2,1,0:T(8,128)(2,1)}, bf16[4,128,512]{2,1,0:T(8,128)(2,1)}, u32[]{:S(2)}, u32[]{:S(2)}) %collective-permute-start.16) | collective-permute-done | bytes 524320 | tf_op jit(solution)/shard_map/ppermute | solution.py:629
  147.2 15.0 %shard_map.274 = (f32[512,1024]{1,0:T(8,128)}, bf16[512,1024]{1,0:T(8,128)(2,1)}, bf16[512,1024]{1,0:T(8,128)(2,1)}, f32[512,1152]{1,0:T(8,128)}, f32[512,1152]{...) custom-call(bf16[512,1152]{1,0:T(8,128)(2,1)} %get-tuple-element.179.refs_0_.h_ref, ...), custom_call_target="tpu_custom_call" | custom-call | flops 3758096384 | bytes 20185088 | tf_op jit(solution)/shard_map/pallas_call | solution.py:228
  164.2 12.3 %collective-permute-done.18 = bf16[256,1152]{1,0:T(8,128)(2,1)S(1)} collective-permute-done((bf16[256,1152]{1,0:T(8,128)(2,1)}, bf16[256,1152]{1,0:T(8,128)(2,1)S(1)}, u32[]{:S(2)}, u32[]{:S(2)}) %collective-permute-start.18) | collective-permute-done | bytes 589856 | tf_op jit(solution)/shard_map/ppermute | solution.py:629
  182.8 20.9 %all-gather.3.cloned.1.call-done = bf16[4,576,1792]{2,1,0:T(8,128)(2,1)} async-done(((bf16[4,72,1792]{2,1,0:T(8,128)(2,1)}), bf16[4,576,1792]{2,1,0:T(8,128)(2,1)}) %all-gather.3.cloned.1.call-update) | async-done | bytes 8257552 | tf_op jit(solution)/shard_map/all_gather | solution.py:689
  203.7 21.2 %shard_map.275 = (bf16[1024,1792]{1,0:T(8,128)(2,1)}, bf16[1024,1792]{1,0:T(8,128)(2,1)}, bf16[1024,1792]{1,0:T(8,128)(2,1)}, bf16[1024,1152]{1,0:T(8,128)(2,1)}) custom-call(bf16[1024,1152]{1,0:T(8,128)(2,1)} %pad_maximum_fusion.1.refs_0_, bf16[2,1152,1792]{2,1,0:T(8,128)(2,1)} %bitcast.90, ...), custom_call_target="tpu_custom_call" | custom-call | flops 12683575296 | bytes 26738688 | tf_op jit(solution)/shard_map/pallas_call | solution.py:391
  225.9 22.7 %shard_map.276 = (bf16[1024,1792]{1,0:T(8,128)(2,1)}, bf16[1024,1792]{1,0:T(8,128)(2,1)}, bf16[1024,1792]{1,0:T(8,128)(2,1)}, bf16[512,1152]{1,0:T(8,128)(2,1)}, bf16[512,1152]{1,0:T(8,128)(2,1)}) custom-call(bf16[512,1152]{1,0:T(8,128)(2,1)} %copy-done.26, bf16[512,1152]{1,0:T(8,128)(2,1)} %collective-permute-done.21.refs_1_.refs_3_, ...), custom_call_target="tpu_custom_call" | custom-call | flops 12683575296 | bytes 26738688 | tf_op jit(solution)/shard_map/pallas_call | solution.py:391
  251.6 25.4 %collective-permute-done.22 = bf16[512,1152]{1,0:T(8,128)(2,1)S(1)} collective-permute-done((bf16[512,1152]{1,0:T(8,128)(2,1)}, bf16[512,1152]{1,0:T(8,128)(2,1)S(1)}, u32[]{:S(2)}, u32[]{:S(2)}) %collective-permute-start.22) | collective-permute-done | bytes 1179680 | tf_op jit(solution)/shard_map/ppermute | solution.py:629
  282.1 12.3 %collective-permute-done.24.far_a = bf16[256,1152]{1,0:T(8,128)(2,1)S(1)} collective-permute-done((bf16[256,1152]{1,0:T(8,128)(2,1)S(1)}, bf16[256,1152]{1,0:T(8,128)(2,1)S(1)}, u32[]{:S(2)}, u32[]{:S(2)}) %collective-permute-start.24) | collective-permute-done | bytes 589856 | tf_op jit(solution)/shard_map/ppermute | solution.py:629
  303.4 12.2 %collective-permute-done.26 = bf16[256,1152]{1,0:T(8,128)(2,1)S(1)} collective-permute-done((bf16[256,1152]{1,0:T(8,128)(2,1)}, bf16[256,1152]{1,0:T(8,128)(2,1)S(1)}, u32[]{:S(2)}, u32[]{:S(2)}) %collective-permute-start.26) | collective-permute-done | bytes 589856 | tf_op jit(solution)/shard_map/ppermute | solution.py:629
  320.9 24.7 %shard_map.278 = (bf16[2,1024,1792]{2,1,0:T(8,128)(2,1)}, bf16[1024,1152]{1,0:T(8,128)(2,1)}) custom-call(bf16[1024,1152]{1,0:T(8,128)(2,1)} %pad_maximum_fusion.2.refs_0_, bf16[1024,1792]{1,0:T(8,128)(2,1)} %get-tuple-element.233.refs_1_, bf16[1024,1792]{1,0:T(8,128)(2,1)} %get-tuple-element.234.refs_2_, bf16[2,1152,1792]{2,1,0:T(8,128)(2,1)} %bitcast.92, ...), custom_call_target="tpu_custom_call" | custom-call | flops 12683575296 | bytes 19398656 | tf_op jit(solution)/shard_map/pallas_call | solution.py:417
  347.0 25.0 %shard_map.279 = (bf16[2,1024,1792]{2,1,0:T(8,128)(2,1)}, bf16[512,1152]{1,0:T(8,128)(2,1)}, bf16[512,1152]{1,0:T(8,128)(2,1)}) custom-call(bf16[512,1152]{1,0:T(8,128)(2,1)} %copy-done.27, bf16[512,1152]{1,0:T(8,128)(2,1)} %copy-done.28, bf16[1024,1792]{1,0:T(8,128)(2,1)} %get-tuple-element.240.refs_2_, bf16[1024,1792]{1,0:T(8,128)(2,1)} %get-tuple-element.241.refs_3_, ...), custom_call_target="tpu_custom_call" | custom-call | flops 12683575296 | bytes 19398656 | tf_op jit(solution)/shard_map/pallas_call | solution.py:417
  374.1 27.0 %shard_map.280 = (bf16[1152,1792]{1,0:T(8,128)(2,1)}, bf16[1152,1792]{1,0:T(8,128)(2,1)}) custom-call(bf16[1024,1152]{1,0:T(8,128)(2,1)} %pad_maximum_fusion.1.refs_0_, bf16[2,1024,1792]{2,1,0:T(8,128)(2,1)} %get-tuple-element.249.refs_1_, bf16[512,1152]{1,0:T(8,128)(2,1)} %copy-done.26, bf16[512,1152]{1,0:T(8,128)(2,1)} %collective-permute-done.21.refs_1_.refs_3_, ...), custom_call_target="tpu_custom_call" | custom-call | flops 16911433728 | bytes 16515072 | tf_op jit(solution)/shard_map/pallas_call | solution.py:474
  404.8 16.7 %shard_map.281 = (bf16[896,1152]{1,0:T(8,128)(2,1)}, bf16[896,1152]{1,0:T(8,128)(2,1)}) custom-call(bf16[1024,1792]{1,0:T(8,128)(2,1)} %get-tuple-element.261.refs_0_, bf16[1,1024,1152]{2,1,0:T(8,128)(2,1)} %bitcast.80, bf16[1024,1792]{1,0:T(8,128)(2,1)} %get-tuple-element.263.refs_2_, bf16[1,512,1152]{2,1,0:T(8,128)(2,1)} %bitcast.96, ...), custom_call_target="tpu_custom_call" | custom-call | flops 8455716864 | bytes 8257536 | tf_op jit(solution)/shard_map/pallas_call | solution.py:474
  427.2 18.2 %shard_map.282 = (f32[512,1152]{1,0:T(8,128)}, bf16[512,1152]{1,0:T(8,128)(2,1)}, bf16[512,1024]{1,0:T(8,128)(2,1)}, f32[8,1152]{1,0:T(8,128)}, f32[8,256]{1,0:T...) custom-call(f32[256,1152]{1,0:T(8,128)} %get-tuple-element.270.refs_, ...), custom_call_target="tpu_custom_call" | custom-call | flops 4563402752 | bytes 17653760 | tf_op jit(solution)/shard_map/pallas_call | solution.py:299
  445.5 9.2 %shard_map.283 = (bf16[16,72,1152]{2,1,0:T(8,128)(2,1)}, bf16[16,72,1152]{2,1,0:T(8,128)(2,1)}) custom-call(bf16[512,1024]{1,0:T(8,128)(2,1)} %get-tuple-element.280.mixed_ref, bf16[512,1152]{1,0:T(8,128)(2,1)} %get-tuple-element.281.dattn_ref, bf16[512,1152]{1,0:T(8,128)(2,1)} %get-tuple-element.179.refs_0_.h_ref, ...), custom_call_target="tpu_custom_call" | custom-call | flops 2415919104 | bytes 10616832 | tf_op jit(solution)/shard_map/pallas_call | solution.py:505
  470.1 10.5 %collective-permute-done.36 = bf16[4,128,512]{2,1,0:T(8,128)(2,1)} collective-permute-done((bf16[4,128,512]{2,1,0:T(8,128)(2,1)}, bf16[4,128,512]{2,1,0:T(8,128)(2,1)}, u32[]{:S(2)}, u32[]{:S(2)}) %collective-permute-start.36) | collective-permute-done | bytes 524320 | tf_op jit(solution)/shard_map/ppermute | solution.py:629
  488.7 23.6 %collective-permute-done.41 = bf16[2,4,72,1152]{3,2,1,0:T(8,128)(2,1)} collective-permute-done((bf16[2,4,72,1152]{3,2,1,0:T(8,128)(2,1)}, bf16[2,4,72,1152]{3,2,1,0:T(8,128)(2,1)}, u32[]{:S(2)}, u32[]{:S(2)}) %collective-permute-start.41) | collective-permute-done | bytes 1327136 | tf_op jit(solution)/shard_map/ppermute | solution.py:629
  515.0 7.9 %collective-permute-done.39.refs_2_ = bf16[4,128,512]{2,1,0:T(8,128)(2,1)} collective-permute-done((bf16[4,128,512]{2,1,0:T(8,128)(2,1)S(1)}, bf16[4,128,512]{2,1,0:T(8,128)(2,1)}, u32[]{:S(2)}, u32[]{:S(2)}) %collective-permute-start.39) | collective-permute-done | bytes 524320 | tf_op jit(solution)/shard_map/ppermute | solution.py:634
  531.2 10.0 %shard_map.284 = (bf16[512,512]{1,0:T(8,128)(2,1)}, bf16[512,1152]{1,0:T(8,128)(2,1)}, f32[8,1152]{1,0:T(8,128)}, f32[8,256]{1,0:T(8,128)}) custom-call(f32[4,128,512]{2,1,0:T(8,128)} %get-tuple-element.294.refs_0_, bf16[4,128,512]{2,1,0:T(8,128)(2,1)} %collective-permute-done.40.refs_1_, bf16[4,128,512]{2,1,0:T(8,128)(2,1)} %collective-permute-done.39.refs_2_, ...), custom_call_target="tpu_custom_call" | custom-call | flops 1811939328 | bytes 3497984 | tf_op jit(solution)/shard_map/pallas_call | solution.py:351
  561.2 14.3 %reduce-scatter.5.cloned.1.call-done = bf16[224,1152]{1,0:T(8,128)(2,1)} async-done(((bf16[896,1152]{1,0:T(8,128)(2,1)}), bf16[224,1152]{1,0:T(8,128)(2,1)}) %reduce-scatter.5.cloned.1.call-update) | async-done | bytes 516112 | tf_op jit(solution)/shard_map/reduce_scatter | solution.py:715
  (246 shorter events, 219.8 us)
Async XLA Ops:
  7.2 175.6 %all-gather.5.cloned.1.call-start = ((), (), s32[]{:S(2)}) async-start(), calls=%async_computation.6 | async-start | bytes 4644864 | tf_op jit(solution)/shard_map/all_gather | solution.py:689
  39.3 31.3 %collective-permute-start.6 = (bf16[16,48,512]{2,1,0:T(8,128)(2,1)S(1)}, bf16[16,48,512]{2,1,0:T(8,128)(2,1)}, u32[]{:S(2)}, u32[]{:S(2)}) collective-permute-start(bf16[16,48,512]{2,1,0:T(8,128)(2,1)S(1)} %pad_maximum_fusion.8.own_ref), channel_id=1, source_target_pairs={{0,8},{8,0},{1,9},{9,1},{2,10},{10,2},{3,11},{11,3},{4,12},{12,4},... | collective-permute-start | bytes 2359304 | tf_op jit(solution)/shard_map/ppermute | solution.py:629
  41.2 37.5 %all-to-all-start = ((bf16[4,2,36,1792]{3,1,2,0:T(2,128)(2,1)}), bf16[4,2,36,1792]{3,1,2,0:T(2,128)(2,1)S(1)}, u32[]{:S(2)}, u32[]{:S(2)}) async-start(bf16[4,2,36,1792]{3,1,2,0:T(2,128)(2,1)} %bitcast.12), calls=%async_computation | async-start | bytes 2064384 | tf_op jit(solution)/shard_map/all_to_all | solution.py:729
  44.7 159.0 %all-gather.3.cloned.1.call-start = ((), (), s32[]{:S(2)}) async-start(), calls=%async_computation.5 | async-start | bytes 9289728 | tf_op jit(solution)/shard_map/all_gather | solution.py:689
  80.6 30.2 %collective-permute-start.13 = (bf16[4,72,1152]{2,1,0:T(8,128)(2,1)S(1)}, bf16[4,72,1152]{2,1,0:T(8,128)(2,1)}, u32[]{:S(2)}, u32[]{:S(2)}) collective-permute-start(bf16[4,72,1152]{2,1,0:T(8,128)(2,1)S(1)} %pad_maximum_fusion.9), channel_id=1, source_target_pairs={{0,1},{1,0},{2,3},{3,2},{4,5},{5,4},{6,7},{7,6},{8,9},{9,8},{10,11... | collective-permute-start | bytes 1990664 | tf_op jit(solution)/shard_map/ppermute | solution.py:629
  82.1 28.7 %collective-permute-start.14 = (bf16[4,72,1152]{2,1,0:T(8,128)(2,1)S(1)}, bf16[4,72,1152]{2,1,0:T(8,128)(2,1)}, u32[]{:S(2)}, u32[]{:S(2)}) collective-permute-start(bf16[4,72,1152]{2,1,0:T(8,128)(2,1)S(1)} %pad_maximum_fusion.9), channel_id=1, source_target_pairs={{0,17},{1,16},{16,1},{17,0},{2,19},{3,18},{18,3},{19,2},{4,21},{5,... | collective-permute-start | bytes 1990664 | tf_op jit(solution)/shard_map/ppermute | solution.py:650
  82.2 30.5 %collective-permute-start.10 = (bf16[4,128,512]{2,1,0:T(8,128)(2,1)}, bf16[4,128,512]{2,1,0:T(8,128)(2,1)}, u32[]{:S(2)}, u32[]{:S(2)}) collective-permute-start(bf16[4,128,512]{2,1,0:T(8,128)(2,1)} %get-tuple-element.183.refs_10_.refs_16_), channel_id=1, source_target_pairs={{0,2},{2,4},{4,6},{1,3},{3,5},{5,7},{8,10},{10,12},{12,14},{9,11},... | collective-permute-start | bytes 1572872 | tf_op jit(solution)/shard_map/ppermute | solution.py:634
  112.7 410.2 %reduce-scatter.3.cloned.1.call-start = ((), (), s32[]{:S(2)}) async-start(), calls=%async_computation.7 | async-start | bytes 5160960 | tf_op jit(solution)/shard_map/reduce_scatter | solution.py:715
  112.8 28.2 %collective-permute-start.17 = (bf16[16,72,1152]{2,1,0:T(8,128)(2,1)S(1)}, bf16[16,72,1152]{2,1,0:T(8,128)(2,1)}, u32[]{:S(2)}, u32[]{:S(2)}) collective-permute-start(bf16[16,72,1152]{2,1,0:T(8,128)(2,1)S(1)} %pad_maximum_fusion.own_ref), channel_id=1, source_target_pairs={{0,8},{8,0},{1,9},{9,1},{2,10},{10,2},{3,11},{11,3},{4,12},{12,4},... | collective-permute-start | bytes 7962632 | tf_op jit(solution)/shard_map/ppermute | solution.py:629
  180.4 44.5 %collective-permute-start.20 = (bf16[512,1152]{1,0:T(8,128)(2,1)S(1)}, bf16[512,1152]{1,0:T(8,128)(2,1)S(1)}, u32[]{:S(2)}, u32[]{:S(2)}) collective-permute-start(bf16[512,1152]{1,0:T(8,128)(2,1)S(1)} %get-tuple-element.202), channel_id=1, source_target_pairs={{0,1},{1,0},{2,3},{3,2},{4,5},{5,4},{6,7},{7,6},{8,9},{9,8},{10,11... | collective-permute-start | bytes 3538952 | tf_op jit(solution)/shard_map/ppermute | solution.py:629
  181.2 43.6 %collective-permute-start.21 = (bf16[512,1152]{1,0:T(8,128)(2,1)S(1)}, bf16[512,1152]{1,0:T(8,128)(2,1)}, u32[]{:S(2)}, u32[]{:S(2)}) collective-permute-start(bf16[512,1152]{1,0:T(8,128)(2,1)S(1)} %get-tuple-element.203), channel_id=1, source_target_pairs={{0,16},{16,0},{1,17},{17,1},{2,18},{18,2},{3,19},{19,3},{4,20},{20... | collective-permute-start | bytes 3538952 | tf_op jit(solution)/shard_map/ppermute | solution.py:629
  248.6 28.3 %collective-permute-start.22 = (bf16[512,1152]{1,0:T(8,128)(2,1)}, bf16[512,1152]{1,0:T(8,128)(2,1)S(1)}, u32[]{:S(2)}, u32[]{:S(2)}) collective-permute-start(bf16[512,1152]{1,0:T(8,128)(2,1)} %get-tuple-element.216), channel_id=1, source_target_pairs={{0,1},{1,0},{2,3},{3,2},{4,5},{5,4},{6,7},{7,6},{8,9},{9,8},{10,11... | collective-permute-start | bytes 3538952 | tf_op jit(solution)/shard_map/ppermute | solution.py:629
  250.1 28.1 %collective-permute-start.23 = (bf16[512,1152]{1,0:T(8,128)(2,1)}, bf16[512,1152]{1,0:T(8,128)(2,1)S(1)}, u32[]{:S(2)}, u32[]{:S(2)}) collective-permute-start(bf16[512,1152]{1,0:T(8,128)(2,1)} %get-tuple-element.217), channel_id=1, source_target_pairs={{0,16},{16,0},{1,17},{17,1},{2,18},{18,2},{3,19},{19,3},{4,20},{20... | collective-permute-start | bytes 3538952 | tf_op jit(solution)/shard_map/ppermute | solution.py:629
  318.9 26.7 %collective-permute-start.28 = (bf16[512,1152]{1,0:T(8,128)(2,1)S(1)}, bf16[512,1152]{1,0:T(8,128)(2,1)S(1)}, u32[]{:S(2)}, u32[]{:S(2)}) collective-permute-start(bf16[512,1152]{1,0:T(8,128)(2,1)S(1)} %pad_maximum_fusion.5), channel_id=1, source_target_pairs={{0,1},{1,0},{2,3},{3,2},{4,5},{5,4},{6,7},{7,6},{8,9},{9,8},{10,11... | collective-permute-start | bytes 3538952 | tf_op jit(solution)/shard_map/ppermute | solution.py:629
  319.6 25.9 %collective-permute-start.29 = (bf16[512,1152]{1,0:T(8,128)(2,1)S(1)}, bf16[512,1152]{1,0:T(8,128)(2,1)S(1)}, u32[]{:S(2)}, u32[]{:S(2)}) collective-permute-start(bf16[512,1152]{1,0:T(8,128)(2,1)S(1)} %pad_maximum_fusion.6), channel_id=1, source_target_pairs={{0,16},{16,0},{1,17},{17,1},{2,18},{18,2},{3,19},{19,3},{4,20},{20... | collective-permute-start | bytes 3538952 | tf_op jit(solution)/shard_map/ppermute | solution.py:629
  371.9 29.2 %collective-permute-start.30 = (bf16[512,1152]{1,0:T(8,128)(2,1)}, bf16[512,1152]{1,0:T(8,128)(2,1)S(1)}, u32[]{:S(2)}, u32[]{:S(2)}) collective-permute-start(bf16[512,1152]{1,0:T(8,128)(2,1)} %get-tuple-element.246), channel_id=1, source_target_pairs={{0,1},{1,0},{2,3},{3,2},{4,5},{5,4},{6,7},{7,6},{8,9},{9,8},{10,11... | collective-permute-start | bytes 3538952 | tf_op jit(solution)/shard_map/ppermute | solution.py:629
  373.4 27.7 %collective-permute-start.31 = (bf16[512,1152]{1,0:T(8,128)(2,1)}, bf16[512,1152]{1,0:T(8,128)(2,1)S(1)}, u32[]{:S(2)}, u32[]{:S(2)}) collective-permute-start(bf16[512,1152]{1,0:T(8,128)(2,1)} %get-tuple-element.247), channel_id=1, source_target_pairs={{0,16},{16,0},{1,17},{17,1},{2,18},{18,2},{3,19},{19,3},{4,20},{20... | collective-permute-start | bytes 3538952 | tf_op jit(solution)/shard_map/ppermute | solution.py:629
  427.1 148.4 %reduce-scatter.5.cloned.1.call-start = ((), (), s32[]{:S(2)}) async-start(), calls=%async_computation.8 | async-start | bytes 2580480 | tf_op jit(solution)/shard_map/reduce_scatter | solution.py:715
  427.1 30.0 %collective-permute-start.38 = (bf16[896,1152]{1,0:T(8,128)(2,1)}, bf16[896,1152]{1,0:T(8,128)(2,1)}, u32[]{:S(2)}, u32[]{:S(2)}) collective-permute-start(bf16[896,1152]{1,0:T(8,128)(2,1)} %get-tuple-element.286), channel_id=1, source_target_pairs={{0,8},{8,0},{1,9},{9,1},{2,10},{10,2},{3,11},{11,3},{4,12},{12,4},... | collective-permute-start | bytes 6193160 | tf_op jit(solution)/shard_map/ppermute | solution.py:629
  456.5 24.1 %collective-permute-start.36 = (bf16[4,128,512]{2,1,0:T(8,128)(2,1)}, bf16[4,128,512]{2,1,0:T(8,128)(2,1)}, u32[]{:S(2)}, u32[]{:S(2)}) collective-permute-start(bf16[4,128,512]{2,1,0:T(8,128)(2,1)} %get-tuple-element.279), channel_id=1, source_target_pairs={{0,1},{1,0},{2,3},{3,2},{4,5},{5,4},{6,7},{7,6},{8,9},{9,8},{10,11... | collective-permute-start | bytes 1572872 | tf_op jit(solution)/shard_map/ppermute | solution.py:629
  481.7 30.6 %collective-permute-start.41 = (bf16[2,4,72,1152]{3,2,1,0:T(8,128)(2,1)}, bf16[2,4,72,1152]{3,2,1,0:T(8,128)(2,1)}, u32[]{:S(2)}, u32[]{:S(2)}) collective-permute-start(bf16[2,4,72,1152]{3,2,1,0:T(8,128)(2,1)} %dynamic-slice_bitcast_fusion), channel_id=1, source_target_pairs={{0,16},{16,0},{1,17},{17,1},{2,18},{18,2},{3,19},{19,3},{4,20},{20... | collective-permute-start | bytes 3981320 | tf_op jit(solution)/shard_map/ppermute | solution.py:629
  486.1 36.9 %collective-permute-start.39 = (bf16[4,128,512]{2,1,0:T(8,128)(2,1)S(1)}, bf16[4,128,512]{2,1,0:T(8,128)(2,1)}, u32[]{:S(2)}, u32[]{:S(2)}) collective-permute-start(bf16[4,128,512]{2,1,0:T(8,128)(2,1)S(1)} %get-tuple-element.344), channel_id=1, source_target_pairs={{4,0},{6,2},{5,1},{7,3},{12,8},{14,10},{13,9},{15,11},{20,16},{22,... | collective-permute-start | bytes 1572872 | tf_op jit(solution)/shard_map/ppermute | solution.py:634
  487.4 35.6 %collective-permute-start.40 = (bf16[4,128,512]{2,1,0:T(8,128)(2,1)S(1)}, bf16[4,128,512]{2,1,0:T(8,128)(2,1)}, u32[]{:S(2)}, u32[]{:S(2)}) collective-permute-start(bf16[4,128,512]{2,1,0:T(8,128)(2,1)S(1)} %get-tuple-element.343), channel_id=1, source_target_pairs={{2,0},{4,2},{6,4},{3,1},{5,3},{7,5},{10,8},{12,10},{14,12},{11,9},... | collective-permute-start | bytes 1572872 | tf_op jit(solution)/shard_map/ppermute | solution.py:634
  527.6 24.2 %all-to-all-start.1 = ((bf16[4,2,36,1792]{3,1,2,0:T(2,128)(2,1)}), bf16[4,2,36,1792]{3,1,2,0:T(2,128)(2,1)S(1)}, u32[]{:S(2)}, u32[]{:S(2)}) async-start(bf16[4,2,36,1792]{3,1,2,0:T(2,128)(2,1)} %copy.51), calls=%async_computation.2 | async-start | bytes 2064384 | tf_op jit(solution)/shard_map/all_to_all | solution.py:729
  (62 other events, 787.1 us)
Sparse Core Ops, SparseCore 0:
  12.7 62.3 all-gather.4
  112.9 90.8 all-gather.2
  427.2 82.4 reduce-scatter.2
  523.1 52.3 reduce-scatter.4

commit v7 on v6

--- a/solution.py
+++ b/solution.py
@@ -990,8 +990,10 @@
         (d_kvproj, links.sum_halves(second, "y", 0), links.exchange(by_member(grad_pair)))
     )
     first_grad = first_grads(links.order("xyz"), shard, h_in, d_kvproj, small_terms)
-    first_core, second, grad_down = lax.optimization_barrier((links.sum_cores(*first_grad), second, grad_down))
-    first_got, second_sum = lax.optimization_barrier((links.to_members(first_core), links.sum_z(second, 0)))
+    first_core = links.sum_cores(*first_grad)
+    first_got, second_sum, grad_down = lax.optimization_barrier(
+        (links.to_members(first_core), links.sum_z(second, 0), grad_down)
+    )
     first_sum = links.sum_z(jnp.sum(first_got.astype(F32), axis=0).astype(BF16), 0)
     grad_pair = unpacked(got_pair)
     return (

time: 632 us -> 625 us (0.989)
  waiting for transfers between devices: 234 us -> 216 us
  starting transfers between devices: 73.3 us -> 83.5 us
    reduce_scatter x2, waiting for transfers between devices: 14.3 us -> 0.01 us  [sum_z_low(): return lax.psum_scatter(array, 'z', scatter_dimension=0, tiled=True)]
    ppermute x12, starting transfers between devices: 18.8 us -> 29.6 us  [turn(): lax.ppermute(array, 'z', [(i, (i + step) % depth) for i in range(depth)])]
  transfers between devices with their start and end apart: 57 -> 57, of which waited for: 27 -> 25; matrix products, arithmetic and copies ran while one was open for 9% -> 10% of each run, Pallas kernels for 26% -> 26%
where the time goes in v7:
time: 625 us; the launch traced here: 616 us
  waiting for transfers between devices  216 us (35%)
  Pallas kernels  214 us (34%)
  starting transfers between devices  83.5 us (13%)
  other arithmetic  52.3 us (8%)
  local copies, waits for them, and re-layouts  35.9 us (6%)
  between operations  14.7 us (2%)
    ppermute x32, waiting for transfers between devices, swap(): return lax.ppermute(array, axis, SWAP)  156 us
    pallas_call x2, Pallas kernels, ffn_backward(): call(functools.partial(down_body, step, len(d)), (count // tile,), specs...  49.6 us
    pallas_call x2, Pallas kernels, ffn_forward(): call(functools.partial(up_body, step, len(h)), (count // tile,), specs +...  43.8 us
    pallas_call x2, Pallas kernels, weight_grads(): call(functools.partial(grads_body, places, [(len(lefts), len(rights)) for...  43.6 us
    ppermute x32, starting transfers between devices, swap(): return lax.ppermute(array, axis, SWAP)  30.1 us
    ppermute x12, starting transfers between devices, turn(): lax.ppermute(array, 'z', [(i, (i + step) % depth) for i in range(depth)])  29.6 us
    ppermute x12, waiting for transfers between devices, turn(): lax.ppermute(array, 'z', [(i, (i + step) % depth) for i in range(depth)])  27.9 us
    all_gather x2, waiting for transfers between devices, gather_cz(): return lax.all_gather(array, ('core', 'z'), axis=dim, tiled=True)  20.9 us
  transfers between devices with their start and end apart: 57, of which 25 were waited for; matrix products, arithmetic and copies ran while one was open for 10% of the time, Pallas kernels for 26%

profile of v7, /device:TPU:0, one launch (start us, length us, event | category | flops | bytes accessed | tf_op | source)
XLA Modules:
  0.0 615.9 jit_solution(17436190737695878742)
XLA Ops:
  48.8 15.4 %collective-permute-done.8 = bf16[72,1152]{1,0:T(8,128)(2,1)S(1)} collective-permute-done((bf16[72,1152]{1,0:T(8,128)(2,1)S(1)}, bf16[72,1152]{1,0:T(8,128)(2,1)S(1)}, u32[]{:S(2)}, u32[]{:S(2)}) %collective-permute-start.8) | collective-permute-done | bytes 165920 | tf_op jit(solution)/shard_map/ppermute | solution.py:638
  83.1 7.2 %collective-permute-start.10 = (bf16[4,128,512]{2,1,0:T(8,128)(2,1)}, bf16[4,128,512]{2,1,0:T(8,128)(2,1)}, u32[]{:S(2)}, u32[]{:S(2)}) collective-permute-start(bf16[4,128,512]{2,1,0:T(8,128)(2,1)} %get-tuple-element.181.refs_10_.refs_16_), channel_id=1, source_target_pairs={{0,2},{2,4},{4,6},{1,3},{3,5},{5,7},{8,10},{10,12},{12,14},{9,11},... | collective-permute-start | bytes 1572872 | tf_op jit(solution)/shard_map/ppermute | solution.py:634
  97.5 14.1 %collective-permute-done.13 = bf16[4,72,1152]{2,1,0:T(8,128)(2,1)} collective-permute-done((bf16[4,72,1152]{2,1,0:T(8,128)(2,1)S(1)}, bf16[4,72,1152]{2,1,0:T(8,128)(2,1)}, u32[]{:S(2)}, u32[]{:S(2)}) %collective-permute-start.13) | collective-permute-done | bytes 663584 | tf_op jit(solution)/shard_map/ppermute | solution.py:629
  119.7 12.1 %collective-permute-done.15.refs_13_.refs_19_ = bf16[4,128,512]{2,1,0:T(8,128)(2,1)S(1)} collective-permute-done((bf16[4,128,512]{2,1,0:T(8,128)(2,1)}, bf16[4,128,512]{2,1,0:T(8,128)(2,1)S(1)}, u32[]{:S(2)}, u32[]{:S(2)}) %collective-permute-start.15) | collective-permute-done | bytes 524320 | tf_op jit(solution)/shard_map/ppermute | solution.py:629
  131.8 10.1 %collective-permute-done.16.refs_14_.refs_20_ = bf16[4,128,512]{2,1,0:T(8,128)(2,1)} collective-permute-done((bf16[4,128,512]{2,1,0:T(8,128)(2,1)}, bf16[4,128,512]{2,1,0:T(8,128)(2,1)}, u32[]{:S(2)}, u32[]{:S(2)}) %collective-permute-start.16) | collective-permute-done | bytes 524320 | tf_op jit(solution)/shard_map/ppermute | solution.py:629
  148.1 15.0 %shard_map.274 = (f32[512,1024]{1,0:T(8,128)}, bf16[512,1024]{1,0:T(8,128)(2,1)}, bf16[512,1024]{1,0:T(8,128)(2,1)}, f32[512,1152]{1,0:T(8,128)}, f32[512,1152]{...) custom-call(bf16[512,1152]{1,0:T(8,128)(2,1)} %get-tuple-element.177.refs_0_.h_ref, ...), custom_call_target="tpu_custom_call" | custom-call | flops 3758096384 | bytes 20185088 | tf_op jit(solution)/shard_map/pallas_call | solution.py:228
  165.1 12.3 %collective-permute-done.18 = bf16[256,1152]{1,0:T(8,128)(2,1)S(1)} collective-permute-done((bf16[256,1152]{1,0:T(8,128)(2,1)}, bf16[256,1152]{1,0:T(8,128)(2,1)S(1)}, u32[]{:S(2)}, u32[]{:S(2)}) %collective-permute-start.18) | collective-permute-done | bytes 589856 | tf_op jit(solution)/shard_map/ppermute | solution.py:629
  183.6 20.9 %all-gather.3.cloned.1.call-done = bf16[4,576,1792]{2,1,0:T(8,128)(2,1)} async-done(((bf16[4,72,1792]{2,1,0:T(8,128)(2,1)}), bf16[4,576,1792]{2,1,0:T(8,128)(2,1)}) %all-gather.3.cloned.1.call-update) | async-done | bytes 8257552 | tf_op jit(solution)/shard_map/all_gather | solution.py:689
  204.6 21.1 %shard_map.275 = (bf16[1024,1792]{1,0:T(8,128)(2,1)}, bf16[1024,1792]{1,0:T(8,128)(2,1)}, bf16[1024,1792]{1,0:T(8,128)(2,1)}, bf16[1024,1152]{1,0:T(8,128)(2,1)}) custom-call(bf16[1024,1152]{1,0:T(8,128)(2,1)} %pad_maximum_fusion.1.refs_0_, bf16[2,1152,1792]{2,1,0:T(8,128)(2,1)} %bitcast.92, ...), custom_call_target="tpu_custom_call" | custom-call | flops 12683575296 | bytes 26738688 | tf_op jit(solution)/shard_map/pallas_call | solution.py:391
  226.7 22.7 %shard_map.276 = (bf16[1024,1792]{1,0:T(8,128)(2,1)}, bf16[1024,1792]{1,0:T(8,128)(2,1)}, bf16[1024,1792]{1,0:T(8,128)(2,1)}, bf16[512,1152]{1,0:T(8,128)(2,1)}, bf16[512,1152]{1,0:T(8,128)(2,1)}) custom-call(bf16[512,1152]{1,0:T(8,128)(2,1)} %copy-done.28, bf16[512,1152]{1,0:T(8,128)(2,1)} %collective-permute-done.21.refs_1_.refs_3_, ...), custom_call_target="tpu_custom_call" | custom-call | flops 12683575296 | bytes 26738688 | tf_op jit(solution)/shard_map/pallas_call | solution.py:391
  252.4 25.4 %collective-permute-done.22 = bf16[512,1152]{1,0:T(8,128)(2,1)S(1)} collective-permute-done((bf16[512,1152]{1,0:T(8,128)(2,1)}, bf16[512,1152]{1,0:T(8,128)(2,1)S(1)}, u32[]{:S(2)}, u32[]{:S(2)}) %collective-permute-start.22) | collective-permute-done | bytes 1179680 | tf_op jit(solution)/shard_map/ppermute | solution.py:629
  282.9 12.3 %collective-permute-done.24.far_a = bf16[256,1152]{1,0:T(8,128)(2,1)S(1)} collective-permute-done((bf16[256,1152]{1,0:T(8,128)(2,1)S(1)}, bf16[256,1152]{1,0:T(8,128)(2,1)S(1)}, u32[]{:S(2)}, u32[]{:S(2)}) %collective-permute-start.24) | collective-permute-done | bytes 589856 | tf_op jit(solution)/shard_map/ppermute | solution.py:629
  304.2 12.2 %collective-permute-done.26 = bf16[256,1152]{1,0:T(8,128)(2,1)S(1)} collective-permute-done((bf16[256,1152]{1,0:T(8,128)(2,1)}, bf16[256,1152]{1,0:T(8,128)(2,1)S(1)}, u32[]{:S(2)}, u32[]{:S(2)}) %collective-permute-start.26) | collective-permute-done | bytes 589856 | tf_op jit(solution)/shard_map/ppermute | solution.py:629
  321.7 24.6 %shard_map.278 = (bf16[2,1024,1792]{2,1,0:T(8,128)(2,1)}, bf16[1024,1152]{1,0:T(8,128)(2,1)}) custom-call(bf16[1024,1152]{1,0:T(8,128)(2,1)} %pad_maximum_fusion.2.refs_0_, bf16[1024,1792]{1,0:T(8,128)(2,1)} %get-tuple-element.231.refs_1_, bf16[1024,1792]{1,0:T(8,128)(2,1)} %get-tuple-element.232.refs_2_, bf16[2,1152,1792]{2,1,0:T(8,128)(2,1)} %bitcast.94, ...), custom_call_target="tpu_custom_call" | custom-call | flops 12683575296 | bytes 19398656 | tf_op jit(solution)/shard_map/pallas_call | solution.py:417
  347.7 25.0 %shard_map.279 = (bf16[2,1024,1792]{2,1,0:T(8,128)(2,1)}, bf16[512,1152]{1,0:T(8,128)(2,1)}, bf16[512,1152]{1,0:T(8,128)(2,1)}) custom-call(bf16[512,1152]{1,0:T(8,128)(2,1)} %copy-done.29, bf16[512,1152]{1,0:T(8,128)(2,1)} %copy-done.30, bf16[1024,1792]{1,0:T(8,128)(2,1)} %get-tuple-element.238.refs_2_, bf16[1024,1792]{1,0:T(8,128)(2,1)} %get-tuple-element.239.refs_3_, ...), custom_call_target="tpu_custom_call" | custom-call | flops 12683575296 | bytes 19398656 | tf_op jit(solution)/shard_map/pallas_call | solution.py:417
  374.9 27.0 %shard_map.280 = (bf16[1152,1792]{1,0:T(8,128)(2,1)}, bf16[1152,1792]{1,0:T(8,128)(2,1)}) custom-call(bf16[1024,1152]{1,0:T(8,128)(2,1)} %pad_maximum_fusion.1.refs_0_, bf16[2,1024,1792]{2,1,0:T(8,128)(2,1)} %get-tuple-element.247.refs_1_, bf16[512,1152]{1,0:T(8,128)(2,1)} %copy-done.28, bf16[512,1152]{1,0:T(8,128)(2,1)} %collective-permute-done.21.refs_1_.refs_3_, ...), custom_call_target="tpu_custom_call" | custom-call | flops 16911433728 | bytes 16515072 | tf_op jit(solution)/shard_map/pallas_call | solution.py:474
  405.5 16.7 %shard_map.281 = (bf16[896,1152]{1,0:T(8,128)(2,1)}, bf16[896,1152]{1,0:T(8,128)(2,1)}) custom-call(bf16[1024,1792]{1,0:T(8,128)(2,1)} %get-tuple-element.259.refs_0_, bf16[1,1024,1152]{2,1,0:T(8,128)(2,1)} %bitcast.82, bf16[1024,1792]{1,0:T(8,128)(2,1)} %get-tuple-element.261.refs_2_, bf16[1,512,1152]{2,1,0:T(8,128)(2,1)} %bitcast.98, ...), custom_call_target="tpu_custom_call" | custom-call | flops 8455716864 | bytes 8257536 | tf_op jit(solution)/shard_map/pallas_call | solution.py:474
  428.0 18.3 %shard_map.282 = (f32[512,1152]{1,0:T(8,128)}, bf16[512,1152]{1,0:T(8,128)(2,1)}, bf16[512,1024]{1,0:T(8,128)(2,1)}, f32[8,1152]{1,0:T(8,128)}, f32[8,256]{1,0:T...) custom-call(f32[256,1152]{1,0:T(8,128)} %get-tuple-element.268.refs_, ...), custom_call_target="tpu_custom_call" | custom-call | flops 4563402752 | bytes 17653760 | tf_op jit(solution)/shard_map/pallas_call | solution.py:299
  446.3 9.1 %shard_map.283 = (bf16[16,72,1152]{2,1,0:T(8,128)(2,1)}, bf16[16,72,1152]{2,1,0:T(8,128)(2,1)}) custom-call(bf16[512,1024]{1,0:T(8,128)(2,1)} %get-tuple-element.278.mixed_ref, bf16[512,1152]{1,0:T(8,128)(2,1)} %get-tuple-element.279.dattn_ref, bf16[512,1152]{1,0:T(8,128)(2,1)} %get-tuple-element.177.refs_0_.h_ref, ...), custom_call_target="tpu_custom_call" | custom-call | flops 2415919104 | bytes 10616832 | tf_op jit(solution)/shard_map/pallas_call | solution.py:505
  470.8 10.5 %collective-permute-done.36 = bf16[4,128,512]{2,1,0:T(8,128)(2,1)} collective-permute-done((bf16[4,128,512]{2,1,0:T(8,128)(2,1)}, bf16[4,128,512]{2,1,0:T(8,128)(2,1)}, u32[]{:S(2)}, u32[]{:S(2)}) %collective-permute-start.36) | collective-permute-done | bytes 524320 | tf_op jit(solution)/shard_map/ppermute | solution.py:629
  489.3 23.7 %collective-permute-done.41 = bf16[2,4,72,1152]{3,2,1,0:T(8,128)(2,1)} collective-permute-done((bf16[2,4,72,1152]{3,2,1,0:T(8,128)(2,1)}, bf16[2,4,72,1152]{3,2,1,0:T(8,128)(2,1)}, u32[]{:S(2)}, u32[]{:S(2)}) %collective-permute-start.41) | collective-permute-done | bytes 1327136 | tf_op jit(solution)/shard_map/ppermute | solution.py:629
  515.7 8.0 %collective-permute-done.39.refs_2_ = bf16[4,128,512]{2,1,0:T(8,128)(2,1)} collective-permute-done((bf16[4,128,512]{2,1,0:T(8,128)(2,1)S(1)}, bf16[4,128,512]{2,1,0:T(8,128)(2,1)}, u32[]{:S(2)}, u32[]{:S(2)}) %collective-permute-start.39) | collective-permute-done | bytes 524320 | tf_op jit(solution)/shard_map/ppermute | solution.py:634
  532.0 10.0 %shard_map.284 = (bf16[512,512]{1,0:T(8,128)(2,1)}, bf16[512,1152]{1,0:T(8,128)(2,1)}, f32[8,1152]{1,0:T(8,128)}, f32[8,256]{1,0:T(8,128)}) custom-call(f32[4,128,512]{2,1,0:T(8,128)} %get-tuple-element.292.refs_0_, bf16[4,128,512]{2,1,0:T(8,128)(2,1)} %collective-permute-done.40.refs_1_, bf16[4,128,512]{2,1,0:T(8,128)(2,1)} %collective-permute-done.39.refs_2_, ...), custom_call_target="tpu_custom_call" | custom-call | flops 1811939328 | bytes 3497984 | tf_op jit(solution)/shard_map/pallas_call | solution.py:351
  559.1 11.8 %collective-permute-start.44 = (bf16[72,1152]{1,0:T(8,128)(2,1)}, bf16[72,1152]{1,0:T(8,128)(2,1)}, u32[]{:S(2)}, u32[]{:S(2)}) collective-permute-start(bf16[72,1152]{1,0:T(8,128)(2,1)} %get-tuple-element.335), channel_id=1, source_target_pairs={{0,2},{2,4},{4,6},{6,0},{1,3},{3,5},{5,7},{7,1},{8,10},{10,12},{12... | collective-permute-start | bytes 497672 | tf_op jit(solution)/shard_map/ppermute | solution.py:638
  (250 shorter events, 215.7 us)
Async XLA Ops:
  7.2 176.4 %all-gather.5.cloned.1.call-start = ((), (), s32[]{:S(2)}) async-start(), calls=%async_computation.6 | async-start | bytes 4644864 | tf_op jit(solution)/shard_map/all_gather | solution.py:689
  39.3 31.3 %collective-permute-start.6 = (bf16[16,48,512]{2,1,0:T(8,128)(2,1)S(1)}, bf16[16,48,512]{2,1,0:T(8,128)(2,1)S(1)}, u32[]{:S(2)}, u32[]{:S(2)}) collective-permute-start(bf16[16,48,512]{2,1,0:T(8,128)(2,1)S(1)} %pad_maximum_fusion.8.own_ref), channel_id=1, source_target_pairs={{0,8},{8,0},{1,9},{9,1},{2,10},{10,2},{3,11},{11,3},{4,12},{12,4},... | collective-permute-start | bytes 2359304 | tf_op jit(solution)/shard_map/ppermute | solution.py:629
  41.2 38.4 %all-to-all-start = ((bf16[4,2,36,1792]{3,1,2,0:T(2,128)(2,1)}), bf16[4,2,36,1792]{3,1,2,0:T(2,128)(2,1)S(1)}, u32[]{:S(2)}, u32[]{:S(2)}) async-start(bf16[4,2,36,1792]{3,1,2,0:T(2,128)(2,1)} %bitcast.12), calls=%async_computation | async-start | bytes 2064384 | tf_op jit(solution)/shard_map/all_to_all | solution.py:729
  44.7 159.9 %all-gather.3.cloned.1.call-start = ((), (), s32[]{:S(2)}) async-start(), calls=%async_computation.5 | async-start | bytes 9289728 | tf_op jit(solution)/shard_map/all_gather | solution.py:689
  81.4 30.2 %collective-permute-start.13 = (bf16[4,72,1152]{2,1,0:T(8,128)(2,1)S(1)}, bf16[4,72,1152]{2,1,0:T(8,128)(2,1)}, u32[]{:S(2)}, u32[]{:S(2)}) collective-permute-start(bf16[4,72,1152]{2,1,0:T(8,128)(2,1)S(1)} %pad_maximum_fusion.9), channel_id=1, source_target_pairs={{0,1},{1,0},{2,3},{3,2},{4,5},{5,4},{6,7},{7,6},{8,9},{9,8},{10,11... | collective-permute-start | bytes 1990664 | tf_op jit(solution)/shard_map/ppermute | solution.py:629
  82.9 28.8 %collective-permute-start.14 = (bf16[4,72,1152]{2,1,0:T(8,128)(2,1)S(1)}, bf16[4,72,1152]{2,1,0:T(8,128)(2,1)}, u32[]{:S(2)}, u32[]{:S(2)}) collective-permute-start(bf16[4,72,1152]{2,1,0:T(8,128)(2,1)S(1)} %pad_maximum_fusion.9), channel_id=1, source_target_pairs={{0,17},{1,16},{16,1},{17,0},{2,19},{3,18},{18,3},{19,2},{4,21},{5,... | collective-permute-start | bytes 1990664 | tf_op jit(solution)/shard_map/ppermute | solution.py:650
  83.1 30.5 %collective-permute-start.10 = (bf16[4,128,512]{2,1,0:T(8,128)(2,1)}, bf16[4,128,512]{2,1,0:T(8,128)(2,1)}, u32[]{:S(2)}, u32[]{:S(2)}) collective-permute-start(bf16[4,128,512]{2,1,0:T(8,128)(2,1)} %get-tuple-element.181.refs_10_.refs_16_), channel_id=1, source_target_pairs={{0,2},{2,4},{4,6},{1,3},{3,5},{5,7},{8,10},{10,12},{12,14},{9,11},... | collective-permute-start | bytes 1572872 | tf_op jit(solution)/shard_map/ppermute | solution.py:634
  113.6 410.1 %reduce-scatter.3.cloned.1.call-start = ((), (), s32[]{:S(2)}) async-start(), calls=%async_computation.7 | async-start | bytes 5160960 | tf_op jit(solution)/shard_map/reduce_scatter | solution.py:715
  113.6 28.2 %collective-permute-start.17 = (bf16[16,72,1152]{2,1,0:T(8,128)(2,1)S(1)}, bf16[16,72,1152]{2,1,0:T(8,128)(2,1)}, u32[]{:S(2)}, u32[]{:S(2)}) collective-permute-start(bf16[16,72,1152]{2,1,0:T(8,128)(2,1)S(1)} %pad_maximum_fusion.own_ref), channel_id=1, source_target_pairs={{0,8},{8,0},{1,9},{9,1},{2,10},{10,2},{3,11},{11,3},{4,12},{12,4},... | collective-permute-start | bytes 7962632 | tf_op jit(solution)/shard_map/ppermute | solution.py:629
  181.2 44.5 %collective-permute-start.20 = (bf16[512,1152]{1,0:T(8,128)(2,1)S(1)}, bf16[512,1152]{1,0:T(8,128)(2,1)S(1)}, u32[]{:S(2)}, u32[]{:S(2)}) collective-permute-start(bf16[512,1152]{1,0:T(8,128)(2,1)S(1)} %get-tuple-element.200), channel_id=1, source_target_pairs={{0,1},{1,0},{2,3},{3,2},{4,5},{5,4},{6,7},{7,6},{8,9},{9,8},{10,11... | collective-permute-start | bytes 3538952 | tf_op jit(solution)/shard_map/ppermute | solution.py:629
  182.1 43.6 %collective-permute-start.21 = (bf16[512,1152]{1,0:T(8,128)(2,1)S(1)}, bf16[512,1152]{1,0:T(8,128)(2,1)}, u32[]{:S(2)}, u32[]{:S(2)}) collective-permute-start(bf16[512,1152]{1,0:T(8,128)(2,1)S(1)} %get-tuple-element.201), channel_id=1, source_target_pairs={{0,16},{16,0},{1,17},{17,1},{2,18},{18,2},{3,19},{19,3},{4,20},{20... | collective-permute-start | bytes 3538952 | tf_op jit(solution)/shard_map/ppermute | solution.py:629
  249.4 28.3 %collective-permute-start.22 = (bf16[512,1152]{1,0:T(8,128)(2,1)}, bf16[512,1152]{1,0:T(8,128)(2,1)S(1)}, u32[]{:S(2)}, u32[]{:S(2)}) collective-permute-start(bf16[512,1152]{1,0:T(8,128)(2,1)} %get-tuple-element.214), channel_id=1, source_target_pairs={{0,1},{1,0},{2,3},{3,2},{4,5},{5,4},{6,7},{7,6},{8,9},{9,8},{10,11... | collective-permute-start | bytes 3538952 | tf_op jit(solution)/shard_map/ppermute | solution.py:629
  250.9 28.1 %collective-permute-start.23 = (bf16[512,1152]{1,0:T(8,128)(2,1)}, bf16[512,1152]{1,0:T(8,128)(2,1)S(1)}, u32[]{:S(2)}, u32[]{:S(2)}) collective-permute-start(bf16[512,1152]{1,0:T(8,128)(2,1)} %get-tuple-element.215), channel_id=1, source_target_pairs={{0,16},{16,0},{1,17},{17,1},{2,18},{18,2},{3,19},{19,3},{4,20},{20... | collective-permute-start | bytes 3538952 | tf_op jit(solution)/shard_map/ppermute | solution.py:629
  319.7 26.6 %collective-permute-start.28 = (bf16[512,1152]{1,0:T(8,128)(2,1)S(1)}, bf16[512,1152]{1,0:T(8,128)(2,1)S(1)}, u32[]{:S(2)}, u32[]{:S(2)}) collective-permute-start(bf16[512,1152]{1,0:T(8,128)(2,1)S(1)} %pad_maximum_fusion.5), channel_id=1, source_target_pairs={{0,1},{1,0},{2,3},{3,2},{4,5},{5,4},{6,7},{7,6},{8,9},{9,8},{10,11... | collective-permute-start | bytes 3538952 | tf_op jit(solution)/shard_map/ppermute | solution.py:629
  320.4 25.9 %collective-permute-start.29 = (bf16[512,1152]{1,0:T(8,128)(2,1)S(1)}, bf16[512,1152]{1,0:T(8,128)(2,1)S(1)}, u32[]{:S(2)}, u32[]{:S(2)}) collective-permute-start(bf16[512,1152]{1,0:T(8,128)(2,1)S(1)} %pad_maximum_fusion.6), channel_id=1, source_target_pairs={{0,16},{16,0},{1,17},{17,1},{2,18},{18,2},{3,19},{19,3},{4,20},{20... | collective-permute-start | bytes 3538952 | tf_op jit(solution)/shard_map/ppermute | solution.py:629
  372.7 29.2 %collective-permute-start.30 = (bf16[512,1152]{1,0:T(8,128)(2,1)}, bf16[512,1152]{1,0:T(8,128)(2,1)S(1)}, u32[]{:S(2)}, u32[]{:S(2)}) collective-permute-start(bf16[512,1152]{1,0:T(8,128)(2,1)} %get-tuple-element.244), channel_id=1, source_target_pairs={{0,1},{1,0},{2,3},{3,2},{4,5},{5,4},{6,7},{7,6},{8,9},{9,8},{10,11... | collective-permute-start | bytes 3538952 | tf_op jit(solution)/shard_map/ppermute | solution.py:629
  374.1 27.7 %collective-permute-start.31 = (bf16[512,1152]{1,0:T(8,128)(2,1)}, bf16[512,1152]{1,0:T(8,128)(2,1)S(1)}, u32[]{:S(2)}, u32[]{:S(2)}) collective-permute-start(bf16[512,1152]{1,0:T(8,128)(2,1)} %get-tuple-element.245), channel_id=1, source_target_pairs={{0,16},{16,0},{1,17},{17,1},{2,18},{18,2},{3,19},{19,3},{4,20},{20... | collective-permute-start | bytes 3538952 | tf_op jit(solution)/shard_map/ppermute | solution.py:629
  427.8 160.1 %reduce-scatter.5.cloned.1.call-start = ((), (), s32[]{:S(2)}) async-start(), calls=%async_computation.8 | async-start | bytes 2580480 | tf_op jit(solution)/shard_map/reduce_scatter | solution.py:715
  427.9 29.9 %collective-permute-start.38 = (bf16[896,1152]{1,0:T(8,128)(2,1)}, bf16[896,1152]{1,0:T(8,128)(2,1)}, u32[]{:S(2)}, u32[]{:S(2)}) collective-permute-start(bf16[896,1152]{1,0:T(8,128)(2,1)} %get-tuple-element.284), channel_id=1, source_target_pairs={{0,8},{8,0},{1,9},{9,1},{2,10},{10,2},{3,11},{11,3},{4,12},{12,4},... | collective-permute-start | bytes 6193160 | tf_op jit(solution)/shard_map/ppermute | solution.py:629
  457.1 24.1 %collective-permute-start.36 = (bf16[4,128,512]{2,1,0:T(8,128)(2,1)}, bf16[4,128,512]{2,1,0:T(8,128)(2,1)}, u32[]{:S(2)}, u32[]{:S(2)}) collective-permute-start(bf16[4,128,512]{2,1,0:T(8,128)(2,1)} %get-tuple-element.277), channel_id=1, source_target_pairs={{0,1},{1,0},{2,3},{3,2},{4,5},{5,4},{6,7},{7,6},{8,9},{9,8},{10,11... | collective-permute-start | bytes 1572872 | tf_op jit(solution)/shard_map/ppermute | solution.py:629
  482.4 30.6 %collective-permute-start.41 = (bf16[2,4,72,1152]{3,2,1,0:T(8,128)(2,1)}, bf16[2,4,72,1152]{3,2,1,0:T(8,128)(2,1)}, u32[]{:S(2)}, u32[]{:S(2)}) collective-permute-start(bf16[2,4,72,1152]{3,2,1,0:T(8,128)(2,1)} %dynamic-slice_bitcast_fusion), channel_id=1, source_target_pairs={{0,16},{16,0},{1,17},{17,1},{2,18},{18,2},{3,19},{19,3},{4,20},{20... | collective-permute-start | bytes 3981320 | tf_op jit(solution)/shard_map/ppermute | solution.py:629
  486.8 36.9 %collective-permute-start.39 = (bf16[4,128,512]{2,1,0:T(8,128)(2,1)S(1)}, bf16[4,128,512]{2,1,0:T(8,128)(2,1)}, u32[]{:S(2)}, u32[]{:S(2)}) collective-permute-start(bf16[4,128,512]{2,1,0:T(8,128)(2,1)S(1)} %get-tuple-element.340), channel_id=1, source_target_pairs={{4,0},{6,2},{5,1},{7,3},{12,8},{14,10},{13,9},{15,11},{20,16},{22,... | collective-permute-start | bytes 1572872 | tf_op jit(solution)/shard_map/ppermute | solution.py:634
  488.0 35.7 %collective-permute-start.40 = (bf16[4,128,512]{2,1,0:T(8,128)(2,1)S(1)}, bf16[4,128,512]{2,1,0:T(8,128)(2,1)}, u32[]{:S(2)}, u32[]{:S(2)}) collective-permute-start(bf16[4,128,512]{2,1,0:T(8,128)(2,1)S(1)} %get-tuple-element.339), channel_id=1, source_target_pairs={{2,0},{4,2},{6,4},{3,1},{5,3},{7,5},{10,8},{12,10},{14,12},{11,9},... | collective-permute-start | bytes 1572872 | tf_op jit(solution)/shard_map/ppermute | solution.py:634
  528.4 24.1 %all-to-all-start.1 = ((bf16[4,2,36,1792]{3,1,2,0:T(2,128)(2,1)}), bf16[4,2,36,1792]{3,1,2,0:T(2,128)(2,1)S(1)}, u32[]{:S(2)}, u32[]{:S(2)}) async-start(bf16[4,2,36,1792]{3,1,2,0:T(2,128)(2,1)} %copy.51), calls=%async_computation.2 | async-start | bytes 2064384 | tf_op jit(solution)/shard_map/all_to_all | solution.py:729
  (64 other events, 809.9 us)
Sparse Core Ops, SparseCore 0:
  12.7 62.3 all-gather.4
  113.7 90.8 all-gather.2
  428.0 82.5 reduce-scatter.2
  523.9 59.7 reduce-scatter.4

commit v8 on v7

--- a/solution.py
+++ b/solution.py
@@ -410,7 +410,7 @@
     store_part(refs[many + 5 :], (mm_t(pair_out[0], pair_ref[0]) + mm_t(pair_out[1], pair_ref[1])).astype(BF16))
 
 
-def ffn_backward(d, turn, act, pair, down, tile=256, step=256):
+def ffn_backward(d, turn, act, pair, down, tile=256, step=512):
     count, width = sum(one.shape[0] for one in d), d[0].shape[1]
     units = pair.shape[2]
     specs = part_specs(tile, width, d)
@@ -867,8 +867,8 @@
     kv_shard = jnp.concatenate([jnp.concatenate([w_key, w_value], axis=1), seg_rows, vectors]).astype(BF16)
     kv_shard = jnp.pad(kv_shard, ((0, eights(used) - used), (0, 0)))
     own_ids = segment_ids.astype(F32).reshape(count, 1)
-    kv_shard, own_ids, w_gate, w_up, w_down, w_query, w_out = lax.optimization_barrier(
-        (kv_shard, own_ids, w_gate, w_up, w_down, w_query, w_out)
+    kv_shard, own_ids, w_gate, w_up, w_query, w_out = lax.optimization_barrier(
+        (kv_shard, own_ids, w_gate, w_up, w_query, w_out)
     )
     kv_along = links.along_z(kv_shard)
     full_down = links.gather_cz(jnp.pad(w_down.astype(BF16), ((0, chunk - hidden_shard), (0, 0))), 0)
@@ -986,10 +986,10 @@
     head_terms = (heads_attn + heads_in)[:2].reshape(2, parts, head_shard)
     head_terms = jnp.pad(head_terms, ((0, 0), (0, 0), (0, shard - head_shard))).reshape(2, width)
     small_terms = jnp.pad(jnp.concatenate([gain_terms, head_terms]), ((0, SMALL - 6), (0, 0)))
-    d_kvproj, second, got_pair = lax.optimization_barrier(
-        (d_kvproj, links.sum_halves(second, "y", 0), links.exchange(by_member(grad_pair)))
-    )
     first_grad = first_grads(links.order("xyz"), shard, h_in, d_kvproj, small_terms)
+    first_grad, second, got_pair = lax.optimization_barrier(
+        (first_grad, links.sum_halves(second, "y", 0), links.exchange(by_member(grad_pair)))
+    )
     first_core = links.sum_cores(*first_grad)
     first_got, second_sum, grad_down = lax.optimization_barrier(
         (links.to_members(first_core), links.sum_z(second, 0), grad_down)

time: 625 us -> 622 us (level)
  transfers between devices with their start and end apart: 57 -> 57, of which waited for: 25 -> 24; matrix products, arithmetic and copies ran while one was open for 10% -> 10% of each run, Pallas kernels for 26% -> 26%
where the time goes in v8:
time: 622 us; the launch traced here: 613 us
  waiting for transfers between devices  216 us (35%)
  Pallas kernels  213 us (34%)
  starting transfers between devices  83.9 us (13%)
  other arithmetic  49.3 us (8%)
  local copies, waits for them, and re-layouts  35.3 us (6%)
  between operations  14.9 us (2%)
    ppermute x32, waiting for transfers between devices, swap(): return lax.ppermute(array, axis, SWAP)  152 us
    pallas_call x2, Pallas kernels, ffn_backward(): call(functools.partial(down_body, step, len(d)), (count // tile,), specs...  49.4 us
    pallas_call x2, Pallas kernels, ffn_forward(): call(functools.partial(up_body, step, len(h)), (count // tile,), specs +...  43.8 us
    pallas_call x2, Pallas kernels, weight_grads(): call(functools.partial(grads_body, places, [(len(lefts), len(rights)) for...  43.6 us
    ppermute x32, starting transfers between devices, swap(): return lax.ppermute(array, axis, SWAP)  30.2 us
    ppermute x12, starting transfers between devices, turn(): lax.ppermute(array, 'z', [(i, (i + step) % depth) for i in range(depth)])  30.2 us
    ppermute x12, waiting for transfers between devices, turn(): lax.ppermute(array, 'z', [(i, (i + step) % depth) for i in range(depth)])  28.5 us
    all_gather x2, waiting for transfers between devices, gather_cz(): return lax.all_gather(array, ('core', 'z'), axis=dim, tiled=True)  20.7 us
  transfers between devices with their start and end apart: 57, of which 24 were waited for; matrix products, arithmetic and copies ran while one was open for 10% of the time, Pallas kernels for 26%

profile of v8, /device:TPU:0, one launch (start us, length us, event | category | flops | bytes accessed | tf_op | source)
XLA Modules:
  0.0 612.6 jit_solution(3936412175723464737)
XLA Ops:
  46.1 15.7 %collective-permute-done.8 = bf16[72,1152]{1,0:T(8,128)(2,1)S(1)} collective-permute-done((bf16[72,1152]{1,0:T(8,128)(2,1)S(1)}, bf16[72,1152]{1,0:T(8,128)(2,1)S(1)}, u32[]{:S(2)}, u32[]{:S(2)}) %collective-permute-start.8) | collective-permute-done | bytes 165920 | tf_op jit(solution)/shard_map/ppermute | solution.py:638
  80.3 7.0 %collective-permute-start.10 = (bf16[4,128,512]{2,1,0:T(8,128)(2,1)}, bf16[4,128,512]{2,1,0:T(8,128)(2,1)}, u32[]{:S(2)}, u32[]{:S(2)}) collective-permute-start(bf16[4,128,512]{2,1,0:T(8,128)(2,1)} %get-tuple-element.181.refs_10_.refs_16_), channel_id=1, source_target_pairs={{0,2},{2,4},{4,6},{1,3},{3,5},{5,7},{8,10},{10,12},{12,14},{9,11},... | collective-permute-start | bytes 1572872 | tf_op jit(solution)/shard_map/ppermute | solution.py:634
  94.8 14.1 %collective-permute-done.13 = bf16[4,72,1152]{2,1,0:T(8,128)(2,1)} collective-permute-done((bf16[4,72,1152]{2,1,0:T(8,128)(2,1)S(1)}, bf16[4,72,1152]{2,1,0:T(8,128)(2,1)}, u32[]{:S(2)}, u32[]{:S(2)}) %collective-permute-start.13) | collective-permute-done | bytes 663584 | tf_op jit(solution)/shard_map/ppermute | solution.py:629
  116.9 12.2 %collective-permute-done.15.refs_13_.refs_19_ = bf16[4,128,512]{2,1,0:T(8,128)(2,1)S(1)} collective-permute-done((bf16[4,128,512]{2,1,0:T(8,128)(2,1)}, bf16[4,128,512]{2,1,0:T(8,128)(2,1)S(1)}, u32[]{:S(2)}, u32[]{:S(2)}) %collective-permute-start.15) | collective-permute-done | bytes 524320 | tf_op jit(solution)/shard_map/ppermute | solution.py:629
  129.0 10.1 %collective-permute-done.16.refs_14_.refs_20_ = bf16[4,128,512]{2,1,0:T(8,128)(2,1)} collective-permute-done((bf16[4,128,512]{2,1,0:T(8,128)(2,1)}, bf16[4,128,512]{2,1,0:T(8,128)(2,1)}, u32[]{:S(2)}, u32[]{:S(2)}) %collective-permute-start.16) | collective-permute-done | bytes 524320 | tf_op jit(solution)/shard_map/ppermute | solution.py:629
  145.3 14.9 %shard_map.274 = (f32[512,1024]{1,0:T(8,128)}, bf16[512,1024]{1,0:T(8,128)(2,1)}, bf16[512,1024]{1,0:T(8,128)(2,1)}, f32[512,1152]{1,0:T(8,128)}, f32[512,1152]{...) custom-call(bf16[512,1152]{1,0:T(8,128)(2,1)} %get-tuple-element.177.refs_0_.h_ref, ...), custom_call_target="tpu_custom_call" | custom-call | flops 3758096384 | bytes 20185088 | tf_op jit(solution)/shard_map/pallas_call | solution.py:228
  162.4 12.3 %collective-permute-done.18 = bf16[256,1152]{1,0:T(8,128)(2,1)S(1)} collective-permute-done((bf16[256,1152]{1,0:T(8,128)(2,1)}, bf16[256,1152]{1,0:T(8,128)(2,1)S(1)}, u32[]{:S(2)}, u32[]{:S(2)}) %collective-permute-start.18) | collective-permute-done | bytes 589856 | tf_op jit(solution)/shard_map/ppermute | solution.py:629
  180.9 20.7 %all-gather.3.cloned.1.call-done = bf16[4,576,1792]{2,1,0:T(8,128)(2,1)} async-done(((bf16[4,72,1792]{2,1,0:T(8,128)(2,1)}), bf16[4,576,1792]{2,1,0:T(8,128)(2,1)}) %all-gather.3.cloned.1.call-update) | async-done | bytes 8257552 | tf_op jit(solution)/shard_map/all_gather | solution.py:689
  201.6 21.1 %shard_map.275 = (bf16[1024,1792]{1,0:T(8,128)(2,1)}, bf16[1024,1792]{1,0:T(8,128)(2,1)}, bf16[1024,1792]{1,0:T(8,128)(2,1)}, bf16[1024,1152]{1,0:T(8,128)(2,1)}) custom-call(bf16[1024,1152]{1,0:T(8,128)(2,1)} %pad_maximum_fusion.1.refs_0_, bf16[2,1152,1792]{2,1,0:T(8,128)(2,1)} %bitcast.92, ...), custom_call_target="tpu_custom_call" | custom-call | flops 12683575296 | bytes 26738688 | tf_op jit(solution)/shard_map/pallas_call | solution.py:391
  223.7 22.7 %shard_map.276 = (bf16[1024,1792]{1,0:T(8,128)(2,1)}, bf16[1024,1792]{1,0:T(8,128)(2,1)}, bf16[1024,1792]{1,0:T(8,128)(2,1)}, bf16[512,1152]{1,0:T(8,128)(2,1)}, bf16[512,1152]{1,0:T(8,128)(2,1)}) custom-call(bf16[512,1152]{1,0:T(8,128)(2,1)} %copy-done.39, bf16[512,1152]{1,0:T(8,128)(2,1)} %collective-permute-done.21.refs_1_.refs_3_, ...), custom_call_target="tpu_custom_call" | custom-call | flops 12683575296 | bytes 26738688 | tf_op jit(solution)/shard_map/pallas_call | solution.py:391
  249.3 25.4 %collective-permute-done.22 = bf16[512,1152]{1,0:T(8,128)(2,1)S(1)} collective-permute-done((bf16[512,1152]{1,0:T(8,128)(2,1)}, bf16[512,1152]{1,0:T(8,128)(2,1)S(1)}, u32[]{:S(2)}, u32[]{:S(2)}) %collective-permute-start.22) | collective-permute-done | bytes 1179680 | tf_op jit(solution)/shard_map/ppermute | solution.py:629
  279.8 12.3 %collective-permute-done.24.far_a = bf16[256,1152]{1,0:T(8,128)(2,1)S(1)} collective-permute-done((bf16[256,1152]{1,0:T(8,128)(2,1)S(1)}, bf16[256,1152]{1,0:T(8,128)(2,1)S(1)}, u32[]{:S(2)}, u32[]{:S(2)}) %collective-permute-start.24) | collective-permute-done | bytes 589856 | tf_op jit(solution)/shard_map/ppermute | solution.py:629
  301.2 12.2 %collective-permute-done.26 = bf16[256,1152]{1,0:T(8,128)(2,1)S(1)} collective-permute-done((bf16[256,1152]{1,0:T(8,128)(2,1)}, bf16[256,1152]{1,0:T(8,128)(2,1)S(1)}, u32[]{:S(2)}, u32[]{:S(2)}) %collective-permute-start.26) | collective-permute-done | bytes 589856 | tf_op jit(solution)/shard_map/ppermute | solution.py:629
  318.7 24.6 %shard_map.278 = (bf16[2,1024,1792]{2,1,0:T(8,128)(2,1)}, bf16[1024,1152]{1,0:T(8,128)(2,1)}) custom-call(bf16[1024,1152]{1,0:T(8,128)(2,1)} %pad_maximum_fusion.2.refs_0_, bf16[1024,1792]{1,0:T(8,128)(2,1)} %get-tuple-element.230.refs_1_, bf16[1024,1792]{1,0:T(8,128)(2,1)} %get-tuple-element.231.refs_2_, bf16[2,1152,1792]{2,1,0:T(8,128)(2,1)} %bitcast.94, ...), custom_call_target="tpu_custom_call" | custom-call | flops 12683575296 | bytes 19398656 | tf_op jit(solution)/shard_map/pallas_call | solution.py:417
  344.7 24.8 %shard_map.279 = (bf16[2,1024,1792]{2,1,0:T(8,128)(2,1)}, bf16[512,1152]{1,0:T(8,128)(2,1)}, bf16[512,1152]{1,0:T(8,128)(2,1)}) custom-call(bf16[512,1152]{1,0:T(8,128)(2,1)} %copy-done.40, bf16[512,1152]{1,0:T(8,128)(2,1)} %copy-done.41, bf16[1024,1792]{1,0:T(8,128)(2,1)} %get-tuple-element.237.refs_2_, bf16[1024,1792]{1,0:T(8,128)(2,1)} %get-tuple-element.238.refs_3_, ...), custom_call_target="tpu_custom_call" | custom-call | flops 12683575296 | bytes 19398656 | tf_op jit(solution)/shard_map/pallas_call | solution.py:417
  371.7 26.9 %shard_map.280 = (bf16[1152,1792]{1,0:T(8,128)(2,1)}, bf16[1152,1792]{1,0:T(8,128)(2,1)}) custom-call(bf16[1024,1152]{1,0:T(8,128)(2,1)} %pad_maximum_fusion.1.refs_0_, bf16[2,1024,1792]{2,1,0:T(8,128)(2,1)} %get-tuple-element.246.refs_1_, bf16[512,1152]{1,0:T(8,128)(2,1)} %copy-done.39, bf16[512,1152]{1,0:T(8,128)(2,1)} %collective-permute-done.21.refs_1_.refs_3_, ...), custom_call_target="tpu_custom_call" | custom-call | flops 16911433728 | bytes 16515072 | tf_op jit(solution)/shard_map/pallas_call | solution.py:474
  402.3 16.7 %shard_map.281 = (bf16[896,1152]{1,0:T(8,128)(2,1)}, bf16[896,1152]{1,0:T(8,128)(2,1)}) custom-call(bf16[1024,1792]{1,0:T(8,128)(2,1)} %get-tuple-element.258.refs_0_, bf16[1,1024,1152]{2,1,0:T(8,128)(2,1)} %bitcast.82, bf16[1024,1792]{1,0:T(8,128)(2,1)} %get-tuple-element.260.refs_2_, bf16[1,512,1152]{2,1,0:T(8,128)(2,1)} %bitcast.98, ...), custom_call_target="tpu_custom_call" | custom-call | flops 8455716864 | bytes 8257536 | tf_op jit(solution)/shard_map/pallas_call | solution.py:474
  424.7 18.3 %shard_map.282 = (f32[512,1152]{1,0:T(8,128)}, bf16[512,1152]{1,0:T(8,128)(2,1)}, bf16[512,1024]{1,0:T(8,128)(2,1)}, f32[8,1152]{1,0:T(8,128)}, f32[8,256]{1,0:T...) custom-call(f32[256,1152]{1,0:T(8,128)} %get-tuple-element.267.refs_, ...), custom_call_target="tpu_custom_call" | custom-call | flops 4563402752 | bytes 17653760 | tf_op jit(solution)/shard_map/pallas_call | solution.py:299
  443.1 9.0 %shard_map.283 = (bf16[16,72,1152]{2,1,0:T(8,128)(2,1)}, bf16[16,72,1152]{2,1,0:T(8,128)(2,1)}) custom-call(bf16[512,1024]{1,0:T(8,128)(2,1)} %get-tuple-element.277.mixed_ref, bf16[512,1152]{1,0:T(8,128)(2,1)} %get-tuple-element.278.dattn_ref, bf16[512,1152]{1,0:T(8,128)(2,1)} %get-tuple-element.177.refs_0_.h_ref, ...), custom_call_target="tpu_custom_call" | custom-call | flops 2415919104 | bytes 10616832 | tf_op jit(solution)/shard_map/pallas_call | solution.py:505
  467.5 10.5 %collective-permute-done.36 = bf16[4,128,512]{2,1,0:T(8,128)(2,1)} collective-permute-done((bf16[4,128,512]{2,1,0:T(8,128)(2,1)}, bf16[4,128,512]{2,1,0:T(8,128)(2,1)}, u32[]{:S(2)}, u32[]{:S(2)}) %collective-permute-start.36) | collective-permute-done | bytes 524320 | tf_op jit(solution)/shard_map/ppermute | solution.py:629
  486.1 23.6 %collective-permute-done.41 = bf16[2,4,72,1152]{3,2,1,0:T(8,128)(2,1)} collective-permute-done((bf16[2,4,72,1152]{3,2,1,0:T(8,128)(2,1)}, bf16[2,4,72,1152]{3,2,1,0:T(8,128)(2,1)}, u32[]{:S(2)}, u32[]{:S(2)}) %collective-permute-start.41) | collective-permute-done | bytes 1327136 | tf_op jit(solution)/shard_map/ppermute | solution.py:629
  512.5 7.8 %collective-permute-done.39.refs_2_ = bf16[4,128,512]{2,1,0:T(8,128)(2,1)S(1)} collective-permute-done((bf16[4,128,512]{2,1,0:T(8,128)(2,1)S(1)}, bf16[4,128,512]{2,1,0:T(8,128)(2,1)S(1)}, u32[]{:S(2)}, u32[]{:S(2)}) %collective-permute-start.39) | collective-permute-done | bytes 524320 | tf_op jit(solution)/shard_map/ppermute | solution.py:634
  522.9 9.9 %shard_map.284 = (bf16[512,512]{1,0:T(8,128)(2,1)}, bf16[512,1152]{1,0:T(8,128)(2,1)}, f32[8,1152]{1,0:T(8,128)}, f32[8,256]{1,0:T(8,128)}) custom-call(f32[4,128,512]{2,1,0:T(8,128)} %get-tuple-element.291.refs_0_, bf16[4,128,512]{2,1,0:T(8,128)(2,1)} %collective-permute-done.40.refs_1_, bf16[4,128,512]{2,1,0:T(8,128)(2,1)} %copy-done.24, ...), custom_call_target="tpu_custom_call" | custom-call | flops 1811939328 | bytes 3497984 | tf_op jit(solution)/shard_map/pallas_call | solution.py:351
  555.3 11.8 %collective-permute-start.44 = (bf16[72,1152]{1,0:T(8,128)(2,1)}, bf16[72,1152]{1,0:T(8,128)(2,1)}, u32[]{:S(2)}, u32[]{:S(2)}) collective-permute-start(bf16[72,1152]{1,0:T(8,128)(2,1)} %get-tuple-element.335), channel_id=1, source_target_pairs={{0,2},{2,4},{4,6},{6,0},{1,3},{3,5},{5,7},{7,1},{8,10},{10,12},{12... | collective-permute-start | bytes 497672 | tf_op jit(solution)/shard_map/ppermute | solution.py:638
  (272 shorter events, 213.0 us)
Async XLA Ops:
  7.3 173.7 %all-gather.5.cloned.1.call-start = ((), (), s32[]{:S(2)}) async-start(), calls=%async_computation.6 | async-start | bytes 4644864 | tf_op jit(solution)/shard_map/all_gather | solution.py:689
  36.6 31.3 %collective-permute-start.6 = (bf16[16,48,512]{2,1,0:T(8,128)(2,1)S(1)}, bf16[16,48,512]{2,1,0:T(8,128)(2,1)S(1)}, u32[]{:S(2)}, u32[]{:S(2)}) collective-permute-start(bf16[16,48,512]{2,1,0:T(8,128)(2,1)S(1)} %pad_maximum_fusion.8.own_ref), channel_id=1, source_target_pairs={{0,8},{8,0},{1,9},{9,1},{2,10},{10,2},{3,11},{11,3},{4,12},{12,4},... | collective-permute-start | bytes 2359304 | tf_op jit(solution)/shard_map/ppermute | solution.py:629
  38.4 38.4 %all-to-all-start = ((bf16[4,2,36,1792]{3,1,2,0:T(2,128)(2,1)}), bf16[4,2,36,1792]{3,1,2,0:T(2,128)(2,1)S(1)}, u32[]{:S(2)}, u32[]{:S(2)}) async-start(bf16[4,2,36,1792]{3,1,2,0:T(2,128)(2,1)} %bitcast.12), calls=%async_computation | async-start | bytes 2064384 | tf_op jit(solution)/shard_map/all_to_all | solution.py:729
  41.9 159.7 %all-gather.3.cloned.1.call-start = ((), (), s32[]{:S(2)}) async-start(), calls=%async_computation.5 | async-start | bytes 9289728 | tf_op jit(solution)/shard_map/all_gather | solution.py:689
  78.7 30.2 %collective-permute-start.13 = (bf16[4,72,1152]{2,1,0:T(8,128)(2,1)S(1)}, bf16[4,72,1152]{2,1,0:T(8,128)(2,1)}, u32[]{:S(2)}, u32[]{:S(2)}) collective-permute-start(bf16[4,72,1152]{2,1,0:T(8,128)(2,1)S(1)} %pad_maximum_fusion.9), channel_id=1, source_target_pairs={{0,1},{1,0},{2,3},{3,2},{4,5},{5,4},{6,7},{7,6},{8,9},{9,8},{10,11... | collective-permute-start | bytes 1990664 | tf_op jit(solution)/shard_map/ppermute | solution.py:629
  80.1 28.8 %collective-permute-start.14 = (bf16[4,72,1152]{2,1,0:T(8,128)(2,1)S(1)}, bf16[4,72,1152]{2,1,0:T(8,128)(2,1)}, u32[]{:S(2)}, u32[]{:S(2)}) collective-permute-start(bf16[4,72,1152]{2,1,0:T(8,128)(2,1)S(1)} %pad_maximum_fusion.9), channel_id=1, source_target_pairs={{0,17},{1,16},{16,1},{17,0},{2,19},{3,18},{18,3},{19,2},{4,21},{5,... | collective-permute-start | bytes 1990664 | tf_op jit(solution)/shard_map/ppermute | solution.py:650
  80.3 30.5 %collective-permute-start.10 = (bf16[4,128,512]{2,1,0:T(8,128)(2,1)}, bf16[4,128,512]{2,1,0:T(8,128)(2,1)}, u32[]{:S(2)}, u32[]{:S(2)}) collective-permute-start(bf16[4,128,512]{2,1,0:T(8,128)(2,1)} %get-tuple-element.181.refs_10_.refs_16_), channel_id=1, source_target_pairs={{0,2},{2,4},{4,6},{1,3},{3,5},{5,7},{8,10},{10,12},{12,14},{9,11},... | collective-permute-start | bytes 1572872 | tf_op jit(solution)/shard_map/ppermute | solution.py:634
  110.8 409.5 %reduce-scatter.3.cloned.1.call-start = ((), (), s32[]{:S(2)}) async-start(), calls=%async_computation.7 | async-start | bytes 5160960 | tf_op jit(solution)/shard_map/reduce_scatter | solution.py:715
  110.9 28.2 %collective-permute-start.17 = (bf16[16,72,1152]{2,1,0:T(8,128)(2,1)S(1)}, bf16[16,72,1152]{2,1,0:T(8,128)(2,1)}, u32[]{:S(2)}, u32[]{:S(2)}) collective-permute-start(bf16[16,72,1152]{2,1,0:T(8,128)(2,1)S(1)} %pad_maximum_fusion.own_ref), channel_id=1, source_target_pairs={{0,8},{8,0},{1,9},{9,1},{2,10},{10,2},{3,11},{11,3},{4,12},{12,4},... | collective-permute-start | bytes 7962632 | tf_op jit(solution)/shard_map/ppermute | solution.py:629
  115.5 23.6 %collective-permute-start.16 = (bf16[4,128,512]{2,1,0:T(8,128)(2,1)}, bf16[4,128,512]{2,1,0:T(8,128)(2,1)}, u32[]{:S(2)}, u32[]{:S(2)}) collective-permute-start(bf16[4,128,512]{2,1,0:T(8,128)(2,1)} %get-tuple-element.341), channel_id=1, source_target_pairs={{0,1},{1,0},{2,3},{3,2},{4,5},{5,4},{6,7},{7,6},{8,9},{9,8},{10,11... | collective-permute-start | bytes 1572872 | tf_op jit(solution)/shard_map/ppermute | solution.py:629
  178.6 44.1 %collective-permute-start.20 = (bf16[512,1152]{1,0:T(8,128)(2,1)S(1)}, bf16[512,1152]{1,0:T(8,128)(2,1)S(1)}, u32[]{:S(2)}, u32[]{:S(2)}) collective-permute-start(bf16[512,1152]{1,0:T(8,128)(2,1)S(1)} %get-tuple-element.200), channel_id=1, source_target_pairs={{0,1},{1,0},{2,3},{3,2},{4,5},{5,4},{6,7},{7,6},{8,9},{9,8},{10,11... | collective-permute-start | bytes 3538952 | tf_op jit(solution)/shard_map/ppermute | solution.py:629
  179.4 43.4 %collective-permute-start.21 = (bf16[512,1152]{1,0:T(8,128)(2,1)S(1)}, bf16[512,1152]{1,0:T(8,128)(2,1)}, u32[]{:S(2)}, u32[]{:S(2)}) collective-permute-start(bf16[512,1152]{1,0:T(8,128)(2,1)S(1)} %get-tuple-element.201), channel_id=1, source_target_pairs={{0,16},{16,0},{1,17},{17,1},{2,18},{18,2},{3,19},{19,3},{4,20},{20... | collective-permute-start | bytes 3538952 | tf_op jit(solution)/shard_map/ppermute | solution.py:629
  246.4 28.3 %collective-permute-start.22 = (bf16[512,1152]{1,0:T(8,128)(2,1)}, bf16[512,1152]{1,0:T(8,128)(2,1)S(1)}, u32[]{:S(2)}, u32[]{:S(2)}) collective-permute-start(bf16[512,1152]{1,0:T(8,128)(2,1)} %get-tuple-element.213), channel_id=1, source_target_pairs={{0,1},{1,0},{2,3},{3,2},{4,5},{5,4},{6,7},{7,6},{8,9},{9,8},{10,11... | collective-permute-start | bytes 3538952 | tf_op jit(solution)/shard_map/ppermute | solution.py:629
  247.9 28.0 %collective-permute-start.23 = (bf16[512,1152]{1,0:T(8,128)(2,1)}, bf16[512,1152]{1,0:T(8,128)(2,1)S(1)}, u32[]{:S(2)}, u32[]{:S(2)}) collective-permute-start(bf16[512,1152]{1,0:T(8,128)(2,1)} %get-tuple-element.214), channel_id=1, source_target_pairs={{0,16},{16,0},{1,17},{17,1},{2,18},{18,2},{3,19},{19,3},{4,20},{20... | collective-permute-start | bytes 3538952 | tf_op jit(solution)/shard_map/ppermute | solution.py:629
  316.7 26.6 %collective-permute-start.28 = (bf16[512,1152]{1,0:T(8,128)(2,1)S(1)}, bf16[512,1152]{1,0:T(8,128)(2,1)S(1)}, u32[]{:S(2)}, u32[]{:S(2)}) collective-permute-start(bf16[512,1152]{1,0:T(8,128)(2,1)S(1)} %pad_maximum_fusion.5), channel_id=1, source_target_pairs={{0,1},{1,0},{2,3},{3,2},{4,5},{5,4},{6,7},{7,6},{8,9},{9,8},{10,11... | collective-permute-start | bytes 3538952 | tf_op jit(solution)/shard_map/ppermute | solution.py:629
  317.4 25.9 %collective-permute-start.29 = (bf16[512,1152]{1,0:T(8,128)(2,1)S(1)}, bf16[512,1152]{1,0:T(8,128)(2,1)S(1)}, u32[]{:S(2)}, u32[]{:S(2)}) collective-permute-start(bf16[512,1152]{1,0:T(8,128)(2,1)S(1)} %pad_maximum_fusion.6), channel_id=1, source_target_pairs={{0,16},{16,0},{1,17},{17,1},{2,18},{18,2},{3,19},{19,3},{4,20},{20... | collective-permute-start | bytes 3538952 | tf_op jit(solution)/shard_map/ppermute | solution.py:629
  369.5 29.1 %collective-permute-start.30 = (bf16[512,1152]{1,0:T(8,128)(2,1)}, bf16[512,1152]{1,0:T(8,128)(2,1)S(1)}, u32[]{:S(2)}, u32[]{:S(2)}) collective-permute-start(bf16[512,1152]{1,0:T(8,128)(2,1)} %get-tuple-element.243), channel_id=1, source_target_pairs={{0,1},{1,0},{2,3},{3,2},{4,5},{5,4},{6,7},{7,6},{8,9},{9,8},{10,11... | collective-permute-start | bytes 3538952 | tf_op jit(solution)/shard_map/ppermute | solution.py:629
  370.9 27.7 %collective-permute-start.31 = (bf16[512,1152]{1,0:T(8,128)(2,1)}, bf16[512,1152]{1,0:T(8,128)(2,1)S(1)}, u32[]{:S(2)}, u32[]{:S(2)}) collective-permute-start(bf16[512,1152]{1,0:T(8,128)(2,1)} %get-tuple-element.244), channel_id=1, source_target_pairs={{0,16},{16,0},{1,17},{17,1},{2,18},{18,2},{3,19},{19,3},{4,20},{20... | collective-permute-start | bytes 3538952 | tf_op jit(solution)/shard_map/ppermute | solution.py:629
  424.6 160.1 %reduce-scatter.5.cloned.1.call-start = ((), (), s32[]{:S(2)}) async-start(), calls=%async_computation.8 | async-start | bytes 2580480 | tf_op jit(solution)/shard_map/reduce_scatter | solution.py:715
  424.7 29.9 %collective-permute-start.38 = (bf16[896,1152]{1,0:T(8,128)(2,1)}, bf16[896,1152]{1,0:T(8,128)(2,1)}, u32[]{:S(2)}, u32[]{:S(2)}) collective-permute-start(bf16[896,1152]{1,0:T(8,128)(2,1)} %get-tuple-element.283), channel_id=1, source_target_pairs={{0,8},{8,0},{1,9},{9,1},{2,10},{10,2},{3,11},{11,3},{4,12},{12,4},... | collective-permute-start | bytes 6193160 | tf_op jit(solution)/shard_map/ppermute | solution.py:629
  453.9 24.1 %collective-permute-start.36 = (bf16[4,128,512]{2,1,0:T(8,128)(2,1)}, bf16[4,128,512]{2,1,0:T(8,128)(2,1)}, u32[]{:S(2)}, u32[]{:S(2)}) collective-permute-start(bf16[4,128,512]{2,1,0:T(8,128)(2,1)} %get-tuple-element.276), channel_id=1, source_target_pairs={{0,1},{1,0},{2,3},{3,2},{4,5},{5,4},{6,7},{7,6},{8,9},{9,8},{10,11... | collective-permute-start | bytes 1572872 | tf_op jit(solution)/shard_map/ppermute | solution.py:629
  479.2 30.6 %collective-permute-start.41 = (bf16[2,4,72,1152]{3,2,1,0:T(8,128)(2,1)}, bf16[2,4,72,1152]{3,2,1,0:T(8,128)(2,1)}, u32[]{:S(2)}, u32[]{:S(2)}) collective-permute-start(bf16[2,4,72,1152]{3,2,1,0:T(8,128)(2,1)} %dynamic-slice_bitcast_fusion), channel_id=1, source_target_pairs={{0,16},{16,0},{1,17},{17,1},{2,18},{18,2},{3,19},{19,3},{4,20},{20... | collective-permute-start | bytes 3981320 | tf_op jit(solution)/shard_map/ppermute | solution.py:629
  483.6 36.8 %collective-permute-start.39 = (bf16[4,128,512]{2,1,0:T(8,128)(2,1)S(1)}, bf16[4,128,512]{2,1,0:T(8,128)(2,1)S(1)}, u32[]{:S(2)}, u32[]{:S(2)}) collective-permute-start(bf16[4,128,512]{2,1,0:T(8,128)(2,1)S(1)} %get-tuple-element.340), channel_id=1, source_target_pairs={{4,0},{6,2},{5,1},{7,3},{12,8},{14,10},{13,9},{15,11},{20,16},{22,... | collective-permute-start | bytes 1572872 | tf_op jit(solution)/shard_map/ppermute | solution.py:634
  484.8 35.5 %collective-permute-start.40 = (bf16[4,128,512]{2,1,0:T(8,128)(2,1)S(1)}, bf16[4,128,512]{2,1,0:T(8,128)(2,1)}, u32[]{:S(2)}, u32[]{:S(2)}) collective-permute-start(bf16[4,128,512]{2,1,0:T(8,128)(2,1)S(1)} %get-tuple-element.339), channel_id=1, source_target_pairs={{2,0},{4,2},{6,4},{3,1},{5,3},{7,5},{10,8},{12,10},{14,12},{11,9},... | collective-permute-start | bytes 1572872 | tf_op jit(solution)/shard_map/ppermute | solution.py:634
  (75 other events, 830.8 us)
Sparse Core Ops, SparseCore 0:
  9.7 62.1 all-gather.4
  111.0 90.6 all-gather.2
  424.7 82.5 reduce-scatter.2
  520.5 60.3 reduce-scatter.4

commit v9 on v8

--- a/solution.py
+++ b/solution.py
@@ -188,7 +188,7 @@
     allowed = jnp.concatenate([allowed.astype(F32)] * HEADS, axis=0) > 0.5
     scores = jnp.where(allowed, mm_t(query, keys) * SCORE_SCALE, NEG_FILL)
     powers = jnp.exp(scores - jnp.max(scores, axis=-1, keepdims=True))
-    return powers / jnp.sum(powers, axis=-1, keepdims=True)
+    return powers * (1.0 / jnp.sum(powers, axis=-1, keepdims=True))
 
 
 def attend_body(links, blocks, *refs):

time: 622 us -> 622 us (level)
  no operation moved by 1% of the time
where the time goes in v9:
time: 622 us; the launch traced here: 613 us
  waiting for transfers between devices  216 us (35%)
  Pallas kernels  213 us (34%)
  starting transfers between devices  83.9 us (13%)
  other arithmetic  49.3 us (8%)
  local copies, waits for them, and re-layouts  35.3 us (6%)
  between operations  14.9 us (2%)
    ppermute x32, waiting for transfers between devices, swap(): return lax.ppermute(array, axis, SWAP)  152 us
    pallas_call x2, Pallas kernels, ffn_backward(): call(functools.partial(down_body, step, len(d)), (count // tile,), specs...  49.4 us
    pallas_call x2, Pallas kernels, ffn_forward(): call(functools.partial(up_body, step, len(h)), (count // tile,), specs +...  43.8 us
    pallas_call x2, Pallas kernels, weight_grads(): call(functools.partial(grads_body, places, [(len(lefts), len(rights)) for...  43.6 us
    ppermute x32, starting transfers between devices, swap(): return lax.ppermute(array, axis, SWAP)  30.2 us
    ppermute x12, starting transfers between devices, turn(): lax.ppermute(array, 'z', [(i, (i + step) % depth) for i in range(depth)])  30.2 us
    ppermute x12, waiting for transfers between devices, turn(): lax.ppermute(array, 'z', [(i, (i + step) % depth) for i in range(depth)])  28.5 us
    all_gather x2, waiting for transfers between devices, gather_cz(): return lax.all_gather(array, ('core', 'z'), axis=dim, tiled=True)  20.7 us
  transfers between devices with their start and end apart: 57, of which 24 were waited for; matrix products, arithmetic and copies ran while one was open for 10% of the time, Pallas kernels for 26%

profile of v9, /device:TPU:0, one launch (start us, length us, event | category | flops | bytes accessed | tf_op | source)
XLA Modules:
  0.0 612.6 jit_solution(3936412175723464737)
XLA Ops:
  46.1 15.7 %collective-permute-done.8 = bf16[72,1152]{1,0:T(8,128)(2,1)S(1)} collective-permute-done((bf16[72,1152]{1,0:T(8,128)(2,1)S(1)}, bf16[72,1152]{1,0:T(8,128)(2,1)S(1)}, u32[]{:S(2)}, u32[]{:S(2)}) %collective-permute-start.8) | collective-permute-done | bytes 165920 | tf_op jit(solution)/shard_map/ppermute | solution.py:638
  80.3 7.0 %collective-permute-start.10 = (bf16[4,128,512]{2,1,0:T(8,128)(2,1)}, bf16[4,128,512]{2,1,0:T(8,128)(2,1)}, u32[]{:S(2)}, u32[]{:S(2)}) collective-permute-start(bf16[4,128,512]{2,1,0:T(8,128)(2,1)} %get-tuple-element.181.refs_10_.refs_16_), channel_id=1, source_target_pairs={{0,2},{2,4},{4,6},{1,3},{3,5},{5,7},{8,10},{10,12},{12,14},{9,11},... | collective-permute-start | bytes 1572872 | tf_op jit(solution)/shard_map/ppermute | solution.py:634
  94.8 14.1 %collective-permute-done.13 = bf16[4,72,1152]{2,1,0:T(8,128)(2,1)} collective-permute-done((bf16[4,72,1152]{2,1,0:T(8,128)(2,1)S(1)}, bf16[4,72,1152]{2,1,0:T(8,128)(2,1)}, u32[]{:S(2)}, u32[]{:S(2)}) %collective-permute-start.13) | collective-permute-done | bytes 663584 | tf_op jit(solution)/shard_map/ppermute | solution.py:629
  116.9 12.2 %collective-permute-done.15.refs_13_.refs_19_ = bf16[4,128,512]{2,1,0:T(8,128)(2,1)S(1)} collective-permute-done((bf16[4,128,512]{2,1,0:T(8,128)(2,1)}, bf16[4,128,512]{2,1,0:T(8,128)(2,1)S(1)}, u32[]{:S(2)}, u32[]{:S(2)}) %collective-permute-start.15) | collective-permute-done | bytes 524320 | tf_op jit(solution)/shard_map/ppermute | solution.py:629
  129.0 10.1 %collective-permute-done.16.refs_14_.refs_20_ = bf16[4,128,512]{2,1,0:T(8,128)(2,1)} collective-permute-done((bf16[4,128,512]{2,1,0:T(8,128)(2,1)}, bf16[4,128,512]{2,1,0:T(8,128)(2,1)}, u32[]{:S(2)}, u32[]{:S(2)}) %collective-permute-start.16) | collective-permute-done | bytes 524320 | tf_op jit(solution)/shard_map/ppermute | solution.py:629
  145.3 14.9 %shard_map.274 = (f32[512,1024]{1,0:T(8,128)}, bf16[512,1024]{1,0:T(8,128)(2,1)}, bf16[512,1024]{1,0:T(8,128)(2,1)}, f32[512,1152]{1,0:T(8,128)}, f32[512,1152]{...) custom-call(bf16[512,1152]{1,0:T(8,128)(2,1)} %get-tuple-element.177.refs_0_.h_ref, ...), custom_call_target="tpu_custom_call" | custom-call | flops 3758096384 | bytes 20185088 | tf_op jit(solution)/shard_map/pallas_call | solution.py:228
  162.4 12.3 %collective-permute-done.18 = bf16[256,1152]{1,0:T(8,128)(2,1)S(1)} collective-permute-done((bf16[256,1152]{1,0:T(8,128)(2,1)}, bf16[256,1152]{1,0:T(8,128)(2,1)S(1)}, u32[]{:S(2)}, u32[]{:S(2)}) %collective-permute-start.18) | collective-permute-done | bytes 589856 | tf_op jit(solution)/shard_map/ppermute | solution.py:629
  180.9 20.7 %all-gather.3.cloned.1.call-done = bf16[4,576,1792]{2,1,0:T(8,128)(2,1)} async-done(((bf16[4,72,1792]{2,1,0:T(8,128)(2,1)}), bf16[4,576,1792]{2,1,0:T(8,128)(2,1)}) %all-gather.3.cloned.1.call-update) | async-done | bytes 8257552 | tf_op jit(solution)/shard_map/all_gather | solution.py:689
  201.6 21.1 %shard_map.275 = (bf16[1024,1792]{1,0:T(8,128)(2,1)}, bf16[1024,1792]{1,0:T(8,128)(2,1)}, bf16[1024,1792]{1,0:T(8,128)(2,1)}, bf16[1024,1152]{1,0:T(8,128)(2,1)}) custom-call(bf16[1024,1152]{1,0:T(8,128)(2,1)} %pad_maximum_fusion.1.refs_0_, bf16[2,1152,1792]{2,1,0:T(8,128)(2,1)} %bitcast.92, ...), custom_call_target="tpu_custom_call" | custom-call | flops 12683575296 | bytes 26738688 | tf_op jit(solution)/shard_map/pallas_call | solution.py:391
  223.7 22.7 %shard_map.276 = (bf16[1024,1792]{1,0:T(8,128)(2,1)}, bf16[1024,1792]{1,0:T(8,128)(2,1)}, bf16[1024,1792]{1,0:T(8,128)(2,1)}, bf16[512,1152]{1,0:T(8,128)(2,1)}, bf16[512,1152]{1,0:T(8,128)(2,1)}) custom-call(bf16[512,1152]{1,0:T(8,128)(2,1)} %copy-done.39, bf16[512,1152]{1,0:T(8,128)(2,1)} %collective-permute-done.21.refs_1_.refs_3_, ...), custom_call_target="tpu_custom_call" | custom-call | flops 12683575296 | bytes 26738688 | tf_op jit(solution)/shard_map/pallas_call | solution.py:391
  249.3 25.4 %collective-permute-done.22 = bf16[512,1152]{1,0:T(8,128)(2,1)S(1)} collective-permute-done((bf16[512,1152]{1,0:T(8,128)(2,1)}, bf16[512,1152]{1,0:T(8,128)(2,1)S(1)}, u32[]{:S(2)}, u32[]{:S(2)}) %collective-permute-start.22) | collective-permute-done | bytes 1179680 | tf_op jit(solution)/shard_map/ppermute | solution.py:629
  279.8 12.3 %collective-permute-done.24.far_a = bf16[256,1152]{1,0:T(8,128)(2,1)S(1)} collective-permute-done((bf16[256,1152]{1,0:T(8,128)(2,1)S(1)}, bf16[256,1152]{1,0:T(8,128)(2,1)S(1)}, u32[]{:S(2)}, u32[]{:S(2)}) %collective-permute-start.24) | collective-permute-done | bytes 589856 | tf_op jit(solution)/shard_map/ppermute | solution.py:629
  301.2 12.2 %collective-permute-done.26 = bf16[256,1152]{1,0:T(8,128)(2,1)S(1)} collective-permute-done((bf16[256,1152]{1,0:T(8,128)(2,1)}, bf16[256,1152]{1,0:T(8,128)(2,1)S(1)}, u32[]{:S(2)}, u32[]{:S(2)}) %collective-permute-start.26) | collective-permute-done | bytes 589856 | tf_op jit(solution)/shard_map/ppermute | solution.py:629
  318.7 24.6 %shard_map.278 = (bf16[2,1024,1792]{2,1,0:T(8,128)(2,1)}, bf16[1024,1152]{1,0:T(8,128)(2,1)}) custom-call(bf16[1024,1152]{1,0:T(8,128)(2,1)} %pad_maximum_fusion.2.refs_0_, bf16[1024,1792]{1,0:T(8,128)(2,1)} %get-tuple-element.230.refs_1_, bf16[1024,1792]{1,0:T(8,128)(2,1)} %get-tuple-element.231.refs_2_, bf16[2,1152,1792]{2,1,0:T(8,128)(2,1)} %bitcast.94, ...), custom_call_target="tpu_custom_call" | custom-call | flops 12683575296 | bytes 19398656 | tf_op jit(solution)/shard_map/pallas_call | solution.py:417
  344.7 24.8 %shard_map.279 = (bf16[2,1024,1792]{2,1,0:T(8,128)(2,1)}, bf16[512,1152]{1,0:T(8,128)(2,1)}, bf16[512,1152]{1,0:T(8,128)(2,1)}) custom-call(bf16[512,1152]{1,0:T(8,128)(2,1)} %copy-done.40, bf16[512,1152]{1,0:T(8,128)(2,1)} %copy-done.41, bf16[1024,1792]{1,0:T(8,128)(2,1)} %get-tuple-element.237.refs_2_, bf16[1024,1792]{1,0:T(8,128)(2,1)} %get-tuple-element.238.refs_3_, ...), custom_call_target="tpu_custom_call" | custom-call | flops 12683575296 | bytes 19398656 | tf_op jit(solution)/shard_map/pallas_call | solution.py:417
  371.7 26.9 %shard_map.280 = (bf16[1152,1792]{1,0:T(8,128)(2,1)}, bf16[1152,1792]{1,0:T(8,128)(2,1)}) custom-call(bf16[1024,1152]{1,0:T(8,128)(2,1)} %pad_maximum_fusion.1.refs_0_, bf16[2,1024,1792]{2,1,0:T(8,128)(2,1)} %get-tuple-element.246.refs_1_, bf16[512,1152]{1,0:T(8,128)(2,1)} %copy-done.39, bf16[512,1152]{1,0:T(8,128)(2,1)} %collective-permute-done.21.refs_1_.refs_3_, ...), custom_call_target="tpu_custom_call" | custom-call | flops 16911433728 | bytes 16515072 | tf_op jit(solution)/shard_map/pallas_call | solution.py:474
  402.3 16.7 %shard_map.281 = (bf16[896,1152]{1,0:T(8,128)(2,1)}, bf16[896,1152]{1,0:T(8,128)(2,1)}) custom-call(bf16[1024,1792]{1,0:T(8,128)(2,1)} %get-tuple-element.258.refs_0_, bf16[1,1024,1152]{2,1,0:T(8,128)(2,1)} %bitcast.82, bf16[1024,1792]{1,0:T(8,128)(2,1)} %get-tuple-element.260.refs_2_, bf16[1,512,1152]{2,1,0:T(8,128)(2,1)} %bitcast.98, ...), custom_call_target="tpu_custom_call" | custom-call | flops 8455716864 | bytes 8257536 | tf_op jit(solution)/shard_map/pallas_call | solution.py:474
  424.7 18.3 %shard_map.282 = (f32[512,1152]{1,0:T(8,128)}, bf16[512,1152]{1,0:T(8,128)(2,1)}, bf16[512,1024]{1,0:T(8,128)(2,1)}, f32[8,1152]{1,0:T(8,128)}, f32[8,256]{1,0:T...) custom-call(f32[256,1152]{1,0:T(8,128)} %get-tuple-element.267.refs_, ...), custom_call_target="tpu_custom_call" | custom-call | flops 4563402752 | bytes 17653760 | tf_op jit(solution)/shard_map/pallas_call | solution.py:299
  443.1 9.0 %shard_map.283 = (bf16[16,72,1152]{2,1,0:T(8,128)(2,1)}, bf16[16,72,1152]{2,1,0:T(8,128)(2,1)}) custom-call(bf16[512,1024]{1,0:T(8,128)(2,1)} %get-tuple-element.277.mixed_ref, bf16[512,1152]{1,0:T(8,128)(2,1)} %get-tuple-element.278.dattn_ref, bf16[512,1152]{1,0:T(8,128)(2,1)} %get-tuple-element.177.refs_0_.h_ref, ...), custom_call_target="tpu_custom_call" | custom-call | flops 2415919104 | bytes 10616832 | tf_op jit(solution)/shard_map/pallas_call | solution.py:505
  467.5 10.5 %collective-permute-done.36 = bf16[4,128,512]{2,1,0:T(8,128)(2,1)} collective-permute-done((bf16[4,128,512]{2,1,0:T(8,128)(2,1)}, bf16[4,128,512]{2,1,0:T(8,128)(2,1)}, u32[]{:S(2)}, u32[]{:S(2)}) %collective-permute-start.36) | collective-permute-done | bytes 524320 | tf_op jit(solution)/shard_map/ppermute | solution.py:629
  486.1 23.6 %collective-permute-done.41 = bf16[2,4,72,1152]{3,2,1,0:T(8,128)(2,1)} collective-permute-done((bf16[2,4,72,1152]{3,2,1,0:T(8,128)(2,1)}, bf16[2,4,72,1152]{3,2,1,0:T(8,128)(2,1)}, u32[]{:S(2)}, u32[]{:S(2)}) %collective-permute-start.41) | collective-permute-done | bytes 1327136 | tf_op jit(solution)/shard_map/ppermute | solution.py:629
  512.5 7.8 %collective-permute-done.39.refs_2_ = bf16[4,128,512]{2,1,0:T(8,128)(2,1)S(1)} collective-permute-done((bf16[4,128,512]{2,1,0:T(8,128)(2,1)S(1)}, bf16[4,128,512]{2,1,0:T(8,128)(2,1)S(1)}, u32[]{:S(2)}, u32[]{:S(2)}) %collective-permute-start.39) | collective-permute-done | bytes 524320 | tf_op jit(solution)/shard_map/ppermute | solution.py:634
  522.9 9.9 %shard_map.284 = (bf16[512,512]{1,0:T(8,128)(2,1)}, bf16[512,1152]{1,0:T(8,128)(2,1)}, f32[8,1152]{1,0:T(8,128)}, f32[8,256]{1,0:T(8,128)}) custom-call(f32[4,128,512]{2,1,0:T(8,128)} %get-tuple-element.291.refs_0_, bf16[4,128,512]{2,1,0:T(8,128)(2,1)} %collective-permute-done.40.refs_1_, bf16[4,128,512]{2,1,0:T(8,128)(2,1)} %copy-done.24, ...), custom_call_target="tpu_custom_call" | custom-call | flops 1811939328 | bytes 3497984 | tf_op jit(solution)/shard_map/pallas_call | solution.py:351
  555.3 11.8 %collective-permute-start.44 = (bf16[72,1152]{1,0:T(8,128)(2,1)}, bf16[72,1152]{1,0:T(8,128)(2,1)}, u32[]{:S(2)}, u32[]{:S(2)}) collective-permute-start(bf16[72,1152]{1,0:T(8,128)(2,1)} %get-tuple-element.335), channel_id=1, source_target_pairs={{0,2},{2,4},{4,6},{6,0},{1,3},{3,5},{5,7},{7,1},{8,10},{10,12},{12... | collective-permute-start | bytes 497672 | tf_op jit(solution)/shard_map/ppermute | solution.py:638
  (272 shorter events, 213.0 us)
Async XLA Ops:
  7.3 173.7 %all-gather.5.cloned.1.call-start = ((), (), s32[]{:S(2)}) async-start(), calls=%async_computation.6 | async-start | bytes 4644864 | tf_op jit(solution)/shard_map/all_gather | solution.py:689
  36.6 31.3 %collective-permute-start.6 = (bf16[16,48,512]{2,1,0:T(8,128)(2,1)S(1)}, bf16[16,48,512]{2,1,0:T(8,128)(2,1)S(1)}, u32[]{:S(2)}, u32[]{:S(2)}) collective-permute-start(bf16[16,48,512]{2,1,0:T(8,128)(2,1)S(1)} %pad_maximum_fusion.8.own_ref), channel_id=1, source_target_pairs={{0,8},{8,0},{1,9},{9,1},{2,10},{10,2},{3,11},{11,3},{4,12},{12,4},... | collective-permute-start | bytes 2359304 | tf_op jit(solution)/shard_map/ppermute | solution.py:629
  38.4 38.4 %all-to-all-start = ((bf16[4,2,36,1792]{3,1,2,0:T(2,128)(2,1)}), bf16[4,2,36,1792]{3,1,2,0:T(2,128)(2,1)S(1)}, u32[]{:S(2)}, u32[]{:S(2)}) async-start(bf16[4,2,36,1792]{3,1,2,0:T(2,128)(2,1)} %bitcast.12), calls=%async_computation | async-start | bytes 2064384 | tf_op jit(solution)/shard_map/all_to_all | solution.py:729
  41.9 159.7 %all-gather.3.cloned.1.call-start = ((), (), s32[]{:S(2)}) async-start(), calls=%async_computation.5 | async-start | bytes 9289728 | tf_op jit(solution)/shard_map/all_gather | solution.py:689
  78.7 30.2 %collective-permute-start.13 = (bf16[4,72,1152]{2,1,0:T(8,128)(2,1)S(1)}, bf16[4,72,1152]{2,1,0:T(8,128)(2,1)}, u32[]{:S(2)}, u32[]{:S(2)}) collective-permute-start(bf16[4,72,1152]{2,1,0:T(8,128)(2,1)S(1)} %pad_maximum_fusion.9), channel_id=1, source_target_pairs={{0,1},{1,0},{2,3},{3,2},{4,5},{5,4},{6,7},{7,6},{8,9},{9,8},{10,11... | collective-permute-start | bytes 1990664 | tf_op jit(solution)/shard_map/ppermute | solution.py:629
  80.1 28.8 %collective-permute-start.14 = (bf16[4,72,1152]{2,1,0:T(8,128)(2,1)S(1)}, bf16[4,72,1152]{2,1,0:T(8,128)(2,1)}, u32[]{:S(2)}, u32[]{:S(2)}) collective-permute-start(bf16[4,72,1152]{2,1,0:T(8,128)(2,1)S(1)} %pad_maximum_fusion.9), channel_id=1, source_target_pairs={{0,17},{1,16},{16,1},{17,0},{2,19},{3,18},{18,3},{19,2},{4,21},{5,... | collective-permute-start | bytes 1990664 | tf_op jit(solution)/shard_map/ppermute | solution.py:650
  80.3 30.5 %collective-permute-start.10 = (bf16[4,128,512]{2,1,0:T(8,128)(2,1)}, bf16[4,128,512]{2,1,0:T(8,128)(2,1)}, u32[]{:S(2)}, u32[]{:S(2)}) collective-permute-start(bf16[4,128,512]{2,1,0:T(8,128)(2,1)} %get-tuple-element.181.refs_10_.refs_16_), channel_id=1, source_target_pairs={{0,2},{2,4},{4,6},{1,3},{3,5},{5,7},{8,10},{10,12},{12,14},{9,11},... | collective-permute-start | bytes 1572872 | tf_op jit(solution)/shard_map/ppermute | solution.py:634
  110.8 409.5 %reduce-scatter.3.cloned.1.call-start = ((), (), s32[]{:S(2)}) async-start(), calls=%async_computation.7 | async-start | bytes 5160960 | tf_op jit(solution)/shard_map/reduce_scatter | solution.py:715
  110.9 28.2 %collective-permute-start.17 = (bf16[16,72,1152]{2,1,0:T(8,128)(2,1)S(1)}, bf16[16,72,1152]{2,1,0:T(8,128)(2,1)}, u32[]{:S(2)}, u32[]{:S(2)}) collective-permute-start(bf16[16,72,1152]{2,1,0:T(8,128)(2,1)S(1)} %pad_maximum_fusion.own_ref), channel_id=1, source_target_pairs={{0,8},{8,0},{1,9},{9,1},{2,10},{10,2},{3,11},{11,3},{4,12},{12,4},... | collective-permute-start | bytes 7962632 | tf_op jit(solution)/shard_map/ppermute | solution.py:629
  115.5 23.6 %collective-permute-start.16 = (bf16[4,128,512]{2,1,0:T(8,128)(2,1)}, bf16[4,128,512]{2,1,0:T(8,128)(2,1)}, u32[]{:S(2)}, u32[]{:S(2)}) collective-permute-start(bf16[4,128,512]{2,1,0:T(8,128)(2,1)} %get-tuple-element.341), channel_id=1, source_target_pairs={{0,1},{1,0},{2,3},{3,2},{4,5},{5,4},{6,7},{7,6},{8,9},{9,8},{10,11... | collective-permute-start | bytes 1572872 | tf_op jit(solution)/shard_map/ppermute | solution.py:629
  178.6 44.1 %collective-permute-start.20 = (bf16[512,1152]{1,0:T(8,128)(2,1)S(1)}, bf16[512,1152]{1,0:T(8,128)(2,1)S(1)}, u32[]{:S(2)}, u32[]{:S(2)}) collective-permute-start(bf16[512,1152]{1,0:T(8,128)(2,1)S(1)} %get-tuple-element.200), channel_id=1, source_target_pairs={{0,1},{1,0},{2,3},{3,2},{4,5},{5,4},{6,7},{7,6},{8,9},{9,8},{10,11... | collective-permute-start | bytes 3538952 | tf_op jit(solution)/shard_map/ppermute | solution.py:629
  179.4 43.4 %collective-permute-start.21 = (bf16[512,1152]{1,0:T(8,128)(2,1)S(1)}, bf16[512,1152]{1,0:T(8,128)(2,1)}, u32[]{:S(2)}, u32[]{:S(2)}) collective-permute-start(bf16[512,1152]{1,0:T(8,128)(2,1)S(1)} %get-tuple-element.201), channel_id=1, source_target_pairs={{0,16},{16,0},{1,17},{17,1},{2,18},{18,2},{3,19},{19,3},{4,20},{20... | collective-permute-start | bytes 3538952 | tf_op jit(solution)/shard_map/ppermute | solution.py:629
  246.4 28.3 %collective-permute-start.22 = (bf16[512,1152]{1,0:T(8,128)(2,1)}, bf16[512,1152]{1,0:T(8,128)(2,1)S(1)}, u32[]{:S(2)}, u32[]{:S(2)}) collective-permute-start(bf16[512,1152]{1,0:T(8,128)(2,1)} %get-tuple-element.213), channel_id=1, source_target_pairs={{0,1},{1,0},{2,3},{3,2},{4,5},{5,4},{6,7},{7,6},{8,9},{9,8},{10,11... | collective-permute-start | bytes 3538952 | tf_op jit(solution)/shard_map/ppermute | solution.py:629
  247.9 28.0 %collective-permute-start.23 = (bf16[512,1152]{1,0:T(8,128)(2,1)}, bf16[512,1152]{1,0:T(8,128)(2,1)S(1)}, u32[]{:S(2)}, u32[]{:S(2)}) collective-permute-start(bf16[512,1152]{1,0:T(8,128)(2,1)} %get-tuple-element.214), channel_id=1, source_target_pairs={{0,16},{16,0},{1,17},{17,1},{2,18},{18,2},{3,19},{19,3},{4,20},{20... | collective-permute-start | bytes 3538952 | tf_op jit(solution)/shard_map/ppermute | solution.py:629
  316.7 26.6 %collective-permute-start.28 = (bf16[512,1152]{1,0:T(8,128)(2,1)S(1)}, bf16[512,1152]{1,0:T(8,128)(2,1)S(1)}, u32[]{:S(2)}, u32[]{:S(2)}) collective-permute-start(bf16[512,1152]{1,0:T(8,128)(2,1)S(1)} %pad_maximum_fusion.5), channel_id=1, source_target_pairs={{0,1},{1,0},{2,3},{3,2},{4,5},{5,4},{6,7},{7,6},{8,9},{9,8},{10,11... | collective-permute-start | bytes 3538952 | tf_op jit(solution)/shard_map/ppermute | solution.py:629
  317.4 25.9 %collective-permute-start.29 = (bf16[512,1152]{1,0:T(8,128)(2,1)S(1)}, bf16[512,1152]{1,0:T(8,128)(2,1)S(1)}, u32[]{:S(2)}, u32[]{:S(2)}) collective-permute-start(bf16[512,1152]{1,0:T(8,128)(2,1)S(1)} %pad_maximum_fusion.6), channel_id=1, source_target_pairs={{0,16},{16,0},{1,17},{17,1},{2,18},{18,2},{3,19},{19,3},{4,20},{20... | collective-permute-start | bytes 3538952 | tf_op jit(solution)/shard_map/ppermute | solution.py:629
  369.5 29.1 %collective-permute-start.30 = (bf16[512,1152]{1,0:T(8,128)(2,1)}, bf16[512,1152]{1,0:T(8,128)(2,1)S(1)}, u32[]{:S(2)}, u32[]{:S(2)}) collective-permute-start(bf16[512,1152]{1,0:T(8,128)(2,1)} %get-tuple-element.243), channel_id=1, source_target_pairs={{0,1},{1,0},{2,3},{3,2},{4,5},{5,4},{6,7},{7,6},{8,9},{9,8},{10,11... | collective-permute-start | bytes 3538952 | tf_op jit(solution)/shard_map/ppermute | solution.py:629
  370.9 27.7 %collective-permute-start.31 = (bf16[512,1152]{1,0:T(8,128)(2,1)}, bf16[512,1152]{1,0:T(8,128)(2,1)S(1)}, u32[]{:S(2)}, u32[]{:S(2)}) collective-permute-start(bf16[512,1152]{1,0:T(8,128)(2,1)} %get-tuple-element.244), channel_id=1, source_target_pairs={{0,16},{16,0},{1,17},{17,1},{2,18},{18,2},{3,19},{19,3},{4,20},{20... | collective-permute-start | bytes 3538952 | tf_op jit(solution)/shard_map/ppermute | solution.py:629
  424.6 160.1 %reduce-scatter.5.cloned.1.call-start = ((), (), s32[]{:S(2)}) async-start(), calls=%async_computation.8 | async-start | bytes 2580480 | tf_op jit(solution)/shard_map/reduce_scatter | solution.py:715
  424.7 29.9 %collective-permute-start.38 = (bf16[896,1152]{1,0:T(8,128)(2,1)}, bf16[896,1152]{1,0:T(8,128)(2,1)}, u32[]{:S(2)}, u32[]{:S(2)}) collective-permute-start(bf16[896,1152]{1,0:T(8,128)(2,1)} %get-tuple-element.283), channel_id=1, source_target_pairs={{0,8},{8,0},{1,9},{9,1},{2,10},{10,2},{3,11},{11,3},{4,12},{12,4},... | collective-permute-start | bytes 6193160 | tf_op jit(solution)/shard_map/ppermute | solution.py:629
  453.9 24.1 %collective-permute-start.36 = (bf16[4,128,512]{2,1,0:T(8,128)(2,1)}, bf16[4,128,512]{2,1,0:T(8,128)(2,1)}, u32[]{:S(2)}, u32[]{:S(2)}) collective-permute-start(bf16[4,128,512]{2,1,0:T(8,128)(2,1)} %get-tuple-element.276), channel_id=1, source_target_pairs={{0,1},{1,0},{2,3},{3,2},{4,5},{5,4},{6,7},{7,6},{8,9},{9,8},{10,11... | collective-permute-start | bytes 1572872 | tf_op jit(solution)/shard_map/ppermute | solution.py:629
  479.2 30.6 %collective-permute-start.41 = (bf16[2,4,72,1152]{3,2,1,0:T(8,128)(2,1)}, bf16[2,4,72,1152]{3,2,1,0:T(8,128)(2,1)}, u32[]{:S(2)}, u32[]{:S(2)}) collective-permute-start(bf16[2,4,72,1152]{3,2,1,0:T(8,128)(2,1)} %dynamic-slice_bitcast_fusion), channel_id=1, source_target_pairs={{0,16},{16,0},{1,17},{17,1},{2,18},{18,2},{3,19},{19,3},{4,20},{20... | collective-permute-start | bytes 3981320 | tf_op jit(solution)/shard_map/ppermute | solution.py:629
  483.6 36.8 %collective-permute-start.39 = (bf16[4,128,512]{2,1,0:T(8,128)(2,1)S(1)}, bf16[4,128,512]{2,1,0:T(8,128)(2,1)S(1)}, u32[]{:S(2)}, u32[]{:S(2)}) collective-permute-start(bf16[4,128,512]{2,1,0:T(8,128)(2,1)S(1)} %get-tuple-element.340), channel_id=1, source_target_pairs={{4,0},{6,2},{5,1},{7,3},{12,8},{14,10},{13,9},{15,11},{20,16},{22,... | collective-permute-start | bytes 1572872 | tf_op jit(solution)/shard_map/ppermute | solution.py:634
  484.8 35.5 %collective-permute-start.40 = (bf16[4,128,512]{2,1,0:T(8,128)(2,1)S(1)}, bf16[4,128,512]{2,1,0:T(8,128)(2,1)}, u32[]{:S(2)}, u32[]{:S(2)}) collective-permute-start(bf16[4,128,512]{2,1,0:T(8,128)(2,1)S(1)} %get-tuple-element.339), channel_id=1, source_target_pairs={{2,0},{4,2},{6,4},{3,1},{5,3},{7,5},{10,8},{12,10},{14,12},{11,9},... | collective-permute-start | bytes 1572872 | tf_op jit(solution)/shard_map/ppermute | solution.py:634
  (75 other events, 830.8 us)
Sparse Core Ops, SparseCore 0:
  9.7 62.1 all-gather.4
  111.0 90.6 all-gather.2
  424.7 82.5 reduce-scatter.2
  520.5 60.3 reduce-scatter.4
